TPU v7x, 32 devices: a whole 2x2x4 slice. The times are simulated.
32 devices in a mesh: req: 2 (over y), patch: 16 (over z, x, core).
Axes of the slice: x: 2, y: 2, z: 4, core: 2. Of those that a mesh axis runs over, the one named last changes fastest.
Arguments:
- queries: bfloat16 [8, 128, 4096], P('req', 'patch'), parts along dimension 0, may hold values from -5 to 5
- keys: bfloat16 [8, 128, 4096], P('req', 'patch'), parts along dimension 0, may hold values from -5 to 5
- values: bfloat16 [8, 128, 4096], P('req', 'patch'), parts along dimension 0, may hold values from -6 to 6
- q_gain: float32 [4096], replicated, may hold values from 1.5 to 6
- k_gain: float32 [4096], replicated, may hold values from 1.5 to 6
- stale_cache: bfloat16 [256, 128, 256], P(('req', 'patch')), parts along dimension 0, may hold values from -8 to 8
- coords: int32 [3, 128], P(None, 'patch'), may hold values from 0 to 63
Outputs:
- attended: bfloat16 [8, 128, 4096], P('req', 'patch'), parts along dimension 0
- next_cache: bfloat16 [256, 128, 256], P(('req', 'patch')), parts along dimension 0
There are 2 independent parts, one for each index of `req`. A program takes and returns all parts, laid end to end along the dimension named above; an argument that names none is the same for every part. Nothing has to cross between parts.
All inputs are finite; a program needn't handle non-finite values.
Results may differ from a plain program's by a relative error of at most 0.012.
The roundings to bfloat16 on the way count: a program that leaves them out, or rounds other values in their place, can miss the bound.
Values may be sent and summed in bfloat16 or wider, within the bound.
No kernel may reach another device: no remote copies, remote signals or barrier semaphores. Data moves between devices by JAX's collectives and lax.ppermute only.
A program may use at most 128 MiB of HBM per device.

v0:
```python
import math

import jax
import jax.numpy as jnp
from jax import lax
from jax.sharding import PartitionSpec as P

DH = 128


def rotate(field, coords):
    videos, rows, width = field.shape
    half = DH // 2
    side = DH // 6
    first = half - 2 * side
    place = coords.astype(jnp.float32)

    def freqs(count):
        return 10000.0 ** (-jnp.arange(count, dtype=jnp.float32) / count)

    angle = jnp.concatenate(
        [
            place[0][:, None] * freqs(first),
            place[1][:, None] * freqs(side),
            place[2][:, None] * freqs(side),
        ],
        axis=1,
    )
    cosine = jnp.cos(angle)[None, :, None, :]
    sine = jnp.sin(angle)[None, :, None, :]
    split = field.reshape(videos, rows, width // DH, half, 2)
    real_part = split[..., 0]
    imag_part = split[..., 1]
    turned = jnp.stack(
        [real_part * cosine - imag_part * sine, real_part * sine + imag_part * cosine], axis=-1
    )
    return turned.reshape(videos, rows, width)


def prepare(field, gain, coords):
    wide = field.astype(jnp.float32)
    meansq = jnp.mean(wide * wide, axis=-1, keepdims=True)
    normed = wide * lax.rsqrt(meansq + 1e-06) * gain
    return rotate(normed, coords).astype(jnp.bfloat16)


def local(queries, keys, values, q_gain, k_gain, stale_cache, coords):
    videos, tok_rows, width = queries.shape
    heads = width // DH
    scale = 1.0 / math.sqrt(DH)
    qn = prepare(queries, q_gain, coords)
    kn = prepare(keys, k_gain, coords)
    query_tokens = jnp.transpose(qn, (1, 0, 2)).reshape(tok_rows, videos * heads, DH)
    fresh_four = jnp.concatenate(
        [kn.reshape(videos, tok_rows, heads, DH), values.reshape(videos, tok_rows, heads, DH)],
        axis=-1,
    )
    fresh_tokens = jnp.transpose(fresh_four, (1, 0, 2, 3)).reshape(tok_rows, videos * heads, 2 * DH)
    query_heads = lax.all_to_all(query_tokens, "patch", split_axis=1, concat_axis=0, tiled=True)
    fresh_heads = lax.all_to_all(fresh_tokens, "patch", split_axis=1, concat_axis=0, tiled=True)
    next_cache = jnp.transpose(fresh_heads, (1, 0, 2))
    total_rows, pairs_here, depth = query_heads.shape
    block = 512 if total_rows % 512 == 0 else total_rows
    starts = jnp.arange(total_rows // block, dtype=jnp.int32) * block
    key_owner = jnp.arange(total_rows) // tok_rows
    stale_keys = stale_cache[:, :, :DH]
    stale_values = stale_cache[:, :, DH:]

    def own_patch(start):
        row_owner = (start + jnp.arange(block)) // tok_rows
        return (row_owner[:, None] == key_owner[None, :])[None]

    def stacked_rows(stacked):
        return stacked.reshape((total_rows,) + stacked.shape[2:])

    def stale_block(start):
        query_rows = lax.dynamic_slice_in_dim(query_heads, start, block, 0)
        scores = (
            jnp.einsum("qpd,pkd->pqk", query_rows, stale_keys, preferred_element_type=jnp.float32)
            * scale
        )
        scores = jnp.where(own_patch(start), -jnp.inf, scores)
        top = jnp.max(scores, axis=-1)
        weights = jnp.exp(scores - top[..., None])
        total = jnp.sum(weights, axis=-1)
        summed = jnp.einsum(
            "pqk,pkd->qpd",
            weights.astype(jnp.bfloat16),
            stale_values,
            preferred_element_type=jnp.float32,
        )
        return (summed, top.T, total.T)

    remote_sum, remote_top, remote_total = lax.map(stale_block, starts)
    remote_sum = stacked_rows(remote_sum)
    remote_top = stacked_rows(remote_top)
    remote_total = stacked_rows(remote_total)
    back_sum, back_top, back_total = (
        lax.all_to_all(remote_sum, "patch", split_axis=0, concat_axis=1, tiled=True),
        lax.all_to_all(remote_top, "patch", split_axis=0, concat_axis=1, tiled=True),
        lax.all_to_all(remote_total, "patch", split_axis=0, concat_axis=1, tiled=True),
    )
    back_sum = jnp.transpose(back_sum.reshape(tok_rows, videos, heads, DH), (1, 0, 2, 3))
    back_top = jnp.transpose(back_top.reshape(tok_rows, videos, heads), (1, 0, 2))
    back_total = jnp.transpose(back_total.reshape(tok_rows, videos, heads), (1, 0, 2))
    query_four = qn.reshape(videos, tok_rows, heads, DH)
    key_four = kn.reshape(videos, tok_rows, heads, DH)
    value_four = values.reshape(videos, tok_rows, heads, DH)
    local_scores = (
        jnp.einsum("vqhd,vkhd->vqhk", query_four, key_four, preferred_element_type=jnp.float32)
        * scale
    )
    local_top = jnp.max(local_scores, axis=-1)
    local_weights = jnp.exp(local_scores - local_top[..., None])
    local_total = jnp.sum(local_weights, axis=-1)
    local_sum = jnp.einsum(
        "vqhk,vkhd->vqhd",
        local_weights.astype(jnp.bfloat16),
        value_four,
        preferred_element_type=jnp.float32,
    )
    joint_top = jnp.maximum(local_top, back_top)
    local_factor = jnp.exp(local_top - joint_top)
    back_factor = jnp.exp(back_top - joint_top)
    joint_sum = local_sum * local_factor[..., None] + back_sum * back_factor[..., None]
    joint_total = local_total * local_factor + back_total * back_factor
    attended = (
        (joint_sum / joint_total[..., None]).astype(jnp.bfloat16).reshape(videos, tok_rows, width)
    )
    return (attended, next_cache)


def solution(mesh):
    in_specs = (
        P("req", "patch", None),
        P("req", "patch", None),
        P("req", "patch", None),
        P(),
        P(),
        P(("req", "patch"), None, None),
        P(None, "patch"),
    )
    out_specs = (P("req", "patch", None), P(("req", "patch"), None, None))
    return jax.shard_map(local, mesh=mesh, in_specs=in_specs, out_specs=out_specs, check_vma=False)
```

profile of v0, /device:TPU:0, one launch (start us, length us, event | category | flops | bytes accessed | tf_op | source)
XLA Modules:
  0.0 207.8 jit_solution(2800768118660183510)
XLA Ops:
  0.7 0.7 convert_element_type.36
  1.4 0.1 broadcast_multiply_fusion.2
  1.4 0.1 broadcast_multiply_fusion.1
  1.5 0.1 fusion.28
  1.6 0.1 copy.111
  1.7 0.1 copy.112
  1.8 1.1 fusion.7
  2.9 1.1 fusion.8
  4.0 0.0 copy-start.3
  4.0 0.0 copy-start.5
  4.0 4.9 %copy.110 = f32[4,8,4096]{1,2,0:T(8,128)} copy(f32[4,8,4096]{2,1,0:T(8,128)S(1)} %fusion.8) | data formatting | bytes 1048576 | tf_op jit(solution)/shard_map/mul | solution.py:43
  8.9 0.1 fusion.9
  9.0 0.1 fusion.10
  9.1 4.9 %copy.118 = f32[4,8,4096]{1,2,0:T(8,128)} copy(f32[4,8,4096]{2,1,0:T(8,128)S(1)} %fusion.10) | data formatting | bytes 1048576 | tf_op jit(solution)/shard_map/mul | solution.py:43
  14.0 37.9 %slice_multiply_fusion.1 = (f32[4,8,32,64,1]{1,4,3,2,0:T(1,128)}, f32[4,8,32,64,1]{1,4,3,2,0:T(1,128)}, f32[4,8,32,64,1]{1,4,3,2,0:T(1,128)}, f32[4,8,32,64,1]{1...) fusion(f32[4,8,32,64,2]{1,4,3,2,0:T(2,128)} %bitcast.97, ...), kind=kLoop, calls=%fused_computation.1 | loop fusion | flops 524288 | bytes 3149824 | tf_op jit(solution)/shard_map/mul | solution.py:35
  51.9 8.9 %copy.119 = f32[4,8,32,64,1]{3,2,4,1,0:T(8,128)S(1)} copy(f32[4,8,32,64,1]{1,4,3,2,0:T(1,128)} %get-tuple-element.46) | data formatting | bytes 524288 | tf_op jit(solution)/shard_map/mul | solution.py:35
  60.8 8.9 %copy.120 = f32[4,8,32,64,1]{3,2,4,1,0:T(8,128)S(1)} copy(f32[4,8,32,64,1]{1,4,3,2,0:T(1,128)} %get-tuple-element.39) | data formatting | bytes 524288 | tf_op jit(solution)/shard_map/mul | solution.py:35
  69.6 8.9 %copy.121 = f32[4,8,32,64,1]{3,2,4,1,0:T(8,128)S(1)} copy(f32[4,8,32,64,1]{1,4,3,2,0:T(1,128)} %get-tuple-element.40) | data formatting | bytes 524288 | tf_op jit(solution)/shard_map/mul | solution.py:35
  78.5 8.9 %copy.122 = f32[4,8,32,64,1]{3,2,4,1,0:T(8,128)S(1)} copy(f32[4,8,32,64,1]{1,4,3,2,0:T(1,128)} %get-tuple-element.45) | data formatting | bytes 524288 | tf_op jit(solution)/shard_map/mul | solution.py:35
  87.4 0.1 sub.45
  87.5 0.1 add.54
  87.6 0.1 maximum_convert_fusion
  87.7 0.0 copy-start
  87.7 7.4 %copy.128 = bf16[4,8,32,64,2]{1,4,3,2,0:T(2,128)(2,1)} copy(bf16[4,8,32,64,2]{3,2,4,1,0:T(8,128)(2,1)S(1)} %maximum_convert_fusion) | data formatting | bytes 524288 | tf_op jit(solution)/shard_map/convert_element_type | solution.py:44
  95.1 4.2 %copy.130 = bf16[8,128,128]{2,0,1:T(8,128)(2,1)} copy(bf16[8,128,128]{0,2,1:T(8,128)(2,1)} %bitcast.98) | data formatting | bytes 524288 | tf_op jit(solution)/shard_map/reshape | solution.py:53
  99.3 7.4 %all-to-all-start = ((bf16[8,128,128]{2,0,1:T(8,128)(2,1)}), bf16[8,128,128]{2,0,1:T(8,128)(2,1)S(1)}, u32[]{:S(2)}, u32[]{:S(2)}) async-start(bf16[8,128,128]{2,0,1:T(8,128)(2,1)} %copy.130), calls=%async_computation | async-start | bytes 524288 | tf_op jit(solution)/shard_map/all_to_all | solution.py:59
  106.6 8.9 %copy.113 = f32[4,8,32,64,1]{3,2,4,1,0:T(8,128)S(1)} copy(f32[4,8,32,64,1]{1,4,3,2,0:T(1,128)} %get-tuple-element.47) | data formatting | bytes 524288 | tf_op jit(solution)/shard_map/mul | solution.py:35
  115.5 8.9 %copy.114 = f32[4,8,32,64,1]{3,2,4,1,0:T(8,128)S(1)} copy(f32[4,8,32,64,1]{1,4,3,2,0:T(1,128)} %get-tuple-element.50) | data formatting | bytes 524288 | tf_op jit(solution)/shard_map/mul | solution.py:35
  124.4 8.9 %copy.115 = f32[4,8,32,64,1]{3,2,4,1,0:T(8,128)S(1)} copy(f32[4,8,32,64,1]{1,4,3,2,0:T(1,128)} %get-tuple-element.49) | data formatting | bytes 524288 | tf_op jit(solution)/shard_map/mul | solution.py:35
  133.2 8.9 %copy.116 = f32[4,8,32,64,1]{3,2,4,1,0:T(8,128)S(1)} copy(f32[4,8,32,64,1]{1,4,3,2,0:T(1,128)} %get-tuple-element.48) | data formatting | bytes 524288 | tf_op jit(solution)/shard_map/mul | solution.py:35
  142.1 0.1 broadcast_compare_fusion
  142.2 0.2 add_convert_fusion
  142.4 0.0 all-to-all-done
  142.5 1.3 fusion.31
  143.7 0.8 copy-done.2
  144.5 0.1 fusion.13
  144.6 0.1 all_to_all.71
  144.7 0.7 copy.139
  145.4 6.0 %all-to-all-start.3 = ((f32[16,8,8]{1,2,0:T(8,128)}), f32[16,8,8]{1,2,0:T(8,128)S(1)}, u32[]{:S(2)}, u32[]{:S(2)}) async-start(f32[16,8,8]{1,2,0:T(8,128)} %copy.139), calls=%async_computation.3 | async-start | bytes 131072 | tf_op jit(solution)/shard_map/all_to_all | solution.py:101
  151.4 0.1 pad_maximum_fusion
  151.5 0.8 copy.117
  152.4 1.5 copy.142
  153.8 0.1 all_to_all.65
  153.9 0.6 copy.133
  154.5 3.7 %all-to-all-done.3 = f32[16,8,8]{1,2,0:T(8,128)S(1)} async-done(((f32[16,8,8]{1,2,0:T(8,128)}), f32[16,8,8]{1,2,0:T(8,128)S(1)}, u32[]{:S(2)}, u32[]{:S(2)}) %all-to-all-start.3) | async-done | bytes 4128 | tf_op jit(solution)/shard_map/all_to_all | solution.py:101
  158.3 3.5 %all-to-all-start.1 = ((f32[16,8,8]{1,2,0:T(8,128)}), f32[16,8,8]{1,2,0:T(8,128)S(1)}, u32[]{:S(2)}, u32[]{:S(2)}) async-start(f32[16,8,8]{1,2,0:T(8,128)} %copy.133), calls=%async_computation.1 | async-start | bytes 131072 | tf_op jit(solution)/shard_map/all_to_all | solution.py:100
  161.8 1.6 maximum_bitcast_fusion
  163.4 2.1 %copy.155 = bf16[8,4,32,256]{3,0,2,1:T(8,128)(2,1)} copy(bf16[8,4,32,256]{2,0,3,1:T(8,128)(2,1)S(1)} %maximum_bitcast_fusion) | data formatting | bytes 1048576 | tf_op jit(solution)/shard_map/reshape | solution.py:58
  165.5 3.1 %all-to-all-done.1 = f32[16,8,8]{1,2,0:T(8,128)S(1)} async-done(((f32[16,8,8]{1,2,0:T(8,128)}), f32[16,8,8]{1,2,0:T(8,128)S(1)}, u32[]{:S(2)}, u32[]{:S(2)}) %all-to-all-start.1) | async-done | bytes 4128 | tf_op jit(solution)/shard_map/all_to_all | solution.py:100
  168.6 3.6 %all-to-all-start.4 = ((bf16[8,128,256]{2,0,1:T(8,128)(2,1)}), bf16[8,128,256]{2,0,1:T(8,128)(2,1)S(1)}, u32[]{:S(2)}, u32[]{:S(2)}) async-start(bf16[8,128,256]{2,0,1:T(8,128)(2,1)} %bitcast.102), calls=%async_computation.4 | async-start | bytes 1048576 | tf_op jit(solution)/shard_map/all_to_all | solution.py:60
  172.2 1.4 convolution_bitcast_fusion
  173.6 1.1 copy.137
  174.7 11.9 %all-to-all-done.4 = bf16[8,128,256]{2,0,1:T(8,128)(2,1)S(1)} async-done(((bf16[8,128,256]{2,0,1:T(8,128)(2,1)}), bf16[8,128,256]{2,0,1:T(8,128)(2,1)S(1)}, u32[]{:S(2)}, u32[]{:S(2)}) %all-to-all-start.4) | async-done | bytes 524320 | tf_op jit(solution)/shard_map/all_to_all | solution.py:60
  186.6 4.4 %all-to-all-start.2 = ((f32[128,8,128]{2,1,0:T(8,128)}), f32[128,8,128]{2,1,0:T(8,128)}, u32[]{:S(2)}, u32[]{:S(2)}) async-start(f32[128,8,128]{2,1,0:T(8,128)} %copy.137), calls=%async_computation.2 | async-start | bytes 1048576 | tf_op jit(solution)/shard_map/all_to_all | solution.py:99
  191.1 0.8 copy.123
  191.9 0.6 copy.124
  192.5 0.6 copy.125
  193.2 0.3 fusion.32
  193.5 0.2 fusion.11
  193.8 0.1 copy.146
  193.9 0.9 copy.147
  194.8 10.6 %all-to-all-done.2 = f32[128,8,128]{2,1,0:T(8,128)} async-done(((f32[128,8,128]{2,1,0:T(8,128)}), f32[128,8,128]{2,1,0:T(8,128)}, u32[]{:S(2)}, u32[]{:S(2)}) %all-to-all-start.2) | async-done | bytes 524320 | tf_op jit(solution)/shard_map/all_to_all | solution.py:99
  205.3 1.1 copy.138
  206.5 1.3 fusion.6
  (16 shorter events, 0.1 us)
Async XLA Ops:
  4.0 4.9 %copy-start.3 = (bf16[4,8,4096]{2,1,0:T(8,128)(2,1)S(1)}, bf16[4,8,4096]{2,1,0:T(8,128)(2,1)}, u32[]{:S(2)}) copy-start(bf16[4,8,4096]{2,1,0:T(8,128)(2,1)} %param.7) | copy-start | bytes 786436
  4.0 5.0 %copy-start.5 = (f32[4096]{0:T(1024)S(1)}, f32[4096]{0:T(1024)}, u32[]{:S(2)}) copy-start(f32[4096]{0:T(1024)} %param.10) | copy-start | bytes 49156
  87.7 11.6 %copy-start = (bf16[4,8,32,64,2]{3,2,4,1,0:T(8,128)(2,1)}, bf16[4,8,32,64,2]{3,2,4,1,0:T(8,128)(2,1)S(1)}, u32[]{:S(2)}) copy-start(bf16[4,8,32,64,2]{3,2,4,1,0:T(8,128)(2,1)S(1)} %maximum_convert_fusion) | copy-start | bytes 786436
  99.3 43.2 %all-to-all-start = ((bf16[8,128,128]{2,0,1:T(8,128)(2,1)}), bf16[8,128,128]{2,0,1:T(8,128)(2,1)S(1)}, u32[]{:S(2)}, u32[]{:S(2)}) async-start(bf16[8,128,128]{2,0,1:T(8,128)(2,1)} %copy.130), calls=%async_computation | async-start | bytes 524288 | tf_op jit(solution)/shard_map/all_to_all | solution.py:59
  142.1 10.2 %copy-start.4 = (bf16[4,8,4096]{2,1,0:T(8,128)(2,1)S(1)}, bf16[4,8,4096]{2,1,0:T(8,128)(2,1)}, u32[]{:S(2)}) copy-start(bf16[4,8,4096]{2,1,0:T(8,128)(2,1)} %param.9) | copy-start | bytes 786436
  143.7 0.8 copy-start.2
  145.4 12.9 %all-to-all-start.3 = ((f32[16,8,8]{1,2,0:T(8,128)}), f32[16,8,8]{1,2,0:T(8,128)S(1)}, u32[]{:S(2)}, u32[]{:S(2)}) async-start(f32[16,8,8]{1,2,0:T(8,128)} %copy.139), calls=%async_computation.3 | async-start | bytes 131072 | tf_op jit(solution)/shard_map/all_to_all | solution.py:101
  158.3 10.4 %all-to-all-start.1 = ((f32[16,8,8]{1,2,0:T(8,128)}), f32[16,8,8]{1,2,0:T(8,128)S(1)}, u32[]{:S(2)}, u32[]{:S(2)}) async-start(f32[16,8,8]{1,2,0:T(8,128)} %copy.133), calls=%async_computation.1 | async-start | bytes 131072 | tf_op jit(solution)/shard_map/all_to_all | solution.py:100
  165.5 25.6 %copy-start.1 = (bf16[4,8,32,64,2]{3,2,4,1,0:T(8,128)(2,1)S(1)}, bf16[4,8,32,64,2]{3,2,4,1,0:T(8,128)(2,1)}, u32[]{:S(2)}) copy-start(bf16[4,8,32,64,2]{3,2,4,1,0:T(8,128)(2,1)} %copy-done) | copy-start | bytes 786436
  168.6 18.0 %all-to-all-start.4 = ((bf16[8,128,256]{2,0,1:T(8,128)(2,1)}), bf16[8,128,256]{2,0,1:T(8,128)(2,1)S(1)}, u32[]{:S(2)}, u32[]{:S(2)}) async-start(bf16[8,128,256]{2,0,1:T(8,128)(2,1)} %bitcast.102), calls=%async_computation.4 | async-start | bytes 1048576 | tf_op jit(solution)/shard_map/all_to_all | solution.py:60
  186.6 18.7 %all-to-all-start.2 = ((f32[128,8,128]{2,1,0:T(8,128)}), f32[128,8,128]{2,1,0:T(8,128)}, u32[]{:S(2)}, u32[]{:S(2)}) async-start(f32[128,8,128]{2,1,0:T(8,128)} %copy.137), calls=%async_computation.2 | async-start | bytes 1048576 | tf_op jit(solution)/shard_map/all_to_all | solution.py:99
where the time goes:
time: 210 us; the launch traced here: 208 us
  local copies, waits for them, and re-layouts  104 us (50%)
  other arithmetic  44 us (21%)
  waiting for transfers between devices  29.3 us (14%)
  starting transfers between devices  24.8 us (12%)
  matrix products  4.31 us (2%)
    mul x1, other arithmetic, rotate(): imag_part * sine  37.9 us
    mul x2, local copies, waits for them, and re-layouts, rotate(): imag_part * cosine  17.7 us
    mul x2, local copies, waits for them, and re-layouts, rotate(): real_part * sine + imag_part * cosine  17.7 us
    mul x2, local copies, waits for them, and re-layouts, rotate(): imag_part * sine  17.7 us
    mul x2, local copies, waits for them, and re-layouts, rotate(): real_part * cosine - imag_part * sine  17.7 us
    all_to_all x1, waiting for transfers between devices, local(): lax.all_to_all(fresh_tokens, 'patch', split_axis=1, concat_axis=0, tiled=...  11.9 us
    all_to_all x1, waiting for transfers between devices, local(): lax.all_to_all(remote_sum, 'patch', split_axis=0, concat_axis=1, tiled=True)  10.6 us
    mul x2, local copies, waits for them, and re-layouts, prepare(): normed = wide * lax.rsqrt(meansq + 1e-06) * gain  9.74 us
  transfers between devices with their start and end apart: 5, of which 4 were waited for; matrix products, arithmetic and copies ran while one was open for 23% of the time, Pallas kernels for 0%

commit v1 on v0

v1 whole, which is shorter than its diff:
```python
import functools
import math

import jax
import jax.numpy as jnp
from jax import lax
from jax.experimental import pallas as pl
from jax.experimental.pallas import tpu as pltpu
from jax.sharding import PartitionSpec as P

DH = 128
VMEM = pl.BlockSpec(memory_space=pltpu.VMEM)
SMEM = pl.BlockSpec(memory_space=pltpu.SMEM)


def rope_tables(coords_ref, tok_rows):
    half = DH // 2
    side = DH // 6
    first = half - 2 * side
    shape = (tok_rows, DH)
    row = lax.broadcasted_iota(jnp.int32, shape, 0)
    lane = lax.broadcasted_iota(jnp.int32, shape, 1)
    pair = lane // 2
    axis = (pair >= first).astype(jnp.int32) + (pair >= first + side).astype(jnp.int32)
    place = jnp.zeros(shape, jnp.int32)
    for which in range(3):
        for token in range(tok_rows):
            place = jnp.where((axis == which) & (row == token), coords_ref[which, token], place)
    step = jnp.where(axis == 0, pair, jnp.where(axis == 1, pair - first, pair - first - side))
    count = jnp.where(axis == 0, float(first), float(side))
    freq = jnp.exp(step.astype(jnp.float32) / count * (-math.log(10000.0)))
    angle = place.astype(jnp.float32) * freq
    sine = jnp.sin(angle)
    even = lane % 2 == 0
    return jnp.cos(angle), jnp.where(even, -sine, 0.0), jnp.where(even, 0.0, sine)


def prepare_kernel(heads_here, q_ref, k_ref, v_ref, q_gain_ref, k_gain_ref, coords_ref, out_ref):
    videos, tok_rows, width = q_ref.shape
    groups = width // (DH * heads_here)
    cosine, sine_even, sine_odd = rope_tables(coords_ref, tok_rows)
    for video in range(videos):
        for part, (ref, gain_ref) in enumerate(((q_ref, q_gain_ref), (k_ref, k_gain_ref))):
            wide = ref[video].astype(jnp.float32)
            meansq = jnp.sum(wide * wide, axis=-1, keepdims=True) * (1.0 / width)
            inverse = lax.rsqrt(meansq + 1e-06)
            for head in range(width // DH):
                here = slice(head * DH, (head + 1) * DH)
                y = ref[video, :, here].astype(jnp.float32) * inverse * gain_ref[:, here]
                turned = (
                    y * cosine
                    + pltpu.roll(y, DH - 1, 1) * sine_even
                    + pltpu.roll(y, 1, 1) * sine_odd
                )
                start = (head % heads_here * 3 + part) * DH
                out_ref[video * groups + head // heads_here, :, start : start + DH] = turned.astype(
                    jnp.bfloat16
                )
        for head in range(width // DH):
            start = (head % heads_here * 3 + 2) * DH
            out_ref[video * groups + head // heads_here, :, start : start + DH] = v_ref[
                video, :, head * DH : (head + 1) * DH
            ]


def attend_kernel(tok_rows, got_ref, stale_ref, attended_ref, cache_ref):
    pairs_here, total_rows, _ = stale_ref.shape
    scale = 1.0 / math.sqrt(DH)
    block = min(total_rows, 128)
    dims = (((1,), (1,)), ((), ()))
    for pair in range(pairs_here):
        fresh = got_ref[:, (pair * 3 + 1) * DH : (pair * 3 + 3) * DH]
        cache_ref[pair] = fresh
        stale = stale_ref[pair]
        for start in range(0, total_rows, block):
            query = got_ref[start : start + block, pair * 3 * DH : (pair * 3 + 1) * DH]
            shape = (block, total_rows)
            same = (start + lax.broadcasted_iota(jnp.int32, shape, 0)) // tok_rows == (
                lax.broadcasted_iota(jnp.int32, shape, 1) // tok_rows
            )
            fresh_scores = lax.dot_general(
                query, fresh[:, :DH], dims, preferred_element_type=jnp.float32
            )
            stale_scores = lax.dot_general(
                query, stale[:, :DH], dims, preferred_element_type=jnp.float32
            )
            scores = jnp.where(same, fresh_scores, stale_scores) * scale
            top = jnp.max(scores, axis=-1, keepdims=True)
            weights = jnp.exp(scores - top)
            total = jnp.sum(weights, axis=-1, keepdims=True)
            summed = jnp.dot(
                jnp.where(same, weights, 0.0).astype(jnp.bfloat16),
                fresh[:, DH:],
                preferred_element_type=jnp.float32,
            ) + jnp.dot(
                jnp.where(same, 0.0, weights).astype(jnp.bfloat16),
                stale[:, DH:],
                preferred_element_type=jnp.float32,
            )
            attended_ref[start : start + block, pair * DH : (pair + 1) * DH] = (
                summed / total
            ).astype(jnp.bfloat16)


def local(queries, keys, values, q_gain, k_gain, stale_cache, coords):
    videos, tok_rows, width = queries.shape
    pairs_here, total_rows, _ = stale_cache.shape
    patches = total_rows // tok_rows
    params = pltpu.CompilerParams(vmem_limit_bytes=40 * 1024 * 1024)
    sent = pl.pallas_call(
        functools.partial(prepare_kernel, pairs_here),
        out_shape=jax.ShapeDtypeStruct((patches, tok_rows, pairs_here * 3 * DH), jnp.bfloat16),
        in_specs=[VMEM] * 5 + [SMEM],
        out_specs=VMEM,
        compiler_params=params,
        name="prepare",
    )(queries, keys, values, q_gain.reshape(1, width), k_gain.reshape(1, width), coords)
    got = lax.all_to_all(sent, "patch", split_axis=0, concat_axis=0, tiled=True)
    attended, next_cache = pl.pallas_call(
        functools.partial(attend_kernel, tok_rows),
        out_shape=(
            jax.ShapeDtypeStruct((total_rows, pairs_here * DH), jnp.bfloat16),
            jax.ShapeDtypeStruct(stale_cache.shape, jnp.bfloat16),
        ),
        in_specs=[VMEM] * 2,
        out_specs=(VMEM, VMEM),
        compiler_params=params,
        name="attend",
    )(got.reshape(total_rows, pairs_here * 3 * DH), stale_cache)
    back = lax.all_to_all(
        attended.reshape(patches, tok_rows, pairs_here * DH), "patch", split_axis=0, concat_axis=0, tiled=True
    )
    attended = jnp.transpose(
        back.reshape(videos, patches // videos, tok_rows, pairs_here * DH), (0, 2, 1, 3)
    ).reshape(videos, tok_rows, width)
    return (attended, next_cache)


def solution(mesh):
    in_specs = (
        P("req", "patch", None),
        P("req", "patch", None),
        P("req", "patch", None),
        P(),
        P(),
        P(("req", "patch"), None, None),
        P(None, "patch"),
    )
    out_specs = (P("req", "patch", None), P(("req", "patch"), None, None))
    return jax.shard_map(local, mesh=mesh, in_specs=in_specs, out_specs=out_specs, check_vma=False)
```

time: 210 us -> 52.5 us (0.25)
  local copies, waits for them, and re-layouts: 104 us -> 5.67 us
  other arithmetic: 44 us -> 0 us
  blocking collectives: 0 us -> 41.3 us
  waiting for transfers between devices: 29.3 us -> 0 us
  starting transfers between devices: 24.8 us -> 0 us
  Pallas kernels: 0 us -> 4.43 us
  matrix products: 4.31 us -> 0 us
    mul x11 -> x0, local copies, waits for them, and re-layouts: 80.7 us -> none  [the longest x2 17.7 us: rotate(): imag_part * cosine]
    all_to_all x0 -> x2, blocking collectives: none -> 41.3 us  [the longest x1 27.6 us: local(): got = lax.all_to_all(sent, 'patch', split_axis=0, concat_axis=0, tiled=True)]
    mul x5 -> x0, other arithmetic: 39.2 us -> none  [the longest x1 37.9 us: rotate(): imag_part * sine]
    all_to_all x5 -> x0, waiting for transfers between devices: 29.3 us -> none  [the longest x1 11.9 us: local(): lax.all_to_all(fresh_tokens, 'patch', split_axis=1, concat_axis=0, tiled=...]
    all_to_all x5 -> x0, starting transfers between devices: 24.8 us -> none  [the longest x1 7.36 us: local(): lax.all_to_all(query_tokens, 'patch', split_axis=1, concat_axis=0, tiled=...]
    convert_element_type x4 -> x0, local copies, waits for them, and re-layouts: 9.46 us -> none  [prepare(): return rotate(normed, coords).astype(jnp.bfloat16)]
    reshape x3 -> x0, local copies, waits for them, and re-layouts: 7.76 us -> none  [the longest x1 4.21 us: local(): jnp.transpose(qn, (1, 0, 2)).reshape(tok_rows, videos * heads, DH)]
    pallas_call x0 -> x2, Pallas kernels: none -> 4.43 us  [the longest x1 2.54 us: local(): pl.pallas_call(functools.partial(attend_kernel, tok_rows), out_shape=(jax...]
  transfers between devices with their start and end apart: 5 -> 0, of which waited for: 4 -> 0; matrix products, arithmetic and copies ran while one was open for 23% -> 0% of each run, Pallas kernels for 0% -> 0%
where the time goes in v1:
time: 52.5 us; the launch traced here: 52.1 us
  blocking collectives  41.3 us (79%)
  local copies, waits for them, and re-layouts  5.67 us (11%)
  Pallas kernels  4.43 us (8%)
  between operations  0.66 us (1%)
    all_to_all x1, blocking collectives, local(): got = lax.all_to_all(sent, 'patch', split_axis=0, concat_axis=0, tiled=True)  27.6 us
    all_to_all x1, blocking collectives, local(): lax.all_to_all(attended.reshape(patches, tok_rows, pairs_here * DH), 'pat...  13.7 us
    unnamed x15, local copies, waits for them, and re-layouts  5.67 us
    pallas_call x1, Pallas kernels, local(): pl.pallas_call(functools.partial(attend_kernel, tok_rows), out_shape=(jax...  2.54 us
    pallas_call x1, Pallas kernels, local(): pl.pallas_call(functools.partial(prepare_kernel, pairs_here), out_shape=j...  1.88 us

profile of v1, /device:TPU:0, one launch (start us, length us, event | category | flops | bytes accessed | tf_op | source)
XLA Modules:
  0.0 52.1 jit_solution(12170775433607935461)
XLA Ops:
  0.6 0.0 copy-start.6
  0.6 0.7 %copy-done.6 = s32[3,8]{1,0:T(4,128)S(1)} copy-done((s32[3,8]{1,0:T(4,128)S(1)}, s32[3,8]{1,0:T(4,128)}, u32[]{:S(2)}) %copy-start.6) | copy-done | bytes 120
  1.3 0.0 copy-start.1
  1.3 0.9 %copy-done.1 = bf16[4,8,4096]{2,1,0:T(8,128)(2,1)S(1)} copy-done((bf16[4,8,4096]{2,1,0:T(8,128)(2,1)S(1)}, bf16[4,8,4096]{2,1,0:T(8,128)(2,1)}, u32[]{:S(2)}) %copy-start.1) | copy-done | bytes 262168
  2.3 0.0 copy-start.2
  2.3 0.9 %copy-done.2 = bf16[4,8,4096]{2,1,0:T(8,128)(2,1)S(1)} copy-done((bf16[4,8,4096]{2,1,0:T(8,128)(2,1)S(1)}, bf16[4,8,4096]{2,1,0:T(8,128)(2,1)}, u32[]{:S(2)}) %copy-start.2) | copy-done | bytes 262168
  3.2 0.0 copy-start.3
  3.2 0.9 %copy-done.3 = bf16[4,8,4096]{2,1,0:T(8,128)(2,1)S(1)} copy-done((bf16[4,8,4096]{2,1,0:T(8,128)(2,1)S(1)}, bf16[4,8,4096]{2,1,0:T(8,128)(2,1)}, u32[]{:S(2)}) %copy-start.3) | copy-done | bytes 262168
  4.2 0.0 copy-start.4
  4.2 0.7 %copy-done.4 = f32[4096]{0:T(1024)S(1)} copy-done((f32[4096]{0:T(1024)S(1)}, f32[4096]{0:T(1024)}, u32[]{:S(2)}) %copy-start.4) | copy-done | bytes 16408
  4.9 0.0 copy-start.5
  4.9 0.7 %copy-done.5 = f32[4096]{0:T(1024)S(1)} copy-done((f32[4096]{0:T(1024)S(1)}, f32[4096]{0:T(1024)}, u32[]{:S(2)}) %copy-start.5) | copy-done | bytes 16408
  5.6 1.9 %prepare.1 = bf16[16,8,3072]{2,1,0:T(8,128)(2,1)S(1)} custom-call(bf16[4,8,4096]{2,1,0:T(8,128)(2,1)S(1)} %copy-done.1, bf16[4,8,4096]{2,1,0:T(8,128)(2,1)S(1)} %copy-done.2, bf16[4,8,4096]{2,1,0:T(8,128)(2,1)S(1)} %copy-done.3, f32[1,4096]{1,0:T(1,128)S(1)} %bitcast.11, f32[1,4096]{1,0:T(1,128)S(1)} %bitcast.12, s32[3,8]{1,0:T(4,128)S(1)} %copy-done.6), custom_call_target="tpu_custom_call" | custom-call | tf_op jit(solution)/shard_map/prepare/pallas_call | solution.py:110
  7.5 0.0 copy-start
  7.5 27.6 %all_to_all.10 = bf16[16,8,3072]{2,1,0:T(8,128)(2,1)S(1)} all-to-all(bf16[16,8,3072]{2,1,0:T(8,128)(2,1)S(1)} %prepare.1), channel_id=1, replica_groups=mesh['req'=2,'patch'=16] {'patch'}, dimensions={0} | all-to-all | bytes 1572864 | tf_op jit(solution)/shard_map/all_to_all | solution.py:118
  35.1 0.0 copy-done
  35.1 2.5 %attend.1 = (bf16[128,1024]{1,0:T(8,128)(2,1)S(1)}, bf16[8,128,256]{2,1,0:T(8,128)(2,1)}) custom-call(bf16[128,3072]{1,0:T(8,128)(2,1)S(1)} %bitcast.9, bf16[8,128,256]{2,1,0:T(8,128)(2,1)S(1)} %copy-done), custom_call_target="tpu_custom_call" | custom-call | tf_op jit(solution)/shard_map/attend/pallas_call | solution.py:119
  37.6 13.7 %all_to_all.11 = bf16[16,8,1024]{2,1,0:T(8,128)(2,1)S(1)} all-to-all(bf16[16,8,1024]{2,1,0:T(8,128)(2,1)S(1)} %bitcast.10), channel_id=1, replica_groups=mesh['req'=2,'patch'=16] {'patch'}, dimensions={0} | all-to-all | bytes 524288 | tf_op jit(solution)/shard_map/all_to_all | solution.py:130
  51.4 0.7 %copy.10 = bf16[4,8,4096]{2,1,0:T(8,128)(2,1)} copy(bf16[4,8,4096]{2,1,0:T(8,128)(2,1)S(1)} %bitcast.13) | data formatting | bytes 524288
Async XLA Ops:
  0.6 0.7 %copy-start.6 = (s32[3,8]{1,0:T(4,128)S(1)}, s32[3,8]{1,0:T(4,128)}, u32[]{:S(2)}) copy-start(s32[3,8]{1,0:T(4,128)} %coords_ref.1) | copy-start | bytes 292
  1.3 0.9 %copy-start.1 = (bf16[4,8,4096]{2,1,0:T(8,128)(2,1)S(1)}, bf16[4,8,4096]{2,1,0:T(8,128)(2,1)}, u32[]{:S(2)}) copy-start(bf16[4,8,4096]{2,1,0:T(8,128)(2,1)} %q_ref.1) | copy-start | bytes 786436
  2.3 0.9 %copy-start.2 = (bf16[4,8,4096]{2,1,0:T(8,128)(2,1)S(1)}, bf16[4,8,4096]{2,1,0:T(8,128)(2,1)}, u32[]{:S(2)}) copy-start(bf16[4,8,4096]{2,1,0:T(8,128)(2,1)} %k_ref.1) | copy-start | bytes 786436
  3.2 0.9 %copy-start.3 = (bf16[4,8,4096]{2,1,0:T(8,128)(2,1)S(1)}, bf16[4,8,4096]{2,1,0:T(8,128)(2,1)}, u32[]{:S(2)}) copy-start(bf16[4,8,4096]{2,1,0:T(8,128)(2,1)} %v_ref.1) | copy-start | bytes 786436
  4.2 0.7 %copy-start.4 = (f32[4096]{0:T(1024)S(1)}, f32[4096]{0:T(1024)}, u32[]{:S(2)}) copy-start(f32[4096]{0:T(1024)} %param.10) | copy-start | bytes 49156
  4.9 0.7 %copy-start.5 = (f32[4096]{0:T(1024)S(1)}, f32[4096]{0:T(1024)}, u32[]{:S(2)}) copy-start(f32[4096]{0:T(1024)} %param.11) | copy-start | bytes 49156
  7.5 27.6 %copy-start = (bf16[8,128,256]{2,1,0:T(8,128)(2,1)S(1)}, bf16[8,128,256]{2,1,0:T(8,128)(2,1)}, u32[]{:S(2)}) copy-start(bf16[8,128,256]{2,1,0:T(8,128)(2,1)} %stale_ref.1) | copy-start | bytes 1572868

commit v2 on v1

v2 whole, which is shorter than its diff:
```python
import functools
import math

import jax
import jax.numpy as jnp
from jax import lax
from jax.experimental import pallas as pl
from jax.experimental.pallas import tpu as pltpu
from jax.sharding import PartitionSpec as P

DH = 128
VMEM = pl.BlockSpec(memory_space=pltpu.VMEM)
HBM = pl.BlockSpec(memory_space=pltpu.HBM)
PARAMS = pltpu.CompilerParams(vmem_limit_bytes=48 * 1024 * 1024)


def rope_tables(coords_ref, tok_rows):
    half = DH // 2
    side = DH // 6
    first = half - 2 * side
    shape = (tok_rows, DH)
    row = lax.broadcasted_iota(jnp.int32, shape, 0)
    lane = lax.broadcasted_iota(jnp.int32, shape, 1)
    pair = lane // 2
    axis = (pair >= first).astype(jnp.int32) + (pair >= first + side).astype(jnp.int32)
    place = jnp.zeros(shape, jnp.int32)
    for which in range(3):
        for token in range(tok_rows):
            place = jnp.where((axis == which) & (row == token), coords_ref[which, token], place)
    step = jnp.where(axis == 0, pair, jnp.where(axis == 1, pair - first, pair - first - side))
    count = jnp.where(axis == 0, float(first), float(side))
    freq = jnp.exp(step.astype(jnp.float32) / count * (-math.log(10000.0)))
    angle = place.astype(jnp.float32) * freq
    sine = jnp.sin(angle)
    even = lane % 2 == 0
    return jnp.cos(angle), jnp.where(even, -sine, 0.0), jnp.where(even, 0.0, sine)


def prepare_kernel(pairs_here, patches, *refs):
    sources, outs, scratch = refs[:6], refs[6 : 6 + patches], refs[6 + patches :]
    held, inverse_ref, sems = scratch[:6], scratch[6], scratch[7]
    copies = [
        pltpu.make_async_copy(source, place, sems.at[i])
        for i, (source, place) in enumerate(zip(sources, held))
    ]
    for i in (5, 0, 3, 1, 4, 2):
        copies[i].start()
    q_ref, k_ref, v_ref, q_gain_ref, k_gain_ref, coords_ref = held
    videos, tok_rows, width = q_ref.shape
    groups = width // (DH * pairs_here)
    span = pairs_here * DH
    me = lax.axis_index("patch")
    copies[5].wait()
    cosine, sine_even, sine_odd = rope_tables(coords_ref, tok_rows)
    for part, ref in enumerate((q_ref, k_ref)):
        copies[part].wait()
        for video in range(videos):
            wide = ref[video].astype(jnp.float32)
            meansq = jnp.sum(wide * wide, axis=-1, keepdims=True) * (1.0 / width)
            inverse_ref[part, video] = jnp.broadcast_to(lax.rsqrt(meansq + 1e-06), (tok_rows, DH))
    for i in (3, 4, 2):
        copies[i].wait()
    for s in range(patches):
        target = me ^ s
        video = target // groups
        lanes = pl.ds(pl.multiple_of((target % groups) * span, DH), span)
        for part, (ref, gain_ref) in enumerate(((q_ref, q_gain_ref), (k_ref, k_gain_ref))):
            wide = ref[video, :, lanes].astype(jnp.float32)
            gain = gain_ref[:, lanes]
            inverse = inverse_ref[part, video]
            for pair in range(pairs_here):
                here = slice(pair * DH, (pair + 1) * DH)
                y = wide[:, here] * inverse * gain[:, here]
                turned = (
                    y * cosine
                    + pltpu.roll(y, DH - 1, 1) * sine_even
                    + pltpu.roll(y, 1, 1) * sine_odd
                )
                start = (pair * 3 + part) * DH
                outs[s][:, start : start + DH] = turned.astype(jnp.bfloat16)
        wide = v_ref[video, :, lanes]
        for pair in range(pairs_here):
            start = (pair * 3 + 2) * DH
            outs[s][:, start : start + DH] = wide[:, pair * DH : (pair + 1) * DH]


def rows_of(refs, start):
    rows = [ref[:, start : start + DH].astype(jnp.float32) for ref in refs]
    return jnp.concatenate(rows, axis=0).astype(jnp.bfloat16)


def attend_kernel(patches, *refs):
    got, stale_ref, outs = refs[:patches], refs[patches], refs[patches + 1 :]
    pairs_here, total_rows, _ = stale_ref.shape
    tok_rows = total_rows // patches
    scale = 1.0 / math.sqrt(DH)
    group = min(patches, max(1, 128 // tok_rows))
    block = group * tok_rows
    dims = (((1,), (1,)), ((), ()))
    me = lax.axis_index("patch")
    row = lax.broadcasted_iota(jnp.int32, (block, block), 0) // tok_rows
    same = row == lax.broadcasted_iota(jnp.int32, (block, block), 1) // tok_rows
    row = lax.broadcasted_iota(jnp.int32, (block, total_rows), 0) // tok_rows
    owner = lax.broadcasted_iota(jnp.int32, (block, total_rows), 1) // tok_rows
    for first in range(0, patches, group):
        here = got[first : first + group]
        own = ((row + first) ^ me) == owner
        for pair in range(pairs_here):
            query = rows_of(here, pair * 3 * DH)
            key = rows_of(here, (pair * 3 + 1) * DH)
            value = rows_of(here, (pair * 3 + 2) * DH)
            stale = stale_ref[pair]
            fresh_scores = lax.dot_general(query, key, dims, preferred_element_type=jnp.float32)
            stale_scores = lax.dot_general(
                query, stale[:, :DH], dims, preferred_element_type=jnp.float32
            )
            scores = jnp.concatenate(
                [
                    jnp.where(same, fresh_scores * scale, -jnp.inf),
                    jnp.where(own, -jnp.inf, stale_scores * scale),
                ],
                axis=1,
            )
            weights = jnp.exp(scores - jnp.max(scores, axis=-1, keepdims=True))
            total = jnp.sum(weights, axis=-1, keepdims=True)
            summed = jnp.dot(
                weights.astype(jnp.bfloat16),
                jnp.concatenate([value, stale[:, DH:]], axis=0),
                preferred_element_type=jnp.float32,
            )
            result = summed * (1.0 / total)
            for i in range(group):
                outs[first + i][:, pair * DH : (pair + 1) * DH] = result[
                    i * tok_rows : (i + 1) * tok_rows
                ].astype(jnp.bfloat16)


def cache_kernel(patches, *refs):
    got, out_ref = refs[:patches], refs[patches]
    me = lax.axis_index("patch")
    for s in range(patches):
        for pair in range(out_ref.shape[0]):
            start = (pair * 3 + 1) * DH
            out_ref[pair, me ^ s] = got[s][:, start : start + 2 * DH]


def gather_kernel(patches, *refs):
    back, out_ref, sem = refs[:patches], refs[patches], refs[patches + 1]
    span = back[0].shape[1]
    groups = out_ref.shape[2] // span
    me = lax.axis_index("patch")
    copies = []
    for s in range(patches):
        source = me ^ s
        lanes = pl.ds(pl.multiple_of((source % groups) * span, DH), span)
        copies.append(
            pltpu.make_async_copy(back[s], out_ref.at[source // groups, :, lanes], sem.at[s])
        )
    for copy in copies:
        copy.start()
    for copy in copies:
        copy.wait()


def exchange(arrays):
    patches = len(arrays)
    return [arrays[0]] + [
        lax.ppermute(arrays[s], "patch", [(i, i ^ s) for i in range(patches)])
        for s in range(1, patches)
    ]


def local(queries, keys, values, q_gain, k_gain, stale_cache, coords):
    videos, tok_rows, width = queries.shape
    pairs_here, total_rows, _ = stale_cache.shape
    patches = total_rows // tok_rows
    span = pairs_here * DH
    sent = pl.pallas_call(
        functools.partial(prepare_kernel, pairs_here, patches),
        out_shape=[jax.ShapeDtypeStruct((tok_rows, span * 3), jnp.bfloat16)] * patches,
        in_specs=[HBM] * 6,
        out_specs=[VMEM] * patches,
        scratch_shapes=[
            pltpu.VMEM(queries.shape, jnp.bfloat16),
            pltpu.VMEM(queries.shape, jnp.bfloat16),
            pltpu.VMEM(queries.shape, jnp.bfloat16),
            pltpu.VMEM((1, width), jnp.float32),
            pltpu.VMEM((1, width), jnp.float32),
            pltpu.SMEM(coords.shape, jnp.int32),
            pltpu.VMEM((2, videos, tok_rows, DH), jnp.float32),
            pltpu.SemaphoreType.DMA((6,)),
        ],
        compiler_params=PARAMS,
        name="prepare",
    )(queries, keys, values, q_gain.reshape(1, width), k_gain.reshape(1, width), coords)
    got = exchange(sent)
    result = pl.pallas_call(
        functools.partial(attend_kernel, patches),
        out_shape=[jax.ShapeDtypeStruct((tok_rows, span), jnp.bfloat16)] * patches,
        in_specs=[VMEM] * (patches + 1),
        out_specs=[VMEM] * patches,
        compiler_params=PARAMS,
        name="attend",
    )(*got, stale_cache)
    back = exchange(result)
    next_cache = pl.pallas_call(
        functools.partial(cache_kernel, patches),
        out_shape=jax.ShapeDtypeStruct((pairs_here, patches, tok_rows, 2 * DH), jnp.bfloat16),
        in_specs=[VMEM] * patches,
        out_specs=VMEM,
        compiler_params=PARAMS,
        cost_estimate=pl.CostEstimate(flops=0, bytes_accessed=stale_cache.size * 4, transcendentals=0),
        name="cache",
    )(*got)
    attended = pl.pallas_call(
        functools.partial(gather_kernel, patches),
        out_shape=jax.ShapeDtypeStruct(queries.shape, jnp.bfloat16),
        in_specs=[VMEM] * patches,
        out_specs=HBM,
        scratch_shapes=[pltpu.SemaphoreType.DMA((patches,))],
        compiler_params=PARAMS,
        name="gather",
    )(*back)
    return (attended, next_cache.reshape(stale_cache.shape))


def solution(mesh):
    in_specs = (
        P("req", "patch", None),
        P("req", "patch", None),
        P("req", "patch", None),
        P(),
        P(),
        P(("req", "patch"), None, None),
        P(None, "patch"),
    )
    out_specs = (P("req", "patch", None), P(("req", "patch"), None, None))
    return jax.shard_map(local, mesh=mesh, in_specs=in_specs, out_specs=out_specs, check_vma=False)
```

time: 52.5 us -> 64.8 us (1.23)
  starting transfers between devices: 0 us -> 45.7 us
  blocking collectives: 41.3 us -> 0 us
  waiting for transfers between devices: 0 us -> 7.61 us
  Pallas kernels: 4.43 us -> 5.35 us
  local copies, waits for them, and re-layouts: 5.67 us -> 5.02 us
    ppermute x0 -> x30, starting transfers between devices: none -> 45.7 us  [exchange(): lax.ppermute(arrays[s], 'patch', [(i, i ^ s) for i in range(patches)])]
    all_to_all x2 -> x0, blocking collectives: 41.3 us -> none  [the longest x1 27.6 us: local(): got = lax.all_to_all(sent, 'patch', split_axis=0, concat_axis=0, tiled=True)]
    ppermute x0 -> x30, waiting for transfers between devices: none -> 7.61 us  [exchange(): lax.ppermute(arrays[s], 'patch', [(i, i ^ s) for i in range(patches)])]
    pallas_call x2 -> x4, Pallas kernels: 4.43 us -> 5.35 us  [the longest x1 2.08 us: local(): pl.pallas_call(functools.partial(attend_kernel, patches), out_shape=[jax....]
    unnamed x15 -> x14, local copies, waits for them, and re-layouts: 5.67 us -> 5.02 us
  transfers between devices with their start and end apart: 0 -> 30, of which waited for: 0 -> 3; matrix products, arithmetic and copies ran while one was open for 0% -> 0% of each run, Pallas kernels for 0% -> 1%
where the time goes in v2:
time: 64.8 us; the launch traced here: 64.4 us
  starting transfers between devices  45.7 us (71%)
  waiting for transfers between devices  7.61 us (12%)
  Pallas kernels  5.35 us (8%)
  local copies, waits for them, and re-layouts  5.02 us (8%)
  between operations  0.71 us (1%)
    ppermute x30, starting transfers between devices, exchange(): lax.ppermute(arrays[s], 'patch', [(i, i ^ s) for i in range(patches)])  45.7 us
    ppermute x30, waiting for transfers between devices, exchange(): lax.ppermute(arrays[s], 'patch', [(i, i ^ s) for i in range(patches)])  7.61 us
    unnamed x14, local copies, waits for them, and re-layouts  5.02 us
    pallas_call x1, Pallas kernels, local(): pl.pallas_call(functools.partial(attend_kernel, patches), out_shape=[jax....  2.08 us
    pallas_call x1, Pallas kernels, local(): pl.pallas_call(functools.partial(prepare_kernel, pairs_here, patches), ou...  1.61 us
  transfers between devices with their start and end apart: 30, of which 3 were waited for; matrix products, arithmetic and copies ran while one was open for 0% of the time, Pallas kernels for 1%

profile of v2, /device:TPU:0, one launch (start us, length us, event | category | flops | bytes accessed | tf_op | source)
XLA Modules:
  0.0 64.4 jit_solution(14801933676706372049)
XLA Ops:
  0.7 1.0 %copy-done.1 = bf16[4,8,4096]{2,1,0:T(8,128)(2,1)S(1)} copy-done((bf16[4,8,4096]{2,1,0:T(8,128)(2,1)S(1)}, bf16[4,8,4096]{2,1,0:T(8,128)(2,1)}, u32[]{:S(2)}) %copy-start.1) | copy-done | bytes 262168
  1.7 0.9 %copy-done.2 = bf16[4,8,4096]{2,1,0:T(8,128)(2,1)S(1)} copy-done((bf16[4,8,4096]{2,1,0:T(8,128)(2,1)S(1)}, bf16[4,8,4096]{2,1,0:T(8,128)(2,1)}, u32[]{:S(2)}) %copy-start.2) | copy-done | bytes 262168
  2.6 0.9 %copy-done.3 = bf16[4,8,4096]{2,1,0:T(8,128)(2,1)S(1)} copy-done((bf16[4,8,4096]{2,1,0:T(8,128)(2,1)S(1)}, bf16[4,8,4096]{2,1,0:T(8,128)(2,1)}, u32[]{:S(2)}) %copy-start.3) | copy-done | bytes 262168
  3.6 0.7 %copy-done.4 = f32[4096]{0:T(1024)S(1)} copy-done((f32[4096]{0:T(1024)S(1)}, f32[4096]{0:T(1024)}, u32[]{:S(2)}) %copy-start.4) | copy-done | bytes 16408
  4.3 0.7 %copy-done.5 = f32[4096]{0:T(1024)S(1)} copy-done((f32[4096]{0:T(1024)S(1)}, f32[4096]{0:T(1024)}, u32[]{:S(2)}) %copy-start.5) | copy-done | bytes 16408
  5.0 0.7 %copy-done.6 = s32[3,8]{1,0:T(4,128)S(1)} copy-done((s32[3,8]{1,0:T(4,128)S(1)}, s32[3,8]{1,0:T(4,128)}, u32[]{:S(2)}) %copy-start.6) | copy-done | bytes 120
  5.7 1.6 %prepare.1 = (bf16[8,3072]{1,0:T(8,128)(2,1)S(1)}, bf16[8,3072]{1,0:T(8,128)(2,1)S(1)}, bf16[8,3072]{1,0:T(8,128)(2,1)S(1)}, bf16[8,3072]{1,0:T(8,128)(2,1)S(1)}...) custom-call(bf16[4,8,4096]{2,1,0:T(8,128)(2,1)S(1)} %copy-done.1, ...), custom_call_target="tpu_custom_call" | custom-call | tf_op jit(solution)/shard_map/prepare/pallas_call | solution.py:178
  7.3 0.5 collective-permute-start
  7.8 2.6 %collective-permute-start.1 = (bf16[8,3072]{1,0:T(8,128)(2,1)S(1)}, bf16[8,3072]{1,0:T(8,128)(2,1)S(1)}, u32[]{:S(2)}, u32[]{:S(2)}) collective-permute-start(bf16[8,3072]{1,0:T(8,128)(2,1)S(1)} %get-tuple-element.36), channel_id=1, source_target_pairs={{0,2},{1,3},{2,0},{3,1},{4,6},{5,7},{6,4},{7,5},{8,10},{9,11},{10,... | collective-permute-start | bytes 147464 | tf_op jit(solution)/shard_map/ppermute | solution.py:168
  10.4 0.1 collective-permute-start.2
  10.4 1.8 %collective-permute-start.3 = (bf16[8,3072]{1,0:T(8,128)(2,1)S(1)}, bf16[8,3072]{1,0:T(8,128)(2,1)S(1)}, u32[]{:S(2)}, u32[]{:S(2)}) collective-permute-start(bf16[8,3072]{1,0:T(8,128)(2,1)S(1)} %get-tuple-element.38), channel_id=1, source_target_pairs={{0,4},{1,5},{2,6},{3,7},{4,0},{5,1},{6,2},{7,3},{8,12},{9,13},{10,... | collective-permute-start | bytes 147464 | tf_op jit(solution)/shard_map/ppermute | solution.py:168
  12.3 0.0 collective-permute-start.4
  12.3 0.0 collective-permute-done.refs_1_
  12.3 2.6 %collective-permute-start.5 = (bf16[8,3072]{1,0:T(8,128)(2,1)S(1)}, bf16[8,3072]{1,0:T(8,128)(2,1)S(1)}, u32[]{:S(2)}, u32[]{:S(2)}) collective-permute-start(bf16[8,3072]{1,0:T(8,128)(2,1)S(1)} %get-tuple-element.40), channel_id=1, source_target_pairs={{0,6},{1,7},{2,4},{3,5},{4,2},{5,3},{6,0},{7,1},{8,14},{9,15},{10,... | collective-permute-start | bytes 147464 | tf_op jit(solution)/shard_map/ppermute | solution.py:168
  14.9 0.0 collective-permute-done.1.refs_2_
  14.9 0.1 collective-permute-start.6
  15.0 0.0 collective-permute-done.2.refs_3_
  15.0 2.7 %collective-permute-start.7 = (bf16[8,3072]{1,0:T(8,128)(2,1)S(1)}, bf16[8,3072]{1,0:T(8,128)(2,1)S(1)}, u32[]{:S(2)}, u32[]{:S(2)}) collective-permute-start(bf16[8,3072]{1,0:T(8,128)(2,1)S(1)} %get-tuple-element.42), channel_id=1, source_target_pairs={{0,8},{1,9},{2,10},{3,11},{4,12},{5,13},{6,14},{7,15},{8,0},{9,1},... | collective-permute-start | bytes 147464 | tf_op jit(solution)/shard_map/ppermute | solution.py:168
  17.7 0.0 collective-permute-done.3.refs_4_
  17.7 0.6 collective-permute-start.8
  18.3 2.9 %collective-permute-start.9 = (bf16[8,3072]{1,0:T(8,128)(2,1)S(1)}, bf16[8,3072]{1,0:T(8,128)(2,1)S(1)}, u32[]{:S(2)}, u32[]{:S(2)}) collective-permute-start(bf16[8,3072]{1,0:T(8,128)(2,1)S(1)} %get-tuple-element.44), channel_id=1, source_target_pairs={{0,10},{1,11},{2,8},{3,9},{4,14},{5,15},{6,12},{7,13},{8,2},{9,3},... | collective-permute-start | bytes 147464 | tf_op jit(solution)/shard_map/ppermute | solution.py:168
  21.2 0.0 collective-permute-done.5.refs_6_
  21.2 0.4 collective-permute-start.10
  21.6 0.0 collective-permute-done.6.refs_7_
  21.6 3.3 %collective-permute-start.11 = (bf16[8,3072]{1,0:T(8,128)(2,1)S(1)}, bf16[8,3072]{1,0:T(8,128)(2,1)S(1)}, u32[]{:S(2)}, u32[]{:S(2)}) collective-permute-start(bf16[8,3072]{1,0:T(8,128)(2,1)S(1)} %get-tuple-element.46), channel_id=1, source_target_pairs={{0,12},{1,13},{2,14},{3,15},{4,8},{5,9},{6,10},{7,11},{8,4},{9,5},... | collective-permute-start | bytes 147464 | tf_op jit(solution)/shard_map/ppermute | solution.py:168
  24.9 0.0 collective-permute-done.7.refs_8_
  24.9 0.5 collective-permute-start.12
  25.4 0.0 collective-permute-done.8.refs_9_
  25.4 4.2 %collective-permute-start.13 = (bf16[8,3072]{1,0:T(8,128)(2,1)S(1)}, bf16[8,3072]{1,0:T(8,128)(2,1)S(1)}, u32[]{:S(2)}, u32[]{:S(2)}) collective-permute-start(bf16[8,3072]{1,0:T(8,128)(2,1)S(1)} %get-tuple-element.48), channel_id=1, source_target_pairs={{0,14},{1,15},{2,12},{3,13},{4,10},{5,11},{6,8},{7,9},{8,6},{9,7},... | collective-permute-start | bytes 147464 | tf_op jit(solution)/shard_map/ppermute | solution.py:168
  29.6 0.0 collective-permute-done.9.refs_10_
  29.6 2.9 %collective-permute-start.14 = (bf16[8,3072]{1,0:T(8,128)(2,1)S(1)}, bf16[8,3072]{1,0:T(8,128)(2,1)S(1)}, u32[]{:S(2)}, u32[]{:S(2)}) collective-permute-start(bf16[8,3072]{1,0:T(8,128)(2,1)S(1)} %get-tuple-element.49), channel_id=1, source_target_pairs={{0,15},{1,14},{2,13},{3,12},{4,11},{5,10},{6,9},{7,8},{8,7},{9,6},... | collective-permute-start | bytes 147464 | tf_op jit(solution)/shard_map/ppermute | solution.py:168
  32.5 0.0 collective-permute-done.10.refs_11_
  32.5 0.0 collective-permute-done.11.refs_12_
  32.5 0.0 collective-permute-done.13.refs_14_
  32.5 3.8 %collective-permute-done.14.refs_15_ = bf16[8,3072]{1,0:T(8,128)(2,1)S(1)} collective-permute-done((bf16[8,3072]{1,0:T(8,128)(2,1)S(1)}, bf16[8,3072]{1,0:T(8,128)(2,1)S(1)}, u32[]{:S(2)}, u32[]{:S(2)}) %collective-permute-start.14) | collective-permute-done | bytes 49184 | tf_op jit(solution)/shard_map/ppermute | solution.py:168
  36.4 2.1 %attend.1 = (bf16[8,1024]{1,0:T(8,128)(2,1)S(1)}, bf16[8,1024]{1,0:T(8,128)(2,1)S(1)}, bf16[8,1024]{1,0:T(8,128)(2,1)S(1)}, bf16[8,1024]{1,0:T(8,128)(2,1)S(1)},...) custom-call(bf16[8,3072]{1,0:T(8,128)(2,1)S(1)} %get-tuple-element.3, ...), custom_call_target="tpu_custom_call" | custom-call | tf_op jit(solution)/shard_map/attend/pallas_call | solution.py:197
  38.5 0.1 collective-permute-start.15
  38.6 0.4 collective-permute-start.16
  39.0 1.4 %collective-permute-start.17 = (bf16[8,1024]{1,0:T(8,128)(2,1)S(1)}, bf16[8,1024]{1,0:T(8,128)(2,1)S(1)}, u32[]{:S(2)}, u32[]{:S(2)}) collective-permute-start(bf16[8,1024]{1,0:T(8,128)(2,1)S(1)} %get-tuple-element.53), channel_id=1, source_target_pairs={{0,3},{1,2},{2,1},{3,0},{4,7},{5,6},{6,5},{7,4},{8,11},{9,10},{10,... | collective-permute-start | bytes 49160 | tf_op jit(solution)/shard_map/ppermute | solution.py:168
  40.4 1.8 %collective-permute-start.18 = (bf16[8,1024]{1,0:T(8,128)(2,1)S(1)}, bf16[8,1024]{1,0:T(8,128)(2,1)S(1)}, u32[]{:S(2)}, u32[]{:S(2)}) collective-permute-start(bf16[8,1024]{1,0:T(8,128)(2,1)S(1)} %get-tuple-element.54), channel_id=1, source_target_pairs={{0,4},{1,5},{2,6},{3,7},{4,0},{5,1},{6,2},{7,3},{8,12},{9,13},{10,... | collective-permute-start | bytes 49160 | tf_op jit(solution)/shard_map/ppermute | solution.py:168
  42.2 0.1 collective-permute-start.19
  42.3 1.4 %collective-permute-start.20 = (bf16[8,1024]{1,0:T(8,128)(2,1)S(1)}, bf16[8,1024]{1,0:T(8,128)(2,1)S(1)}, u32[]{:S(2)}, u32[]{:S(2)}) collective-permute-start(bf16[8,1024]{1,0:T(8,128)(2,1)S(1)} %get-tuple-element.56), channel_id=1, source_target_pairs={{0,6},{1,7},{2,4},{3,5},{4,2},{5,3},{6,0},{7,1},{8,14},{9,15},{10,... | collective-permute-start | bytes 49160 | tf_op jit(solution)/shard_map/ppermute | solution.py:168
  43.7 1.1 %collective-permute-start.21 = (bf16[8,1024]{1,0:T(8,128)(2,1)S(1)}, bf16[8,1024]{1,0:T(8,128)(2,1)S(1)}, u32[]{:S(2)}, u32[]{:S(2)}) collective-permute-start(bf16[8,1024]{1,0:T(8,128)(2,1)S(1)} %get-tuple-element.57), channel_id=1, source_target_pairs={{0,7},{1,6},{2,5},{3,4},{4,3},{5,2},{6,1},{7,0},{8,15},{9,14},{10,... | collective-permute-start | bytes 49160 | tf_op jit(solution)/shard_map/ppermute | solution.py:168
  44.8 0.0 collective-permute-done.17.refs_3_
  44.8 2.9 %collective-permute-start.22 = (bf16[8,1024]{1,0:T(8,128)(2,1)S(1)}, bf16[8,1024]{1,0:T(8,128)(2,1)S(1)}, u32[]{:S(2)}, u32[]{:S(2)}) collective-permute-start(bf16[8,1024]{1,0:T(8,128)(2,1)S(1)} %get-tuple-element.58), channel_id=1, source_target_pairs={{0,8},{1,9},{2,10},{3,11},{4,12},{5,13},{6,14},{7,15},{8,0},{9,1},... | collective-permute-start | bytes 49160 | tf_op jit(solution)/shard_map/ppermute | solution.py:168
  47.7 0.0 collective-permute-done.18.refs_4_
  47.7 0.0 collective-permute-start.23
  47.7 0.0 collective-permute-done.19.refs_5_
  47.7 2.4 %collective-permute-start.24 = (bf16[8,1024]{1,0:T(8,128)(2,1)S(1)}, bf16[8,1024]{1,0:T(8,128)(2,1)S(1)}, u32[]{:S(2)}, u32[]{:S(2)}) collective-permute-start(bf16[8,1024]{1,0:T(8,128)(2,1)S(1)} %get-tuple-element.60), channel_id=1, source_target_pairs={{0,10},{1,11},{2,8},{3,9},{4,14},{5,15},{6,12},{7,13},{8,2},{9,3},... | collective-permute-start | bytes 49160 | tf_op jit(solution)/shard_map/ppermute | solution.py:168
  50.1 0.9 %collective-permute-start.25 = (bf16[8,1024]{1,0:T(8,128)(2,1)S(1)}, bf16[8,1024]{1,0:T(8,128)(2,1)S(1)}, u32[]{:S(2)}, u32[]{:S(2)}) collective-permute-start(bf16[8,1024]{1,0:T(8,128)(2,1)S(1)} %get-tuple-element.61), channel_id=1, source_target_pairs={{0,11},{1,10},{2,9},{3,8},{4,15},{5,14},{6,13},{7,12},{8,3},{9,2},... | collective-permute-start | bytes 49160 | tf_op jit(solution)/shard_map/ppermute | solution.py:168
  51.0 2.3 %collective-permute-start.26 = (bf16[8,1024]{1,0:T(8,128)(2,1)S(1)}, bf16[8,1024]{1,0:T(8,128)(2,1)S(1)}, u32[]{:S(2)}, u32[]{:S(2)}) collective-permute-start(bf16[8,1024]{1,0:T(8,128)(2,1)S(1)} %get-tuple-element.62), channel_id=1, source_target_pairs={{0,12},{1,13},{2,14},{3,15},{4,8},{5,9},{6,10},{7,11},{8,4},{9,5},... | collective-permute-start | bytes 49160 | tf_op jit(solution)/shard_map/ppermute | solution.py:168
  53.4 0.0 collective-permute-done.22.refs_8_
  53.4 1.5 %collective-permute-start.27 = (bf16[8,1024]{1,0:T(8,128)(2,1)S(1)}, bf16[8,1024]{1,0:T(8,128)(2,1)S(1)}, u32[]{:S(2)}, u32[]{:S(2)}) collective-permute-start(bf16[8,1024]{1,0:T(8,128)(2,1)S(1)} %get-tuple-element.63), channel_id=1, source_target_pairs={{0,13},{1,12},{2,15},{3,14},{4,9},{5,8},{6,11},{7,10},{8,5},{9,4},... | collective-permute-start | bytes 49160 | tf_op jit(solution)/shard_map/ppermute | solution.py:168
  54.9 0.0 collective-permute-done.23.refs_9_
  54.9 2.8 %collective-permute-start.28 = (bf16[8,1024]{1,0:T(8,128)(2,1)S(1)}, bf16[8,1024]{1,0:T(8,128)(2,1)S(1)}, u32[]{:S(2)}, u32[]{:S(2)}) collective-permute-start(bf16[8,1024]{1,0:T(8,128)(2,1)S(1)} %get-tuple-element.64), channel_id=1, source_target_pairs={{0,14},{1,15},{2,12},{3,13},{4,10},{5,11},{6,8},{7,9},{8,6},{9,7},... | collective-permute-start | bytes 49160 | tf_op jit(solution)/shard_map/ppermute | solution.py:168
  57.7 0.0 collective-permute-done.24.refs_10_
  57.7 1.3 %collective-permute-start.29 = (bf16[8,1024]{1,0:T(8,128)(2,1)S(1)}, bf16[8,1024]{1,0:T(8,128)(2,1)S(1)}, u32[]{:S(2)}, u32[]{:S(2)}) collective-permute-start(bf16[8,1024]{1,0:T(8,128)(2,1)S(1)} %get-tuple-element.65), channel_id=1, source_target_pairs={{0,15},{1,14},{2,13},{3,12},{4,11},{5,10},{6,9},{7,8},{8,7},{9,6},... | collective-permute-start | bytes 49160 | tf_op jit(solution)/shard_map/ppermute | solution.py:168
  59.0 0.8 %cache.1 = bf16[8,16,8,256]{3,2,1,0:T(8,128)(2,1)} custom-call(bf16[8,3072]{1,0:T(8,128)(2,1)S(1)} %get-tuple-element.34.refs_0_, bf16[8,3072]{1,0:T(8,128)(2,1)S(1)} %collective-permute-done.refs_1_, bf16[8,3072]{1,0:T(8,128)(2,1)S(1)} %collective-permute-done.1.refs_2_, bf16[8,3072]{1,0:T(8,128)(2,1)S(1)} %collective-permute-done.2.refs_3_, ...), custom_call_target="tpu_custom_call" | custom-call | bytes 1048576 | tf_op jit(solution)/shard_map/cache/pallas_call | solution.py:206
  59.9 0.0 collective-permute-done.25.refs_11_
  59.9 0.0 collective-permute-done.26.refs_12_
  59.9 0.0 collective-permute-done.27.refs_13_
  59.9 1.5 %collective-permute-done.28.refs_14_ = bf16[8,1024]{1,0:T(8,128)(2,1)S(1)} collective-permute-done((bf16[8,1024]{1,0:T(8,128)(2,1)S(1)}, bf16[8,1024]{1,0:T(8,128)(2,1)S(1)}, u32[]{:S(2)}, u32[]{:S(2)}) %collective-permute-start.28) | collective-permute-done | bytes 16416 | tf_op jit(solution)/shard_map/ppermute | solution.py:168
  61.3 2.2 %collective-permute-done.29.refs_15_ = bf16[8,1024]{1,0:T(8,128)(2,1)S(1)} collective-permute-done((bf16[8,1024]{1,0:T(8,128)(2,1)S(1)}, bf16[8,1024]{1,0:T(8,128)(2,1)S(1)}, u32[]{:S(2)}, u32[]{:S(2)}) %collective-permute-start.29) | collective-permute-done | bytes 16416 | tf_op jit(solution)/shard_map/ppermute | solution.py:168
  63.6 0.8 %gather.1 = bf16[4,8,4096]{2,1,0:T(8,128)(2,1)} custom-call(bf16[8,1024]{1,0:T(8,128)(2,1)S(1)} %get-tuple-element.50.refs_0_, bf16[8,1024]{1,0:T(8,128)(2,1)S(1)} %collective-permute-done.15.refs_1_, bf16[8,1024]{1,0:T(8,128)(2,1)S(1)} %collective-permute-done.16.refs_2_, bf16[8,1024]{1,0:T(8,128)(2,1)S(1)} %collective-permute-done.17.refs_3_, ...), custom_call_target="tpu_custom_call" | custom-call | tf_op jit(solution)/shard_map/gather/pallas_call | solution.py:215
  (14 shorter events, 0.0 us)
Async XLA Ops:
  0.6 35.7 %copy-start = (bf16[8,128,256]{2,1,0:T(8,128)(2,1)S(1)}, bf16[8,128,256]{2,1,0:T(8,128)(2,1)}, u32[]{:S(2)}) copy-start(bf16[8,128,256]{2,1,0:T(8,128)(2,1)} %refs_16_.1) | copy-start | bytes 1572868
  0.6 1.0 %copy-start.1 = (bf16[4,8,4096]{2,1,0:T(8,128)(2,1)S(1)}, bf16[4,8,4096]{2,1,0:T(8,128)(2,1)}, u32[]{:S(2)}) copy-start(bf16[4,8,4096]{2,1,0:T(8,128)(2,1)} %refs_0_.1) | copy-start | bytes 786436
  1.6 0.9 %copy-start.2 = (bf16[4,8,4096]{2,1,0:T(8,128)(2,1)S(1)}, bf16[4,8,4096]{2,1,0:T(8,128)(2,1)}, u32[]{:S(2)}) copy-start(bf16[4,8,4096]{2,1,0:T(8,128)(2,1)} %refs_1_.1) | copy-start | bytes 786436
  2.6 0.9 %copy-start.3 = (bf16[4,8,4096]{2,1,0:T(8,128)(2,1)S(1)}, bf16[4,8,4096]{2,1,0:T(8,128)(2,1)}, u32[]{:S(2)}) copy-start(bf16[4,8,4096]{2,1,0:T(8,128)(2,1)} %refs_2_.1) | copy-start | bytes 786436
  3.6 0.7 %copy-start.4 = (f32[4096]{0:T(1024)S(1)}, f32[4096]{0:T(1024)}, u32[]{:S(2)}) copy-start(f32[4096]{0:T(1024)} %param.10) | copy-start | bytes 49156
  4.3 0.7 %copy-start.5 = (f32[4096]{0:T(1024)S(1)}, f32[4096]{0:T(1024)}, u32[]{:S(2)}) copy-start(f32[4096]{0:T(1024)} %param.11) | copy-start | bytes 49156
  5.0 0.7 %copy-start.6 = (s32[3,8]{1,0:T(4,128)S(1)}, s32[3,8]{1,0:T(4,128)}, u32[]{:S(2)}) copy-start(s32[3,8]{1,0:T(4,128)} %refs_5_.1) | copy-start | bytes 292
  7.3 5.0 %collective-permute-start = (bf16[8,3072]{1,0:T(8,128)(2,1)S(1)}, bf16[8,3072]{1,0:T(8,128)(2,1)S(1)}, u32[]{:S(2)}, u32[]{:S(2)}) collective-permute-start(bf16[8,3072]{1,0:T(8,128)(2,1)S(1)} %get-tuple-element.35), channel_id=1, source_target_pairs={{0,1},{1,0},{2,3},{3,2},{4,5},{5,4},{6,7},{7,6},{8,9},{9,8},{10,11... | collective-permute-start | bytes 147464 | tf_op jit(solution)/shard_map/ppermute | solution.py:168
  7.8 7.1 %collective-permute-start.1 = (bf16[8,3072]{1,0:T(8,128)(2,1)S(1)}, bf16[8,3072]{1,0:T(8,128)(2,1)S(1)}, u32[]{:S(2)}, u32[]{:S(2)}) collective-permute-start(bf16[8,3072]{1,0:T(8,128)(2,1)S(1)} %get-tuple-element.36), channel_id=1, source_target_pairs={{0,2},{1,3},{2,0},{3,1},{4,6},{5,7},{6,4},{7,5},{8,10},{9,11},{10,... | collective-permute-start | bytes 147464 | tf_op jit(solution)/shard_map/ppermute | solution.py:168
  10.4 4.6 %collective-permute-start.2 = (bf16[8,3072]{1,0:T(8,128)(2,1)S(1)}, bf16[8,3072]{1,0:T(8,128)(2,1)S(1)}, u32[]{:S(2)}, u32[]{:S(2)}) collective-permute-start(bf16[8,3072]{1,0:T(8,128)(2,1)S(1)} %get-tuple-element.37), channel_id=1, source_target_pairs={{0,3},{1,2},{2,1},{3,0},{4,7},{5,6},{6,5},{7,4},{8,11},{9,10},{10,... | collective-permute-start | bytes 147464 | tf_op jit(solution)/shard_map/ppermute | solution.py:168
  10.4 7.2 %collective-permute-start.3 = (bf16[8,3072]{1,0:T(8,128)(2,1)S(1)}, bf16[8,3072]{1,0:T(8,128)(2,1)S(1)}, u32[]{:S(2)}, u32[]{:S(2)}) collective-permute-start(bf16[8,3072]{1,0:T(8,128)(2,1)S(1)} %get-tuple-element.38), channel_id=1, source_target_pairs={{0,4},{1,5},{2,6},{3,7},{4,0},{5,1},{6,2},{7,3},{8,12},{9,13},{10,... | collective-permute-start | bytes 147464 | tf_op jit(solution)/shard_map/ppermute | solution.py:168
  12.3 6.0 %collective-permute-start.4 = (bf16[8,3072]{1,0:T(8,128)(2,1)S(1)}, bf16[8,3072]{1,0:T(8,128)(2,1)S(1)}, u32[]{:S(2)}, u32[]{:S(2)}) collective-permute-start(bf16[8,3072]{1,0:T(8,128)(2,1)S(1)} %get-tuple-element.39), channel_id=1, source_target_pairs={{0,5},{1,4},{2,7},{3,6},{4,1},{5,0},{6,3},{7,2},{8,13},{9,12},{10,... | collective-permute-start | bytes 147464 | tf_op jit(solution)/shard_map/ppermute | solution.py:168
  12.3 8.9 %collective-permute-start.5 = (bf16[8,3072]{1,0:T(8,128)(2,1)S(1)}, bf16[8,3072]{1,0:T(8,128)(2,1)S(1)}, u32[]{:S(2)}, u32[]{:S(2)}) collective-permute-start(bf16[8,3072]{1,0:T(8,128)(2,1)S(1)} %get-tuple-element.40), channel_id=1, source_target_pairs={{0,6},{1,7},{2,4},{3,5},{4,2},{5,3},{6,0},{7,1},{8,14},{9,15},{10,... | collective-permute-start | bytes 147464 | tf_op jit(solution)/shard_map/ppermute | solution.py:168
  14.9 6.7 %collective-permute-start.6 = (bf16[8,3072]{1,0:T(8,128)(2,1)S(1)}, bf16[8,3072]{1,0:T(8,128)(2,1)S(1)}, u32[]{:S(2)}, u32[]{:S(2)}) collective-permute-start(bf16[8,3072]{1,0:T(8,128)(2,1)S(1)} %get-tuple-element.41), channel_id=1, source_target_pairs={{0,7},{1,6},{2,5},{3,4},{4,3},{5,2},{6,1},{7,0},{8,15},{9,14},{10,... | collective-permute-start | bytes 147464 | tf_op jit(solution)/shard_map/ppermute | solution.py:168
  15.0 9.9 %collective-permute-start.7 = (bf16[8,3072]{1,0:T(8,128)(2,1)S(1)}, bf16[8,3072]{1,0:T(8,128)(2,1)S(1)}, u32[]{:S(2)}, u32[]{:S(2)}) collective-permute-start(bf16[8,3072]{1,0:T(8,128)(2,1)S(1)} %get-tuple-element.42), channel_id=1, source_target_pairs={{0,8},{1,9},{2,10},{3,11},{4,12},{5,13},{6,14},{7,15},{8,0},{9,1},... | collective-permute-start | bytes 147464 | tf_op jit(solution)/shard_map/ppermute | solution.py:168
  17.7 7.7 %collective-permute-start.8 = (bf16[8,3072]{1,0:T(8,128)(2,1)S(1)}, bf16[8,3072]{1,0:T(8,128)(2,1)S(1)}, u32[]{:S(2)}, u32[]{:S(2)}) collective-permute-start(bf16[8,3072]{1,0:T(8,128)(2,1)S(1)} %get-tuple-element.43), channel_id=1, source_target_pairs={{0,9},{1,8},{2,11},{3,10},{4,13},{5,12},{6,15},{7,14},{8,1},{9,0},... | collective-permute-start | bytes 147464 | tf_op jit(solution)/shard_map/ppermute | solution.py:168
  18.3 11.3 %collective-permute-start.9 = (bf16[8,3072]{1,0:T(8,128)(2,1)S(1)}, bf16[8,3072]{1,0:T(8,128)(2,1)S(1)}, u32[]{:S(2)}, u32[]{:S(2)}) collective-permute-start(bf16[8,3072]{1,0:T(8,128)(2,1)S(1)} %get-tuple-element.44), channel_id=1, source_target_pairs={{0,10},{1,11},{2,8},{3,9},{4,14},{5,15},{6,12},{7,13},{8,2},{9,3},... | collective-permute-start | bytes 147464 | tf_op jit(solution)/shard_map/ppermute | solution.py:168
  21.2 11.3 %collective-permute-start.10 = (bf16[8,3072]{1,0:T(8,128)(2,1)S(1)}, bf16[8,3072]{1,0:T(8,128)(2,1)S(1)}, u32[]{:S(2)}, u32[]{:S(2)}) collective-permute-start(bf16[8,3072]{1,0:T(8,128)(2,1)S(1)} %get-tuple-element.45), channel_id=1, source_target_pairs={{0,11},{1,10},{2,9},{3,8},{4,15},{5,14},{6,13},{7,12},{8,3},{9,2},... | collective-permute-start | bytes 147464 | tf_op jit(solution)/shard_map/ppermute | solution.py:168
  21.6 10.9 %collective-permute-start.11 = (bf16[8,3072]{1,0:T(8,128)(2,1)S(1)}, bf16[8,3072]{1,0:T(8,128)(2,1)S(1)}, u32[]{:S(2)}, u32[]{:S(2)}) collective-permute-start(bf16[8,3072]{1,0:T(8,128)(2,1)S(1)} %get-tuple-element.46), channel_id=1, source_target_pairs={{0,12},{1,13},{2,14},{3,15},{4,8},{5,9},{6,10},{7,11},{8,4},{9,5},... | collective-permute-start | bytes 147464 | tf_op jit(solution)/shard_map/ppermute | solution.py:168
  24.9 7.6 %collective-permute-start.12 = (bf16[8,3072]{1,0:T(8,128)(2,1)S(1)}, bf16[8,3072]{1,0:T(8,128)(2,1)S(1)}, u32[]{:S(2)}, u32[]{:S(2)}) collective-permute-start(bf16[8,3072]{1,0:T(8,128)(2,1)S(1)} %get-tuple-element.47), channel_id=1, source_target_pairs={{0,13},{1,12},{2,15},{3,14},{4,9},{5,8},{6,11},{7,10},{8,5},{9,4},... | collective-permute-start | bytes 147464 | tf_op jit(solution)/shard_map/ppermute | solution.py:168
  25.4 7.1 %collective-permute-start.13 = (bf16[8,3072]{1,0:T(8,128)(2,1)S(1)}, bf16[8,3072]{1,0:T(8,128)(2,1)S(1)}, u32[]{:S(2)}, u32[]{:S(2)}) collective-permute-start(bf16[8,3072]{1,0:T(8,128)(2,1)S(1)} %get-tuple-element.48), channel_id=1, source_target_pairs={{0,14},{1,15},{2,12},{3,13},{4,10},{5,11},{6,8},{7,9},{8,6},{9,7},... | collective-permute-start | bytes 147464 | tf_op jit(solution)/shard_map/ppermute | solution.py:168
  29.6 6.8 %collective-permute-start.14 = (bf16[8,3072]{1,0:T(8,128)(2,1)S(1)}, bf16[8,3072]{1,0:T(8,128)(2,1)S(1)}, u32[]{:S(2)}, u32[]{:S(2)}) collective-permute-start(bf16[8,3072]{1,0:T(8,128)(2,1)S(1)} %get-tuple-element.49), channel_id=1, source_target_pairs={{0,15},{1,14},{2,13},{3,12},{4,11},{5,10},{6,9},{7,8},{8,7},{9,6},... | collective-permute-start | bytes 147464 | tf_op jit(solution)/shard_map/ppermute | solution.py:168
  38.5 3.8 %collective-permute-start.15 = (bf16[8,1024]{1,0:T(8,128)(2,1)S(1)}, bf16[8,1024]{1,0:T(8,128)(2,1)S(1)}, u32[]{:S(2)}, u32[]{:S(2)}) collective-permute-start(bf16[8,1024]{1,0:T(8,128)(2,1)S(1)} %get-tuple-element.51), channel_id=1, source_target_pairs={{0,1},{1,0},{2,3},{3,2},{4,5},{5,4},{6,7},{7,6},{8,9},{9,8},{10,11... | collective-permute-start | bytes 49160 | tf_op jit(solution)/shard_map/ppermute | solution.py:168
  38.6 5.1 %collective-permute-start.16 = (bf16[8,1024]{1,0:T(8,128)(2,1)S(1)}, bf16[8,1024]{1,0:T(8,128)(2,1)S(1)}, u32[]{:S(2)}, u32[]{:S(2)}) collective-permute-start(bf16[8,1024]{1,0:T(8,128)(2,1)S(1)} %get-tuple-element.52), channel_id=1, source_target_pairs={{0,2},{1,3},{2,0},{3,1},{4,6},{5,7},{6,4},{7,5},{8,10},{9,11},{10,... | collective-permute-start | bytes 49160 | tf_op jit(solution)/shard_map/ppermute | solution.py:168
  39.0 5.8 %collective-permute-start.17 = (bf16[8,1024]{1,0:T(8,128)(2,1)S(1)}, bf16[8,1024]{1,0:T(8,128)(2,1)S(1)}, u32[]{:S(2)}, u32[]{:S(2)}) collective-permute-start(bf16[8,1024]{1,0:T(8,128)(2,1)S(1)} %get-tuple-element.53), channel_id=1, source_target_pairs={{0,3},{1,2},{2,1},{3,0},{4,7},{5,6},{6,5},{7,4},{8,11},{9,10},{10,... | collective-permute-start | bytes 49160 | tf_op jit(solution)/shard_map/ppermute | solution.py:168
  40.4 7.3 %collective-permute-start.18 = (bf16[8,1024]{1,0:T(8,128)(2,1)S(1)}, bf16[8,1024]{1,0:T(8,128)(2,1)S(1)}, u32[]{:S(2)}, u32[]{:S(2)}) collective-permute-start(bf16[8,1024]{1,0:T(8,128)(2,1)S(1)} %get-tuple-element.54), channel_id=1, source_target_pairs={{0,4},{1,5},{2,6},{3,7},{4,0},{5,1},{6,2},{7,3},{8,12},{9,13},{10,... | collective-permute-start | bytes 49160 | tf_op jit(solution)/shard_map/ppermute | solution.py:168
  42.2 5.5 %collective-permute-start.19 = (bf16[8,1024]{1,0:T(8,128)(2,1)S(1)}, bf16[8,1024]{1,0:T(8,128)(2,1)S(1)}, u32[]{:S(2)}, u32[]{:S(2)}) collective-permute-start(bf16[8,1024]{1,0:T(8,128)(2,1)S(1)} %get-tuple-element.55), channel_id=1, source_target_pairs={{0,5},{1,4},{2,7},{3,6},{4,1},{5,0},{6,3},{7,2},{8,13},{9,12},{10,... | collective-permute-start | bytes 49160 | tf_op jit(solution)/shard_map/ppermute | solution.py:168
  42.3 7.9 %collective-permute-start.20 = (bf16[8,1024]{1,0:T(8,128)(2,1)S(1)}, bf16[8,1024]{1,0:T(8,128)(2,1)S(1)}, u32[]{:S(2)}, u32[]{:S(2)}) collective-permute-start(bf16[8,1024]{1,0:T(8,128)(2,1)S(1)} %get-tuple-element.56), channel_id=1, source_target_pairs={{0,6},{1,7},{2,4},{3,5},{4,2},{5,3},{6,0},{7,1},{8,14},{9,15},{10,... | collective-permute-start | bytes 49160 | tf_op jit(solution)/shard_map/ppermute | solution.py:168
  43.7 7.4 %collective-permute-start.21 = (bf16[8,1024]{1,0:T(8,128)(2,1)S(1)}, bf16[8,1024]{1,0:T(8,128)(2,1)S(1)}, u32[]{:S(2)}, u32[]{:S(2)}) collective-permute-start(bf16[8,1024]{1,0:T(8,128)(2,1)S(1)} %get-tuple-element.57), channel_id=1, source_target_pairs={{0,7},{1,6},{2,5},{3,4},{4,3},{5,2},{6,1},{7,0},{8,15},{9,14},{10,... | collective-permute-start | bytes 49160 | tf_op jit(solution)/shard_map/ppermute | solution.py:168
  44.8 8.6 %collective-permute-start.22 = (bf16[8,1024]{1,0:T(8,128)(2,1)S(1)}, bf16[8,1024]{1,0:T(8,128)(2,1)S(1)}, u32[]{:S(2)}, u32[]{:S(2)}) collective-permute-start(bf16[8,1024]{1,0:T(8,128)(2,1)S(1)} %get-tuple-element.58), channel_id=1, source_target_pairs={{0,8},{1,9},{2,10},{3,11},{4,12},{5,13},{6,14},{7,15},{8,0},{9,1},... | collective-permute-start | bytes 49160 | tf_op jit(solution)/shard_map/ppermute | solution.py:168
  47.7 7.2 %collective-permute-start.23 = (bf16[8,1024]{1,0:T(8,128)(2,1)S(1)}, bf16[8,1024]{1,0:T(8,128)(2,1)S(1)}, u32[]{:S(2)}, u32[]{:S(2)}) collective-permute-start(bf16[8,1024]{1,0:T(8,128)(2,1)S(1)} %get-tuple-element.59), channel_id=1, source_target_pairs={{0,9},{1,8},{2,11},{3,10},{4,13},{5,12},{6,15},{7,14},{8,1},{9,0},... | collective-permute-start | bytes 49160 | tf_op jit(solution)/shard_map/ppermute | solution.py:168
  47.7 10.0 %collective-permute-start.24 = (bf16[8,1024]{1,0:T(8,128)(2,1)S(1)}, bf16[8,1024]{1,0:T(8,128)(2,1)S(1)}, u32[]{:S(2)}, u32[]{:S(2)}) collective-permute-start(bf16[8,1024]{1,0:T(8,128)(2,1)S(1)} %get-tuple-element.60), channel_id=1, source_target_pairs={{0,10},{1,11},{2,8},{3,9},{4,14},{5,15},{6,12},{7,13},{8,2},{9,3},... | collective-permute-start | bytes 49160 | tf_op jit(solution)/shard_map/ppermute | solution.py:168
  50.1 9.7 %collective-permute-start.25 = (bf16[8,1024]{1,0:T(8,128)(2,1)S(1)}, bf16[8,1024]{1,0:T(8,128)(2,1)S(1)}, u32[]{:S(2)}, u32[]{:S(2)}) collective-permute-start(bf16[8,1024]{1,0:T(8,128)(2,1)S(1)} %get-tuple-element.61), channel_id=1, source_target_pairs={{0,11},{1,10},{2,9},{3,8},{4,15},{5,14},{6,13},{7,12},{8,3},{9,2},... | collective-permute-start | bytes 49160 | tf_op jit(solution)/shard_map/ppermute | solution.py:168
  51.0 8.8 %collective-permute-start.26 = (bf16[8,1024]{1,0:T(8,128)(2,1)S(1)}, bf16[8,1024]{1,0:T(8,128)(2,1)S(1)}, u32[]{:S(2)}, u32[]{:S(2)}) collective-permute-start(bf16[8,1024]{1,0:T(8,128)(2,1)S(1)} %get-tuple-element.62), channel_id=1, source_target_pairs={{0,12},{1,13},{2,14},{3,15},{4,8},{5,9},{6,10},{7,11},{8,4},{9,5},... | collective-permute-start | bytes 49160 | tf_op jit(solution)/shard_map/ppermute | solution.py:168
  53.4 6.5 %collective-permute-start.27 = (bf16[8,1024]{1,0:T(8,128)(2,1)S(1)}, bf16[8,1024]{1,0:T(8,128)(2,1)S(1)}, u32[]{:S(2)}, u32[]{:S(2)}) collective-permute-start(bf16[8,1024]{1,0:T(8,128)(2,1)S(1)} %get-tuple-element.63), channel_id=1, source_target_pairs={{0,13},{1,12},{2,15},{3,14},{4,9},{5,8},{6,11},{7,10},{8,5},{9,4},... | collective-permute-start | bytes 49160 | tf_op jit(solution)/shard_map/ppermute | solution.py:168
  54.9 6.4 %collective-permute-start.28 = (bf16[8,1024]{1,0:T(8,128)(2,1)S(1)}, bf16[8,1024]{1,0:T(8,128)(2,1)S(1)}, u32[]{:S(2)}, u32[]{:S(2)}) collective-permute-start(bf16[8,1024]{1,0:T(8,128)(2,1)S(1)} %get-tuple-element.64), channel_id=1, source_target_pairs={{0,14},{1,15},{2,12},{3,13},{4,10},{5,11},{6,8},{7,9},{8,6},{9,7},... | collective-permute-start | bytes 49160 | tf_op jit(solution)/shard_map/ppermute | solution.py:168
  57.7 5.9 %collective-permute-start.29 = (bf16[8,1024]{1,0:T(8,128)(2,1)S(1)}, bf16[8,1024]{1,0:T(8,128)(2,1)S(1)}, u32[]{:S(2)}, u32[]{:S(2)}) collective-permute-start(bf16[8,1024]{1,0:T(8,128)(2,1)S(1)} %get-tuple-element.65), channel_id=1, source_target_pairs={{0,15},{1,14},{2,13},{3,12},{4,11},{5,10},{6,9},{7,8},{8,7},{9,6},... | collective-permute-start | bytes 49160 | tf_op jit(solution)/shard_map/ppermute | solution.py:168

commit v3 on v1

v3 whole, which is shorter than its diff:
```python
import functools
import math

import jax
import jax.numpy as jnp
from jax import lax
from jax.experimental import pallas as pl
from jax.experimental.pallas import tpu as pltpu
from jax.sharding import PartitionSpec as P

DH = 128
VMEM = pl.BlockSpec(memory_space=pltpu.VMEM)
HBM = pl.BlockSpec(memory_space=pltpu.HBM)
MIB = 1024 * 1024


def rope_tables(coords_ref, tok_rows):
    half = DH // 2
    side = DH // 6
    first = half - 2 * side
    shape = (tok_rows, DH)
    row = lax.broadcasted_iota(jnp.int32, shape, 0)
    lane = lax.broadcasted_iota(jnp.int32, shape, 1)
    pair = lane // 2
    axis = (pair >= first).astype(jnp.int32) + (pair >= first + side).astype(jnp.int32)
    place = jnp.zeros(shape, jnp.int32)
    for which in range(3):
        for token in range(tok_rows):
            place = jnp.where((axis == which) & (row == token), coords_ref[which, token], place)
    step = jnp.where(axis == 0, pair, jnp.where(axis == 1, pair - first, pair - first - side))
    count = jnp.where(axis == 0, float(first), float(side))
    freq = jnp.exp(step.astype(jnp.float32) / count * (-math.log(10000.0)))
    angle = place.astype(jnp.float32) * freq
    sine = jnp.sin(angle)
    even = lane % 2 == 0
    return jnp.cos(angle), jnp.where(even, -sine, 0.0), jnp.where(even, 0.0, sine)


def prepare_kernel(groups, *refs):
    sources, refs = refs[:6], refs[6:]
    videos, tok_rows, width = sources[0].shape
    queries, fresh, refs = refs[:videos], refs[videos : 2 * videos], refs[2 * videos :]
    held, sems = refs[:6], refs[6]
    copies = [
        pltpu.make_async_copy(source, place, sems.at[i])
        for i, (source, place) in enumerate(zip(sources, held))
    ]
    for i in (5, 1, 4, 2, 0, 3):
        copies[i].start()
    q_ref, k_ref, v_ref, q_gain_ref, k_gain_ref, coords_ref = held
    own = lax.axis_index("patch") // groups
    copies[5].wait()
    cosine, sine_even, sine_odd = rope_tables(coords_ref, tok_rows)

    def turned(ref, gain_ref, video):
        wide = ref[video].astype(jnp.float32)
        meansq = jnp.sum(wide * wide, axis=-1, keepdims=True) * (1.0 / width)
        inverse = lax.rsqrt(meansq + 1e-06)
        for head in range(width // DH):
            here = slice(head * DH, (head + 1) * DH)
            y = wide[:, here] * inverse * gain_ref[:, here]
            y = (
                y * cosine
                + pltpu.roll(y, DH - 1, 1) * sine_even
                + pltpu.roll(y, 1, 1) * sine_odd
            )
            yield head, y.astype(jnp.bfloat16)

    for i in (1, 4, 2):
        copies[i].wait()
    for s in range(videos):
        for head, y in turned(k_ref, k_gain_ref, own ^ s):
            fresh[s][:, 2 * head * DH : (2 * head + 1) * DH] = y
            fresh[s][:, (2 * head + 1) * DH : (2 * head + 2) * DH] = v_ref[
                own ^ s, :, head * DH : (head + 1) * DH
            ]
    for i in (0, 3):
        copies[i].wait()
    for s in range(videos):
        for head, y in turned(q_ref, q_gain_ref, own ^ s):
            queries[s][:, head * DH : (head + 1) * DH] = y


def rows_of(refs, start):
    rows = [ref[:, start : start + DH].astype(jnp.float32) for ref in refs]
    return jnp.concatenate(rows, axis=0).astype(jnp.bfloat16)


def attend_kernel(groups, videos, *refs):
    queries, fresh, refs = refs[:videos], refs[videos : 2 * videos], refs[2 * videos :]
    stale_ref, outs = refs[0], refs[1:]
    heads, total_rows, _ = stale_ref.shape
    tok_rows = queries[0].shape[0]
    rows = videos * tok_rows
    scale = 1.0 / math.sqrt(DH)
    dims = (((1,), (1,)), ((), ()))
    me = lax.axis_index("patch")
    row = lax.broadcasted_iota(jnp.int32, (rows, rows), 0) // tok_rows
    same = row == lax.broadcasted_iota(jnp.int32, (rows, rows), 1) // tok_rows
    row = lax.broadcasted_iota(jnp.int32, (rows, total_rows), 0) // tok_rows
    owner = lax.broadcasted_iota(jnp.int32, (rows, total_rows), 1) // tok_rows
    own = (row * groups) ^ me == owner
    for head in range(heads):
        query = rows_of(queries, head * DH)
        key = rows_of(fresh, 2 * head * DH)
        value = rows_of(fresh, (2 * head + 1) * DH)
        stale = stale_ref[head]
        fresh_scores = lax.dot_general(query, key, dims, preferred_element_type=jnp.float32)
        stale_scores = lax.dot_general(
            query, stale[:, :DH], dims, preferred_element_type=jnp.float32
        )
        fresh_scores = jnp.where(same, fresh_scores * scale, -jnp.inf)
        stale_scores = jnp.where(own, -jnp.inf, stale_scores * scale)
        top = jnp.maximum(
            jnp.max(fresh_scores, axis=-1, keepdims=True),
            jnp.max(stale_scores, axis=-1, keepdims=True),
        )
        fresh_weights = jnp.exp(fresh_scores - top)
        stale_weights = jnp.exp(stale_scores - top)
        total = jnp.sum(fresh_weights, axis=-1, keepdims=True) + jnp.sum(
            stale_weights, axis=-1, keepdims=True
        )
        summed = jnp.dot(
            fresh_weights.astype(jnp.bfloat16), value, preferred_element_type=jnp.float32
        ) + jnp.dot(
            stale_weights.astype(jnp.bfloat16), stale[:, DH:], preferred_element_type=jnp.float32
        )
        result = (summed * (1.0 / total)).astype(jnp.bfloat16)
        for s in range(videos):
            outs[s][:, head * DH : (head + 1) * DH] = result[s * tok_rows : (s + 1) * tok_rows]


def pack_kernel(groups, videos, *refs):
    fresh, outs = refs[:videos], refs[videos:]
    span = outs[0].shape[2]
    mine = lax.axis_index("patch") % groups
    for t in range(groups):
        lanes = pl.ds(pl.multiple_of((mine ^ t) * span, DH), span)
        for s in range(videos):
            outs[t][s] = fresh[s][:, lanes]


def cache_kernel(groups, *refs):
    got, out_ref = refs[:groups], refs[groups]
    me = lax.axis_index("patch")
    for t in range(groups):
        for s in range(got[0].shape[0]):
            for pair in range(out_ref.shape[0]):
                out_ref[pair, me ^ (s * groups) ^ t] = got[t][s, :, 2 * pair * DH : 2 * (pair + 1) * DH]


def gather_kernel(groups, videos, *refs):
    back, out_ref, sem = refs[:videos], refs[videos], refs[videos + 1]
    own = lax.axis_index("patch") // groups
    copies = [
        pltpu.make_async_copy(back[s], out_ref.at[own ^ s], sem.at[s]) for s in range(videos)
    ]
    for copy in copies:
        copy.start()
    for copy in copies:
        copy.wait()


def exchange(arrays, stride, patches):
    return [arrays[0]] + [
        lax.ppermute(arrays[s], "patch", [(i, i ^ (s * stride)) for i in range(patches)])
        for s in range(1, len(arrays))
    ]


def local(queries, keys, values, q_gain, k_gain, stale_cache, coords):
    videos, tok_rows, width = queries.shape
    pairs_here, total_rows, _ = stale_cache.shape
    patches = total_rows // tok_rows
    groups = patches // videos
    heads = width // DH
    bf16 = jnp.bfloat16

    def kernel(body, name, limit, **kwargs):
        return pl.pallas_call(
            body, name=name, compiler_params=pltpu.CompilerParams(vmem_limit_bytes=limit * MIB), **kwargs
        )

    planes = [[v * groups + g for g in range(groups)] for v in range(videos)]
    stale_all = lax.all_gather(
        stale_cache, "patch", axis_index_groups=planes, axis=0, tiled=True
    )
    sent = kernel(
        functools.partial(prepare_kernel, groups),
        "prepare",
        61,
        out_shape=[jax.ShapeDtypeStruct((tok_rows, width), bf16)] * videos
        + [jax.ShapeDtypeStruct((tok_rows, 2 * width), bf16)] * videos,
        in_specs=[HBM] * 6,
        out_specs=[VMEM] * (2 * videos),
        scratch_shapes=[
            pltpu.VMEM(queries.shape, bf16),
            pltpu.VMEM(queries.shape, bf16),
            pltpu.VMEM(queries.shape, bf16),
            pltpu.VMEM((1, width), jnp.float32),
            pltpu.VMEM((1, width), jnp.float32),
            pltpu.SMEM(coords.shape, jnp.int32),
            pltpu.SemaphoreType.DMA((6,)),
        ],
    )(queries, keys, values, q_gain.reshape(1, width), k_gain.reshape(1, width), coords)
    fresh = exchange(sent[videos:], groups, patches)
    query = exchange(sent[:videos], groups, patches)
    result = kernel(
        functools.partial(attend_kernel, groups, videos),
        "attend",
        40,
        out_shape=[jax.ShapeDtypeStruct((tok_rows, width), bf16)] * videos,
        in_specs=[VMEM] * (2 * videos + 1),
        out_specs=[VMEM] * videos,
    )(*query, *fresh, stale_all)
    packed = kernel(
        functools.partial(pack_kernel, groups, videos),
        "pack",
        16,
        out_shape=[jax.ShapeDtypeStruct((videos, tok_rows, pairs_here * 2 * DH), bf16)] * groups,
        in_specs=[VMEM] * videos,
        out_specs=[VMEM] * groups,
    )(*fresh)
    spread = exchange(packed, 1, patches)
    back = exchange(result, groups, patches)
    next_cache = kernel(
        functools.partial(cache_kernel, groups),
        "cache",
        16,
        out_shape=jax.ShapeDtypeStruct((pairs_here, patches, tok_rows, 2 * DH), bf16),
        in_specs=[VMEM] * groups,
        out_specs=VMEM,
        cost_estimate=pl.CostEstimate(flops=0, bytes_accessed=stale_cache.size * 4, transcendentals=0),
    )(*spread)
    attended = kernel(
        functools.partial(gather_kernel, groups, videos),
        "gather",
        16,
        out_shape=jax.ShapeDtypeStruct(queries.shape, bf16),
        in_specs=[VMEM] * videos,
        out_specs=HBM,
        scratch_shapes=[pltpu.SemaphoreType.DMA((videos,))],
    )(*back)
    return (attended, next_cache.reshape(stale_cache.shape))


def solution(mesh):
    in_specs = (
        P("req", "patch", None),
        P("req", "patch", None),
        P("req", "patch", None),
        P(),
        P(),
        P(("req", "patch"), None, None),
        P(None, "patch"),
    )
    out_specs = (P("req", "patch", None), P(("req", "patch"), None, None))
    return jax.shard_map(local, mesh=mesh, in_specs=in_specs, out_specs=out_specs, check_vma=False)
```

time: 52.5 us -> 66.2 us (1.26)
  blocking collectives: 41.3 us -> 0 us
  waiting for transfers between devices: 0 us -> 17.8 us
  starting transfers between devices: 0 us -> 17 us
  between operations: 0.66 us -> 14.1 us
  Pallas kernels: 4.43 us -> 12.8 us
  local copies, waits for them, and re-layouts: 5.67 us -> 4.24 us
    all_to_all x2 -> x0, blocking collectives: 41.3 us -> none  [the longest x1 27.6 us: local(): got = lax.all_to_all(sent, 'patch', split_axis=0, concat_axis=0, tiled=True)]
    ppermute x0 -> x12, waiting for transfers between devices: none -> 17.1 us  [exchange(): lax.ppermute(arrays[s], 'patch', [(i, i ^ s * stride) for i in range(patc...]
    ppermute x0 -> x12, starting transfers between devices: none -> 17 us  [exchange(): lax.ppermute(arrays[s], 'patch', [(i, i ^ s * stride) for i in range(patc...]
    pallas_call x2 -> x5, Pallas kernels: 4.43 us -> 12.8 us  [the longest x1 8.14 us: local(): kernel(functools.partial(attend_kernel, groups, videos), 'attend', 40, ou...]
    unnamed x15 -> x8, local copies, waits for them, and re-layouts: 5.67 us -> 4.24 us
    unnamed x0 -> x1, waiting for transfers between devices: none -> 0.68 us
  transfers between devices with their start and end apart: 0 -> 13, of which waited for: 0 -> 5; matrix products, arithmetic and copies ran while one was open for 0% -> 0% of each run, Pallas kernels for 0% -> 18%
where the time goes in v3:
time: 66.2 us; the launch traced here: 65.9 us
  waiting for transfers between devices  17.8 us (27%)
  starting transfers between devices  17 us (26%)
  between operations  14.1 us (21%)
  Pallas kernels  12.8 us (19%)
  local copies, waits for them, and re-layouts  4.24 us (6%)
    ppermute x12, waiting for transfers between devices, exchange(): lax.ppermute(arrays[s], 'patch', [(i, i ^ s * stride) for i in range(patc...  17.1 us
    ppermute x12, starting transfers between devices, exchange(): lax.ppermute(arrays[s], 'patch', [(i, i ^ s * stride) for i in range(patc...  17 us
    pallas_call x1, Pallas kernels, local(): kernel(functools.partial(attend_kernel, groups, videos), 'attend', 40, ou...  8.14 us
    unnamed x8, local copies, waits for them, and re-layouts  4.24 us
    pallas_call x1, Pallas kernels, local(): kernel(functools.partial(prepare_kernel, groups), 'prepare', 61, out_shap...  3.07 us
  transfers between devices with their start and end apart: 13, of which 5 were waited for; matrix products, arithmetic and copies ran while one was open for 0% of the time, Pallas kernels for 18%

profile of v3, /device:TPU:0, one launch (start us, length us, event | category | flops | bytes accessed | tf_op | source)
XLA Modules:
  0.0 65.9 jit_solution(2712553095483240404)
XLA Ops:
  7.2 0.0 all-gather.2.cloned.1.call-start
  7.2 0.7 %all-gather.2.cloned.1.call-update = ((bf16[8,128,256]{2,1,0:T(8,128)(2,1)}), bf16[32,128,256]{2,1,0:T(8,128)(2,1)}) async-update(((), (), s32[]{:S(2)}) %all-gather.2.cloned.1.call-start, bf16[8,128,256]{2,1,0:T(8,128)(2,1)} %param.12) | async-update | bytes 3145752
  7.9 3.1 %prepare.1 = (bf16[8,4096]{1,0:T(8,128)(2,1)}, bf16[8,4096]{1,0:T(8,128)(2,1)}, bf16[8,4096]{1,0:T(8,128)(2,1)}, bf16[8,4096]{1,0:T(8,128)(2,1)}, bf16[8,8192]{1...) custom-call(bf16[4,8,4096]{2,1,0:T(8,128)(2,1)} %refs_0_.1, ...), custom_call_target="tpu_custom_call" | custom-call | tf_op jit(solution)/shard_map/prepare/pallas_call | solution.py:188
  11.0 3.1 %collective-permute-start.3 = (bf16[8,8192]{1,0:T(8,128)(2,1)}, bf16[8,8192]{1,0:T(8,128)(2,1)S(1)}, u32[]{:S(2)}, u32[]{:S(2)}) collective-permute-start(bf16[8,8192]{1,0:T(8,128)(2,1)} %get-tuple-element.23), channel_id=1, source_target_pairs={{0,4},{1,5},{2,6},{3,7},{4,0},{5,1},{6,2},{7,3},{8,12},{9,13},{10,... | collective-permute-start | bytes 393224 | tf_op jit(solution)/shard_map/ppermute | solution.py:166
  14.1 2.6 %collective-permute-start.4 = (bf16[8,8192]{1,0:T(8,128)(2,1)}, bf16[8,8192]{1,0:T(8,128)(2,1)S(1)}, u32[]{:S(2)}, u32[]{:S(2)}) collective-permute-start(bf16[8,8192]{1,0:T(8,128)(2,1)} %get-tuple-element.24), channel_id=1, source_target_pairs={{0,8},{1,9},{2,10},{3,11},{4,12},{5,13},{6,14},{7,15},{8,0},{9,1},... | collective-permute-start | bytes 393224 | tf_op jit(solution)/shard_map/ppermute | solution.py:166
  16.7 0.0 collective-permute-start.5
  16.7 0.9 %collective-permute-start = (bf16[8,4096]{1,0:T(8,128)(2,1)}, bf16[8,4096]{1,0:T(8,128)(2,1)S(1)}, u32[]{:S(2)}, u32[]{:S(2)}) collective-permute-start(bf16[8,4096]{1,0:T(8,128)(2,1)} %get-tuple-element.19), channel_id=1, source_target_pairs={{0,4},{1,5},{2,6},{3,7},{4,0},{5,1},{6,2},{7,3},{8,12},{9,13},{10,... | collective-permute-start | bytes 196616 | tf_op jit(solution)/shard_map/ppermute | solution.py:166
  17.6 2.1 %collective-permute-done.3.refs_5_.refs_1_ = bf16[8,8192]{1,0:T(8,128)(2,1)S(1)} collective-permute-done((bf16[8,8192]{1,0:T(8,128)(2,1)}, bf16[8,8192]{1,0:T(8,128)(2,1)S(1)}, u32[]{:S(2)}, u32[]{:S(2)}) %collective-permute-start.3) | collective-permute-done | bytes 131104 | tf_op jit(solution)/shard_map/ppermute | solution.py:166
  19.7 7.5 %collective-permute-done.4.refs_6_.refs_2_ = bf16[8,8192]{1,0:T(8,128)(2,1)S(1)} collective-permute-done((bf16[8,8192]{1,0:T(8,128)(2,1)}, bf16[8,8192]{1,0:T(8,128)(2,1)S(1)}, u32[]{:S(2)}, u32[]{:S(2)}) %collective-permute-start.4) | collective-permute-done | bytes 131104 | tf_op jit(solution)/shard_map/ppermute | solution.py:166
  27.2 0.0 collective-permute-done.5.refs_7_.refs_3_
  27.2 0.0 copy-start.1
  27.2 0.9 %copy-done.1 = bf16[8,8192]{1,0:T(8,128)(2,1)S(1)} copy-done((bf16[8,8192]{1,0:T(8,128)(2,1)S(1)}, bf16[8,8192]{1,0:T(8,128)(2,1)}, u32[]{:S(2)}) %copy-start.1) | copy-done | bytes 131096
  28.2 0.1 collective-permute-start.9
  28.2 3.1 %collective-permute-start.1 = (bf16[8,4096]{1,0:T(8,128)(2,1)}, bf16[8,4096]{1,0:T(8,128)(2,1)S(1)}, u32[]{:S(2)}, u32[]{:S(2)}) collective-permute-start(bf16[8,4096]{1,0:T(8,128)(2,1)} %get-tuple-element.20), channel_id=1, source_target_pairs={{0,8},{1,9},{2,10},{3,11},{4,12},{5,13},{6,14},{7,15},{8,0},{9,1},... | collective-permute-start | bytes 196616 | tf_op jit(solution)/shard_map/ppermute | solution.py:166
  31.3 1.3 %collective-permute-start.2 = (bf16[8,4096]{1,0:T(8,128)(2,1)}, bf16[8,4096]{1,0:T(8,128)(2,1)S(1)}, u32[]{:S(2)}, u32[]{:S(2)}) collective-permute-start(bf16[8,4096]{1,0:T(8,128)(2,1)} %get-tuple-element.21), channel_id=1, source_target_pairs={{0,12},{1,13},{2,14},{3,15},{4,8},{5,9},{6,10},{7,11},{8,4},{9,5},... | collective-permute-start | bytes 196616 | tf_op jit(solution)/shard_map/ppermute | solution.py:166
  32.6 1.5 %collective-permute-start.10 = (bf16[4,8,2048]{2,1,0:T(8,128)(2,1)S(1)}, bf16[4,8,2048]{2,1,0:T(8,128)(2,1)S(1)}, u32[]{:S(2)}, u32[]{:S(2)}) collective-permute-start(bf16[4,8,2048]{2,1,0:T(8,128)(2,1)S(1)} %get-tuple-element.32), channel_id=1, source_target_pairs={{0,2},{1,3},{2,0},{3,1},{4,6},{5,7},{6,4},{7,5},{8,10},{9,11},{10,... | collective-permute-start | bytes 393224 | tf_op jit(solution)/shard_map/ppermute | solution.py:166
  34.1 0.0 collective-permute-done.refs_1_
  34.1 0.0 collective-permute-start.11
  34.1 1.7 %collective-permute-done.1.refs_2_ = bf16[8,4096]{1,0:T(8,128)(2,1)S(1)} collective-permute-done((bf16[8,4096]{1,0:T(8,128)(2,1)}, bf16[8,4096]{1,0:T(8,128)(2,1)S(1)}, u32[]{:S(2)}, u32[]{:S(2)}) %collective-permute-start.1) | collective-permute-done | bytes 65568 | tf_op jit(solution)/shard_map/ppermute | solution.py:166
  35.9 1.8 %collective-permute-done.2.refs_3_ = bf16[8,4096]{1,0:T(8,128)(2,1)S(1)} collective-permute-done((bf16[8,4096]{1,0:T(8,128)(2,1)}, bf16[8,4096]{1,0:T(8,128)(2,1)S(1)}, u32[]{:S(2)}, u32[]{:S(2)}) %collective-permute-start.2) | collective-permute-done | bytes 65568 | tf_op jit(solution)/shard_map/ppermute | solution.py:166
  37.6 0.0 all-gather.2.cloned.1.call-done.refs_8_
  37.6 0.0 copy-start
  37.6 1.6 %copy-done = bf16[32,128,256]{2,1,0:T(8,128)(2,1)S(1)} copy-done((bf16[32,128,256]{2,1,0:T(8,128)(2,1)S(1)}, bf16[32,128,256]{2,1,0:T(8,128)(2,1)}, u32[]{:S(2)}) %copy-start) | copy-done | bytes 2097176
  39.2 0.0 copy-start.2
  39.2 0.9 %copy-done.2 = bf16[8,8192]{1,0:T(8,128)(2,1)S(1)} copy-done((bf16[8,8192]{1,0:T(8,128)(2,1)S(1)}, bf16[8,8192]{1,0:T(8,128)(2,1)}, u32[]{:S(2)}) %copy-start.2) | copy-done | bytes 131096
  40.1 0.0 copy-start.3
  40.1 0.8 %copy-done.3 = bf16[8,4096]{1,0:T(8,128)(2,1)S(1)} copy-done((bf16[8,4096]{1,0:T(8,128)(2,1)S(1)}, bf16[8,4096]{1,0:T(8,128)(2,1)}, u32[]{:S(2)}) %copy-start.3) | copy-done | bytes 65560
  41.0 8.1 %attend.1 = (bf16[8,4096]{1,0:T(8,128)(2,1)S(1)}, bf16[8,4096]{1,0:T(8,128)(2,1)S(1)}, bf16[8,4096]{1,0:T(8,128)(2,1)S(1)}, bf16[8,4096]{1,0:T(8,128)(2,1)S(1)}) custom-call(bf16[8,4096]{1,0:T(8,128)(2,1)S(1)} %copy-done.3, bf16[8,4096]{1,0:T(8,128)(2,1)S(1)} %collective-permute-done.refs_1_, bf16[8,4096]{1,0:T(8,128)(2,1)S(1)} %collective-permute-done.1.refs_2_, ...), custom_call_target="tpu_custom_call" | custom-call | tf_op jit(solution)/shard_map/attend/pallas_call | solution.py:208
  49.1 1.4 %collective-permute-start.6 = (bf16[8,4096]{1,0:T(8,128)(2,1)S(1)}, bf16[8,4096]{1,0:T(8,128)(2,1)S(1)}, u32[]{:S(2)}, u32[]{:S(2)}) collective-permute-start(bf16[8,4096]{1,0:T(8,128)(2,1)S(1)} %get-tuple-element.27), channel_id=1, source_target_pairs={{0,4},{1,5},{2,6},{3,7},{4,0},{5,1},{6,2},{7,3},{8,12},{9,13},{10,... | collective-permute-start | bytes 196616 | tf_op jit(solution)/shard_map/ppermute | solution.py:166
  50.5 1.0 %collective-permute-start.7 = (bf16[8,4096]{1,0:T(8,128)(2,1)S(1)}, bf16[8,4096]{1,0:T(8,128)(2,1)S(1)}, u32[]{:S(2)}, u32[]{:S(2)}) collective-permute-start(bf16[8,4096]{1,0:T(8,128)(2,1)S(1)} %get-tuple-element.28), channel_id=1, source_target_pairs={{0,8},{1,9},{2,10},{3,11},{4,12},{5,13},{6,14},{7,15},{8,0},{9,1},... | collective-permute-start | bytes 196616 | tf_op jit(solution)/shard_map/ppermute | solution.py:166
  51.6 0.0 collective-permute-done.9.refs_1_
  51.6 2.0 %collective-permute-start.8 = (bf16[8,4096]{1,0:T(8,128)(2,1)S(1)}, bf16[8,4096]{1,0:T(8,128)(2,1)S(1)}, u32[]{:S(2)}, u32[]{:S(2)}) collective-permute-start(bf16[8,4096]{1,0:T(8,128)(2,1)S(1)} %get-tuple-element.29), channel_id=1, source_target_pairs={{0,12},{1,13},{2,14},{3,15},{4,8},{5,9},{6,10},{7,11},{8,4},{9,5},... | collective-permute-start | bytes 196616 | tf_op jit(solution)/shard_map/ppermute | solution.py:166
  53.6 0.0 collective-permute-done.10.refs_2_
  53.6 0.0 collective-permute-done.11.refs_3_
  53.6 0.9 %cache.1 = bf16[8,16,8,256]{3,2,1,0:T(8,128)(2,1)} custom-call(bf16[4,8,2048]{2,1,0:T(8,128)(2,1)S(1)} %get-tuple-element.30.refs_0_, bf16[4,8,2048]{2,1,0:T(8,128)(2,1)S(1)} %collective-permute-done.9.refs_1_, bf16[4,8,2048]{2,1,0:T(8,128)(2,1)S(1)} %collective-permute-done.10.refs_2_, bf16[4,8,2048]{2,1,0:T(8,128)(2,1)S(1)} %collective-permute-done.11.refs_3_), custom_call_target="tpu_custom_call" | custom-call | bytes 1048576 | tf_op jit(solution)/shard_map/cache/pallas_call | solution.py:226
  54.4 0.0 collective-permute-done.6.refs_1_
  54.5 3.9 %collective-permute-done.7.refs_2_ = bf16[8,4096]{1,0:T(8,128)(2,1)S(1)} collective-permute-done((bf16[8,4096]{1,0:T(8,128)(2,1)S(1)}, bf16[8,4096]{1,0:T(8,128)(2,1)S(1)}, u32[]{:S(2)}, u32[]{:S(2)}) %collective-permute-start.7) | collective-permute-done | bytes 65568 | tf_op jit(solution)/shard_map/ppermute | solution.py:166
  58.4 0.0 collective-permute-done.8.refs_3_
  58.4 0.7 %gather.1 = bf16[4,8,4096]{2,1,0:T(8,128)(2,1)} custom-call(bf16[8,4096]{1,0:T(8,128)(2,1)S(1)} %get-tuple-element.26.refs_0_, bf16[8,4096]{1,0:T(8,128)(2,1)S(1)} %collective-permute-done.6.refs_1_, bf16[8,4096]{1,0:T(8,128)(2,1)S(1)} %collective-permute-done.7.refs_2_, bf16[8,4096]{1,0:T(8,128)(2,1)S(1)} %collective-permute-done.8.refs_3_), custom_call_target="tpu_custom_call" | custom-call | tf_op jit(solution)/shard_map/gather/pallas_call | solution.py:235
  (1 shorter events, 0.0 us)
Async XLA Ops:
  7.2 30.5 %all-gather.2.cloned.1.call-start = ((), (), s32[]{:S(2)}) async-start(), calls=%async_computation | async-start | bytes 2621440 | tf_op jit(solution)/shard_map/all_gather | solution.py:185
  11.0 8.7 %collective-permute-start.3 = (bf16[8,8192]{1,0:T(8,128)(2,1)}, bf16[8,8192]{1,0:T(8,128)(2,1)S(1)}, u32[]{:S(2)}, u32[]{:S(2)}) collective-permute-start(bf16[8,8192]{1,0:T(8,128)(2,1)} %get-tuple-element.23), channel_id=1, source_target_pairs={{0,4},{1,5},{2,6},{3,7},{4,0},{5,1},{6,2},{7,3},{8,12},{9,13},{10,... | collective-permute-start | bytes 393224 | tf_op jit(solution)/shard_map/ppermute | solution.py:166
  14.1 13.1 %collective-permute-start.4 = (bf16[8,8192]{1,0:T(8,128)(2,1)}, bf16[8,8192]{1,0:T(8,128)(2,1)S(1)}, u32[]{:S(2)}, u32[]{:S(2)}) collective-permute-start(bf16[8,8192]{1,0:T(8,128)(2,1)} %get-tuple-element.24), channel_id=1, source_target_pairs={{0,8},{1,9},{2,10},{3,11},{4,12},{5,13},{6,14},{7,15},{8,0},{9,1},... | collective-permute-start | bytes 393224 | tf_op jit(solution)/shard_map/ppermute | solution.py:166
  16.7 10.6 %collective-permute-start.5 = (bf16[8,8192]{1,0:T(8,128)(2,1)}, bf16[8,8192]{1,0:T(8,128)(2,1)S(1)}, u32[]{:S(2)}, u32[]{:S(2)}) collective-permute-start(bf16[8,8192]{1,0:T(8,128)(2,1)} %get-tuple-element.25), channel_id=1, source_target_pairs={{0,12},{1,13},{2,14},{3,15},{4,8},{5,9},{6,10},{7,11},{8,4},{9,5},... | collective-permute-start | bytes 393224 | tf_op jit(solution)/shard_map/ppermute | solution.py:166
  16.7 17.5 %collective-permute-start = (bf16[8,4096]{1,0:T(8,128)(2,1)}, bf16[8,4096]{1,0:T(8,128)(2,1)S(1)}, u32[]{:S(2)}, u32[]{:S(2)}) collective-permute-start(bf16[8,4096]{1,0:T(8,128)(2,1)} %get-tuple-element.19), channel_id=1, source_target_pairs={{0,4},{1,5},{2,6},{3,7},{4,0},{5,1},{6,2},{7,3},{8,12},{9,13},{10,... | collective-permute-start | bytes 196616 | tf_op jit(solution)/shard_map/ppermute | solution.py:166
  27.2 0.9 %copy-start.1 = (bf16[8,8192]{1,0:T(8,128)(2,1)S(1)}, bf16[8,8192]{1,0:T(8,128)(2,1)}, u32[]{:S(2)}) copy-start(bf16[8,8192]{1,0:T(8,128)(2,1)} %get-tuple-element.22.refs_4_.refs_0_) | copy-start | bytes 393220
  28.2 23.4 %collective-permute-start.9 = (bf16[4,8,2048]{2,1,0:T(8,128)(2,1)S(1)}, bf16[4,8,2048]{2,1,0:T(8,128)(2,1)S(1)}, u32[]{:S(2)}, u32[]{:S(2)}) collective-permute-start(bf16[4,8,2048]{2,1,0:T(8,128)(2,1)S(1)} %get-tuple-element.31), channel_id=1, source_target_pairs={{0,1},{1,0},{2,3},{3,2},{4,5},{5,4},{6,7},{7,6},{8,9},{9,8},{10,11... | collective-permute-start | bytes 393224 | tf_op jit(solution)/shard_map/ppermute | solution.py:166
  28.2 7.6 %collective-permute-start.1 = (bf16[8,4096]{1,0:T(8,128)(2,1)}, bf16[8,4096]{1,0:T(8,128)(2,1)S(1)}, u32[]{:S(2)}, u32[]{:S(2)}) collective-permute-start(bf16[8,4096]{1,0:T(8,128)(2,1)} %get-tuple-element.20), channel_id=1, source_target_pairs={{0,8},{1,9},{2,10},{3,11},{4,12},{5,13},{6,14},{7,15},{8,0},{9,1},... | collective-permute-start | bytes 196616 | tf_op jit(solution)/shard_map/ppermute | solution.py:166
  31.3 6.3 %collective-permute-start.2 = (bf16[8,4096]{1,0:T(8,128)(2,1)}, bf16[8,4096]{1,0:T(8,128)(2,1)S(1)}, u32[]{:S(2)}, u32[]{:S(2)}) collective-permute-start(bf16[8,4096]{1,0:T(8,128)(2,1)} %get-tuple-element.21), channel_id=1, source_target_pairs={{0,12},{1,13},{2,14},{3,15},{4,8},{5,9},{6,10},{7,11},{8,4},{9,5},... | collective-permute-start | bytes 196616 | tf_op jit(solution)/shard_map/ppermute | solution.py:166
  32.6 21.0 %collective-permute-start.10 = (bf16[4,8,2048]{2,1,0:T(8,128)(2,1)S(1)}, bf16[4,8,2048]{2,1,0:T(8,128)(2,1)S(1)}, u32[]{:S(2)}, u32[]{:S(2)}) collective-permute-start(bf16[4,8,2048]{2,1,0:T(8,128)(2,1)S(1)} %get-tuple-element.32), channel_id=1, source_target_pairs={{0,2},{1,3},{2,0},{3,1},{4,6},{5,7},{6,4},{7,5},{8,10},{9,11},{10,... | collective-permute-start | bytes 393224 | tf_op jit(solution)/shard_map/ppermute | solution.py:166
  34.1 19.5 %collective-permute-start.11 = (bf16[4,8,2048]{2,1,0:T(8,128)(2,1)S(1)}, bf16[4,8,2048]{2,1,0:T(8,128)(2,1)S(1)}, u32[]{:S(2)}, u32[]{:S(2)}) collective-permute-start(bf16[4,8,2048]{2,1,0:T(8,128)(2,1)S(1)} %get-tuple-element.33), channel_id=1, source_target_pairs={{0,3},{1,2},{2,1},{3,0},{4,7},{5,6},{6,5},{7,4},{8,11},{9,10},{10,... | collective-permute-start | bytes 393224 | tf_op jit(solution)/shard_map/ppermute | solution.py:166
  37.6 1.6 %copy-start = (bf16[32,128,256]{2,1,0:T(8,128)(2,1)S(1)}, bf16[32,128,256]{2,1,0:T(8,128)(2,1)}, u32[]{:S(2)}) copy-start(bf16[32,128,256]{2,1,0:T(8,128)(2,1)} %all-gather.2.cloned.1.call-done.refs_8_) | copy-start | bytes 6291460
  39.2 0.9 %copy-start.2 = (bf16[8,8192]{1,0:T(8,128)(2,1)S(1)}, bf16[8,8192]{1,0:T(8,128)(2,1)}, u32[]{:S(2)}) copy-start(bf16[8,8192]{1,0:T(8,128)(2,1)} %get-tuple-element.22.refs_4_.refs_0_) | copy-start | bytes 393220
  40.1 0.8 %copy-start.3 = (bf16[8,4096]{1,0:T(8,128)(2,1)S(1)}, bf16[8,4096]{1,0:T(8,128)(2,1)}, u32[]{:S(2)}) copy-start(bf16[8,4096]{1,0:T(8,128)(2,1)} %get-tuple-element.18.refs_0_) | copy-start | bytes 196612
  49.1 5.3 %collective-permute-start.6 = (bf16[8,4096]{1,0:T(8,128)(2,1)S(1)}, bf16[8,4096]{1,0:T(8,128)(2,1)S(1)}, u32[]{:S(2)}, u32[]{:S(2)}) collective-permute-start(bf16[8,4096]{1,0:T(8,128)(2,1)S(1)} %get-tuple-element.27), channel_id=1, source_target_pairs={{0,4},{1,5},{2,6},{3,7},{4,0},{5,1},{6,2},{7,3},{8,12},{9,13},{10,... | collective-permute-start | bytes 196616 | tf_op jit(solution)/shard_map/ppermute | solution.py:166
  50.5 7.8 %collective-permute-start.7 = (bf16[8,4096]{1,0:T(8,128)(2,1)S(1)}, bf16[8,4096]{1,0:T(8,128)(2,1)S(1)}, u32[]{:S(2)}, u32[]{:S(2)}) collective-permute-start(bf16[8,4096]{1,0:T(8,128)(2,1)S(1)} %get-tuple-element.28), channel_id=1, source_target_pairs={{0,8},{1,9},{2,10},{3,11},{4,12},{5,13},{6,14},{7,15},{8,0},{9,1},... | collective-permute-start | bytes 196616 | tf_op jit(solution)/shard_map/ppermute | solution.py:166
  51.6 6.8 %collective-permute-start.8 = (bf16[8,4096]{1,0:T(8,128)(2,1)S(1)}, bf16[8,4096]{1,0:T(8,128)(2,1)S(1)}, u32[]{:S(2)}, u32[]{:S(2)}) collective-permute-start(bf16[8,4096]{1,0:T(8,128)(2,1)S(1)} %get-tuple-element.29), channel_id=1, source_target_pairs={{0,12},{1,13},{2,14},{3,15},{4,8},{5,9},{6,10},{7,11},{8,4},{9,5},... | collective-permute-start | bytes 196616 | tf_op jit(solution)/shard_map/ppermute | solution.py:166
Sparse Core Ops, SparseCore 0:
  9.6 25.2 all-gather.1

commit v4 on v1

v4 whole, which is shorter than its diff:
```python
import functools
import math

import jax
import jax.numpy as jnp
from jax import lax
from jax.experimental import pallas as pl
from jax.experimental.pallas import tpu as pltpu
from jax.sharding import PartitionSpec as P

DH = 128
VMEM = pl.BlockSpec(memory_space=pltpu.VMEM)
HBM = pl.BlockSpec(memory_space=pltpu.HBM)
SMEM = pl.BlockSpec(memory_space=pltpu.SMEM)
MIB = 1024 * 1024
BF16 = jnp.bfloat16
F32 = jnp.float32
TRANSPOSED = (((1,), (1,)), ((), ()))


def rope_tables(coords_ref, tok_rows):
    half = DH // 2
    side = DH // 6
    first = half - 2 * side
    shape = (tok_rows, DH)
    row = lax.broadcasted_iota(jnp.int32, shape, 0)
    lane = lax.broadcasted_iota(jnp.int32, shape, 1)
    pair = lane // 2
    axis = (pair >= first).astype(jnp.int32) + (pair >= first + side).astype(jnp.int32)
    place = jnp.zeros(shape, jnp.int32)
    for which in range(3):
        for token in range(tok_rows):
            place = jnp.where((axis == which) & (row == token), coords_ref[which, token], place)
    step = jnp.where(axis == 0, pair, jnp.where(axis == 1, pair - first, pair - first - side))
    count = jnp.where(axis == 0, float(first), float(side))
    freq = jnp.exp(step.astype(F32) / count * (-math.log(10000.0)))
    angle = place.astype(F32) * freq
    sine = jnp.sin(angle)
    even = lane % 2 == 0
    return jnp.cos(angle), jnp.where(even, -sine, 0.0), jnp.where(even, 0.0, sine)


def normed_heads(wide, gain_ref, tables):
    cosine, sine_even, sine_odd = tables
    width = wide.shape[-1]
    meansq = jnp.sum(wide * wide, axis=-1, keepdims=True) * (1.0 / width)
    inverse = lax.rsqrt(meansq + 1e-06)
    for head in range(width // DH):
        here = slice(head * DH, (head + 1) * DH)
        y = wide[:, here] * inverse * gain_ref[:, here]
        y = y * cosine + pltpu.roll(y, DH - 1, 1) * sine_even + pltpu.roll(y, 1, 1) * sine_odd
        yield head, y.astype(BF16)


def query_kernel(groups, q_hbm, gain_hbm, coords_hbm, *refs):
    videos, tok_rows, width = q_hbm.shape
    outs, tables_ref, refs = refs[:videos], refs[videos], refs[videos + 1 :]
    q_ref, gain_ref, coords_ref, done_ref, sems, out_sems = refs
    own = lax.axis_index("patch") // groups
    copies = [
        pltpu.make_async_copy(source, place, sems.at[i])
        for i, (source, place) in enumerate(
            ((coords_hbm, coords_ref), (q_hbm, q_ref), (gain_hbm, gain_ref))
        )
    ]
    for copy in copies:
        copy.start()
    copies[0].wait()
    tables = rope_tables(coords_ref, tok_rows)
    for i in range(3):
        tables_ref[i] = tables[i]
    copies[1].wait()
    copies[2].wait()
    sends = []
    for s in range(videos):
        for head, y in normed_heads(q_ref[own ^ s].astype(F32), gain_ref, tables):
            done_ref[s, :, head * DH : (head + 1) * DH] = y
        sends.append(pltpu.make_async_copy(done_ref.at[s], outs[s], out_sems.at[s]))
        sends[-1].start()
    for send in sends:
        send.wait()


def key_kernel(k_ref, v_ref, gain_ref, tables_ref, out_ref):
    videos, tok_rows, width = k_ref.shape
    tables = [tables_ref[i] for i in range(3)]
    span = out_ref.shape[2]
    groups = out_ref.shape[0] // videos
    pairs = span // (2 * DH)
    for video in range(videos):
        for head, y in normed_heads(k_ref[video].astype(F32), gain_ref, tables):
            target, start = video * groups + head // pairs, head % pairs * 2 * DH
            out_ref[target, :, start : start + DH] = y
            out_ref[target, :, start + DH : start + 2 * DH] = v_ref[
                video, :, head * DH : (head + 1) * DH
            ]


def softmax_parts(scores):
    top = jnp.max(scores, axis=-1, keepdims=True)
    weights = jnp.exp(scores - top)
    total = jnp.sum(weights, axis=-1, keepdims=True)
    return weights.astype(BF16), 1.0 / total, top + jnp.log(total)


def stacked(refs, lanes):
    rows = [ref[:, lanes].astype(F32) for ref in refs]
    return jnp.concatenate(rows, axis=0).astype(BF16)


def fresh_kernel(groups, videos, *refs):
    queries, fresh_ref, out_ref, log_ref = refs[:videos], refs[videos], refs[videos + 1], refs[videos + 2]
    own = lax.axis_index("patch") // groups
    _, tok_rows, width = out_ref.shape
    span = width // groups
    pairs = span // DH
    rows = videos * tok_rows
    scale = 1.0 / math.sqrt(DH)
    shape = (pairs * rows, rows)
    same = lax.broadcasted_iota(jnp.int32, shape, 0) % rows // tok_rows == (
        lax.broadcasted_iota(jnp.int32, shape, 1) // tok_rows
    )
    lane = lax.broadcasted_iota(jnp.int32, (rows, DH), 1)
    logs = jnp.zeros((rows, DH), F32)
    for group in range(groups):
        query = stacked(queries, slice(group * span, (group + 1) * span))
        fresh = jnp.concatenate(
            [fresh_ref[(own ^ s) * groups + group].astype(F32) for s in range(videos)], axis=0
        ).astype(BF16)
        scores = jnp.concatenate(
            [
                lax.dot_general(
                    query[:, pair * DH : (pair + 1) * DH],
                    fresh[:, 2 * pair * DH : (2 * pair + 1) * DH],
                    TRANSPOSED,
                    preferred_element_type=F32,
                )
                for pair in range(pairs)
            ],
            axis=0,
        )
        weights, inverse, log = softmax_parts(jnp.where(same, scores * scale, -jnp.inf))
        for pair in range(pairs):
            here = slice(pair * rows, (pair + 1) * rows)
            head = group * pairs + pair
            result = inverse[here] * jnp.dot(
                weights[here],
                fresh[:, (2 * pair + 1) * DH : (2 * pair + 2) * DH],
                preferred_element_type=F32,
            )
            logs = jnp.where(lane == head, log[here], logs)
            for s in range(videos):
                out_ref[s, :, head * DH : (head + 1) * DH] = result[s * tok_rows : (s + 1) * tok_rows]
    for s in range(videos):
        log_ref[s] = logs[s * tok_rows : (s + 1) * tok_rows]


def stale_kernel(groups, videos, *refs):
    queries, pieces, outs = refs[:videos], refs[videos : videos + groups], refs[videos + groups :]
    me = lax.axis_index("patch")
    mine = me % groups
    pairs, total_rows, _ = pieces[0].shape
    tok_rows, width = queries[0].shape
    span = pairs * DH
    rows = videos * tok_rows
    scale = 1.0 / math.sqrt(DH)
    shape = (pairs * rows, total_rows)
    patch = (lax.broadcasted_iota(jnp.int32, shape, 0) % rows // tok_rows * groups) ^ me
    own = patch == lax.broadcasted_iota(jnp.int32, shape, 1) // tok_rows
    lane = lax.broadcasted_iota(jnp.int32, (rows, DH), 1)
    logs = jnp.zeros((rows, DH), F32)
    for t in range(groups):
        start = pl.multiple_of((mine ^ t) * span, DH)
        query = stacked(queries, pl.ds(start, span))
        scores = jnp.concatenate(
            [
                lax.dot_general(
                    query[:, pair * DH : (pair + 1) * DH],
                    pieces[t][pair, :, :DH],
                    TRANSPOSED,
                    preferred_element_type=F32,
                )
                for pair in range(pairs)
            ],
            axis=0,
        )
        weights, inverse, log = softmax_parts(jnp.where(own, -jnp.inf, scores * scale))
        results = []
        for pair in range(pairs):
            here = slice(pair * rows, (pair + 1) * rows)
            results.append(
                inverse[here]
                * jnp.dot(weights[here], pieces[t][pair, :, DH:], preferred_element_type=F32)
            )
            logs = jnp.where(lane == t * pairs + pair, log[here], logs)
        result = jnp.concatenate(results, axis=1).astype(BF16)
        for s in range(videos):
            outs[s][:, pl.ds(start, span)] = result[s * tok_rows : (s + 1) * tok_rows]
    high = logs.astype(BF16).astype(F32)
    middle = (logs - high).astype(BF16).astype(F32)
    low = (logs - high - middle).astype(BF16).astype(F32)
    heads = groups * pairs
    terms = (high + pltpu.roll(middle, heads, 1) + pltpu.roll(low, 2 * heads, 1)).astype(BF16)
    for s in range(videos):
        outs[s][:, width:] = terms[s * tok_rows : (s + 1) * tok_rows]


def join_kernel(groups, videos, *refs):
    back = refs[:videos]
    fresh_ref, log_ref, out_ref, done_ref, sems = refs[videos:]
    me = lax.axis_index("patch")
    own, mine = me // groups, me % groups
    _, tok_rows, width = fresh_ref.shape
    heads = width // DH
    pairs = heads // groups
    copies = []
    for s in range(videos):
        terms = back[s][:, width:].astype(F32)
        stale_log = terms + pltpu.roll(terms, DH - heads, 1) + pltpu.roll(terms, DH - 2 * heads, 1)
        fresh_log = log_ref[s]
        for t in range(groups):
            start = pl.multiple_of((mine ^ t) * pairs * DH, DH)
            stale = back[s][:, pl.ds(start, pairs * DH)].astype(F32)
            fresh = fresh_ref[s, :, pl.ds(start, pairs * DH)]
            shift = DH + t * pairs - (mine ^ t) * pairs
            gap = stale_log - pltpu.roll(fresh_log, shift % DH, 1)
            share = 1.0 / (1.0 + jnp.exp(gap))
            parts = []
            for pair in range(pairs):
                here = slice(pair * DH, (pair + 1) * DH)
                of = share[:, t * pairs + pair : t * pairs + pair + 1]
                parts.append(of * fresh[:, here] + (1.0 - of) * stale[:, here])
            done_ref[s, :, pl.ds(start, pairs * DH)] = jnp.concatenate(parts, axis=1).astype(BF16)
        copies.append(pltpu.make_async_copy(done_ref.at[s], out_ref.at[own ^ s], sems.at[s]))
        copies[-1].start()
    for copy in copies:
        copy.wait()


def cache_kernel(got_ref, out_ref, sems):
    copies = []
    for pair in range(out_ref.shape[0]):
        lanes = pl.ds(2 * pair * DH, 2 * DH)
        copies.append(
            pltpu.make_async_copy(got_ref.at[:, :, lanes], out_ref.at[pair], sems.at[pair])
        )
        copies[-1].start()
    for copy in copies:
        copy.wait()


def permuted(array, offset, patches):
    return lax.ppermute(array, "patch", [(i, i ^ offset) for i in range(patches)])


def exchange(arrays, stride, patches):
    return [arrays[0]] + [
        permuted(arrays[s], s * stride, patches) for s in range(1, len(arrays))
    ]


def local(queries, keys, values, q_gain, k_gain, stale_cache, coords):
    videos, tok_rows, width = queries.shape
    pairs_here, total_rows, _ = stale_cache.shape
    patches = total_rows // tok_rows
    groups = patches // videos
    rows = jax.ShapeDtypeStruct((tok_rows, width), BF16)

    def kernel(body, name, limit, cost=0, **kwargs):
        return pl.pallas_call(
            body,
            name=name,
            compiler_params=pltpu.CompilerParams(vmem_limit_bytes=limit * MIB),
            cost_estimate=pl.CostEstimate(flops=0, bytes_accessed=cost, transcendentals=0),
            **kwargs,
        )

    pieces = {0: stale_cache}
    bit = groups // 2
    pieces[bit] = permuted(stale_cache, bit, patches)
    *query, tables = kernel(
        functools.partial(query_kernel, groups),
        "query",
        56,
        out_shape=[rows] * videos + [jax.ShapeDtypeStruct((3, tok_rows, DH), F32)],
        in_specs=[HBM] * 3,
        out_specs=[HBM] * videos + [VMEM],
        scratch_shapes=[
            pltpu.VMEM(queries.shape, BF16),
            pltpu.VMEM((1, width), F32),
            pltpu.SMEM(coords.shape, jnp.int32),
            pltpu.VMEM(queries.shape, BF16),
            pltpu.SemaphoreType.DMA((3,)),
            pltpu.SemaphoreType.DMA((videos,)),
        ],
    )(queries, q_gain.reshape(1, width), coords)
    query_got = exchange(query, groups, patches)
    fresh = kernel(
        key_kernel,
        "key",
        16,
        out_shape=jax.ShapeDtypeStruct((patches, tok_rows, 2 * pairs_here * DH), BF16),
        in_specs=[VMEM] * 4,
        out_specs=VMEM,
    )(keys, values, k_gain.reshape(1, width), tables)
    cached = lax.all_to_all(fresh, "patch", split_axis=0, concat_axis=0, tiled=True)
    fresh_sum, fresh_log = kernel(
        functools.partial(fresh_kernel, groups, videos),
        "fresh",
        16,
        out_shape=(
            jax.ShapeDtypeStruct((videos, tok_rows, width), F32),
            jax.ShapeDtypeStruct((videos, tok_rows, DH), F32),
        ),
        in_specs=[VMEM] * (videos + 1),
        out_specs=(VMEM, VMEM),
    )(*query, fresh)
    pieces, query_got, fresh_log = lax.optimization_barrier((pieces, query_got, fresh_log))
    while bit > 1:
        bit //= 2
        pieces.update({t | bit: permuted(piece, bit, patches) for t, piece in list(pieces.items())})
    result = kernel(
        functools.partial(stale_kernel, groups, videos),
        "stale",
        32,
        out_shape=[jax.ShapeDtypeStruct((tok_rows, width + DH), BF16)] * videos,
        in_specs=[VMEM] * (videos + groups),
        out_specs=[VMEM] * videos,
    )(*query_got, *[pieces[t] for t in range(groups)])
    back = exchange(result, groups, patches)
    next_cache = kernel(
        cache_kernel,
        "cache",
        16,
        out_shape=jax.ShapeDtypeStruct((pairs_here, patches, tok_rows, 2 * DH), BF16),
        in_specs=[VMEM],
        out_specs=HBM,
        scratch_shapes=[pltpu.SemaphoreType.DMA((pairs_here,))],
    )(cached)
    attended = kernel(
        functools.partial(join_kernel, groups, videos),
        "join",
        16,
        out_shape=jax.ShapeDtypeStruct(queries.shape, BF16),
        in_specs=[VMEM] * (videos + 2),
        out_specs=HBM,
        scratch_shapes=[
            pltpu.VMEM(queries.shape, BF16),
            pltpu.SemaphoreType.DMA((videos,)),
        ],
    )(*back, fresh_sum, fresh_log)
    return (attended, next_cache.reshape(stale_cache.shape))


def solution(mesh):
    in_specs = (
        P("req", "patch", None),
        P("req", "patch", None),
        P("req", "patch", None),
        P(),
        P(),
        P(("req", "patch"), None, None),
        P(None, "patch"),
    )
    out_specs = (P("req", "patch", None), P(("req", "patch"), None, None))
    return jax.shard_map(local, mesh=mesh, in_specs=in_specs, out_specs=out_specs, check_vma=False)
```

time: 52.5 us -> 50.7 us (0.966)
  blocking collectives: 41.3 us -> 0 us
  waiting for transfers between devices: 0 us -> 19.8 us
  starting transfers between devices: 0 us -> 17.6 us
  Pallas kernels: 4.43 us -> 10.6 us
  local copies, waits for them, and re-layouts: 5.67 us -> 1.68 us
    all_to_all x2 -> x0, blocking collectives: 41.3 us -> none  [the longest x1 27.6 us: local(): got = lax.all_to_all(sent, 'patch', split_axis=0, concat_axis=0, tiled=True)]
    ppermute x0 -> x9, waiting for transfers between devices: none -> 19.8 us  [permuted(): lax.ppermute(array, 'patch', [(i, i ^ offset) for i in range(patches)])]
    ppermute x0 -> x9, starting transfers between devices: none -> 12.4 us  [permuted(): lax.ppermute(array, 'patch', [(i, i ^ offset) for i in range(patches)])]
    pallas_call x2 -> x6, Pallas kernels: 4.43 us -> 10.6 us  [the longest x1 2.87 us: local(): kernel(functools.partial(query_kernel, groups), 'query', 56, out_shape=[r...]
    all_to_all x0 -> x1, starting transfers between devices: none -> 5.13 us  [local(): lax.all_to_all(fresh, 'patch', split_axis=0, concat_axis=0, tiled=True)]
    unnamed x15 -> x18, local copies, waits for them, and re-layouts: 5.67 us -> 1.68 us
  transfers between devices with their start and end apart: 0 -> 10, of which waited for: 0 -> 5; matrix products, arithmetic and copies ran while one was open for 0% -> 0% of each run, Pallas kernels for 0% -> 18%
where the time goes in v4:
time: 50.7 us; the launch traced here: 50.3 us
  waiting for transfers between devices  19.8 us (39%)
  starting transfers between devices  17.6 us (35%)
  Pallas kernels  10.6 us (21%)
  local copies, waits for them, and re-layouts  1.68 us (3%)
  between operations  0.75 us (1%)
    ppermute x9, waiting for transfers between devices, permuted(): lax.ppermute(array, 'patch', [(i, i ^ offset) for i in range(patches)])  19.8 us
    ppermute x9, starting transfers between devices, permuted(): lax.ppermute(array, 'patch', [(i, i ^ offset) for i in range(patches)])  12.4 us
    all_to_all x1, starting transfers between devices, local(): lax.all_to_all(fresh, 'patch', split_axis=0, concat_axis=0, tiled=True)  5.13 us
    pallas_call x1, Pallas kernels, local(): kernel(functools.partial(query_kernel, groups), 'query', 56, out_shape=[r...  2.87 us
    pallas_call x1, Pallas kernels, local(): kernel(functools.partial(fresh_kernel, groups, videos), 'fresh', 16, out_...  2.15 us
    pallas_call x1, Pallas kernels, local(): kernel(functools.partial(join_kernel, groups, videos), 'join', 16, out_sh...  1.77 us
    unnamed x18, local copies, waits for them, and re-layouts  1.68 us
    pallas_call x1, Pallas kernels, local(): kernel(functools.partial(stale_kernel, groups, videos), 'stale', 32, out_...  1.52 us
  transfers between devices with their start and end apart: 10, of which 5 were waited for; matrix products, arithmetic and copies ran while one was open for 0% of the time, Pallas kernels for 18%

profile of v4, /device:TPU:0, one launch (start us, length us, event | category | flops | bytes accessed | tf_op | source)
XLA Modules:
  0.0 50.3 jit_solution(8942739421545285694)
XLA Ops:
  0.6 0.0 copy-start.2
  0.6 3.0 %collective-permute-start = (bf16[8,128,256]{2,1,0:T(8,128)(2,1)}, bf16[8,128,256]{2,1,0:T(8,128)(2,1)S(1)}, u32[]{:S(2)}, u32[]{:S(2)}) collective-permute-start(bf16[8,128,256]{2,1,0:T(8,128)(2,1)} %refs_4_), channel_id=1, source_target_pairs={{0,2},{1,3},{2,0},{3,1},{4,6},{5,7},{6,4},{7,5},{8,10},{9,11},{10,... | collective-permute-start | bytes 1572872 | tf_op jit(solution)/shard_map/ppermute | solution.py:253
  3.6 0.0 copy-start.7
  3.6 2.9 %query.1 = (bf16[8,4096]{1,0:T(8,128)(2,1)}, bf16[8,4096]{1,0:T(8,128)(2,1)}, bf16[8,4096]{1,0:T(8,128)(2,1)}, bf16[8,4096]{1,0:T(8,128)(2,1)}, f32[3,8,128]{2,1,0:T(8,128)}) custom-call(bf16[4,8,4096]{2,1,0:T(8,128)(2,1)} %q_hbm.1, f32[1,4096]{1,0:T(1,128)} %bitcast.5, s32[3,8]{1,0:T(4,128)} %coords_hbm.1), custom_call_target="tpu_custom_call" | custom-call | tf_op jit(solution)/shard_map/query/pallas_call | solution.py:281
  6.5 0.0 copy-done.2
  6.5 0.0 copy-done.7
  6.5 0.0 copy-start.3
  6.6 0.9 %copy-done.3 = bf16[4,8,4096]{2,1,0:T(8,128)(2,1)S(1)} copy-done((bf16[4,8,4096]{2,1,0:T(8,128)(2,1)S(1)}, bf16[4,8,4096]{2,1,0:T(8,128)(2,1)}, u32[]{:S(2)}) %copy-start.3) | copy-done | bytes 262168
  7.5 0.0 copy-start.8
  7.5 0.7 %copy-done.8 = f32[3,8,128]{2,1,0:T(8,128)S(1)} copy-done((f32[3,8,128]{2,1,0:T(8,128)S(1)}, f32[3,8,128]{2,1,0:T(8,128)}, u32[]{:S(2)}) %copy-start.8) | copy-done | bytes 12312
  8.2 1.4 %key.1.refs_4_ = bf16[16,8,2048]{2,1,0:T(8,128)(2,1)} custom-call(bf16[4,8,4096]{2,1,0:T(8,128)(2,1)S(1)} %copy-done.2, bf16[4,8,4096]{2,1,0:T(8,128)(2,1)S(1)} %copy-done.3, f32[1,4096]{1,0:T(1,128)S(1)} %bitcast.3, f32[3,8,128]{2,1,0:T(8,128)S(1)} %copy-done.8), custom_call_target="tpu_custom_call" | custom-call | tf_op jit(solution)/shard_map/key/pallas_call | solution.py:298
  9.6 0.0 copy-start.6
  9.6 0.0 copy-start.5
  9.6 0.0 copy-start.4
  9.6 0.0 copy-start.1
  9.6 5.1 %all-to-all-start = ((bf16[16,8,2048]{2,1,0:T(8,128)(2,1)}), bf16[16,8,2048]{2,1,0:T(8,128)(2,1)S(1)}, u32[]{:S(2)}, u32[]{:S(2)}) async-start(bf16[16,8,2048]{2,1,0:T(8,128)(2,1)} %key.1.refs_4_), calls=%async_computation | async-start | bytes 1048576 | tf_op jit(solution)/shard_map/all_to_all | solution.py:306
  14.8 0.0 copy-start
  14.8 0.0 copy-done.6
  14.8 2.0 %collective-permute-start.1 = (bf16[8,4096]{1,0:T(8,128)(2,1)S(1)}, bf16[8,4096]{1,0:T(8,128)(2,1)S(1)}, u32[]{:S(2)}, u32[]{:S(2)}) collective-permute-start(bf16[8,4096]{1,0:T(8,128)(2,1)S(1)} %copy-done.6), channel_id=1, source_target_pairs={{0,4},{1,5},{2,6},{3,7},{4,0},{5,1},{6,2},{7,3},{8,12},{9,13},{10,... | collective-permute-start | bytes 196616 | tf_op jit(solution)/shard_map/ppermute | solution.py:253
  16.8 0.0 copy-done.5
  16.8 2.4 %collective-permute-start.2 = (bf16[8,4096]{1,0:T(8,128)(2,1)S(1)}, bf16[8,4096]{1,0:T(8,128)(2,1)S(1)}, u32[]{:S(2)}, u32[]{:S(2)}) collective-permute-start(bf16[8,4096]{1,0:T(8,128)(2,1)S(1)} %copy-done.5), channel_id=1, source_target_pairs={{0,8},{1,9},{2,10},{3,11},{4,12},{5,13},{6,14},{7,15},{8,0},{9,1},... | collective-permute-start | bytes 196616 | tf_op jit(solution)/shard_map/ppermute | solution.py:253
  19.2 0.0 copy-done.4
  19.2 0.1 collective-permute-start.3
  19.3 0.0 copy-done.1
  19.3 2.1 %fresh.1 = (f32[4,8,4096]{2,1,0:T(8,128)S(1)}, f32[4,8,128]{2,1,0:T(8,128)S(1)}) custom-call(bf16[8,4096]{1,0:T(8,128)(2,1)S(1)} %copy-done.1, bf16[8,4096]{1,0:T(8,128)(2,1)S(1)} %copy-done.6, bf16[8,4096]{1,0:T(8,128)(2,1)S(1)} %copy-done.5, bf16[8,4096]{1,0:T(8,128)(2,1)S(1)} %copy-done.4, bf16[16,8,2048]{2,1,0:T(8,128)(2,1)} %key.1.refs_4_), custom_call_target="tpu_custom_call" | custom-call | tf_op jit(solution)/shard_map/fresh/pallas_call | solution.py:307
  21.4 5.0 %collective-permute-done.1.refs_1_ = bf16[8,4096]{1,0:T(8,128)(2,1)S(1)} collective-permute-done((bf16[8,4096]{1,0:T(8,128)(2,1)S(1)}, bf16[8,4096]{1,0:T(8,128)(2,1)S(1)}, u32[]{:S(2)}, u32[]{:S(2)}) %collective-permute-start.1) | collective-permute-done | bytes 65568 | tf_op jit(solution)/shard_map/ppermute | solution.py:253
  26.4 8.4 %collective-permute-done.2.refs_2_ = bf16[8,4096]{1,0:T(8,128)(2,1)S(1)} collective-permute-done((bf16[8,4096]{1,0:T(8,128)(2,1)S(1)}, bf16[8,4096]{1,0:T(8,128)(2,1)S(1)}, u32[]{:S(2)}, u32[]{:S(2)}) %collective-permute-start.2) | collective-permute-done | bytes 65568 | tf_op jit(solution)/shard_map/ppermute | solution.py:253
  34.7 0.0 collective-permute-done.3.refs_3_
  34.7 0.0 collective-permute-done.refs_6_
  34.7 0.0 copy-done
  34.8 0.1 collective-permute-start.4
  34.8 0.5 collective-permute-start.5
  35.3 1.4 %collective-permute-done.4.refs_5_ = bf16[8,128,256]{2,1,0:T(8,128)(2,1)S(1)} collective-permute-done((bf16[8,128,256]{2,1,0:T(8,128)(2,1)S(1)}, bf16[8,128,256]{2,1,0:T(8,128)(2,1)S(1)}, u32[]{:S(2)}, u32[]{:S(2)}) %collective-permute-start.4) | collective-permute-done | bytes 524320 | tf_op jit(solution)/shard_map/ppermute | solution.py:253
  36.7 0.7 %collective-permute-done.5.refs_7_ = bf16[8,128,256]{2,1,0:T(8,128)(2,1)S(1)} collective-permute-done((bf16[8,128,256]{2,1,0:T(8,128)(2,1)S(1)}, bf16[8,128,256]{2,1,0:T(8,128)(2,1)S(1)}, u32[]{:S(2)}, u32[]{:S(2)}) %collective-permute-start.5) | collective-permute-done | bytes 524320 | tf_op jit(solution)/shard_map/ppermute | solution.py:253
  37.5 1.5 %stale.1 = (bf16[8,4224]{1,0:T(8,128)(2,1)S(1)}, bf16[8,4224]{1,0:T(8,128)(2,1)S(1)}, bf16[8,4224]{1,0:T(8,128)(2,1)S(1)}, bf16[8,4224]{1,0:T(8,128)(2,1)S(1)}) custom-call(bf16[8,4096]{1,0:T(8,128)(2,1)S(1)} %copy-done.1, bf16[8,4096]{1,0:T(8,128)(2,1)S(1)} %collective-permute-done.1.refs_1_, bf16[8,4096]{1,0:T(8,128)(2,1)S(1)} %collective-permute-done.2.refs_2_, ...), custom_call_target="tpu_custom_call" | custom-call | tf_op jit(solution)/shard_map/stale/pallas_call | solution.py:322
  39.0 1.5 %collective-permute-start.6 = (bf16[8,4224]{1,0:T(8,128)(2,1)S(1)}, bf16[8,4224]{1,0:T(8,128)(2,1)S(1)}, u32[]{:S(2)}, u32[]{:S(2)}) collective-permute-start(bf16[8,4224]{1,0:T(8,128)(2,1)S(1)} %get-tuple-element.33), channel_id=1, source_target_pairs={{0,4},{1,5},{2,6},{3,7},{4,0},{5,1},{6,2},{7,3},{8,12},{9,13},{10,... | collective-permute-start | bytes 202760 | tf_op jit(solution)/shard_map/ppermute | solution.py:253
  40.5 0.6 %collective-permute-start.7 = (bf16[8,4224]{1,0:T(8,128)(2,1)S(1)}, bf16[8,4224]{1,0:T(8,128)(2,1)S(1)}, u32[]{:S(2)}, u32[]{:S(2)}) collective-permute-start(bf16[8,4224]{1,0:T(8,128)(2,1)S(1)} %get-tuple-element.34), channel_id=1, source_target_pairs={{0,8},{1,9},{2,10},{3,11},{4,12},{5,13},{6,14},{7,15},{8,0},{9,1},... | collective-permute-start | bytes 202760 | tf_op jit(solution)/shard_map/ppermute | solution.py:253
  41.1 2.3 %collective-permute-start.8 = (bf16[8,4224]{1,0:T(8,128)(2,1)S(1)}, bf16[8,4224]{1,0:T(8,128)(2,1)S(1)}, u32[]{:S(2)}, u32[]{:S(2)}) collective-permute-start(bf16[8,4224]{1,0:T(8,128)(2,1)S(1)} %get-tuple-element.35), channel_id=1, source_target_pairs={{0,12},{1,13},{2,14},{3,15},{4,8},{5,9},{6,10},{7,11},{8,4},{9,5},... | collective-permute-start | bytes 202760 | tf_op jit(solution)/shard_map/ppermute | solution.py:253
  43.4 0.0 all-to-all-done.got_ref
  43.4 0.8 %cache.1 = bf16[8,16,8,256]{3,2,1,0:T(8,128)(2,1)} custom-call(bf16[16,8,2048]{2,1,0:T(8,128)(2,1)S(1)} %all-to-all-done.got_ref), custom_call_target="tpu_custom_call" | custom-call | tf_op jit(solution)/shard_map/cache/pallas_call | solution.py:331
  44.3 0.0 collective-permute-done.6.refs_1_
  44.3 4.3 %collective-permute-done.7.refs_2_ = bf16[8,4224]{1,0:T(8,128)(2,1)S(1)} collective-permute-done((bf16[8,4224]{1,0:T(8,128)(2,1)S(1)}, bf16[8,4224]{1,0:T(8,128)(2,1)S(1)}, u32[]{:S(2)}, u32[]{:S(2)}) %collective-permute-start.7) | collective-permute-done | bytes 67616 | tf_op jit(solution)/shard_map/ppermute | solution.py:253
  48.6 0.0 collective-permute-done.8.refs_3_
  48.6 1.8 %join.1 = bf16[4,8,4096]{2,1,0:T(8,128)(2,1)} custom-call(bf16[8,4224]{1,0:T(8,128)(2,1)S(1)} %get-tuple-element.32.refs_0_, bf16[8,4224]{1,0:T(8,128)(2,1)S(1)} %collective-permute-done.6.refs_1_, bf16[8,4224]{1,0:T(8,128)(2,1)S(1)} %collective-permute-done.7.refs_2_, bf16[8,4224]{1,0:T(8,128)(2,1)S(1)} %collective-permute-done.8.refs_3_, ...), custom_call_target="tpu_custom_call" | custom-call | tf_op jit(solution)/shard_map/join/pallas_call | solution.py:340
Async XLA Ops:
  0.6 5.9 %copy-start.2 = (bf16[4,8,4096]{2,1,0:T(8,128)(2,1)S(1)}, bf16[4,8,4096]{2,1,0:T(8,128)(2,1)}, u32[]{:S(2)}) copy-start(bf16[4,8,4096]{2,1,0:T(8,128)(2,1)} %k_ref.1) | copy-start | bytes 786436
  0.6 34.1 %collective-permute-start = (bf16[8,128,256]{2,1,0:T(8,128)(2,1)}, bf16[8,128,256]{2,1,0:T(8,128)(2,1)S(1)}, u32[]{:S(2)}, u32[]{:S(2)}) collective-permute-start(bf16[8,128,256]{2,1,0:T(8,128)(2,1)} %refs_4_), channel_id=1, source_target_pairs={{0,2},{1,3},{2,0},{3,1},{4,6},{5,7},{6,4},{7,5},{8,10},{9,11},{10,... | collective-permute-start | bytes 1572872 | tf_op jit(solution)/shard_map/ppermute | solution.py:253
  3.6 2.9 %copy-start.7 = (f32[4096]{0:T(1024)S(1)}, f32[4096]{0:T(1024)}, u32[]{:S(2)}) copy-start(f32[4096]{0:T(1024)} %param.11) | copy-start | bytes 49156
  6.5 1.0 %copy-start.3 = (bf16[4,8,4096]{2,1,0:T(8,128)(2,1)S(1)}, bf16[4,8,4096]{2,1,0:T(8,128)(2,1)}, u32[]{:S(2)}) copy-start(bf16[4,8,4096]{2,1,0:T(8,128)(2,1)} %v_ref.1) | copy-start | bytes 786436
  7.5 0.7 %copy-start.8 = (f32[3,8,128]{2,1,0:T(8,128)S(1)}, f32[3,8,128]{2,1,0:T(8,128)}, u32[]{:S(2)}) copy-start(f32[3,8,128]{2,1,0:T(8,128)} %get-tuple-element.24.tables_ref) | copy-start | bytes 36868
  9.6 5.2 %copy-start.6 = (bf16[8,4096]{1,0:T(8,128)(2,1)S(1)}, bf16[8,4096]{1,0:T(8,128)(2,1)}, u32[]{:S(2)}) copy-start(bf16[8,4096]{1,0:T(8,128)(2,1)} %get-tuple-element.21.refs_1_) | copy-start | bytes 196612
  9.6 7.2 %copy-start.5 = (bf16[8,4096]{1,0:T(8,128)(2,1)S(1)}, bf16[8,4096]{1,0:T(8,128)(2,1)}, u32[]{:S(2)}) copy-start(bf16[8,4096]{1,0:T(8,128)(2,1)} %get-tuple-element.22.refs_2_) | copy-start | bytes 196612
  9.6 9.5 %copy-start.4 = (bf16[8,4096]{1,0:T(8,128)(2,1)S(1)}, bf16[8,4096]{1,0:T(8,128)(2,1)}, u32[]{:S(2)}) copy-start(bf16[8,4096]{1,0:T(8,128)(2,1)} %get-tuple-element.23.refs_3_) | copy-start | bytes 196612
  9.6 9.6 %copy-start.1 = (bf16[8,4096]{1,0:T(8,128)(2,1)S(1)}, bf16[8,4096]{1,0:T(8,128)(2,1)}, u32[]{:S(2)}) copy-start(bf16[8,4096]{1,0:T(8,128)(2,1)} %get-tuple-element.26.refs_0_) | copy-start | bytes 196612
  9.6 33.8 %all-to-all-start = ((bf16[16,8,2048]{2,1,0:T(8,128)(2,1)}), bf16[16,8,2048]{2,1,0:T(8,128)(2,1)S(1)}, u32[]{:S(2)}, u32[]{:S(2)}) async-start(bf16[16,8,2048]{2,1,0:T(8,128)(2,1)} %key.1.refs_4_), calls=%async_computation | async-start | bytes 1048576 | tf_op jit(solution)/shard_map/all_to_all | solution.py:306
  14.8 20.0 %copy-start = (bf16[8,128,256]{2,1,0:T(8,128)(2,1)S(1)}, bf16[8,128,256]{2,1,0:T(8,128)(2,1)}, u32[]{:S(2)}) copy-start(bf16[8,128,256]{2,1,0:T(8,128)(2,1)} %refs_4_) | copy-start | bytes 1572868
  14.8 11.6 %collective-permute-start.1 = (bf16[8,4096]{1,0:T(8,128)(2,1)S(1)}, bf16[8,4096]{1,0:T(8,128)(2,1)S(1)}, u32[]{:S(2)}, u32[]{:S(2)}) collective-permute-start(bf16[8,4096]{1,0:T(8,128)(2,1)S(1)} %copy-done.6), channel_id=1, source_target_pairs={{0,4},{1,5},{2,6},{3,7},{4,0},{5,1},{6,2},{7,3},{8,12},{9,13},{10,... | collective-permute-start | bytes 196616 | tf_op jit(solution)/shard_map/ppermute | solution.py:253
  16.8 18.0 %collective-permute-start.2 = (bf16[8,4096]{1,0:T(8,128)(2,1)S(1)}, bf16[8,4096]{1,0:T(8,128)(2,1)S(1)}, u32[]{:S(2)}, u32[]{:S(2)}) collective-permute-start(bf16[8,4096]{1,0:T(8,128)(2,1)S(1)} %copy-done.5), channel_id=1, source_target_pairs={{0,8},{1,9},{2,10},{3,11},{4,12},{5,13},{6,14},{7,15},{8,0},{9,1},... | collective-permute-start | bytes 196616 | tf_op jit(solution)/shard_map/ppermute | solution.py:253
  19.2 15.6 %collective-permute-start.3 = (bf16[8,4096]{1,0:T(8,128)(2,1)S(1)}, bf16[8,4096]{1,0:T(8,128)(2,1)S(1)}, u32[]{:S(2)}, u32[]{:S(2)}) collective-permute-start(bf16[8,4096]{1,0:T(8,128)(2,1)S(1)} %copy-done.4), channel_id=1, source_target_pairs={{0,12},{1,13},{2,14},{3,15},{4,8},{5,9},{6,10},{7,11},{8,4},{9,5},... | collective-permute-start | bytes 196616 | tf_op jit(solution)/shard_map/ppermute | solution.py:253
  34.8 2.0 %collective-permute-start.4 = (bf16[8,128,256]{2,1,0:T(8,128)(2,1)S(1)}, bf16[8,128,256]{2,1,0:T(8,128)(2,1)S(1)}, u32[]{:S(2)}, u32[]{:S(2)}) collective-permute-start(bf16[8,128,256]{2,1,0:T(8,128)(2,1)S(1)} %copy-done), channel_id=1, source_target_pairs={{0,1},{1,0},{2,3},{3,2},{4,5},{5,4},{6,7},{7,6},{8,9},{9,8},{10,11... | collective-permute-start | bytes 1572872 | tf_op jit(solution)/shard_map/ppermute | solution.py:253
  34.8 2.6 %collective-permute-start.5 = (bf16[8,128,256]{2,1,0:T(8,128)(2,1)S(1)}, bf16[8,128,256]{2,1,0:T(8,128)(2,1)S(1)}, u32[]{:S(2)}, u32[]{:S(2)}) collective-permute-start(bf16[8,128,256]{2,1,0:T(8,128)(2,1)S(1)} %collective-permute-done.refs_6_), channel_id=1, source_target_pairs={{0,1},{1,0},{2,3},{3,2},{4,5},{5,4},{6,7},{7,6},{8,9},{9,8},{10,11... | collective-permute-start | bytes 1572872 | tf_op jit(solution)/shard_map/ppermute | solution.py:253
  39.0 5.3 %collective-permute-start.6 = (bf16[8,4224]{1,0:T(8,128)(2,1)S(1)}, bf16[8,4224]{1,0:T(8,128)(2,1)S(1)}, u32[]{:S(2)}, u32[]{:S(2)}) collective-permute-start(bf16[8,4224]{1,0:T(8,128)(2,1)S(1)} %get-tuple-element.33), channel_id=1, source_target_pairs={{0,4},{1,5},{2,6},{3,7},{4,0},{5,1},{6,2},{7,3},{8,12},{9,13},{10,... | collective-permute-start | bytes 202760 | tf_op jit(solution)/shard_map/ppermute | solution.py:253
  40.5 8.1 %collective-permute-start.7 = (bf16[8,4224]{1,0:T(8,128)(2,1)S(1)}, bf16[8,4224]{1,0:T(8,128)(2,1)S(1)}, u32[]{:S(2)}, u32[]{:S(2)}) collective-permute-start(bf16[8,4224]{1,0:T(8,128)(2,1)S(1)} %get-tuple-element.34), channel_id=1, source_target_pairs={{0,8},{1,9},{2,10},{3,11},{4,12},{5,13},{6,14},{7,15},{8,0},{9,1},... | collective-permute-start | bytes 202760 | tf_op jit(solution)/shard_map/ppermute | solution.py:253
  41.1 7.5 %collective-permute-start.8 = (bf16[8,4224]{1,0:T(8,128)(2,1)S(1)}, bf16[8,4224]{1,0:T(8,128)(2,1)S(1)}, u32[]{:S(2)}, u32[]{:S(2)}) collective-permute-start(bf16[8,4224]{1,0:T(8,128)(2,1)S(1)} %get-tuple-element.35), channel_id=1, source_target_pairs={{0,12},{1,13},{2,14},{3,15},{4,8},{5,9},{6,10},{7,11},{8,4},{9,5},... | collective-permute-start | bytes 202760 | tf_op jit(solution)/shard_map/ppermute | solution.py:253

commit v5 on v4

--- a/solution.py
+++ b/solution.py
@@ -323,6 +323,7 @@
         functools.partial(stale_kernel, groups, videos),
         "stale",
         32,
+        cost=36 * MIB,
         out_shape=[jax.ShapeDtypeStruct((tok_rows, width + DH), BF16)] * videos,
         in_specs=[VMEM] * (videos + groups),
         out_specs=[VMEM] * videos,

time: 50.7 us -> 50.7 us (level)
  no operation moved by 1% of the time
where the time goes in v5:
time: 50.7 us; the launch traced here: 50.3 us
  waiting for transfers between devices  19.8 us (39%)
  starting transfers between devices  17.6 us (35%)
  Pallas kernels  10.6 us (21%)
  local copies, waits for them, and re-layouts  1.68 us (3%)
  between operations  0.75 us (1%)
    ppermute x9, waiting for transfers between devices, permuted(): lax.ppermute(array, 'patch', [(i, i ^ offset) for i in range(patches)])  19.8 us
    ppermute x9, starting transfers between devices, permuted(): lax.ppermute(array, 'patch', [(i, i ^ offset) for i in range(patches)])  12.4 us
    all_to_all x1, starting transfers between devices, local(): lax.all_to_all(fresh, 'patch', split_axis=0, concat_axis=0, tiled=True)  5.13 us
    pallas_call x1, Pallas kernels, local(): kernel(functools.partial(query_kernel, groups), 'query', 56, out_shape=[r...  2.87 us
    pallas_call x1, Pallas kernels, local(): kernel(functools.partial(fresh_kernel, groups, videos), 'fresh', 16, out_...  2.15 us
    pallas_call x1, Pallas kernels, local(): kernel(functools.partial(join_kernel, groups, videos), 'join', 16, out_sh...  1.77 us
    unnamed x18, local copies, waits for them, and re-layouts  1.68 us
    pallas_call x1, Pallas kernels, local(): kernel(functools.partial(stale_kernel, groups, videos), 'stale', 32, cost...  1.52 us
  transfers between devices with their start and end apart: 10, of which 5 were waited for; matrix products, arithmetic and copies ran while one was open for 0% of the time, Pallas kernels for 18%

profile of v5, /device:TPU:0, one launch (start us, length us, event | category | flops | bytes accessed | tf_op | source)
XLA Modules:
  0.0 50.3 jit_solution(8942739421545285694)
XLA Ops:
  0.6 0.0 copy-start.2
  0.6 3.0 %collective-permute-start = (bf16[8,128,256]{2,1,0:T(8,128)(2,1)}, bf16[8,128,256]{2,1,0:T(8,128)(2,1)S(1)}, u32[]{:S(2)}, u32[]{:S(2)}) collective-permute-start(bf16[8,128,256]{2,1,0:T(8,128)(2,1)} %refs_4_), channel_id=1, source_target_pairs={{0,2},{1,3},{2,0},{3,1},{4,6},{5,7},{6,4},{7,5},{8,10},{9,11},{10,... | collective-permute-start | bytes 1572872 | tf_op jit(solution)/shard_map/ppermute | solution.py:253
  3.6 0.0 copy-start.7
  3.6 2.9 %query.1 = (bf16[8,4096]{1,0:T(8,128)(2,1)}, bf16[8,4096]{1,0:T(8,128)(2,1)}, bf16[8,4096]{1,0:T(8,128)(2,1)}, bf16[8,4096]{1,0:T(8,128)(2,1)}, f32[3,8,128]{2,1,0:T(8,128)}) custom-call(bf16[4,8,4096]{2,1,0:T(8,128)(2,1)} %q_hbm.1, f32[1,4096]{1,0:T(1,128)} %bitcast.5, s32[3,8]{1,0:T(4,128)} %coords_hbm.1), custom_call_target="tpu_custom_call" | custom-call | tf_op jit(solution)/shard_map/query/pallas_call | solution.py:281
  6.5 0.0 copy-done.2
  6.5 0.0 copy-done.7
  6.5 0.0 copy-start.3
  6.6 0.9 %copy-done.3 = bf16[4,8,4096]{2,1,0:T(8,128)(2,1)S(1)} copy-done((bf16[4,8,4096]{2,1,0:T(8,128)(2,1)S(1)}, bf16[4,8,4096]{2,1,0:T(8,128)(2,1)}, u32[]{:S(2)}) %copy-start.3) | copy-done | bytes 262168
  7.5 0.0 copy-start.8
  7.5 0.7 %copy-done.8 = f32[3,8,128]{2,1,0:T(8,128)S(1)} copy-done((f32[3,8,128]{2,1,0:T(8,128)S(1)}, f32[3,8,128]{2,1,0:T(8,128)}, u32[]{:S(2)}) %copy-start.8) | copy-done | bytes 12312
  8.2 1.4 %key.1.refs_4_ = bf16[16,8,2048]{2,1,0:T(8,128)(2,1)} custom-call(bf16[4,8,4096]{2,1,0:T(8,128)(2,1)S(1)} %copy-done.2, bf16[4,8,4096]{2,1,0:T(8,128)(2,1)S(1)} %copy-done.3, f32[1,4096]{1,0:T(1,128)S(1)} %bitcast.3, f32[3,8,128]{2,1,0:T(8,128)S(1)} %copy-done.8), custom_call_target="tpu_custom_call" | custom-call | tf_op jit(solution)/shard_map/key/pallas_call | solution.py:298
  9.6 0.0 copy-start.6
  9.6 0.0 copy-start.5
  9.6 0.0 copy-start.4
  9.6 0.0 copy-start.1
  9.6 5.1 %all-to-all-start = ((bf16[16,8,2048]{2,1,0:T(8,128)(2,1)}), bf16[16,8,2048]{2,1,0:T(8,128)(2,1)S(1)}, u32[]{:S(2)}, u32[]{:S(2)}) async-start(bf16[16,8,2048]{2,1,0:T(8,128)(2,1)} %key.1.refs_4_), calls=%async_computation | async-start | bytes 1048576 | tf_op jit(solution)/shard_map/all_to_all | solution.py:306
  14.8 0.0 copy-start
  14.8 0.0 copy-done.6
  14.8 2.0 %collective-permute-start.1 = (bf16[8,4096]{1,0:T(8,128)(2,1)S(1)}, bf16[8,4096]{1,0:T(8,128)(2,1)S(1)}, u32[]{:S(2)}, u32[]{:S(2)}) collective-permute-start(bf16[8,4096]{1,0:T(8,128)(2,1)S(1)} %copy-done.6), channel_id=1, source_target_pairs={{0,4},{1,5},{2,6},{3,7},{4,0},{5,1},{6,2},{7,3},{8,12},{9,13},{10,... | collective-permute-start | bytes 196616 | tf_op jit(solution)/shard_map/ppermute | solution.py:253
  16.8 0.0 copy-done.5
  16.8 2.4 %collective-permute-start.2 = (bf16[8,4096]{1,0:T(8,128)(2,1)S(1)}, bf16[8,4096]{1,0:T(8,128)(2,1)S(1)}, u32[]{:S(2)}, u32[]{:S(2)}) collective-permute-start(bf16[8,4096]{1,0:T(8,128)(2,1)S(1)} %copy-done.5), channel_id=1, source_target_pairs={{0,8},{1,9},{2,10},{3,11},{4,12},{5,13},{6,14},{7,15},{8,0},{9,1},... | collective-permute-start | bytes 196616 | tf_op jit(solution)/shard_map/ppermute | solution.py:253
  19.2 0.0 copy-done.4
  19.2 0.1 collective-permute-start.3
  19.3 0.0 copy-done.1
  19.3 2.1 %fresh.1 = (f32[4,8,4096]{2,1,0:T(8,128)S(1)}, f32[4,8,128]{2,1,0:T(8,128)S(1)}) custom-call(bf16[8,4096]{1,0:T(8,128)(2,1)S(1)} %copy-done.1, bf16[8,4096]{1,0:T(8,128)(2,1)S(1)} %copy-done.6, bf16[8,4096]{1,0:T(8,128)(2,1)S(1)} %copy-done.5, bf16[8,4096]{1,0:T(8,128)(2,1)S(1)} %copy-done.4, bf16[16,8,2048]{2,1,0:T(8,128)(2,1)} %key.1.refs_4_), custom_call_target="tpu_custom_call" | custom-call | tf_op jit(solution)/shard_map/fresh/pallas_call | solution.py:307
  21.4 5.0 %collective-permute-done.1.refs_1_ = bf16[8,4096]{1,0:T(8,128)(2,1)S(1)} collective-permute-done((bf16[8,4096]{1,0:T(8,128)(2,1)S(1)}, bf16[8,4096]{1,0:T(8,128)(2,1)S(1)}, u32[]{:S(2)}, u32[]{:S(2)}) %collective-permute-start.1) | collective-permute-done | bytes 65568 | tf_op jit(solution)/shard_map/ppermute | solution.py:253
  26.4 8.4 %collective-permute-done.2.refs_2_ = bf16[8,4096]{1,0:T(8,128)(2,1)S(1)} collective-permute-done((bf16[8,4096]{1,0:T(8,128)(2,1)S(1)}, bf16[8,4096]{1,0:T(8,128)(2,1)S(1)}, u32[]{:S(2)}, u32[]{:S(2)}) %collective-permute-start.2) | collective-permute-done | bytes 65568 | tf_op jit(solution)/shard_map/ppermute | solution.py:253
  34.7 0.0 collective-permute-done.3.refs_3_
  34.7 0.0 collective-permute-done.refs_6_
  34.7 0.0 copy-done
  34.8 0.1 collective-permute-start.4
  34.8 0.5 collective-permute-start.5
  35.3 1.4 %collective-permute-done.4.refs_5_ = bf16[8,128,256]{2,1,0:T(8,128)(2,1)S(1)} collective-permute-done((bf16[8,128,256]{2,1,0:T(8,128)(2,1)S(1)}, bf16[8,128,256]{2,1,0:T(8,128)(2,1)S(1)}, u32[]{:S(2)}, u32[]{:S(2)}) %collective-permute-start.4) | collective-permute-done | bytes 524320 | tf_op jit(solution)/shard_map/ppermute | solution.py:253
  36.7 0.7 %collective-permute-done.5.refs_7_ = bf16[8,128,256]{2,1,0:T(8,128)(2,1)S(1)} collective-permute-done((bf16[8,128,256]{2,1,0:T(8,128)(2,1)S(1)}, bf16[8,128,256]{2,1,0:T(8,128)(2,1)S(1)}, u32[]{:S(2)}, u32[]{:S(2)}) %collective-permute-start.5) | collective-permute-done | bytes 524320 | tf_op jit(solution)/shard_map/ppermute | solution.py:253
  37.5 1.5 %stale.1 = (bf16[8,4224]{1,0:T(8,128)(2,1)S(1)}, bf16[8,4224]{1,0:T(8,128)(2,1)S(1)}, bf16[8,4224]{1,0:T(8,128)(2,1)S(1)}, bf16[8,4224]{1,0:T(8,128)(2,1)S(1)}) custom-call(bf16[8,4096]{1,0:T(8,128)(2,1)S(1)} %copy-done.1, bf16[8,4096]{1,0:T(8,128)(2,1)S(1)} %collective-permute-done.1.refs_1_, bf16[8,4096]{1,0:T(8,128)(2,1)S(1)} %collective-permute-done.2.refs_2_, ...), custom_call_target="tpu_custom_call" | custom-call | bytes 37748736 | tf_op jit(solution)/shard_map/stale/pallas_call | solution.py:322
  39.0 1.5 %collective-permute-start.6 = (bf16[8,4224]{1,0:T(8,128)(2,1)S(1)}, bf16[8,4224]{1,0:T(8,128)(2,1)S(1)}, u32[]{:S(2)}, u32[]{:S(2)}) collective-permute-start(bf16[8,4224]{1,0:T(8,128)(2,1)S(1)} %get-tuple-element.33), channel_id=1, source_target_pairs={{0,4},{1,5},{2,6},{3,7},{4,0},{5,1},{6,2},{7,3},{8,12},{9,13},{10,... | collective-permute-start | bytes 202760 | tf_op jit(solution)/shard_map/ppermute | solution.py:253
  40.5 0.6 %collective-permute-start.7 = (bf16[8,4224]{1,0:T(8,128)(2,1)S(1)}, bf16[8,4224]{1,0:T(8,128)(2,1)S(1)}, u32[]{:S(2)}, u32[]{:S(2)}) collective-permute-start(bf16[8,4224]{1,0:T(8,128)(2,1)S(1)} %get-tuple-element.34), channel_id=1, source_target_pairs={{0,8},{1,9},{2,10},{3,11},{4,12},{5,13},{6,14},{7,15},{8,0},{9,1},... | collective-permute-start | bytes 202760 | tf_op jit(solution)/shard_map/ppermute | solution.py:253
  41.1 2.3 %collective-permute-start.8 = (bf16[8,4224]{1,0:T(8,128)(2,1)S(1)}, bf16[8,4224]{1,0:T(8,128)(2,1)S(1)}, u32[]{:S(2)}, u32[]{:S(2)}) collective-permute-start(bf16[8,4224]{1,0:T(8,128)(2,1)S(1)} %get-tuple-element.35), channel_id=1, source_target_pairs={{0,12},{1,13},{2,14},{3,15},{4,8},{5,9},{6,10},{7,11},{8,4},{9,5},... | collective-permute-start | bytes 202760 | tf_op jit(solution)/shard_map/ppermute | solution.py:253
  43.4 0.0 all-to-all-done.got_ref
  43.4 0.8 %cache.1 = bf16[8,16,8,256]{3,2,1,0:T(8,128)(2,1)} custom-call(bf16[16,8,2048]{2,1,0:T(8,128)(2,1)S(1)} %all-to-all-done.got_ref), custom_call_target="tpu_custom_call" | custom-call | tf_op jit(solution)/shard_map/cache/pallas_call | solution.py:332
  44.3 0.0 collective-permute-done.6.refs_1_
  44.3 4.3 %collective-permute-done.7.refs_2_ = bf16[8,4224]{1,0:T(8,128)(2,1)S(1)} collective-permute-done((bf16[8,4224]{1,0:T(8,128)(2,1)S(1)}, bf16[8,4224]{1,0:T(8,128)(2,1)S(1)}, u32[]{:S(2)}, u32[]{:S(2)}) %collective-permute-start.7) | collective-permute-done | bytes 67616 | tf_op jit(solution)/shard_map/ppermute | solution.py:253
  48.6 0.0 collective-permute-done.8.refs_3_
  48.6 1.8 %join.1 = bf16[4,8,4096]{2,1,0:T(8,128)(2,1)} custom-call(bf16[8,4224]{1,0:T(8,128)(2,1)S(1)} %get-tuple-element.32.refs_0_, bf16[8,4224]{1,0:T(8,128)(2,1)S(1)} %collective-permute-done.6.refs_1_, bf16[8,4224]{1,0:T(8,128)(2,1)S(1)} %collective-permute-done.7.refs_2_, bf16[8,4224]{1,0:T(8,128)(2,1)S(1)} %collective-permute-done.8.refs_3_, ...), custom_call_target="tpu_custom_call" | custom-call | tf_op jit(solution)/shard_map/join/pallas_call | solution.py:341
Async XLA Ops:
  0.6 5.9 %copy-start.2 = (bf16[4,8,4096]{2,1,0:T(8,128)(2,1)S(1)}, bf16[4,8,4096]{2,1,0:T(8,128)(2,1)}, u32[]{:S(2)}) copy-start(bf16[4,8,4096]{2,1,0:T(8,128)(2,1)} %k_ref.1) | copy-start | bytes 786436
  0.6 34.1 %collective-permute-start = (bf16[8,128,256]{2,1,0:T(8,128)(2,1)}, bf16[8,128,256]{2,1,0:T(8,128)(2,1)S(1)}, u32[]{:S(2)}, u32[]{:S(2)}) collective-permute-start(bf16[8,128,256]{2,1,0:T(8,128)(2,1)} %refs_4_), channel_id=1, source_target_pairs={{0,2},{1,3},{2,0},{3,1},{4,6},{5,7},{6,4},{7,5},{8,10},{9,11},{10,... | collective-permute-start | bytes 1572872 | tf_op jit(solution)/shard_map/ppermute | solution.py:253
  3.6 2.9 %copy-start.7 = (f32[4096]{0:T(1024)S(1)}, f32[4096]{0:T(1024)}, u32[]{:S(2)}) copy-start(f32[4096]{0:T(1024)} %param.11) | copy-start | bytes 49156
  6.5 1.0 %copy-start.3 = (bf16[4,8,4096]{2,1,0:T(8,128)(2,1)S(1)}, bf16[4,8,4096]{2,1,0:T(8,128)(2,1)}, u32[]{:S(2)}) copy-start(bf16[4,8,4096]{2,1,0:T(8,128)(2,1)} %v_ref.1) | copy-start | bytes 786436
  7.5 0.7 %copy-start.8 = (f32[3,8,128]{2,1,0:T(8,128)S(1)}, f32[3,8,128]{2,1,0:T(8,128)}, u32[]{:S(2)}) copy-start(f32[3,8,128]{2,1,0:T(8,128)} %get-tuple-element.24.tables_ref) | copy-start | bytes 36868
  9.6 5.2 %copy-start.6 = (bf16[8,4096]{1,0:T(8,128)(2,1)S(1)}, bf16[8,4096]{1,0:T(8,128)(2,1)}, u32[]{:S(2)}) copy-start(bf16[8,4096]{1,0:T(8,128)(2,1)} %get-tuple-element.21.refs_1_) | copy-start | bytes 196612
  9.6 7.2 %copy-start.5 = (bf16[8,4096]{1,0:T(8,128)(2,1)S(1)}, bf16[8,4096]{1,0:T(8,128)(2,1)}, u32[]{:S(2)}) copy-start(bf16[8,4096]{1,0:T(8,128)(2,1)} %get-tuple-element.22.refs_2_) | copy-start | bytes 196612
  9.6 9.5 %copy-start.4 = (bf16[8,4096]{1,0:T(8,128)(2,1)S(1)}, bf16[8,4096]{1,0:T(8,128)(2,1)}, u32[]{:S(2)}) copy-start(bf16[8,4096]{1,0:T(8,128)(2,1)} %get-tuple-element.23.refs_3_) | copy-start | bytes 196612
  9.6 9.6 %copy-start.1 = (bf16[8,4096]{1,0:T(8,128)(2,1)S(1)}, bf16[8,4096]{1,0:T(8,128)(2,1)}, u32[]{:S(2)}) copy-start(bf16[8,4096]{1,0:T(8,128)(2,1)} %get-tuple-element.26.refs_0_) | copy-start | bytes 196612
  9.6 33.8 %all-to-all-start = ((bf16[16,8,2048]{2,1,0:T(8,128)(2,1)}), bf16[16,8,2048]{2,1,0:T(8,128)(2,1)S(1)}, u32[]{:S(2)}, u32[]{:S(2)}) async-start(bf16[16,8,2048]{2,1,0:T(8,128)(2,1)} %key.1.refs_4_), calls=%async_computation | async-start | bytes 1048576 | tf_op jit(solution)/shard_map/all_to_all | solution.py:306
  14.8 20.0 %copy-start = (bf16[8,128,256]{2,1,0:T(8,128)(2,1)S(1)}, bf16[8,128,256]{2,1,0:T(8,128)(2,1)}, u32[]{:S(2)}) copy-start(bf16[8,128,256]{2,1,0:T(8,128)(2,1)} %refs_4_) | copy-start | bytes 1572868
  14.8 11.6 %collective-permute-start.1 = (bf16[8,4096]{1,0:T(8,128)(2,1)S(1)}, bf16[8,4096]{1,0:T(8,128)(2,1)S(1)}, u32[]{:S(2)}, u32[]{:S(2)}) collective-permute-start(bf16[8,4096]{1,0:T(8,128)(2,1)S(1)} %copy-done.6), channel_id=1, source_target_pairs={{0,4},{1,5},{2,6},{3,7},{4,0},{5,1},{6,2},{7,3},{8,12},{9,13},{10,... | collective-permute-start | bytes 196616 | tf_op jit(solution)/shard_map/ppermute | solution.py:253
  16.8 18.0 %collective-permute-start.2 = (bf16[8,4096]{1,0:T(8,128)(2,1)S(1)}, bf16[8,4096]{1,0:T(8,128)(2,1)S(1)}, u32[]{:S(2)}, u32[]{:S(2)}) collective-permute-start(bf16[8,4096]{1,0:T(8,128)(2,1)S(1)} %copy-done.5), channel_id=1, source_target_pairs={{0,8},{1,9},{2,10},{3,11},{4,12},{5,13},{6,14},{7,15},{8,0},{9,1},... | collective-permute-start | bytes 196616 | tf_op jit(solution)/shard_map/ppermute | solution.py:253
  19.2 15.6 %collective-permute-start.3 = (bf16[8,4096]{1,0:T(8,128)(2,1)S(1)}, bf16[8,4096]{1,0:T(8,128)(2,1)S(1)}, u32[]{:S(2)}, u32[]{:S(2)}) collective-permute-start(bf16[8,4096]{1,0:T(8,128)(2,1)S(1)} %copy-done.4), channel_id=1, source_target_pairs={{0,12},{1,13},{2,14},{3,15},{4,8},{5,9},{6,10},{7,11},{8,4},{9,5},... | collective-permute-start | bytes 196616 | tf_op jit(solution)/shard_map/ppermute | solution.py:253
  34.8 2.0 %collective-permute-start.4 = (bf16[8,128,256]{2,1,0:T(8,128)(2,1)S(1)}, bf16[8,128,256]{2,1,0:T(8,128)(2,1)S(1)}, u32[]{:S(2)}, u32[]{:S(2)}) collective-permute-start(bf16[8,128,256]{2,1,0:T(8,128)(2,1)S(1)} %copy-done), channel_id=1, source_target_pairs={{0,1},{1,0},{2,3},{3,2},{4,5},{5,4},{6,7},{7,6},{8,9},{9,8},{10,11... | collective-permute-start | bytes 1572872 | tf_op jit(solution)/shard_map/ppermute | solution.py:253
  34.8 2.6 %collective-permute-start.5 = (bf16[8,128,256]{2,1,0:T(8,128)(2,1)S(1)}, bf16[8,128,256]{2,1,0:T(8,128)(2,1)S(1)}, u32[]{:S(2)}, u32[]{:S(2)}) collective-permute-start(bf16[8,128,256]{2,1,0:T(8,128)(2,1)S(1)} %collective-permute-done.refs_6_), channel_id=1, source_target_pairs={{0,1},{1,0},{2,3},{3,2},{4,5},{5,4},{6,7},{7,6},{8,9},{9,8},{10,11... | collective-permute-start | bytes 1572872 | tf_op jit(solution)/shard_map/ppermute | solution.py:253
  39.0 5.3 %collective-permute-start.6 = (bf16[8,4224]{1,0:T(8,128)(2,1)S(1)}, bf16[8,4224]{1,0:T(8,128)(2,1)S(1)}, u32[]{:S(2)}, u32[]{:S(2)}) collective-permute-start(bf16[8,4224]{1,0:T(8,128)(2,1)S(1)} %get-tuple-element.33), channel_id=1, source_target_pairs={{0,4},{1,5},{2,6},{3,7},{4,0},{5,1},{6,2},{7,3},{8,12},{9,13},{10,... | collective-permute-start | bytes 202760 | tf_op jit(solution)/shard_map/ppermute | solution.py:253
  40.5 8.1 %collective-permute-start.7 = (bf16[8,4224]{1,0:T(8,128)(2,1)S(1)}, bf16[8,4224]{1,0:T(8,128)(2,1)S(1)}, u32[]{:S(2)}, u32[]{:S(2)}) collective-permute-start(bf16[8,4224]{1,0:T(8,128)(2,1)S(1)} %get-tuple-element.34), channel_id=1, source_target_pairs={{0,8},{1,9},{2,10},{3,11},{4,12},{5,13},{6,14},{7,15},{8,0},{9,1},... | collective-permute-start | bytes 202760 | tf_op jit(solution)/shard_map/ppermute | solution.py:253
  41.1 7.5 %collective-permute-start.8 = (bf16[8,4224]{1,0:T(8,128)(2,1)S(1)}, bf16[8,4224]{1,0:T(8,128)(2,1)S(1)}, u32[]{:S(2)}, u32[]{:S(2)}) collective-permute-start(bf16[8,4224]{1,0:T(8,128)(2,1)S(1)} %get-tuple-element.35), channel_id=1, source_target_pairs={{0,12},{1,13},{2,14},{3,15},{4,8},{5,9},{6,10},{7,11},{8,4},{9,5},... | collective-permute-start | bytes 202760 | tf_op jit(solution)/shard_map/ppermute | solution.py:253

commit v6 on v4

--- a/solution.py
+++ b/solution.py
@@ -81,19 +81,15 @@
         send.wait()
 
 
-def key_kernel(k_ref, v_ref, gain_ref, tables_ref, out_ref):
-    videos, tok_rows, width = k_ref.shape
+def key_kernel(k_ref, gain_ref, tables_ref, out_ref):
+    videos = k_ref.shape[0]
     tables = [tables_ref[i] for i in range(3)]
-    span = out_ref.shape[2]
     groups = out_ref.shape[0] // videos
-    pairs = span // (2 * DH)
+    pairs = out_ref.shape[2] // DH
     for video in range(videos):
         for head, y in normed_heads(k_ref[video].astype(F32), gain_ref, tables):
-            target, start = video * groups + head // pairs, head % pairs * 2 * DH
-            out_ref[target, :, start : start + DH] = y
-            out_ref[target, :, start + DH : start + 2 * DH] = v_ref[
-                video, :, head * DH : (head + 1) * DH
-            ]
+            start = head % pairs * DH
+            out_ref[video * groups + head // pairs, :, start : start + DH] = y
 
 
 def softmax_parts(scores):
@@ -109,7 +105,8 @@
 
 
 def fresh_kernel(groups, videos, *refs):
-    queries, fresh_ref, out_ref, log_ref = refs[:videos], refs[videos], refs[videos + 1], refs[videos + 2]
+    queries = refs[:videos]
+    key_ref, value_ref, out_ref, log_ref = refs[videos:]
     own = lax.axis_index("patch") // groups
     _, tok_rows, width = out_ref.shape
     span = width // groups
@@ -124,14 +121,14 @@
     logs = jnp.zeros((rows, DH), F32)
     for group in range(groups):
         query = stacked(queries, slice(group * span, (group + 1) * span))
-        fresh = jnp.concatenate(
-            [fresh_ref[(own ^ s) * groups + group].astype(F32) for s in range(videos)], axis=0
-        ).astype(BF16)
+        lanes = slice(group * span, (group + 1) * span)
+        key = stacked([key_ref.at[(own ^ s) * groups + group] for s in range(videos)], slice(None))
+        value = stacked([value_ref.at[own ^ s] for s in range(videos)], lanes)
         scores = jnp.concatenate(
             [
                 lax.dot_general(
                     query[:, pair * DH : (pair + 1) * DH],
-                    fresh[:, 2 * pair * DH : (2 * pair + 1) * DH],
+                    key[:, pair * DH : (pair + 1) * DH],
                     TRANSPOSED,
                     preferred_element_type=F32,
                 )
@@ -145,7 +142,7 @@
             head = group * pairs + pair
             result = inverse[here] * jnp.dot(
                 weights[here],
-                fresh[:, (2 * pair + 1) * DH : (2 * pair + 2) * DH],
+                value[:, pair * DH : (pair + 1) * DH],
                 preferred_element_type=F32,
             )
             logs = jnp.where(lane == head, log[here], logs)
@@ -237,14 +234,18 @@
         copy.wait()
 
 
-def cache_kernel(got_ref, out_ref, sems):
+def cache_kernel(key_ref, value_ref, out_ref, sems):
     copies = []
     for pair in range(out_ref.shape[0]):
-        lanes = pl.ds(2 * pair * DH, 2 * DH)
-        copies.append(
-            pltpu.make_async_copy(got_ref.at[:, :, lanes], out_ref.at[pair], sems.at[pair])
-        )
-        copies[-1].start()
+        for part, ref in enumerate((key_ref, value_ref)):
+            copies.append(
+                pltpu.make_async_copy(
+                    ref.at[:, :, pl.ds(pair * DH, DH)],
+                    out_ref.at[pair, :, :, pl.ds(part * DH, DH)],
+                    sems.at[part, pair],
+                )
+            )
+            copies[-1].start()
     for copy in copies:
         copy.wait()
 
@@ -275,6 +276,10 @@
             **kwargs,
         )
 
+    value_sent = jnp.transpose(
+        values.reshape(videos, tok_rows, groups, pairs_here * DH), (0, 2, 1, 3)
+    ).reshape(patches, tok_rows, pairs_here * DH)
+    value_got = lax.all_to_all(value_sent, "patch", split_axis=0, concat_axis=0, tiled=True)
     pieces = {0: stale_cache}
     bit = groups // 2
     pieces[bit] = permuted(stale_cache, bit, patches)
@@ -295,15 +300,16 @@
         ],
     )(queries, q_gain.reshape(1, width), coords)
     query_got = exchange(query, groups, patches)
-    fresh = kernel(
+    key = kernel(
         key_kernel,
         "key",
         16,
-        out_shape=jax.ShapeDtypeStruct((patches, tok_rows, 2 * pairs_here * DH), BF16),
-        in_specs=[VMEM] * 4,
+        out_shape=jax.ShapeDtypeStruct((patches, tok_rows, pairs_here * DH), BF16),
+        in_specs=[VMEM] * 3,
         out_specs=VMEM,
-    )(keys, values, k_gain.reshape(1, width), tables)
-    cached = lax.all_to_all(fresh, "patch", split_axis=0, concat_axis=0, tiled=True)
+    )(keys, k_gain.reshape(1, width), tables)
+    key_sent, query_got = lax.optimization_barrier((key, query_got))
+    key_got = lax.all_to_all(key_sent, "patch", split_axis=0, concat_axis=0, tiled=True)
     fresh_sum, fresh_log = kernel(
         functools.partial(fresh_kernel, groups, videos),
         "fresh",
@@ -312,9 +318,9 @@
             jax.ShapeDtypeStruct((videos, tok_rows, width), F32),
             jax.ShapeDtypeStruct((videos, tok_rows, DH), F32),
         ),
-        in_specs=[VMEM] * (videos + 1),
+        in_specs=[VMEM] * (videos + 2),
         out_specs=(VMEM, VMEM),
-    )(*query, fresh)
+    )(*query, key, values)
     pieces, query_got, fresh_log = lax.optimization_barrier((pieces, query_got, fresh_log))
     while bit > 1:
         bit //= 2
@@ -333,10 +339,10 @@
         "cache",
         16,
         out_shape=jax.ShapeDtypeStruct((pairs_here, patches, tok_rows, 2 * DH), BF16),
-        in_specs=[VMEM],
+        in_specs=[VMEM, VMEM],
         out_specs=HBM,
-        scratch_shapes=[pltpu.SemaphoreType.DMA((pairs_here,))],
-    )(cached)
+        scratch_shapes=[pltpu.SemaphoreType.DMA((2, pairs_here))],
+    )(key_got, value_got)
     attended = kernel(
         functools.partial(join_kernel, groups, videos),
         "join",

time: 50.7 us -> 45.9 us (0.905)
  waiting for transfers between devices: 19.8 us -> 9.65 us
  starting transfers between devices: 17.6 us -> 21.4 us
  other arithmetic: 0 us -> 0.72 us
  Pallas kernels: 10.6 us -> 11.2 us
    ppermute x9, waiting for transfers between devices: 19.8 us -> 5.75 us  [permuted(): lax.ppermute(array, 'patch', [(i, i ^ offset) for i in range(patches)])]
    all_to_all x1 -> x2, waiting for transfers between devices: 0.01 us -> 3.89 us  [the longest x1 3.89 us: local(): lax.all_to_all(key_sent, 'patch', split_axis=0, concat_axis=0, tiled=True)]
    all_to_all x1 -> x2, starting transfers between devices: 5.13 us -> 8.95 us  [the longest x1 4.98 us: local(): lax.all_to_all(value_sent, 'patch', split_axis=0, concat_axis=0, tiled=True)]
    slice x0 -> x1, local copies, waits for them, and re-layouts: none -> 0.95 us
    unnamed x18, local copies, waits for them, and re-layouts: 1.68 us -> 0.74 us
    concatenate x0 -> x1, other arithmetic: none -> 0.72 us
    pallas_call x1, Pallas kernels: 1.52 us -> 2.22 us  [local(): kernel(functools.partial(stale_kernel, groups, videos), 'stale', 32, out_...]
  transfers between devices with their start and end apart: 10 -> 11, of which waited for: 5 -> 3; matrix products, arithmetic and copies ran while one was open for 0% -> 4% of each run, Pallas kernels for 18% -> 21%
where the time goes in v6:
time: 45.9 us; the launch traced here: 45.4 us
  starting transfers between devices  21.4 us (47%)
  Pallas kernels  11.2 us (24%)
  waiting for transfers between devices  9.65 us (21%)
  local copies, waits for them, and re-layouts  1.7 us (4%)
  between operations  0.77 us (2%)
  other arithmetic  0.72 us (2%)
    ppermute x9, starting transfers between devices, permuted(): lax.ppermute(array, 'patch', [(i, i ^ offset) for i in range(patches)])  12.4 us
    ppermute x9, waiting for transfers between devices, permuted(): lax.ppermute(array, 'patch', [(i, i ^ offset) for i in range(patches)])  5.75 us
    all_to_all x1, starting transfers between devices, local(): lax.all_to_all(value_sent, 'patch', split_axis=0, concat_axis=0, tiled=True)  4.98 us
    all_to_all x1, starting transfers between devices, local(): lax.all_to_all(key_sent, 'patch', split_axis=0, concat_axis=0, tiled=True)  3.97 us
    all_to_all x1, waiting for transfers between devices, local(): lax.all_to_all(key_sent, 'patch', split_axis=0, concat_axis=0, tiled=True)  3.89 us
    pallas_call x1, Pallas kernels, local(): kernel(functools.partial(query_kernel, groups), 'query', 56, out_shape=[r...  2.89 us
    pallas_call x1, Pallas kernels, local(): kernel(functools.partial(stale_kernel, groups, videos), 'stale', 32, out_...  2.22 us
    pallas_call x1, Pallas kernels, local(): kernel(functools.partial(fresh_kernel, groups, videos), 'fresh', 16, out_...  2.11 us
  transfers between devices with their start and end apart: 11, of which 3 were waited for; matrix products, arithmetic and copies ran while one was open for 4% of the time, Pallas kernels for 21%

profile of v6, /device:TPU:0, one launch (start us, length us, event | category | flops | bytes accessed | tf_op | source)
XLA Modules:
  0.0 45.4 jit_solution(12518680931911474363)
XLA Ops:
  0.6 3.0 %collective-permute-start = (bf16[8,128,256]{2,1,0:T(8,128)(2,1)}, bf16[8,128,256]{2,1,0:T(8,128)(2,1)S(1)}, u32[]{:S(2)}, u32[]{:S(2)}) collective-permute-start(bf16[8,128,256]{2,1,0:T(8,128)(2,1)} %refs_4_), channel_id=1, source_target_pairs={{0,2},{1,3},{2,0},{3,1},{4,6},{5,7},{6,4},{7,5},{8,10},{9,11},{10,... | collective-permute-start | bytes 1572872 | tf_op jit(solution)/shard_map/ppermute | solution.py:254
  3.6 1.0 %fusion = (bf16[4,8,1024]{2,1,0:T(8,128)(2,1)S(1)}, bf16[4,8,1024]{2,1,0:T(8,128)(2,1)S(1)}, bf16[4,8,1024]{2,1,0:T(8,128)(2,1)S(1)}, bf16[4,8,1024]{2,1,0:T(8,128)(2,1)S(1)}) fusion(bf16[4,8,4096]{2,1,0:T(8,128)(2,1)} %refs_5_.1), kind=kLoop, calls=%fused_computation.1 | loop fusion | bytes 524288 | tf_op jit(solution)/shard_map/slice
  4.6 0.7 %pad_maximum_fusion = bf16[4,32,1024]{2,1,0:T(8,128)(2,1)} fusion(bf16[4,8,1024]{2,1,0:T(8,128)(2,1)S(1)} %get-tuple-element.50, bf16[4,8,1024]{2,1,0:T(8,128)(2,1)S(1)} %get-tuple-element.51, bf16[4,8,1024]{2,1,0:T(8,128)(2,1)S(1)} %get-tuple-element.49, bf16[4,8,1024]{2,1,0:T(8,128)(2,1)S(1)} %get-tuple-element.48), kind=kLoop, calls=%fused_computation | loop fusion | flops 1048576 | bytes 524288 | tf_op jit(solution)/shard_map/concatenate
  5.3 5.0 %all-to-all-start.1 = ((bf16[16,8,1024]{2,1,0:T(8,128)(2,1)}), bf16[16,8,1024]{2,1,0:T(8,128)(2,1)S(1)}, u32[]{:S(2)}, u32[]{:S(2)}) async-start(bf16[16,8,1024]{2,1,0:T(8,128)(2,1)} %bitcast.2), calls=%async_computation.1 | async-start | bytes 524288 | tf_op jit(solution)/shard_map/all_to_all | solution.py:282
  10.3 0.0 copy-start.3
  10.3 0.0 copy-start.7
  10.3 2.9 %query.1 = (bf16[8,4096]{1,0:T(8,128)(2,1)}, bf16[8,4096]{1,0:T(8,128)(2,1)}, bf16[8,4096]{1,0:T(8,128)(2,1)}, bf16[8,4096]{1,0:T(8,128)(2,1)}, f32[3,8,128]{2,1,0:T(8,128)}) custom-call(bf16[4,8,4096]{2,1,0:T(8,128)(2,1)} %q_hbm.1, f32[1,4096]{1,0:T(1,128)} %bitcast.6, s32[3,8]{1,0:T(4,128)} %coords_hbm.1), custom_call_target="tpu_custom_call" | custom-call | tf_op jit(solution)/shard_map/query/pallas_call | solution.py:286
  13.2 2.0 %collective-permute-start.1 = (bf16[8,4096]{1,0:T(8,128)(2,1)}, bf16[8,4096]{1,0:T(8,128)(2,1)S(1)}, u32[]{:S(2)}, u32[]{:S(2)}) collective-permute-start(bf16[8,4096]{1,0:T(8,128)(2,1)} %get-tuple-element.27.refs_1_), channel_id=1, source_target_pairs={{0,4},{1,5},{2,6},{3,7},{4,0},{5,1},{6,2},{7,3},{8,12},{9,13},{10,... | collective-permute-start | bytes 196616 | tf_op jit(solution)/shard_map/ppermute | solution.py:254
  15.2 2.4 %collective-permute-start.2 = (bf16[8,4096]{1,0:T(8,128)(2,1)}, bf16[8,4096]{1,0:T(8,128)(2,1)S(1)}, u32[]{:S(2)}, u32[]{:S(2)}) collective-permute-start(bf16[8,4096]{1,0:T(8,128)(2,1)} %get-tuple-element.28.refs_2_), channel_id=1, source_target_pairs={{0,8},{1,9},{2,10},{3,11},{4,12},{5,13},{6,14},{7,15},{8,0},{9,1},... | collective-permute-start | bytes 196616 | tf_op jit(solution)/shard_map/ppermute | solution.py:254
  17.6 0.1 collective-permute-start.3
  17.7 0.0 copy-done.3
  17.7 0.0 copy-done.7
  17.7 0.0 copy-start.8
  17.7 0.7 %copy-done.8 = f32[3,8,128]{2,1,0:T(8,128)S(1)} copy-done((f32[3,8,128]{2,1,0:T(8,128)S(1)}, f32[3,8,128]{2,1,0:T(8,128)}, u32[]{:S(2)}) %copy-start.8) | copy-done | bytes 12312
  18.4 0.0 copy-start
  18.4 0.0 copy-start.2
  18.4 0.0 copy-start.4
  18.4 0.0 copy-start.5
  18.4 0.0 copy-start.6
  18.4 1.3 %key.1.refs_4_ = bf16[16,8,1024]{2,1,0:T(8,128)(2,1)} custom-call(bf16[4,8,4096]{2,1,0:T(8,128)(2,1)S(1)} %copy-done.3, f32[1,4096]{1,0:T(1,128)S(1)} %bitcast.4, f32[3,8,128]{2,1,0:T(8,128)S(1)} %copy-done.8), custom_call_target="tpu_custom_call" | custom-call | tf_op jit(solution)/shard_map/key/pallas_call | solution.py:303
  19.7 0.0 copy-start.1
  19.7 0.0 copy-done
  19.7 0.0 copy-done.2
  19.8 0.0 copy-done.4
  19.8 0.0 copy-done.5
  19.8 0.0 copy-done.6
  19.8 2.1 %fresh.1 = (f32[4,8,4096]{2,1,0:T(8,128)S(1)}, f32[4,8,128]{2,1,0:T(8,128)S(1)}) custom-call(bf16[8,4096]{1,0:T(8,128)(2,1)S(1)} %copy-done.2, bf16[8,4096]{1,0:T(8,128)(2,1)S(1)} %copy-done.6, bf16[8,4096]{1,0:T(8,128)(2,1)S(1)} %copy-done.5, bf16[8,4096]{1,0:T(8,128)(2,1)S(1)} %copy-done.4, bf16[16,8,1024]{2,1,0:T(8,128)(2,1)} %key.1.refs_4_, ...), custom_call_target="tpu_custom_call" | custom-call | tf_op jit(solution)/shard_map/fresh/pallas_call | solution.py:313
  21.9 0.0 collective-permute-done.1.refs_1_
  21.9 2.7 %collective-permute-done.2.refs_2_ = bf16[8,4096]{1,0:T(8,128)(2,1)S(1)} collective-permute-done((bf16[8,4096]{1,0:T(8,128)(2,1)}, bf16[8,4096]{1,0:T(8,128)(2,1)S(1)}, u32[]{:S(2)}, u32[]{:S(2)}) %collective-permute-start.2) | collective-permute-done | bytes 65568 | tf_op jit(solution)/shard_map/ppermute | solution.py:254
  24.6 0.0 collective-permute-done.3.refs_3_
  24.6 0.0 collective-permute-done.refs_6_
  24.6 0.0 copy-done.1
  24.6 0.1 collective-permute-start.4
  24.7 0.5 %collective-permute-start.5 = (bf16[8,128,256]{2,1,0:T(8,128)(2,1)S(1)}, bf16[8,128,256]{2,1,0:T(8,128)(2,1)S(1)}, u32[]{:S(2)}, u32[]{:S(2)}) collective-permute-start(bf16[8,128,256]{2,1,0:T(8,128)(2,1)S(1)} %collective-permute-done.refs_6_), channel_id=1, source_target_pairs={{0,1},{1,0},{2,3},{3,2},{4,5},{5,4},{6,7},{7,6},{8,9},{9,8},{10,11... | collective-permute-start | bytes 1572872 | tf_op jit(solution)/shard_map/ppermute | solution.py:254
  25.2 0.0 all-to-all-done.1.value_ref
  25.2 4.0 %all-to-all-start = ((bf16[16,8,1024]{2,1,0:T(8,128)(2,1)}), bf16[16,8,1024]{2,1,0:T(8,128)(2,1)S(1)}, u32[]{:S(2)}, u32[]{:S(2)}) async-start(bf16[16,8,1024]{2,1,0:T(8,128)(2,1)} %key.1.refs_4_), calls=%async_computation | async-start | bytes 524288 | tf_op jit(solution)/shard_map/all_to_all | solution.py:312
  29.2 0.0 collective-permute-done.4.refs_5_
  29.2 0.0 collective-permute-done.5.refs_7_
  29.2 2.2 %stale.1 = (bf16[8,4224]{1,0:T(8,128)(2,1)S(1)}, bf16[8,4224]{1,0:T(8,128)(2,1)}, bf16[8,4224]{1,0:T(8,128)(2,1)}, bf16[8,4224]{1,0:T(8,128)(2,1)}) custom-call(bf16[8,4096]{1,0:T(8,128)(2,1)S(1)} %copy-done.2, bf16[8,4096]{1,0:T(8,128)(2,1)S(1)} %collective-permute-done.1.refs_1_, bf16[8,4096]{1,0:T(8,128)(2,1)S(1)} %collective-permute-done.2.refs_2_, ...), custom_call_target="tpu_custom_call" | custom-call | tf_op jit(solution)/shard_map/stale/pallas_call | solution.py:328
  31.4 1.9 %collective-permute-start.6 = (bf16[8,4224]{1,0:T(8,128)(2,1)}, bf16[8,4224]{1,0:T(8,128)(2,1)S(1)}, u32[]{:S(2)}, u32[]{:S(2)}) collective-permute-start(bf16[8,4224]{1,0:T(8,128)(2,1)} %get-tuple-element.42), channel_id=1, source_target_pairs={{0,4},{1,5},{2,6},{3,7},{4,0},{5,1},{6,2},{7,3},{8,12},{9,13},{10,... | collective-permute-start | bytes 202760 | tf_op jit(solution)/shard_map/ppermute | solution.py:254
  33.4 2.4 %collective-permute-start.7 = (bf16[8,4224]{1,0:T(8,128)(2,1)}, bf16[8,4224]{1,0:T(8,128)(2,1)S(1)}, u32[]{:S(2)}, u32[]{:S(2)}) collective-permute-start(bf16[8,4224]{1,0:T(8,128)(2,1)} %get-tuple-element.43), channel_id=1, source_target_pairs={{0,8},{1,9},{2,10},{3,11},{4,12},{5,13},{6,14},{7,15},{8,0},{9,1},... | collective-permute-start | bytes 202760 | tf_op jit(solution)/shard_map/ppermute | solution.py:254
  35.7 0.1 collective-permute-start.8
  35.8 3.9 %all-to-all-done.key_ref = bf16[16,8,1024]{2,1,0:T(8,128)(2,1)S(1)} async-done(((bf16[16,8,1024]{2,1,0:T(8,128)(2,1)}), bf16[16,8,1024]{2,1,0:T(8,128)(2,1)S(1)}, u32[]{:S(2)}, u32[]{:S(2)}) %all-to-all-start) | async-done | bytes 262176 | tf_op jit(solution)/shard_map/all_to_all | solution.py:312
  39.7 0.9 %cache.1 = bf16[8,16,8,256]{3,2,1,0:T(8,128)(2,1)} custom-call(bf16[16,8,1024]{2,1,0:T(8,128)(2,1)S(1)} %all-to-all-done.key_ref, bf16[16,8,1024]{2,1,0:T(8,128)(2,1)S(1)} %all-to-all-done.1.value_ref), custom_call_target="tpu_custom_call" | custom-call | tf_op jit(solution)/shard_map/cache/pallas_call | solution.py:337
  40.6 0.0 collective-permute-done.6.refs_1_
  40.7 3.0 %collective-permute-done.7.refs_2_ = bf16[8,4224]{1,0:T(8,128)(2,1)S(1)} collective-permute-done((bf16[8,4224]{1,0:T(8,128)(2,1)}, bf16[8,4224]{1,0:T(8,128)(2,1)S(1)}, u32[]{:S(2)}, u32[]{:S(2)}) %collective-permute-start.7) | collective-permute-done | bytes 67616 | tf_op jit(solution)/shard_map/ppermute | solution.py:254
  43.7 0.0 collective-permute-done.8.refs_3_
  43.7 1.8 %join.1 = bf16[4,8,4096]{2,1,0:T(8,128)(2,1)} custom-call(bf16[8,4224]{1,0:T(8,128)(2,1)S(1)} %get-tuple-element.41.refs_0_, bf16[8,4224]{1,0:T(8,128)(2,1)S(1)} %collective-permute-done.6.refs_1_, bf16[8,4224]{1,0:T(8,128)(2,1)S(1)} %collective-permute-done.7.refs_2_, bf16[8,4224]{1,0:T(8,128)(2,1)S(1)} %collective-permute-done.8.refs_3_, ...), custom_call_target="tpu_custom_call" | custom-call | tf_op jit(solution)/shard_map/join/pallas_call | solution.py:346
Async XLA Ops:
  0.6 24.0 %collective-permute-start = (bf16[8,128,256]{2,1,0:T(8,128)(2,1)}, bf16[8,128,256]{2,1,0:T(8,128)(2,1)S(1)}, u32[]{:S(2)}, u32[]{:S(2)}) collective-permute-start(bf16[8,128,256]{2,1,0:T(8,128)(2,1)} %refs_4_), channel_id=1, source_target_pairs={{0,2},{1,3},{2,0},{3,1},{4,6},{5,7},{6,4},{7,5},{8,10},{9,11},{10,... | collective-permute-start | bytes 1572872 | tf_op jit(solution)/shard_map/ppermute | solution.py:254
  5.3 19.9 %all-to-all-start.1 = ((bf16[16,8,1024]{2,1,0:T(8,128)(2,1)}), bf16[16,8,1024]{2,1,0:T(8,128)(2,1)S(1)}, u32[]{:S(2)}, u32[]{:S(2)}) async-start(bf16[16,8,1024]{2,1,0:T(8,128)(2,1)} %bitcast.2), calls=%async_computation.1 | async-start | bytes 524288 | tf_op jit(solution)/shard_map/all_to_all | solution.py:282
  10.3 7.4 %copy-start.3 = (bf16[4,8,4096]{2,1,0:T(8,128)(2,1)S(1)}, bf16[4,8,4096]{2,1,0:T(8,128)(2,1)}, u32[]{:S(2)}) copy-start(bf16[4,8,4096]{2,1,0:T(8,128)(2,1)} %k_ref.1) | copy-start | bytes 786436
  10.3 7.4 %copy-start.7 = (f32[4096]{0:T(1024)S(1)}, f32[4096]{0:T(1024)}, u32[]{:S(2)}) copy-start(f32[4096]{0:T(1024)} %param.11) | copy-start | bytes 49156
  13.2 8.7 %collective-permute-start.1 = (bf16[8,4096]{1,0:T(8,128)(2,1)}, bf16[8,4096]{1,0:T(8,128)(2,1)S(1)}, u32[]{:S(2)}, u32[]{:S(2)}) collective-permute-start(bf16[8,4096]{1,0:T(8,128)(2,1)} %get-tuple-element.27.refs_1_), channel_id=1, source_target_pairs={{0,4},{1,5},{2,6},{3,7},{4,0},{5,1},{6,2},{7,3},{8,12},{9,13},{10,... | collective-permute-start | bytes 196616 | tf_op jit(solution)/shard_map/ppermute | solution.py:254
  15.2 9.4 %collective-permute-start.2 = (bf16[8,4096]{1,0:T(8,128)(2,1)}, bf16[8,4096]{1,0:T(8,128)(2,1)S(1)}, u32[]{:S(2)}, u32[]{:S(2)}) collective-permute-start(bf16[8,4096]{1,0:T(8,128)(2,1)} %get-tuple-element.28.refs_2_), channel_id=1, source_target_pairs={{0,8},{1,9},{2,10},{3,11},{4,12},{5,13},{6,14},{7,15},{8,0},{9,1},... | collective-permute-start | bytes 196616 | tf_op jit(solution)/shard_map/ppermute | solution.py:254
  17.6 7.1 %collective-permute-start.3 = (bf16[8,4096]{1,0:T(8,128)(2,1)}, bf16[8,4096]{1,0:T(8,128)(2,1)S(1)}, u32[]{:S(2)}, u32[]{:S(2)}) collective-permute-start(bf16[8,4096]{1,0:T(8,128)(2,1)} %get-tuple-element.29.refs_3_), channel_id=1, source_target_pairs={{0,12},{1,13},{2,14},{3,15},{4,8},{5,9},{6,10},{7,11},{8,4},{9,5},... | collective-permute-start | bytes 196616 | tf_op jit(solution)/shard_map/ppermute | solution.py:254
  17.7 0.7 %copy-start.8 = (f32[3,8,128]{2,1,0:T(8,128)S(1)}, f32[3,8,128]{2,1,0:T(8,128)}, u32[]{:S(2)}) copy-start(f32[3,8,128]{2,1,0:T(8,128)} %get-tuple-element.25.tables_ref) | copy-start | bytes 36868
  18.4 1.4 %copy-start = (bf16[4,8,4096]{2,1,0:T(8,128)(2,1)S(1)}, bf16[4,8,4096]{2,1,0:T(8,128)(2,1)}, u32[]{:S(2)}) copy-start(bf16[4,8,4096]{2,1,0:T(8,128)(2,1)} %refs_5_.1) | copy-start | bytes 786436
  18.4 1.4 %copy-start.2 = (bf16[8,4096]{1,0:T(8,128)(2,1)S(1)}, bf16[8,4096]{1,0:T(8,128)(2,1)}, u32[]{:S(2)}) copy-start(bf16[8,4096]{1,0:T(8,128)(2,1)} %get-tuple-element.35.refs_0_) | copy-start | bytes 196612
  18.4 1.4 %copy-start.4 = (bf16[8,4096]{1,0:T(8,128)(2,1)S(1)}, bf16[8,4096]{1,0:T(8,128)(2,1)}, u32[]{:S(2)}) copy-start(bf16[8,4096]{1,0:T(8,128)(2,1)} %get-tuple-element.29.refs_3_) | copy-start | bytes 196612
  18.4 1.4 %copy-start.5 = (bf16[8,4096]{1,0:T(8,128)(2,1)S(1)}, bf16[8,4096]{1,0:T(8,128)(2,1)}, u32[]{:S(2)}) copy-start(bf16[8,4096]{1,0:T(8,128)(2,1)} %get-tuple-element.28.refs_2_) | copy-start | bytes 196612
  18.4 1.4 %copy-start.6 = (bf16[8,4096]{1,0:T(8,128)(2,1)S(1)}, bf16[8,4096]{1,0:T(8,128)(2,1)}, u32[]{:S(2)}) copy-start(bf16[8,4096]{1,0:T(8,128)(2,1)} %get-tuple-element.27.refs_1_) | copy-start | bytes 196612
  19.7 4.9 %copy-start.1 = (bf16[8,128,256]{2,1,0:T(8,128)(2,1)S(1)}, bf16[8,128,256]{2,1,0:T(8,128)(2,1)}, u32[]{:S(2)}) copy-start(bf16[8,128,256]{2,1,0:T(8,128)(2,1)} %refs_4_) | copy-start | bytes 1572868
  24.6 4.6 %collective-permute-start.4 = (bf16[8,128,256]{2,1,0:T(8,128)(2,1)S(1)}, bf16[8,128,256]{2,1,0:T(8,128)(2,1)S(1)}, u32[]{:S(2)}, u32[]{:S(2)}) collective-permute-start(bf16[8,128,256]{2,1,0:T(8,128)(2,1)S(1)} %copy-done.1), channel_id=1, source_target_pairs={{0,1},{1,0},{2,3},{3,2},{4,5},{5,4},{6,7},{7,6},{8,9},{9,8},{10,11... | collective-permute-start | bytes 1572872 | tf_op jit(solution)/shard_map/ppermute | solution.py:254
  24.7 4.5 %collective-permute-start.5 = (bf16[8,128,256]{2,1,0:T(8,128)(2,1)S(1)}, bf16[8,128,256]{2,1,0:T(8,128)(2,1)S(1)}, u32[]{:S(2)}, u32[]{:S(2)}) collective-permute-start(bf16[8,128,256]{2,1,0:T(8,128)(2,1)S(1)} %collective-permute-done.refs_6_), channel_id=1, source_target_pairs={{0,1},{1,0},{2,3},{3,2},{4,5},{5,4},{6,7},{7,6},{8,9},{9,8},{10,11... | collective-permute-start | bytes 1572872 | tf_op jit(solution)/shard_map/ppermute | solution.py:254
  25.2 14.5 %all-to-all-start = ((bf16[16,8,1024]{2,1,0:T(8,128)(2,1)}), bf16[16,8,1024]{2,1,0:T(8,128)(2,1)S(1)}, u32[]{:S(2)}, u32[]{:S(2)}) async-start(bf16[16,8,1024]{2,1,0:T(8,128)(2,1)} %key.1.refs_4_), calls=%async_computation | async-start | bytes 524288 | tf_op jit(solution)/shard_map/all_to_all | solution.py:312
  31.4 9.2 %collective-permute-start.6 = (bf16[8,4224]{1,0:T(8,128)(2,1)}, bf16[8,4224]{1,0:T(8,128)(2,1)S(1)}, u32[]{:S(2)}, u32[]{:S(2)}) collective-permute-start(bf16[8,4224]{1,0:T(8,128)(2,1)} %get-tuple-element.42), channel_id=1, source_target_pairs={{0,4},{1,5},{2,6},{3,7},{4,0},{5,1},{6,2},{7,3},{8,12},{9,13},{10,... | collective-permute-start | bytes 202760 | tf_op jit(solution)/shard_map/ppermute | solution.py:254
  33.4 10.3 %collective-permute-start.7 = (bf16[8,4224]{1,0:T(8,128)(2,1)}, bf16[8,4224]{1,0:T(8,128)(2,1)S(1)}, u32[]{:S(2)}, u32[]{:S(2)}) collective-permute-start(bf16[8,4224]{1,0:T(8,128)(2,1)} %get-tuple-element.43), channel_id=1, source_target_pairs={{0,8},{1,9},{2,10},{3,11},{4,12},{5,13},{6,14},{7,15},{8,0},{9,1},... | collective-permute-start | bytes 202760 | tf_op jit(solution)/shard_map/ppermute | solution.py:254
  35.7 7.9 %collective-permute-start.8 = (bf16[8,4224]{1,0:T(8,128)(2,1)}, bf16[8,4224]{1,0:T(8,128)(2,1)S(1)}, u32[]{:S(2)}, u32[]{:S(2)}) collective-permute-start(bf16[8,4224]{1,0:T(8,128)(2,1)} %get-tuple-element.44), channel_id=1, source_target_pairs={{0,12},{1,13},{2,14},{3,15},{4,8},{5,9},{6,10},{7,11},{8,4},{9,5},... | collective-permute-start | bytes 202760 | tf_op jit(solution)/shard_map/ppermute | solution.py:254

commit v7 on v6

--- a/solution.py
+++ b/solution.py
@@ -52,10 +52,10 @@
         yield head, y.astype(BF16)
 
 
-def query_kernel(groups, q_hbm, gain_hbm, coords_hbm, *refs):
+def query_kernel(groups, q_hbm, gain_hbm, coords_hbm, value_hbm, *refs):
     videos, tok_rows, width = q_hbm.shape
-    outs, tables_ref, refs = refs[:videos], refs[videos], refs[videos + 1 :]
-    q_ref, gain_ref, coords_ref, done_ref, sems, out_sems = refs
+    outs, tables_ref, value_out, refs = refs[:videos], refs[videos], refs[videos + 1], refs[videos + 2 :]
+    q_ref, gain_ref, coords_ref, done_ref, sems, out_sems, value_sems = refs
     own = lax.axis_index("patch") // groups
     copies = [
         pltpu.make_async_copy(source, place, sems.at[i])
@@ -65,6 +65,15 @@
     ]
     for copy in copies:
         copy.start()
+    span = width // groups
+    spreads = [
+        pltpu.make_async_copy(
+            value_hbm.at[:, :, pl.ds(group * span, span)], value_out.at[:, group], value_sems.at[group]
+        )
+        for group in range(groups)
+    ]
+    for spread in spreads:
+        spread.start()
     copies[0].wait()
     tables = rope_tables(coords_ref, tok_rows)
     for i in range(3):
@@ -77,8 +86,8 @@
             done_ref[s, :, head * DH : (head + 1) * DH] = y
         sends.append(pltpu.make_async_copy(done_ref.at[s], outs[s], out_sems.at[s]))
         sends[-1].start()
-    for send in sends:
-        send.wait()
+    for copy in sends + spreads:
+        copy.wait()
 
 
 def key_kernel(k_ref, gain_ref, tables_ref, out_ref):
@@ -107,7 +116,8 @@
 def fresh_kernel(groups, videos, *refs):
     queries = refs[:videos]
     key_ref, value_ref, out_ref, log_ref = refs[videos:]
-    own = lax.axis_index("patch") // groups
+    me = lax.axis_index("patch")
+    own, mine = me // groups, me % groups
     _, tok_rows, width = out_ref.shape
     span = width // groups
     pairs = span // DH
@@ -119,10 +129,10 @@
     )
     lane = lax.broadcasted_iota(jnp.int32, (rows, DH), 1)
     logs = jnp.zeros((rows, DH), F32)
-    for group in range(groups):
-        query = stacked(queries, slice(group * span, (group + 1) * span))
-        lanes = slice(group * span, (group + 1) * span)
-        key = stacked([key_ref.at[(own ^ s) * groups + group] for s in range(videos)], slice(None))
+    for t in range(groups):
+        lanes = pl.ds(pl.multiple_of((mine ^ t) * span, DH), span)
+        query = stacked(queries, lanes)
+        key = stacked([key_ref.at[me ^ (s * groups) ^ t] for s in range(videos)], slice(None))
         value = stacked([value_ref.at[own ^ s] for s in range(videos)], lanes)
         scores = jnp.concatenate(
             [
@@ -139,7 +149,7 @@
         weights, inverse, log = softmax_parts(jnp.where(same, scores * scale, -jnp.inf))
         for pair in range(pairs):
             here = slice(pair * rows, (pair + 1) * rows)
-            head = group * pairs + pair
+            head = t * pairs + pair
             result = inverse[here] * jnp.dot(
                 weights[here],
                 value[:, pair * DH : (pair + 1) * DH],
@@ -192,7 +202,7 @@
             logs = jnp.where(lane == t * pairs + pair, log[here], logs)
         result = jnp.concatenate(results, axis=1).astype(BF16)
         for s in range(videos):
-            outs[s][:, pl.ds(start, span)] = result[s * tok_rows : (s + 1) * tok_rows]
+            outs[s][:, t * span : (t + 1) * span] = result[s * tok_rows : (s + 1) * tok_rows]
     high = logs.astype(BF16).astype(F32)
     middle = (logs - high).astype(BF16).astype(F32)
     low = (logs - high - middle).astype(BF16).astype(F32)
@@ -210,24 +220,21 @@
     _, tok_rows, width = fresh_ref.shape
     heads = width // DH
     pairs = heads // groups
+    span = pairs * DH
     copies = []
     for s in range(videos):
         terms = back[s][:, width:].astype(F32)
         stale_log = terms + pltpu.roll(terms, DH - heads, 1) + pltpu.roll(terms, DH - 2 * heads, 1)
-        fresh_log = log_ref[s]
+        share = 1.0 / (1.0 + jnp.exp(stale_log - log_ref[s]))
         for t in range(groups):
-            start = pl.multiple_of((mine ^ t) * pairs * DH, DH)
-            stale = back[s][:, pl.ds(start, pairs * DH)].astype(F32)
-            fresh = fresh_ref[s, :, pl.ds(start, pairs * DH)]
-            shift = DH + t * pairs - (mine ^ t) * pairs
-            gap = stale_log - pltpu.roll(fresh_log, shift % DH, 1)
-            share = 1.0 / (1.0 + jnp.exp(gap))
             parts = []
             for pair in range(pairs):
-                here = slice(pair * DH, (pair + 1) * DH)
-                of = share[:, t * pairs + pair : t * pairs + pair + 1]
-                parts.append(of * fresh[:, here] + (1.0 - of) * stale[:, here])
-            done_ref[s, :, pl.ds(start, pairs * DH)] = jnp.concatenate(parts, axis=1).astype(BF16)
+                head = t * pairs + pair
+                here = slice(head * DH, (head + 1) * DH)
+                stale = back[s][:, here].astype(F32)
+                parts.append(stale + share[:, head : head + 1] * (fresh_ref[s, :, here] - stale))
+            lanes = pl.ds(pl.multiple_of((mine ^ t) * span, DH), span)
+            done_ref[s, :, lanes] = jnp.concatenate(parts, axis=1).astype(BF16)
         copies.append(pltpu.make_async_copy(done_ref.at[s], out_ref.at[own ^ s], sems.at[s]))
         copies[-1].start()
     for copy in copies:
@@ -276,20 +283,20 @@
             **kwargs,
         )
 
-    value_sent = jnp.transpose(
-        values.reshape(videos, tok_rows, groups, pairs_here * DH), (0, 2, 1, 3)
-    ).reshape(patches, tok_rows, pairs_here * DH)
-    value_got = lax.all_to_all(value_sent, "patch", split_axis=0, concat_axis=0, tiled=True)
     pieces = {0: stale_cache}
     bit = groups // 2
     pieces[bit] = permuted(stale_cache, bit, patches)
-    *query, tables = kernel(
+    *query, tables, value_sent = kernel(
         functools.partial(query_kernel, groups),
         "query",
         56,
-        out_shape=[rows] * videos + [jax.ShapeDtypeStruct((3, tok_rows, DH), F32)],
-        in_specs=[HBM] * 3,
-        out_specs=[HBM] * videos + [VMEM],
+        out_shape=[rows] * videos
+        + [
+            jax.ShapeDtypeStruct((3, tok_rows, DH), F32),
+            jax.ShapeDtypeStruct((videos, groups, tok_rows, pairs_here * DH), BF16),
+        ],
+        in_specs=[HBM] * 4,
+        out_specs=[HBM] * videos + [VMEM, HBM],
         scratch_shapes=[
             pltpu.VMEM(queries.shape, BF16),
             pltpu.VMEM((1, width), F32),
@@ -297,8 +304,12 @@
             pltpu.VMEM(queries.shape, BF16),
             pltpu.SemaphoreType.DMA((3,)),
             pltpu.SemaphoreType.DMA((videos,)),
+            pltpu.SemaphoreType.DMA((groups,)),
         ],
-    )(queries, q_gain.reshape(1, width), coords)
+    )(queries, q_gain.reshape(1, width), coords, values)
+    value_got = lax.all_to_all(
+        value_sent.reshape(patches, tok_rows, pairs_here * DH), "patch", split_axis=0, concat_axis=0, tiled=True
+    )
     query_got = exchange(query, groups, patches)
     key = kernel(
         key_kernel,

time: 45.9 us -> 53.3 us (1.16)
  Pallas kernels: 11.2 us -> 17.4 us
  waiting for transfers between devices: 9.65 us -> 13.3 us
  local copies, waits for them, and re-layouts: 1.7 us -> 0.04 us
  other arithmetic: 0.72 us -> 0 us
    pallas_call x1, Pallas kernels: 2.89 us -> 9.73 us  [local(): kernel(functools.partial(query_kernel, groups), 'query', 56, out_shape=[r...]
    ppermute x9, waiting for transfers between devices: 5.75 us -> 9.41 us  [permuted(): lax.ppermute(array, 'patch', [(i, i ^ offset) for i in range(patches)])]
    slice x1 -> x0, local copies, waits for them, and re-layouts: 0.95 us -> none
    concatenate x1 -> x0, other arithmetic: 0.72 us -> none
    unnamed x18, local copies, waits for them, and re-layouts: 0.74 us -> 0.04 us
    pallas_call x1, Pallas kernels: 1.77 us -> 1.16 us  [local(): kernel(functools.partial(join_kernel, groups, videos), 'join', 16, out_sh...]
  transfers between devices with their start and end apart: 11 -> 11, of which waited for: 3 -> 4; matrix products, arithmetic and copies ran while one was open for 4% -> 0% of each run, Pallas kernels for 21% -> 31%
where the time goes in v7:
time: 53.3 us; the launch traced here: 52.8 us
  starting transfers between devices  21.2 us (40%)
  Pallas kernels  17.4 us (33%)
  waiting for transfers between devices  13.3 us (25%)
  between operations  0.79 us (1%)
    ppermute x9, starting transfers between devices, permuted(): lax.ppermute(array, 'patch', [(i, i ^ offset) for i in range(patches)])  12.4 us
    pallas_call x1, Pallas kernels, local(): kernel(functools.partial(query_kernel, groups), 'query', 56, out_shape=[r...  9.73 us
    ppermute x9, waiting for transfers between devices, permuted(): lax.ppermute(array, 'patch', [(i, i ^ offset) for i in range(patches)])  9.41 us
    all_to_all x1, starting transfers between devices, local(): lax.all_to_all(value_sent.reshape(patches, tok_rows, pairs_here * DH), 'p...  5.13 us
    all_to_all x1, waiting for transfers between devices, local(): lax.all_to_all(key_sent, 'patch', split_axis=0, concat_axis=0, tiled=True)  3.91 us
    all_to_all x1, starting transfers between devices, local(): lax.all_to_all(key_sent, 'patch', split_axis=0, concat_axis=0, tiled=True)  3.71 us
    pallas_call x1, Pallas kernels, local(): kernel(functools.partial(stale_kernel, groups, videos), 'stale', 32, out_...  2.2 us
    pallas_call x1, Pallas kernels, local(): kernel(functools.partial(fresh_kernel, groups, videos), 'fresh', 16, out_...  2.11 us
  transfers between devices with their start and end apart: 11, of which 4 were waited for; matrix products, arithmetic and copies ran while one was open for 0% of the time, Pallas kernels for 31%

profile of v7, /device:TPU:0, one launch (start us, length us, event | category | flops | bytes accessed | tf_op | source)
XLA Modules:
  0.0 52.8 jit_solution(8751501213580101216)
XLA Ops:
  0.6 3.0 %collective-permute-start = (bf16[8,128,256]{2,1,0:T(8,128)(2,1)}, bf16[8,128,256]{2,1,0:T(8,128)(2,1)S(1)}, u32[]{:S(2)}, u32[]{:S(2)}) collective-permute-start(bf16[8,128,256]{2,1,0:T(8,128)(2,1)} %refs_4_), channel_id=1, source_target_pairs={{0,2},{1,3},{2,0},{3,1},{4,6},{5,7},{6,4},{7,5},{8,10},{9,11},{10,... | collective-permute-start | bytes 1572872 | tf_op jit(solution)/shard_map/ppermute | solution.py:261
  3.6 9.7 %query.1 = (bf16[8,4096]{1,0:T(8,128)(2,1)}, bf16[8,4096]{1,0:T(8,128)(2,1)}, bf16[8,4096]{1,0:T(8,128)(2,1)}, bf16[8,4096]{1,0:T(8,128)(2,1)}, f32[3,8,128]{2,1,0:T(8,128)}, /*index=5*/bf16[4,4,8,1024]{3,2,1,0:T(8,128)(2,1)}) custom-call(bf16[4,8,4096]{2,1,0:T(8,128)(2,1)} %q_hbm.1, f32[1,4096]{1,0:T(1,128)} %bitcast.7, s32[3,8]{1,0:T(4,128)} %coords_hbm.1, ...), custom_call_target="tpu_custom_call" | custom-call | tf_op jit(solution)/shard_map/query/pallas_call | solution.py:289
  13.4 0.0 copy-start.6
  13.4 0.0 copy-start.5
  13.4 0.0 copy-start.4
  13.4 0.0 copy-start.3
  13.4 0.0 copy-start.7
  13.4 0.0 copy-start.8
  13.4 5.1 %all-to-all-start.1 = ((bf16[16,8,1024]{2,1,0:T(8,128)(2,1)}), bf16[16,8,1024]{2,1,0:T(8,128)(2,1)S(1)}, u32[]{:S(2)}, u32[]{:S(2)}) async-start(bf16[16,8,1024]{2,1,0:T(8,128)(2,1)} %bitcast.6), calls=%async_computation.1 | async-start | bytes 524288 | tf_op jit(solution)/shard_map/all_to_all | solution.py:310
  18.6 0.0 copy-done.6
  18.6 2.0 %collective-permute-start.1 = (bf16[8,4096]{1,0:T(8,128)(2,1)S(1)}, bf16[8,4096]{1,0:T(8,128)(2,1)S(1)}, u32[]{:S(2)}, u32[]{:S(2)}) collective-permute-start(bf16[8,4096]{1,0:T(8,128)(2,1)S(1)} %copy-done.6), channel_id=1, source_target_pairs={{0,4},{1,5},{2,6},{3,7},{4,0},{5,1},{6,2},{7,3},{8,12},{9,13},{10,... | collective-permute-start | bytes 196616 | tf_op jit(solution)/shard_map/ppermute | solution.py:261
  20.6 0.0 copy-done.5
  20.6 2.4 %collective-permute-start.2 = (bf16[8,4096]{1,0:T(8,128)(2,1)S(1)}, bf16[8,4096]{1,0:T(8,128)(2,1)S(1)}, u32[]{:S(2)}, u32[]{:S(2)}) collective-permute-start(bf16[8,4096]{1,0:T(8,128)(2,1)S(1)} %copy-done.5), channel_id=1, source_target_pairs={{0,8},{1,9},{2,10},{3,11},{4,12},{5,13},{6,14},{7,15},{8,0},{9,1},... | collective-permute-start | bytes 196616 | tf_op jit(solution)/shard_map/ppermute | solution.py:261
  22.9 0.0 copy-done.4
  22.9 0.1 collective-permute-start.3
  23.0 0.0 copy-done.3
  23.0 0.0 copy-done.7
  23.0 0.0 copy-done.8
  23.1 0.0 copy-start
  23.1 0.0 copy-start.2
  23.1 1.3 %key.1.refs_4_ = bf16[16,8,1024]{2,1,0:T(8,128)(2,1)} custom-call(bf16[4,8,4096]{2,1,0:T(8,128)(2,1)S(1)} %copy-done.3, f32[1,4096]{1,0:T(1,128)S(1)} %bitcast.4, f32[3,8,128]{2,1,0:T(8,128)S(1)} %copy-done.8), custom_call_target="tpu_custom_call" | custom-call | tf_op jit(solution)/shard_map/key/pallas_call | solution.py:314
  24.4 0.0 copy-start.1
  24.4 0.0 copy-done
  24.4 0.0 copy-done.2
  24.4 2.1 %fresh.1 = (f32[4,8,4096]{2,1,0:T(8,128)S(1)}, f32[4,8,128]{2,1,0:T(8,128)S(1)}) custom-call(bf16[8,4096]{1,0:T(8,128)(2,1)S(1)} %copy-done.2, bf16[8,4096]{1,0:T(8,128)(2,1)S(1)} %copy-done.6, bf16[8,4096]{1,0:T(8,128)(2,1)S(1)} %copy-done.5, bf16[8,4096]{1,0:T(8,128)(2,1)S(1)} %copy-done.4, bf16[16,8,1024]{2,1,0:T(8,128)(2,1)} %key.1.refs_4_, ...), custom_call_target="tpu_custom_call" | custom-call | tf_op jit(solution)/shard_map/fresh/pallas_call | solution.py:324
  26.5 0.5 collective-permute-done.1.refs_1_
  27.0 5.9 %collective-permute-done.2.refs_2_ = bf16[8,4096]{1,0:T(8,128)(2,1)S(1)} collective-permute-done((bf16[8,4096]{1,0:T(8,128)(2,1)S(1)}, bf16[8,4096]{1,0:T(8,128)(2,1)S(1)}, u32[]{:S(2)}, u32[]{:S(2)}) %collective-permute-start.2) | collective-permute-done | bytes 65568 | tf_op jit(solution)/shard_map/ppermute | solution.py:261
  32.9 0.0 collective-permute-done.3.refs_3_
  32.9 0.0 collective-permute-done.refs_6_
  32.9 0.0 copy-done.1
  32.9 0.1 collective-permute-start.4
  33.0 0.5 collective-permute-start.5
  33.5 0.0 all-to-all-done.1.value_ref
  33.5 3.7 %all-to-all-start = ((bf16[16,8,1024]{2,1,0:T(8,128)(2,1)}), bf16[16,8,1024]{2,1,0:T(8,128)(2,1)S(1)}, u32[]{:S(2)}, u32[]{:S(2)}) async-start(bf16[16,8,1024]{2,1,0:T(8,128)(2,1)} %key.1.refs_4_), calls=%async_computation | async-start | bytes 524288 | tf_op jit(solution)/shard_map/all_to_all | solution.py:323
  37.2 0.0 collective-permute-done.4.refs_5_
  37.2 0.0 collective-permute-done.5.refs_7_
  37.2 2.2 %stale.1 = (bf16[8,4224]{1,0:T(8,128)(2,1)S(1)}, bf16[8,4224]{1,0:T(8,128)(2,1)}, bf16[8,4224]{1,0:T(8,128)(2,1)}, bf16[8,4224]{1,0:T(8,128)(2,1)}) custom-call(bf16[8,4096]{1,0:T(8,128)(2,1)S(1)} %copy-done.2, bf16[8,4096]{1,0:T(8,128)(2,1)S(1)} %collective-permute-done.1.refs_1_, bf16[8,4096]{1,0:T(8,128)(2,1)S(1)} %collective-permute-done.2.refs_2_, ...), custom_call_target="tpu_custom_call" | custom-call | tf_op jit(solution)/shard_map/stale/pallas_call | solution.py:339
  39.4 1.9 %collective-permute-start.6 = (bf16[8,4224]{1,0:T(8,128)(2,1)}, bf16[8,4224]{1,0:T(8,128)(2,1)S(1)}, u32[]{:S(2)}, u32[]{:S(2)}) collective-permute-start(bf16[8,4224]{1,0:T(8,128)(2,1)} %get-tuple-element.43), channel_id=1, source_target_pairs={{0,4},{1,5},{2,6},{3,7},{4,0},{5,1},{6,2},{7,3},{8,12},{9,13},{10,... | collective-permute-start | bytes 202760 | tf_op jit(solution)/shard_map/ppermute | solution.py:261
  41.4 2.4 %collective-permute-start.7 = (bf16[8,4224]{1,0:T(8,128)(2,1)}, bf16[8,4224]{1,0:T(8,128)(2,1)S(1)}, u32[]{:S(2)}, u32[]{:S(2)}) collective-permute-start(bf16[8,4224]{1,0:T(8,128)(2,1)} %get-tuple-element.44), channel_id=1, source_target_pairs={{0,8},{1,9},{2,10},{3,11},{4,12},{5,13},{6,14},{7,15},{8,0},{9,1},... | collective-permute-start | bytes 202760 | tf_op jit(solution)/shard_map/ppermute | solution.py:261
  43.7 0.1 collective-permute-start.8
  43.8 3.9 %all-to-all-done.key_ref = bf16[16,8,1024]{2,1,0:T(8,128)(2,1)S(1)} async-done(((bf16[16,8,1024]{2,1,0:T(8,128)(2,1)}), bf16[16,8,1024]{2,1,0:T(8,128)(2,1)S(1)}, u32[]{:S(2)}, u32[]{:S(2)}) %all-to-all-start) | async-done | bytes 262176 | tf_op jit(solution)/shard_map/all_to_all | solution.py:323
  47.7 0.9 %cache.1 = bf16[8,16,8,256]{3,2,1,0:T(8,128)(2,1)} custom-call(bf16[16,8,1024]{2,1,0:T(8,128)(2,1)S(1)} %all-to-all-done.key_ref, bf16[16,8,1024]{2,1,0:T(8,128)(2,1)S(1)} %all-to-all-done.1.value_ref), custom_call_target="tpu_custom_call" | custom-call | tf_op jit(solution)/shard_map/cache/pallas_call | solution.py:348
  48.7 0.0 collective-permute-done.6.refs_1_
  48.7 3.0 %collective-permute-done.7.refs_2_ = bf16[8,4224]{1,0:T(8,128)(2,1)S(1)} collective-permute-done((bf16[8,4224]{1,0:T(8,128)(2,1)}, bf16[8,4224]{1,0:T(8,128)(2,1)S(1)}, u32[]{:S(2)}, u32[]{:S(2)}) %collective-permute-start.7) | collective-permute-done | bytes 67616 | tf_op jit(solution)/shard_map/ppermute | solution.py:261
  51.7 0.0 collective-permute-done.8.refs_3_
  51.7 1.2 %join.1 = bf16[4,8,4096]{2,1,0:T(8,128)(2,1)} custom-call(bf16[8,4224]{1,0:T(8,128)(2,1)S(1)} %get-tuple-element.42.refs_0_, bf16[8,4224]{1,0:T(8,128)(2,1)S(1)} %collective-permute-done.6.refs_1_, bf16[8,4224]{1,0:T(8,128)(2,1)S(1)} %collective-permute-done.7.refs_2_, bf16[8,4224]{1,0:T(8,128)(2,1)S(1)} %collective-permute-done.8.refs_3_, ...), custom_call_target="tpu_custom_call" | custom-call | tf_op jit(solution)/shard_map/join/pallas_call | solution.py:357
Async XLA Ops:
  0.6 32.3 %collective-permute-start = (bf16[8,128,256]{2,1,0:T(8,128)(2,1)}, bf16[8,128,256]{2,1,0:T(8,128)(2,1)S(1)}, u32[]{:S(2)}, u32[]{:S(2)}) collective-permute-start(bf16[8,128,256]{2,1,0:T(8,128)(2,1)} %refs_4_), channel_id=1, source_target_pairs={{0,2},{1,3},{2,0},{3,1},{4,6},{5,7},{6,4},{7,5},{8,10},{9,11},{10,... | collective-permute-start | bytes 1572872 | tf_op jit(solution)/shard_map/ppermute | solution.py:261
  13.4 5.2 %copy-start.6 = (bf16[8,4096]{1,0:T(8,128)(2,1)S(1)}, bf16[8,4096]{1,0:T(8,128)(2,1)}, u32[]{:S(2)}) copy-start(bf16[8,4096]{1,0:T(8,128)(2,1)} %get-tuple-element.28.refs_1_) | copy-start | bytes 196612
  13.4 7.2 %copy-start.5 = (bf16[8,4096]{1,0:T(8,128)(2,1)S(1)}, bf16[8,4096]{1,0:T(8,128)(2,1)}, u32[]{:S(2)}) copy-start(bf16[8,4096]{1,0:T(8,128)(2,1)} %get-tuple-element.29.refs_2_) | copy-start | bytes 196612
  13.4 9.5 %copy-start.4 = (bf16[8,4096]{1,0:T(8,128)(2,1)S(1)}, bf16[8,4096]{1,0:T(8,128)(2,1)}, u32[]{:S(2)}) copy-start(bf16[8,4096]{1,0:T(8,128)(2,1)} %get-tuple-element.30.refs_3_) | copy-start | bytes 196612
  13.4 9.6 %copy-start.3 = (bf16[4,8,4096]{2,1,0:T(8,128)(2,1)S(1)}, bf16[4,8,4096]{2,1,0:T(8,128)(2,1)}, u32[]{:S(2)}) copy-start(bf16[4,8,4096]{2,1,0:T(8,128)(2,1)} %k_ref.1) | copy-start | bytes 786436
  13.4 9.6 %copy-start.7 = (f32[4096]{0:T(1024)S(1)}, f32[4096]{0:T(1024)}, u32[]{:S(2)}) copy-start(f32[4096]{0:T(1024)} %param.11) | copy-start | bytes 49156
  13.4 9.6 %copy-start.8 = (f32[3,8,128]{2,1,0:T(8,128)S(1)}, f32[3,8,128]{2,1,0:T(8,128)}, u32[]{:S(2)}) copy-start(f32[3,8,128]{2,1,0:T(8,128)} %get-tuple-element.26.tables_ref) | copy-start | bytes 36868
  13.4 20.1 %all-to-all-start.1 = ((bf16[16,8,1024]{2,1,0:T(8,128)(2,1)}), bf16[16,8,1024]{2,1,0:T(8,128)(2,1)S(1)}, u32[]{:S(2)}, u32[]{:S(2)}) async-start(bf16[16,8,1024]{2,1,0:T(8,128)(2,1)} %bitcast.6), calls=%async_computation.1 | async-start | bytes 524288 | tf_op jit(solution)/shard_map/all_to_all | solution.py:310
  18.6 8.4 %collective-permute-start.1 = (bf16[8,4096]{1,0:T(8,128)(2,1)S(1)}, bf16[8,4096]{1,0:T(8,128)(2,1)S(1)}, u32[]{:S(2)}, u32[]{:S(2)}) collective-permute-start(bf16[8,4096]{1,0:T(8,128)(2,1)S(1)} %copy-done.6), channel_id=1, source_target_pairs={{0,4},{1,5},{2,6},{3,7},{4,0},{5,1},{6,2},{7,3},{8,12},{9,13},{10,... | collective-permute-start | bytes 196616 | tf_op jit(solution)/shard_map/ppermute | solution.py:261
  20.6 12.3 %collective-permute-start.2 = (bf16[8,4096]{1,0:T(8,128)(2,1)S(1)}, bf16[8,4096]{1,0:T(8,128)(2,1)S(1)}, u32[]{:S(2)}, u32[]{:S(2)}) collective-permute-start(bf16[8,4096]{1,0:T(8,128)(2,1)S(1)} %copy-done.5), channel_id=1, source_target_pairs={{0,8},{1,9},{2,10},{3,11},{4,12},{5,13},{6,14},{7,15},{8,0},{9,1},... | collective-permute-start | bytes 196616 | tf_op jit(solution)/shard_map/ppermute | solution.py:261
  22.9 10.0 %collective-permute-start.3 = (bf16[8,4096]{1,0:T(8,128)(2,1)S(1)}, bf16[8,4096]{1,0:T(8,128)(2,1)S(1)}, u32[]{:S(2)}, u32[]{:S(2)}) collective-permute-start(bf16[8,4096]{1,0:T(8,128)(2,1)S(1)} %copy-done.4), channel_id=1, source_target_pairs={{0,12},{1,13},{2,14},{3,15},{4,8},{5,9},{6,10},{7,11},{8,4},{9,5},... | collective-permute-start | bytes 196616 | tf_op jit(solution)/shard_map/ppermute | solution.py:261
  23.1 1.4 %copy-start = (bf16[4,8,4096]{2,1,0:T(8,128)(2,1)S(1)}, bf16[4,8,4096]{2,1,0:T(8,128)(2,1)}, u32[]{:S(2)}) copy-start(bf16[4,8,4096]{2,1,0:T(8,128)(2,1)} %refs_5_.1) | copy-start | bytes 786436
  23.1 1.3 %copy-start.2 = (bf16[8,4096]{1,0:T(8,128)(2,1)S(1)}, bf16[8,4096]{1,0:T(8,128)(2,1)}, u32[]{:S(2)}) copy-start(bf16[8,4096]{1,0:T(8,128)(2,1)} %get-tuple-element.36.refs_0_) | copy-start | bytes 196612
  24.4 8.5 %copy-start.1 = (bf16[8,128,256]{2,1,0:T(8,128)(2,1)S(1)}, bf16[8,128,256]{2,1,0:T(8,128)(2,1)}, u32[]{:S(2)}) copy-start(bf16[8,128,256]{2,1,0:T(8,128)(2,1)} %refs_4_) | copy-start | bytes 1572868
  32.9 4.3 %collective-permute-start.4 = (bf16[8,128,256]{2,1,0:T(8,128)(2,1)S(1)}, bf16[8,128,256]{2,1,0:T(8,128)(2,1)S(1)}, u32[]{:S(2)}, u32[]{:S(2)}) collective-permute-start(bf16[8,128,256]{2,1,0:T(8,128)(2,1)S(1)} %copy-done.1), channel_id=1, source_target_pairs={{0,1},{1,0},{2,3},{3,2},{4,5},{5,4},{6,7},{7,6},{8,9},{9,8},{10,11... | collective-permute-start | bytes 1572872 | tf_op jit(solution)/shard_map/ppermute | solution.py:261
  33.0 4.2 %collective-permute-start.5 = (bf16[8,128,256]{2,1,0:T(8,128)(2,1)S(1)}, bf16[8,128,256]{2,1,0:T(8,128)(2,1)S(1)}, u32[]{:S(2)}, u32[]{:S(2)}) collective-permute-start(bf16[8,128,256]{2,1,0:T(8,128)(2,1)S(1)} %collective-permute-done.refs_6_), channel_id=1, source_target_pairs={{0,1},{1,0},{2,3},{3,2},{4,5},{5,4},{6,7},{7,6},{8,9},{9,8},{10,11... | collective-permute-start | bytes 1572872 | tf_op jit(solution)/shard_map/ppermute | solution.py:261
  33.5 14.2 %all-to-all-start = ((bf16[16,8,1024]{2,1,0:T(8,128)(2,1)}), bf16[16,8,1024]{2,1,0:T(8,128)(2,1)S(1)}, u32[]{:S(2)}, u32[]{:S(2)}) async-start(bf16[16,8,1024]{2,1,0:T(8,128)(2,1)} %key.1.refs_4_), calls=%async_computation | async-start | bytes 524288 | tf_op jit(solution)/shard_map/all_to_all | solution.py:323
  39.4 9.2 %collective-permute-start.6 = (bf16[8,4224]{1,0:T(8,128)(2,1)}, bf16[8,4224]{1,0:T(8,128)(2,1)S(1)}, u32[]{:S(2)}, u32[]{:S(2)}) collective-permute-start(bf16[8,4224]{1,0:T(8,128)(2,1)} %get-tuple-element.43), channel_id=1, source_target_pairs={{0,4},{1,5},{2,6},{3,7},{4,0},{5,1},{6,2},{7,3},{8,12},{9,13},{10,... | collective-permute-start | bytes 202760 | tf_op jit(solution)/shard_map/ppermute | solution.py:261
  41.4 10.3 %collective-permute-start.7 = (bf16[8,4224]{1,0:T(8,128)(2,1)}, bf16[8,4224]{1,0:T(8,128)(2,1)S(1)}, u32[]{:S(2)}, u32[]{:S(2)}) collective-permute-start(bf16[8,4224]{1,0:T(8,128)(2,1)} %get-tuple-element.44), channel_id=1, source_target_pairs={{0,8},{1,9},{2,10},{3,11},{4,12},{5,13},{6,14},{7,15},{8,0},{9,1},... | collective-permute-start | bytes 202760 | tf_op jit(solution)/shard_map/ppermute | solution.py:261
  43.7 8.0 %collective-permute-start.8 = (bf16[8,4224]{1,0:T(8,128)(2,1)}, bf16[8,4224]{1,0:T(8,128)(2,1)S(1)}, u32[]{:S(2)}, u32[]{:S(2)}) collective-permute-start(bf16[8,4224]{1,0:T(8,128)(2,1)} %get-tuple-element.45), channel_id=1, source_target_pairs={{0,12},{1,13},{2,14},{3,15},{4,8},{5,9},{6,10},{7,11},{8,4},{9,5},... | collective-permute-start | bytes 202760 | tf_op jit(solution)/shard_map/ppermute | solution.py:261

commit v8 on v7

--- a/solution.py
+++ b/solution.py
@@ -52,10 +52,10 @@
         yield head, y.astype(BF16)
 
 
-def query_kernel(groups, q_hbm, gain_hbm, coords_hbm, value_hbm, *refs):
+def query_kernel(groups, q_hbm, gain_hbm, coords_hbm, *refs):
     videos, tok_rows, width = q_hbm.shape
-    outs, tables_ref, value_out, refs = refs[:videos], refs[videos], refs[videos + 1], refs[videos + 2 :]
-    q_ref, gain_ref, coords_ref, done_ref, sems, out_sems, value_sems = refs
+    outs, tables_ref, refs = refs[:videos], refs[videos], refs[videos + 1 :]
+    q_ref, gain_ref, coords_ref, done_ref, sems, out_sems = refs
     own = lax.axis_index("patch") // groups
     copies = [
         pltpu.make_async_copy(source, place, sems.at[i])
@@ -65,15 +65,6 @@
     ]
     for copy in copies:
         copy.start()
-    span = width // groups
-    spreads = [
-        pltpu.make_async_copy(
-            value_hbm.at[:, :, pl.ds(group * span, span)], value_out.at[:, group], value_sems.at[group]
-        )
-        for group in range(groups)
-    ]
-    for spread in spreads:
-        spread.start()
     copies[0].wait()
     tables = rope_tables(coords_ref, tok_rows)
     for i in range(3):
@@ -86,8 +77,8 @@
             done_ref[s, :, head * DH : (head + 1) * DH] = y
         sends.append(pltpu.make_async_copy(done_ref.at[s], outs[s], out_sems.at[s]))
         sends[-1].start()
-    for copy in sends + spreads:
-        copy.wait()
+    for send in sends:
+        send.wait()
 
 
 def key_kernel(k_ref, gain_ref, tables_ref, out_ref):
@@ -244,14 +235,9 @@
 def cache_kernel(key_ref, value_ref, out_ref, sems):
     copies = []
     for pair in range(out_ref.shape[0]):
-        for part, ref in enumerate((key_ref, value_ref)):
-            copies.append(
-                pltpu.make_async_copy(
-                    ref.at[:, :, pl.ds(pair * DH, DH)],
-                    out_ref.at[pair, :, :, pl.ds(part * DH, DH)],
-                    sems.at[part, pair],
-                )
-            )
+        for part, source in enumerate((key_ref.at[:, :, pl.ds(pair * DH, DH)], value_ref.at[:, pair])):
+            target = out_ref.at[pair, :, :, pl.ds(part * DH, DH)]
+            copies.append(pltpu.make_async_copy(source, target, sems.at[part, pair]))
             copies[-1].start()
     for copy in copies:
         copy.wait()
@@ -286,17 +272,17 @@
     pieces = {0: stale_cache}
     bit = groups // 2
     pieces[bit] = permuted(stale_cache, bit, patches)
-    *query, tables, value_sent = kernel(
+    value_sent = jnp.transpose(values.reshape(videos, tok_rows, width // DH, DH), (0, 2, 1, 3))
+    value_got = lax.all_to_all(
+        value_sent.reshape(patches, pairs_here, tok_rows, DH), "patch", split_axis=0, concat_axis=0, tiled=True
+    )
+    *query, tables = kernel(
         functools.partial(query_kernel, groups),
         "query",
         56,
-        out_shape=[rows] * videos
-        + [
-            jax.ShapeDtypeStruct((3, tok_rows, DH), F32),
-            jax.ShapeDtypeStruct((videos, groups, tok_rows, pairs_here * DH), BF16),
-        ],
-        in_specs=[HBM] * 4,
-        out_specs=[HBM] * videos + [VMEM, HBM],
+        out_shape=[rows] * videos + [jax.ShapeDtypeStruct((3, tok_rows, DH), F32)],
+        in_specs=[HBM] * 3,
+        out_specs=[HBM] * videos + [VMEM],
         scratch_shapes=[
             pltpu.VMEM(queries.shape, BF16),
             pltpu.VMEM((1, width), F32),
@@ -304,12 +290,8 @@
             pltpu.VMEM(queries.shape, BF16),
             pltpu.SemaphoreType.DMA((3,)),
             pltpu.SemaphoreType.DMA((videos,)),
-            pltpu.SemaphoreType.DMA((groups,)),
         ],
-    )(queries, q_gain.reshape(1, width), coords, values)
-    value_got = lax.all_to_all(
-        value_sent.reshape(patches, tok_rows, pairs_here * DH), "patch", split_axis=0, concat_axis=0, tiled=True
-    )
+    )(queries, q_gain.reshape(1, width), coords)
     query_got = exchange(query, groups, patches)
     key = kernel(
         key_kernel,

time: 53.3 us -> 43.7 us (0.82)
  Pallas kernels: 17.4 us -> 10.6 us
  waiting for transfers between devices: 13.3 us -> 9.64 us
  local copies, waits for them, and re-layouts: 0.04 us -> 0.74 us
    pallas_call x1, Pallas kernels: 9.73 us -> 2.92 us  [local(): kernel(functools.partial(query_kernel, groups), 'query', 56, out_shape=[r...]
    ppermute x9, waiting for transfers between devices: 9.41 us -> 5.74 us  [permuted(): lax.ppermute(array, 'patch', [(i, i ^ offset) for i in range(patches)])]
    unnamed x18, local copies, waits for them, and re-layouts: 0.04 us -> 0.74 us
  transfers between devices with their start and end apart: 11 -> 11, of which waited for: 4 -> 3; matrix products, arithmetic and copies ran while one was open for 0% -> 0% of each run, Pallas kernels for 31% -> 22%
where the time goes in v8:
time: 43.7 us; the launch traced here: 43.2 us
  starting transfers between devices  21.4 us (49%)
  Pallas kernels  10.6 us (24%)
  waiting for transfers between devices  9.64 us (22%)
  between operations  0.77 us (2%)
  local copies, waits for them, and re-layouts  0.74 us (2%)
    ppermute x9, starting transfers between devices, permuted(): lax.ppermute(array, 'patch', [(i, i ^ offset) for i in range(patches)])  12.4 us
    ppermute x9, waiting for transfers between devices, permuted(): lax.ppermute(array, 'patch', [(i, i ^ offset) for i in range(patches)])  5.74 us
    all_to_all x1, starting transfers between devices, local(): lax.all_to_all(value_sent.reshape(patches, pairs_here, tok_rows, DH), 'pa...  4.98 us
    all_to_all x1, starting transfers between devices, local(): lax.all_to_all(key_sent, 'patch', split_axis=0, concat_axis=0, tiled=True)  3.97 us
    all_to_all x1, waiting for transfers between devices, local(): lax.all_to_all(key_sent, 'patch', split_axis=0, concat_axis=0, tiled=True)  3.9 us
    pallas_call x1, Pallas kernels, local(): kernel(functools.partial(query_kernel, groups), 'query', 56, out_shape=[r...  2.92 us
    pallas_call x1, Pallas kernels, local(): kernel(functools.partial(stale_kernel, groups, videos), 'stale', 32, out_...  2.2 us
    pallas_call x1, Pallas kernels, local(): kernel(functools.partial(fresh_kernel, groups, videos), 'fresh', 16, out_...  2.11 us
  transfers between devices with their start and end apart: 11, of which 3 were waited for; matrix products, arithmetic and copies ran while one was open for 0% of the time, Pallas kernels for 22%

profile of v8, /device:TPU:0, one launch (start us, length us, event | category | flops | bytes accessed | tf_op | source)
XLA Modules:
  0.0 43.2 jit_solution(18356204679689500008)
XLA Ops:
  0.6 3.0 %collective-permute-start = (bf16[8,128,256]{2,1,0:T(8,128)(2,1)}, bf16[8,128,256]{2,1,0:T(8,128)(2,1)S(1)}, u32[]{:S(2)}, u32[]{:S(2)}) collective-permute-start(bf16[8,128,256]{2,1,0:T(8,128)(2,1)} %refs_4_), channel_id=1, source_target_pairs={{0,2},{1,3},{2,0},{3,1},{4,6},{5,7},{6,4},{7,5},{8,10},{9,11},{10,... | collective-permute-start | bytes 1572872 | tf_op jit(solution)/shard_map/ppermute | solution.py:247
  3.6 5.0 %all-to-all-start.1 = ((bf16[16,8,8,128]{3,2,1,0:T(8,128)(2,1)}), bf16[16,8,8,128]{3,2,1,0:T(8,128)(2,1)S(1)}, u32[]{:S(2)}, u32[]{:S(2)}) async-start(bf16[16,8,8,128]{3,2,1,0:T(8,128)(2,1)} %bitcast.8), calls=%async_computation.1 | async-start | bytes 524288 | tf_op jit(solution)/shard_map/all_to_all | solution.py:276
  8.6 0.0 copy-start.3
  8.6 0.0 copy-start.7
  8.6 2.9 %query.1 = (bf16[8,4096]{1,0:T(8,128)(2,1)}, bf16[8,4096]{1,0:T(8,128)(2,1)}, bf16[8,4096]{1,0:T(8,128)(2,1)}, bf16[8,4096]{1,0:T(8,128)(2,1)}, f32[3,8,128]{2,1,0:T(8,128)}) custom-call(bf16[4,8,4096]{2,1,0:T(8,128)(2,1)} %q_hbm.1, f32[1,4096]{1,0:T(1,128)} %bitcast.11, s32[3,8]{1,0:T(4,128)} %coords_hbm.1), custom_call_target="tpu_custom_call" | custom-call | tf_op jit(solution)/shard_map/query/pallas_call | solution.py:279
  11.6 2.0 %collective-permute-start.1 = (bf16[8,4096]{1,0:T(8,128)(2,1)}, bf16[8,4096]{1,0:T(8,128)(2,1)S(1)}, u32[]{:S(2)}, u32[]{:S(2)}) collective-permute-start(bf16[8,4096]{1,0:T(8,128)(2,1)} %get-tuple-element.27.refs_1_), channel_id=1, source_target_pairs={{0,4},{1,5},{2,6},{3,7},{4,0},{5,1},{6,2},{7,3},{8,12},{9,13},{10,... | collective-permute-start | bytes 196616 | tf_op jit(solution)/shard_map/ppermute | solution.py:247
  13.6 2.4 %collective-permute-start.2 = (bf16[8,4096]{1,0:T(8,128)(2,1)}, bf16[8,4096]{1,0:T(8,128)(2,1)S(1)}, u32[]{:S(2)}, u32[]{:S(2)}) collective-permute-start(bf16[8,4096]{1,0:T(8,128)(2,1)} %get-tuple-element.28.refs_2_), channel_id=1, source_target_pairs={{0,8},{1,9},{2,10},{3,11},{4,12},{5,13},{6,14},{7,15},{8,0},{9,1},... | collective-permute-start | bytes 196616 | tf_op jit(solution)/shard_map/ppermute | solution.py:247
  15.9 0.1 collective-permute-start.3
  16.0 0.0 copy-done.3
  16.0 0.0 copy-done.7
  16.0 0.0 copy-start.8
  16.0 0.7 %copy-done.8 = f32[3,8,128]{2,1,0:T(8,128)S(1)} copy-done((f32[3,8,128]{2,1,0:T(8,128)S(1)}, f32[3,8,128]{2,1,0:T(8,128)}, u32[]{:S(2)}) %copy-start.8) | copy-done | bytes 12312
  16.7 0.0 copy-start
  16.7 0.0 copy-start.2
  16.7 0.0 copy-start.4
  16.7 0.0 copy-start.5
  16.7 0.0 copy-start.6
  16.8 1.3 %key.1.refs_4_ = bf16[16,8,1024]{2,1,0:T(8,128)(2,1)} custom-call(bf16[4,8,4096]{2,1,0:T(8,128)(2,1)S(1)} %copy-done.3, f32[1,4096]{1,0:T(1,128)S(1)} %bitcast.9, f32[3,8,128]{2,1,0:T(8,128)S(1)} %copy-done.8), custom_call_target="tpu_custom_call" | custom-call | tf_op jit(solution)/shard_map/key/pallas_call | solution.py:296
  18.1 0.0 copy-start.1
  18.1 0.0 copy-done
  18.1 0.0 copy-done.2
  18.1 0.0 copy-done.4
  18.1 0.0 copy-done.5
  18.1 0.0 copy-done.6
  18.1 2.1 %fresh.1 = (f32[4,8,4096]{2,1,0:T(8,128)S(1)}, f32[4,8,128]{2,1,0:T(8,128)S(1)}) custom-call(bf16[8,4096]{1,0:T(8,128)(2,1)S(1)} %copy-done.2, bf16[8,4096]{1,0:T(8,128)(2,1)S(1)} %copy-done.6, bf16[8,4096]{1,0:T(8,128)(2,1)S(1)} %copy-done.5, bf16[8,4096]{1,0:T(8,128)(2,1)S(1)} %copy-done.4, bf16[16,8,1024]{2,1,0:T(8,128)(2,1)} %key.1.refs_4_, ...), custom_call_target="tpu_custom_call" | custom-call | tf_op jit(solution)/shard_map/fresh/pallas_call | solution.py:306
  20.2 0.0 collective-permute-done.1.refs_1_
  20.2 2.7 %collective-permute-done.2.refs_2_ = bf16[8,4096]{1,0:T(8,128)(2,1)S(1)} collective-permute-done((bf16[8,4096]{1,0:T(8,128)(2,1)}, bf16[8,4096]{1,0:T(8,128)(2,1)S(1)}, u32[]{:S(2)}, u32[]{:S(2)}) %collective-permute-start.2) | collective-permute-done | bytes 65568 | tf_op jit(solution)/shard_map/ppermute | solution.py:247
  23.0 0.0 collective-permute-done.3.refs_3_
  23.0 0.0 collective-permute-done.refs_6_
  23.0 0.0 copy-done.1
  23.0 0.1 collective-permute-start.4
  23.0 0.5 %collective-permute-start.5 = (bf16[8,128,256]{2,1,0:T(8,128)(2,1)S(1)}, bf16[8,128,256]{2,1,0:T(8,128)(2,1)S(1)}, u32[]{:S(2)}, u32[]{:S(2)}) collective-permute-start(bf16[8,128,256]{2,1,0:T(8,128)(2,1)S(1)} %collective-permute-done.refs_6_), channel_id=1, source_target_pairs={{0,1},{1,0},{2,3},{3,2},{4,5},{5,4},{6,7},{7,6},{8,9},{9,8},{10,11... | collective-permute-start | bytes 1572872 | tf_op jit(solution)/shard_map/ppermute | solution.py:247
  23.5 0.0 all-to-all-done.1.value_ref
  23.5 4.0 %all-to-all-start = ((bf16[16,8,1024]{2,1,0:T(8,128)(2,1)}), bf16[16,8,1024]{2,1,0:T(8,128)(2,1)S(1)}, u32[]{:S(2)}, u32[]{:S(2)}) async-start(bf16[16,8,1024]{2,1,0:T(8,128)(2,1)} %key.1.refs_4_), calls=%async_computation | async-start | bytes 524288 | tf_op jit(solution)/shard_map/all_to_all | solution.py:305
  27.5 0.0 collective-permute-done.4.refs_5_
  27.5 0.0 collective-permute-done.5.refs_7_
  27.5 2.2 %stale.1 = (bf16[8,4224]{1,0:T(8,128)(2,1)S(1)}, bf16[8,4224]{1,0:T(8,128)(2,1)}, bf16[8,4224]{1,0:T(8,128)(2,1)}, bf16[8,4224]{1,0:T(8,128)(2,1)}) custom-call(bf16[8,4096]{1,0:T(8,128)(2,1)S(1)} %copy-done.2, bf16[8,4096]{1,0:T(8,128)(2,1)S(1)} %collective-permute-done.1.refs_1_, bf16[8,4096]{1,0:T(8,128)(2,1)S(1)} %collective-permute-done.2.refs_2_, ...), custom_call_target="tpu_custom_call" | custom-call | tf_op jit(solution)/shard_map/stale/pallas_call | solution.py:321
  29.7 1.9 %collective-permute-start.6 = (bf16[8,4224]{1,0:T(8,128)(2,1)}, bf16[8,4224]{1,0:T(8,128)(2,1)S(1)}, u32[]{:S(2)}, u32[]{:S(2)}) collective-permute-start(bf16[8,4224]{1,0:T(8,128)(2,1)} %get-tuple-element.42), channel_id=1, source_target_pairs={{0,4},{1,5},{2,6},{3,7},{4,0},{5,1},{6,2},{7,3},{8,12},{9,13},{10,... | collective-permute-start | bytes 202760 | tf_op jit(solution)/shard_map/ppermute | solution.py:247
  31.7 2.4 %collective-permute-start.7 = (bf16[8,4224]{1,0:T(8,128)(2,1)}, bf16[8,4224]{1,0:T(8,128)(2,1)S(1)}, u32[]{:S(2)}, u32[]{:S(2)}) collective-permute-start(bf16[8,4224]{1,0:T(8,128)(2,1)} %get-tuple-element.43), channel_id=1, source_target_pairs={{0,8},{1,9},{2,10},{3,11},{4,12},{5,13},{6,14},{7,15},{8,0},{9,1},... | collective-permute-start | bytes 202760 | tf_op jit(solution)/shard_map/ppermute | solution.py:247
  34.0 0.1 collective-permute-start.8
  34.1 3.9 %all-to-all-done.key_ref = bf16[16,8,1024]{2,1,0:T(8,128)(2,1)S(1)} async-done(((bf16[16,8,1024]{2,1,0:T(8,128)(2,1)}), bf16[16,8,1024]{2,1,0:T(8,128)(2,1)S(1)}, u32[]{:S(2)}, u32[]{:S(2)}) %all-to-all-start) | async-done | bytes 262176 | tf_op jit(solution)/shard_map/all_to_all | solution.py:305
  38.0 0.9 %cache.1 = bf16[8,16,8,256]{3,2,1,0:T(8,128)(2,1)} custom-call(bf16[16,8,1024]{2,1,0:T(8,128)(2,1)S(1)} %all-to-all-done.key_ref, bf16[16,8,8,128]{3,2,1,0:T(8,128)(2,1)S(1)} %all-to-all-done.1.value_ref), custom_call_target="tpu_custom_call" | custom-call | tf_op jit(solution)/shard_map/cache/pallas_call | solution.py:330
  39.0 0.0 collective-permute-done.6.refs_1_
  39.0 3.0 %collective-permute-done.7.refs_2_ = bf16[8,4224]{1,0:T(8,128)(2,1)S(1)} collective-permute-done((bf16[8,4224]{1,0:T(8,128)(2,1)}, bf16[8,4224]{1,0:T(8,128)(2,1)S(1)}, u32[]{:S(2)}, u32[]{:S(2)}) %collective-permute-start.7) | collective-permute-done | bytes 67616 | tf_op jit(solution)/shard_map/ppermute | solution.py:247
  42.0 0.0 collective-permute-done.8.refs_3_
  42.0 1.2 %join.1 = bf16[4,8,4096]{2,1,0:T(8,128)(2,1)} custom-call(bf16[8,4224]{1,0:T(8,128)(2,1)S(1)} %get-tuple-element.41.refs_0_, bf16[8,4224]{1,0:T(8,128)(2,1)S(1)} %collective-permute-done.6.refs_1_, bf16[8,4224]{1,0:T(8,128)(2,1)S(1)} %collective-permute-done.7.refs_2_, bf16[8,4224]{1,0:T(8,128)(2,1)S(1)} %collective-permute-done.8.refs_3_, ...), custom_call_target="tpu_custom_call" | custom-call | tf_op jit(solution)/shard_map/join/pallas_call | solution.py:339
Async XLA Ops:
  0.6 22.3 %collective-permute-start = (bf16[8,128,256]{2,1,0:T(8,128)(2,1)}, bf16[8,128,256]{2,1,0:T(8,128)(2,1)S(1)}, u32[]{:S(2)}, u32[]{:S(2)}) collective-permute-start(bf16[8,128,256]{2,1,0:T(8,128)(2,1)} %refs_4_), channel_id=1, source_target_pairs={{0,2},{1,3},{2,0},{3,1},{4,6},{5,7},{6,4},{7,5},{8,10},{9,11},{10,... | collective-permute-start | bytes 1572872 | tf_op jit(solution)/shard_map/ppermute | solution.py:247
  3.6 19.9 %all-to-all-start.1 = ((bf16[16,8,8,128]{3,2,1,0:T(8,128)(2,1)}), bf16[16,8,8,128]{3,2,1,0:T(8,128)(2,1)S(1)}, u32[]{:S(2)}, u32[]{:S(2)}) async-start(bf16[16,8,8,128]{3,2,1,0:T(8,128)(2,1)} %bitcast.8), calls=%async_computation.1 | async-start | bytes 524288 | tf_op jit(solution)/shard_map/all_to_all | solution.py:276
  8.6 7.4 %copy-start.3 = (bf16[4,8,4096]{2,1,0:T(8,128)(2,1)S(1)}, bf16[4,8,4096]{2,1,0:T(8,128)(2,1)}, u32[]{:S(2)}) copy-start(bf16[4,8,4096]{2,1,0:T(8,128)(2,1)} %k_ref.1) | copy-start | bytes 786436
  8.6 7.4 %copy-start.7 = (f32[4096]{0:T(1024)S(1)}, f32[4096]{0:T(1024)}, u32[]{:S(2)}) copy-start(f32[4096]{0:T(1024)} %param.11) | copy-start | bytes 49156
  11.6 8.7 %collective-permute-start.1 = (bf16[8,4096]{1,0:T(8,128)(2,1)}, bf16[8,4096]{1,0:T(8,128)(2,1)S(1)}, u32[]{:S(2)}, u32[]{:S(2)}) collective-permute-start(bf16[8,4096]{1,0:T(8,128)(2,1)} %get-tuple-element.27.refs_1_), channel_id=1, source_target_pairs={{0,4},{1,5},{2,6},{3,7},{4,0},{5,1},{6,2},{7,3},{8,12},{9,13},{10,... | collective-permute-start | bytes 196616 | tf_op jit(solution)/shard_map/ppermute | solution.py:247
  13.6 9.4 %collective-permute-start.2 = (bf16[8,4096]{1,0:T(8,128)(2,1)}, bf16[8,4096]{1,0:T(8,128)(2,1)S(1)}, u32[]{:S(2)}, u32[]{:S(2)}) collective-permute-start(bf16[8,4096]{1,0:T(8,128)(2,1)} %get-tuple-element.28.refs_2_), channel_id=1, source_target_pairs={{0,8},{1,9},{2,10},{3,11},{4,12},{5,13},{6,14},{7,15},{8,0},{9,1},... | collective-permute-start | bytes 196616 | tf_op jit(solution)/shard_map/ppermute | solution.py:247
  15.9 7.0 %collective-permute-start.3 = (bf16[8,4096]{1,0:T(8,128)(2,1)}, bf16[8,4096]{1,0:T(8,128)(2,1)S(1)}, u32[]{:S(2)}, u32[]{:S(2)}) collective-permute-start(bf16[8,4096]{1,0:T(8,128)(2,1)} %get-tuple-element.29.refs_3_), channel_id=1, source_target_pairs={{0,12},{1,13},{2,14},{3,15},{4,8},{5,9},{6,10},{7,11},{8,4},{9,5},... | collective-permute-start | bytes 196616 | tf_op jit(solution)/shard_map/ppermute | solution.py:247
  16.0 0.7 %copy-start.8 = (f32[3,8,128]{2,1,0:T(8,128)S(1)}, f32[3,8,128]{2,1,0:T(8,128)}, u32[]{:S(2)}) copy-start(f32[3,8,128]{2,1,0:T(8,128)} %get-tuple-element.25.tables_ref) | copy-start | bytes 36868
  16.7 1.4 %copy-start = (bf16[4,8,4096]{2,1,0:T(8,128)(2,1)S(1)}, bf16[4,8,4096]{2,1,0:T(8,128)(2,1)}, u32[]{:S(2)}) copy-start(bf16[4,8,4096]{2,1,0:T(8,128)(2,1)} %refs_5_.1) | copy-start | bytes 786436
  16.7 1.4 %copy-start.2 = (bf16[8,4096]{1,0:T(8,128)(2,1)S(1)}, bf16[8,4096]{1,0:T(8,128)(2,1)}, u32[]{:S(2)}) copy-start(bf16[8,4096]{1,0:T(8,128)(2,1)} %get-tuple-element.35.refs_0_) | copy-start | bytes 196612
  16.7 1.4 %copy-start.4 = (bf16[8,4096]{1,0:T(8,128)(2,1)S(1)}, bf16[8,4096]{1,0:T(8,128)(2,1)}, u32[]{:S(2)}) copy-start(bf16[8,4096]{1,0:T(8,128)(2,1)} %get-tuple-element.29.refs_3_) | copy-start | bytes 196612
  16.7 1.4 %copy-start.5 = (bf16[8,4096]{1,0:T(8,128)(2,1)S(1)}, bf16[8,4096]{1,0:T(8,128)(2,1)}, u32[]{:S(2)}) copy-start(bf16[8,4096]{1,0:T(8,128)(2,1)} %get-tuple-element.28.refs_2_) | copy-start | bytes 196612
  16.7 1.4 %copy-start.6 = (bf16[8,4096]{1,0:T(8,128)(2,1)S(1)}, bf16[8,4096]{1,0:T(8,128)(2,1)}, u32[]{:S(2)}) copy-start(bf16[8,4096]{1,0:T(8,128)(2,1)} %get-tuple-element.27.refs_1_) | copy-start | bytes 196612
  18.1 4.9 %copy-start.1 = (bf16[8,128,256]{2,1,0:T(8,128)(2,1)S(1)}, bf16[8,128,256]{2,1,0:T(8,128)(2,1)}, u32[]{:S(2)}) copy-start(bf16[8,128,256]{2,1,0:T(8,128)(2,1)} %refs_4_) | copy-start | bytes 1572868
  23.0 4.6 %collective-permute-start.4 = (bf16[8,128,256]{2,1,0:T(8,128)(2,1)S(1)}, bf16[8,128,256]{2,1,0:T(8,128)(2,1)S(1)}, u32[]{:S(2)}, u32[]{:S(2)}) collective-permute-start(bf16[8,128,256]{2,1,0:T(8,128)(2,1)S(1)} %copy-done.1), channel_id=1, source_target_pairs={{0,1},{1,0},{2,3},{3,2},{4,5},{5,4},{6,7},{7,6},{8,9},{9,8},{10,11... | collective-permute-start | bytes 1572872 | tf_op jit(solution)/shard_map/ppermute | solution.py:247
  23.0 4.5 %collective-permute-start.5 = (bf16[8,128,256]{2,1,0:T(8,128)(2,1)S(1)}, bf16[8,128,256]{2,1,0:T(8,128)(2,1)S(1)}, u32[]{:S(2)}, u32[]{:S(2)}) collective-permute-start(bf16[8,128,256]{2,1,0:T(8,128)(2,1)S(1)} %collective-permute-done.refs_6_), channel_id=1, source_target_pairs={{0,1},{1,0},{2,3},{3,2},{4,5},{5,4},{6,7},{7,6},{8,9},{9,8},{10,11... | collective-permute-start | bytes 1572872 | tf_op jit(solution)/shard_map/ppermute | solution.py:247
  23.5 14.5 %all-to-all-start = ((bf16[16,8,1024]{2,1,0:T(8,128)(2,1)}), bf16[16,8,1024]{2,1,0:T(8,128)(2,1)S(1)}, u32[]{:S(2)}, u32[]{:S(2)}) async-start(bf16[16,8,1024]{2,1,0:T(8,128)(2,1)} %key.1.refs_4_), calls=%async_computation | async-start | bytes 524288 | tf_op jit(solution)/shard_map/all_to_all | solution.py:305
  29.7 9.2 %collective-permute-start.6 = (bf16[8,4224]{1,0:T(8,128)(2,1)}, bf16[8,4224]{1,0:T(8,128)(2,1)S(1)}, u32[]{:S(2)}, u32[]{:S(2)}) collective-permute-start(bf16[8,4224]{1,0:T(8,128)(2,1)} %get-tuple-element.42), channel_id=1, source_target_pairs={{0,4},{1,5},{2,6},{3,7},{4,0},{5,1},{6,2},{7,3},{8,12},{9,13},{10,... | collective-permute-start | bytes 202760 | tf_op jit(solution)/shard_map/ppermute | solution.py:247
  31.7 10.3 %collective-permute-start.7 = (bf16[8,4224]{1,0:T(8,128)(2,1)}, bf16[8,4224]{1,0:T(8,128)(2,1)S(1)}, u32[]{:S(2)}, u32[]{:S(2)}) collective-permute-start(bf16[8,4224]{1,0:T(8,128)(2,1)} %get-tuple-element.43), channel_id=1, source_target_pairs={{0,8},{1,9},{2,10},{3,11},{4,12},{5,13},{6,14},{7,15},{8,0},{9,1},... | collective-permute-start | bytes 202760 | tf_op jit(solution)/shard_map/ppermute | solution.py:247
  34.0 8.0 %collective-permute-start.8 = (bf16[8,4224]{1,0:T(8,128)(2,1)}, bf16[8,4224]{1,0:T(8,128)(2,1)S(1)}, u32[]{:S(2)}, u32[]{:S(2)}) collective-permute-start(bf16[8,4224]{1,0:T(8,128)(2,1)} %get-tuple-element.44), channel_id=1, source_target_pairs={{0,12},{1,13},{2,14},{3,15},{4,8},{5,9},{6,10},{7,11},{8,4},{9,5},... | collective-permute-start | bytes 202760 | tf_op jit(solution)/shard_map/ppermute | solution.py:247

commit v9 on v8

--- a/solution.py
+++ b/solution.py
@@ -301,20 +301,8 @@
         in_specs=[VMEM] * 3,
         out_specs=VMEM,
     )(keys, k_gain.reshape(1, width), tables)
-    key_sent, query_got = lax.optimization_barrier((key, query_got))
-    key_got = lax.all_to_all(key_sent, "patch", split_axis=0, concat_axis=0, tiled=True)
-    fresh_sum, fresh_log = kernel(
-        functools.partial(fresh_kernel, groups, videos),
-        "fresh",
-        16,
-        out_shape=(
-            jax.ShapeDtypeStruct((videos, tok_rows, width), F32),
-            jax.ShapeDtypeStruct((videos, tok_rows, DH), F32),
-        ),
-        in_specs=[VMEM] * (videos + 2),
-        out_specs=(VMEM, VMEM),
-    )(*query, key, values)
-    pieces, query_got, fresh_log = lax.optimization_barrier((pieces, query_got, fresh_log))
+    key_got = lax.all_to_all(key, "patch", split_axis=0, concat_axis=0, tiled=True)
+    pieces, query_got = lax.optimization_barrier((pieces, query_got))
     while bit > 1:
         bit //= 2
         pieces.update({t | bit: permuted(piece, bit, patches) for t, piece in list(pieces.items())})
@@ -326,16 +314,19 @@
         in_specs=[VMEM] * (videos + groups),
         out_specs=[VMEM] * videos,
     )(*query_got, *[pieces[t] for t in range(groups)])
+    result, key_late = lax.optimization_barrier((result, key))
     back = exchange(result, groups, patches)
-    next_cache = kernel(
-        cache_kernel,
-        "cache",
+    fresh_sum, fresh_log = kernel(
+        functools.partial(fresh_kernel, groups, videos),
+        "fresh",
         16,
-        out_shape=jax.ShapeDtypeStruct((pairs_here, patches, tok_rows, 2 * DH), BF16),
-        in_specs=[VMEM, VMEM],
-        out_specs=HBM,
-        scratch_shapes=[pltpu.SemaphoreType.DMA((2, pairs_here))],
-    )(key_got, value_got)
+        out_shape=(
+            jax.ShapeDtypeStruct((videos, tok_rows, width), F32),
+            jax.ShapeDtypeStruct((videos, tok_rows, DH), F32),
+        ),
+        in_specs=[VMEM] * (videos + 2),
+        out_specs=(VMEM, VMEM),
+    )(*query, key_late, values)
     attended = kernel(
         functools.partial(join_kernel, groups, videos),
         "join",
@@ -348,6 +339,16 @@
             pltpu.SemaphoreType.DMA((videos,)),
         ],
     )(*back, fresh_sum, fresh_log)
+    attended, key_got, value_got = lax.optimization_barrier((attended, key_got, value_got))
+    next_cache = kernel(
+        cache_kernel,
+        "cache",
+        16,
+        out_shape=jax.ShapeDtypeStruct((pairs_here, patches, tok_rows, 2 * DH), BF16),
+        in_specs=[VMEM, VMEM],
+        out_specs=HBM,
+        scratch_shapes=[pltpu.SemaphoreType.DMA((2, pairs_here))],
+    )(key_got, value_got)
     return (attended, next_cache.reshape(stale_cache.shape))
 
 

time: 43.7 us -> 49.5 us (1.13)
  waiting for transfers between devices: 9.64 us -> 16.2 us
  Pallas kernels: 10.6 us -> 9.92 us
    ppermute x9, waiting for transfers between devices: 5.74 us -> 16.2 us  [permuted(): lax.ppermute(array, 'patch', [(i, i ^ offset) for i in range(patches)])]
    all_to_all x1, waiting for transfers between devices: 3.9 us -> 0.01 us  [local(): lax.all_to_all(key, 'patch', split_axis=0, concat_axis=0, tiled=True)]
    all_to_all x1, starting transfers between devices: 4.98 us -> 3.84 us  [local(): lax.all_to_all(value_sent.reshape(patches, pairs_here, tok_rows, DH), 'pa...]
    all_to_all x1, starting transfers between devices: 3.97 us -> 5.11 us  [local(): lax.all_to_all(key, 'patch', split_axis=0, concat_axis=0, tiled=True)]
    pallas_call x1, Pallas kernels: 2.2 us -> 1.52 us  [local(): kernel(functools.partial(stale_kernel, groups, videos), 'stale', 32, out_...]
  transfers between devices with their start and end apart: 11 -> 11, of which waited for: 3 -> 4; matrix products, arithmetic and copies ran while one was open for 0% -> 0% of each run, Pallas kernels for 22% -> 18%
where the time goes in v9:
time: 49.5 us; the launch traced here: 49 us
  starting transfers between devices  21.4 us (43%)
  waiting for transfers between devices  16.2 us (33%)
  Pallas kernels  9.92 us (20%)
  between operations  0.77 us (2%)
  local copies, waits for them, and re-layouts  0.73 us (1%)
    ppermute x9, waiting for transfers between devices, permuted(): lax.ppermute(array, 'patch', [(i, i ^ offset) for i in range(patches)])  16.2 us
    ppermute x9, starting transfers between devices, permuted(): lax.ppermute(array, 'patch', [(i, i ^ offset) for i in range(patches)])  12.4 us
    all_to_all x1, starting transfers between devices, local(): lax.all_to_all(key, 'patch', split_axis=0, concat_axis=0, tiled=True)  5.11 us
    all_to_all x1, starting transfers between devices, local(): lax.all_to_all(value_sent.reshape(patches, pairs_here, tok_rows, DH), 'pa...  3.84 us
    pallas_call x1, Pallas kernels, local(): kernel(functools.partial(query_kernel, groups), 'query', 56, out_shape=[r...  2.87 us
    pallas_call x1, Pallas kernels, local(): kernel(functools.partial(fresh_kernel, groups, videos), 'fresh', 16, out_...  2.13 us
    pallas_call x1, Pallas kernels, local(): kernel(functools.partial(stale_kernel, groups, videos), 'stale', 32, out_...  1.52 us
    pallas_call x1, Pallas kernels, local(): kernel(key_kernel, 'key', 16, out_shape=jax.ShapeDtypeStruct((patches, to...  1.33 us
  transfers between devices with their start and end apart: 11, of which 4 were waited for; matrix products, arithmetic and copies ran while one was open for 0% of the time, Pallas kernels for 18%

profile of v9, /device:TPU:0, one launch (start us, length us, event | category | flops | bytes accessed | tf_op | source)
XLA Modules:
  0.0 49.0 jit_solution(12086077522436768148)
XLA Ops:
  0.6 0.0 copy-start.2
  0.6 3.0 %collective-permute-start = (bf16[8,128,256]{2,1,0:T(8,128)(2,1)}, bf16[8,128,256]{2,1,0:T(8,128)(2,1)S(1)}, u32[]{:S(2)}, u32[]{:S(2)}) collective-permute-start(bf16[8,128,256]{2,1,0:T(8,128)(2,1)} %refs_4_), channel_id=1, source_target_pairs={{0,2},{1,3},{2,0},{3,1},{4,6},{5,7},{6,4},{7,5},{8,10},{9,11},{10,... | collective-permute-start | bytes 1572872 | tf_op jit(solution)/shard_map/ppermute | solution.py:247
  3.6 0.0 copy-start.6
  3.6 2.9 %query.1 = (bf16[8,4096]{1,0:T(8,128)(2,1)}, bf16[8,4096]{1,0:T(8,128)(2,1)}, bf16[8,4096]{1,0:T(8,128)(2,1)}, bf16[8,4096]{1,0:T(8,128)(2,1)}, f32[3,8,128]{2,1,0:T(8,128)}) custom-call(bf16[4,8,4096]{2,1,0:T(8,128)(2,1)} %q_hbm.1, f32[1,4096]{1,0:T(1,128)} %bitcast.10, s32[3,8]{1,0:T(4,128)} %coords_hbm.1), custom_call_target="tpu_custom_call" | custom-call | tf_op jit(solution)/shard_map/query/pallas_call | solution.py:279
  6.5 0.0 copy-done.2
  6.5 0.0 copy-done.6
  6.5 0.0 copy-start.7
  6.6 0.7 %copy-done.7 = f32[3,8,128]{2,1,0:T(8,128)S(1)} copy-done((f32[3,8,128]{2,1,0:T(8,128)S(1)}, f32[3,8,128]{2,1,0:T(8,128)}, u32[]{:S(2)}) %copy-start.7) | copy-done | bytes 12312
  7.3 0.0 copy-start
  7.3 1.3 %key.1.refs_4_ = bf16[16,8,1024]{2,1,0:T(8,128)(2,1)} custom-call(bf16[4,8,4096]{2,1,0:T(8,128)(2,1)S(1)} %copy-done.2, f32[1,4096]{1,0:T(1,128)S(1)} %bitcast.8, f32[3,8,128]{2,1,0:T(8,128)S(1)} %copy-done.7), custom_call_target="tpu_custom_call" | custom-call | tf_op jit(solution)/shard_map/key/pallas_call | solution.py:296
  8.6 0.0 copy-start.3
  8.6 0.0 copy-start.4
  8.6 0.0 copy-start.5
  8.6 5.1 %all-to-all-start = ((bf16[16,8,1024]{2,1,0:T(8,128)(2,1)}), bf16[16,8,1024]{2,1,0:T(8,128)(2,1)S(1)}, u32[]{:S(2)}, u32[]{:S(2)}) async-start(bf16[16,8,1024]{2,1,0:T(8,128)(2,1)} %key.1.refs_4_), calls=%async_computation | async-start | bytes 524288 | tf_op jit(solution)/shard_map/all_to_all | solution.py:304
  13.7 0.0 copy-done.3
  13.7 2.0 %collective-permute-start.1 = (bf16[8,4096]{1,0:T(8,128)(2,1)S(1)}, bf16[8,4096]{1,0:T(8,128)(2,1)S(1)}, u32[]{:S(2)}, u32[]{:S(2)}) collective-permute-start(bf16[8,4096]{1,0:T(8,128)(2,1)S(1)} %copy-done.3), channel_id=1, source_target_pairs={{0,4},{1,5},{2,6},{3,7},{4,0},{5,1},{6,2},{7,3},{8,12},{9,13},{10,... | collective-permute-start | bytes 196616 | tf_op jit(solution)/shard_map/ppermute | solution.py:247
  15.7 0.0 copy-done.4
  15.7 2.4 %collective-permute-start.2 = (bf16[8,4096]{1,0:T(8,128)(2,1)S(1)}, bf16[8,4096]{1,0:T(8,128)(2,1)S(1)}, u32[]{:S(2)}, u32[]{:S(2)}) collective-permute-start(bf16[8,4096]{1,0:T(8,128)(2,1)S(1)} %copy-done.4), channel_id=1, source_target_pairs={{0,8},{1,9},{2,10},{3,11},{4,12},{5,13},{6,14},{7,15},{8,0},{9,1},... | collective-permute-start | bytes 196616 | tf_op jit(solution)/shard_map/ppermute | solution.py:247
  18.1 0.0 copy-done.5
  18.1 0.1 collective-permute-start.3
  18.2 3.9 %collective-permute-done.1.refs_1_ = bf16[8,4096]{1,0:T(8,128)(2,1)S(1)} collective-permute-done((bf16[8,4096]{1,0:T(8,128)(2,1)S(1)}, bf16[8,4096]{1,0:T(8,128)(2,1)S(1)}, u32[]{:S(2)}, u32[]{:S(2)}) %collective-permute-start.1) | collective-permute-done | bytes 65568 | tf_op jit(solution)/shard_map/ppermute | solution.py:247
  22.1 5.9 %collective-permute-done.2.refs_2_ = bf16[8,4096]{1,0:T(8,128)(2,1)S(1)} collective-permute-done((bf16[8,4096]{1,0:T(8,128)(2,1)S(1)}, bf16[8,4096]{1,0:T(8,128)(2,1)S(1)}, u32[]{:S(2)}, u32[]{:S(2)}) %collective-permute-start.2) | collective-permute-done | bytes 65568 | tf_op jit(solution)/shard_map/ppermute | solution.py:247
  28.0 0.0 collective-permute-done.3.refs_3_
  28.0 0.0 collective-permute-done.refs_6_
  28.0 0.0 copy-done
  28.1 0.1 collective-permute-start.4
  28.1 0.5 %collective-permute-start.5 = (bf16[8,128,256]{2,1,0:T(8,128)(2,1)S(1)}, bf16[8,128,256]{2,1,0:T(8,128)(2,1)S(1)}, u32[]{:S(2)}, u32[]{:S(2)}) collective-permute-start(bf16[8,128,256]{2,1,0:T(8,128)(2,1)S(1)} %collective-permute-done.refs_6_), channel_id=1, source_target_pairs={{0,1},{1,0},{2,3},{3,2},{4,5},{5,4},{6,7},{7,6},{8,9},{9,8},{10,11... | collective-permute-start | bytes 1572872 | tf_op jit(solution)/shard_map/ppermute | solution.py:247
  28.6 0.0 all-to-all-done.key_ref
  28.6 0.0 copy-start.1
  28.6 3.8 %all-to-all-start.1 = ((bf16[16,8,8,128]{3,2,1,0:T(8,128)(2,1)}), bf16[16,8,8,128]{3,2,1,0:T(8,128)(2,1)S(1)}, u32[]{:S(2)}, u32[]{:S(2)}) async-start(bf16[16,8,8,128]{3,2,1,0:T(8,128)(2,1)} %bitcast.4), calls=%async_computation.1 | async-start | bytes 524288 | tf_op jit(solution)/shard_map/all_to_all | solution.py:276
  32.5 0.0 collective-permute-done.4.refs_5_
  32.5 0.0 collective-permute-done.5.refs_7_
  32.5 0.0 copy-done.1
  32.5 1.5 %stale.1 = (bf16[8,4224]{1,0:T(8,128)(2,1)S(1)}, bf16[8,4224]{1,0:T(8,128)(2,1)S(1)}, bf16[8,4224]{1,0:T(8,128)(2,1)S(1)}, bf16[8,4224]{1,0:T(8,128)(2,1)S(1)}) custom-call(bf16[8,4096]{1,0:T(8,128)(2,1)S(1)} %copy-done.1, bf16[8,4096]{1,0:T(8,128)(2,1)S(1)} %collective-permute-done.1.refs_1_, bf16[8,4096]{1,0:T(8,128)(2,1)S(1)} %collective-permute-done.2.refs_2_, ...), custom_call_target="tpu_custom_call" | custom-call | tf_op jit(solution)/shard_map/stale/pallas_call | solution.py:309
  34.0 2.0 %collective-permute-start.6 = (bf16[8,4224]{1,0:T(8,128)(2,1)S(1)}, bf16[8,4224]{1,0:T(8,128)(2,1)S(1)}, u32[]{:S(2)}, u32[]{:S(2)}) collective-permute-start(bf16[8,4224]{1,0:T(8,128)(2,1)S(1)} %get-tuple-element.43), channel_id=1, source_target_pairs={{0,4},{1,5},{2,6},{3,7},{4,0},{5,1},{6,2},{7,3},{8,12},{9,13},{10,... | collective-permute-start | bytes 202760 | tf_op jit(solution)/shard_map/ppermute | solution.py:247
  36.0 2.4 %collective-permute-start.7 = (bf16[8,4224]{1,0:T(8,128)(2,1)S(1)}, bf16[8,4224]{1,0:T(8,128)(2,1)S(1)}, u32[]{:S(2)}, u32[]{:S(2)}) collective-permute-start(bf16[8,4224]{1,0:T(8,128)(2,1)S(1)} %get-tuple-element.44), channel_id=1, source_target_pairs={{0,8},{1,9},{2,10},{3,11},{4,12},{5,13},{6,14},{7,15},{8,0},{9,1},... | collective-permute-start | bytes 202760 | tf_op jit(solution)/shard_map/ppermute | solution.py:247
  38.4 0.1 collective-permute-start.8
  38.5 2.1 %fresh.1 = (f32[4,8,4096]{2,1,0:T(8,128)S(1)}, f32[4,8,128]{2,1,0:T(8,128)S(1)}) custom-call(bf16[8,4096]{1,0:T(8,128)(2,1)S(1)} %copy-done.1, bf16[8,4096]{1,0:T(8,128)(2,1)S(1)} %copy-done.3, bf16[8,4096]{1,0:T(8,128)(2,1)S(1)} %copy-done.4, bf16[8,4096]{1,0:T(8,128)(2,1)S(1)} %copy-done.5, bf16[16,8,1024]{2,1,0:T(8,128)(2,1)} %key.1.refs_4_, ...), custom_call_target="tpu_custom_call" | custom-call | tf_op jit(solution)/shard_map/fresh/pallas_call | solution.py:319
  40.6 0.3 collective-permute-done.6.refs_1_
  40.9 6.0 %collective-permute-done.7.refs_2_ = bf16[8,4224]{1,0:T(8,128)(2,1)S(1)} collective-permute-done((bf16[8,4224]{1,0:T(8,128)(2,1)S(1)}, bf16[8,4224]{1,0:T(8,128)(2,1)S(1)}, u32[]{:S(2)}, u32[]{:S(2)}) %collective-permute-start.7) | collective-permute-done | bytes 67616 | tf_op jit(solution)/shard_map/ppermute | solution.py:247
  46.9 0.0 collective-permute-done.8.refs_3_
  46.9 1.2 %join.1 = bf16[4,8,4096]{2,1,0:T(8,128)(2,1)} custom-call(bf16[8,4224]{1,0:T(8,128)(2,1)S(1)} %get-tuple-element.42.refs_0_, bf16[8,4224]{1,0:T(8,128)(2,1)S(1)} %collective-permute-done.6.refs_1_, bf16[8,4224]{1,0:T(8,128)(2,1)S(1)} %collective-permute-done.7.refs_2_, bf16[8,4224]{1,0:T(8,128)(2,1)S(1)} %collective-permute-done.8.refs_3_, ...), custom_call_target="tpu_custom_call" | custom-call | tf_op jit(solution)/shard_map/join/pallas_call | solution.py:330
  48.1 0.0 all-to-all-done.1.value_ref
  48.1 0.9 %cache.1 = bf16[8,16,8,256]{3,2,1,0:T(8,128)(2,1)} custom-call(bf16[16,8,1024]{2,1,0:T(8,128)(2,1)S(1)} %all-to-all-done.key_ref, bf16[16,8,8,128]{3,2,1,0:T(8,128)(2,1)S(1)} %all-to-all-done.1.value_ref), custom_call_target="tpu_custom_call" | custom-call | tf_op jit(solution)/shard_map/cache/pallas_call | solution.py:343
Async XLA Ops:
  0.6 5.9 %copy-start.2 = (bf16[4,8,4096]{2,1,0:T(8,128)(2,1)S(1)}, bf16[4,8,4096]{2,1,0:T(8,128)(2,1)}, u32[]{:S(2)}) copy-start(bf16[4,8,4096]{2,1,0:T(8,128)(2,1)} %k_ref.1) | copy-start | bytes 786436
  0.6 27.4 %collective-permute-start = (bf16[8,128,256]{2,1,0:T(8,128)(2,1)}, bf16[8,128,256]{2,1,0:T(8,128)(2,1)S(1)}, u32[]{:S(2)}, u32[]{:S(2)}) collective-permute-start(bf16[8,128,256]{2,1,0:T(8,128)(2,1)} %refs_4_), channel_id=1, source_target_pairs={{0,2},{1,3},{2,0},{3,1},{4,6},{5,7},{6,4},{7,5},{8,10},{9,11},{10,... | collective-permute-start | bytes 1572872 | tf_op jit(solution)/shard_map/ppermute | solution.py:247
  3.6 2.9 %copy-start.6 = (f32[4096]{0:T(1024)S(1)}, f32[4096]{0:T(1024)}, u32[]{:S(2)}) copy-start(f32[4096]{0:T(1024)} %param.11) | copy-start | bytes 49156
  6.5 0.7 %copy-start.7 = (f32[3,8,128]{2,1,0:T(8,128)S(1)}, f32[3,8,128]{2,1,0:T(8,128)}, u32[]{:S(2)}) copy-start(f32[3,8,128]{2,1,0:T(8,128)} %get-tuple-element.41.tables_ref) | copy-start | bytes 36868
  7.3 20.8 %copy-start = (bf16[8,128,256]{2,1,0:T(8,128)(2,1)S(1)}, bf16[8,128,256]{2,1,0:T(8,128)(2,1)}, u32[]{:S(2)}) copy-start(bf16[8,128,256]{2,1,0:T(8,128)(2,1)} %refs_4_) | copy-start | bytes 1572868
  8.6 5.1 %copy-start.3 = (bf16[8,4096]{1,0:T(8,128)(2,1)S(1)}, bf16[8,4096]{1,0:T(8,128)(2,1)}, u32[]{:S(2)}) copy-start(bf16[8,4096]{1,0:T(8,128)(2,1)} %get-tuple-element.28.refs_1_) | copy-start | bytes 196612
  8.6 7.1 %copy-start.4 = (bf16[8,4096]{1,0:T(8,128)(2,1)S(1)}, bf16[8,4096]{1,0:T(8,128)(2,1)}, u32[]{:S(2)}) copy-start(bf16[8,4096]{1,0:T(8,128)(2,1)} %get-tuple-element.29.refs_2_) | copy-start | bytes 196612
  8.6 9.5 %copy-start.5 = (bf16[8,4096]{1,0:T(8,128)(2,1)S(1)}, bf16[8,4096]{1,0:T(8,128)(2,1)}, u32[]{:S(2)}) copy-start(bf16[8,4096]{1,0:T(8,128)(2,1)} %get-tuple-element.30.refs_3_) | copy-start | bytes 196612
  8.6 20.0 %all-to-all-start = ((bf16[16,8,1024]{2,1,0:T(8,128)(2,1)}), bf16[16,8,1024]{2,1,0:T(8,128)(2,1)S(1)}, u32[]{:S(2)}, u32[]{:S(2)}) async-start(bf16[16,8,1024]{2,1,0:T(8,128)(2,1)} %key.1.refs_4_), calls=%async_computation | async-start | bytes 524288 | tf_op jit(solution)/shard_map/all_to_all | solution.py:304
  13.7 8.4 %collective-permute-start.1 = (bf16[8,4096]{1,0:T(8,128)(2,1)S(1)}, bf16[8,4096]{1,0:T(8,128)(2,1)S(1)}, u32[]{:S(2)}, u32[]{:S(2)}) collective-permute-start(bf16[8,4096]{1,0:T(8,128)(2,1)S(1)} %copy-done.3), channel_id=1, source_target_pairs={{0,4},{1,5},{2,6},{3,7},{4,0},{5,1},{6,2},{7,3},{8,12},{9,13},{10,... | collective-permute-start | bytes 196616 | tf_op jit(solution)/shard_map/ppermute | solution.py:247
  15.7 12.3 %collective-permute-start.2 = (bf16[8,4096]{1,0:T(8,128)(2,1)S(1)}, bf16[8,4096]{1,0:T(8,128)(2,1)S(1)}, u32[]{:S(2)}, u32[]{:S(2)}) collective-permute-start(bf16[8,4096]{1,0:T(8,128)(2,1)S(1)} %copy-done.4), channel_id=1, source_target_pairs={{0,8},{1,9},{2,10},{3,11},{4,12},{5,13},{6,14},{7,15},{8,0},{9,1},... | collective-permute-start | bytes 196616 | tf_op jit(solution)/shard_map/ppermute | solution.py:247
  18.1 10.0 %collective-permute-start.3 = (bf16[8,4096]{1,0:T(8,128)(2,1)S(1)}, bf16[8,4096]{1,0:T(8,128)(2,1)S(1)}, u32[]{:S(2)}, u32[]{:S(2)}) collective-permute-start(bf16[8,4096]{1,0:T(8,128)(2,1)S(1)} %copy-done.5), channel_id=1, source_target_pairs={{0,12},{1,13},{2,14},{3,15},{4,8},{5,9},{6,10},{7,11},{8,4},{9,5},... | collective-permute-start | bytes 196616 | tf_op jit(solution)/shard_map/ppermute | solution.py:247
  28.1 4.4 %collective-permute-start.4 = (bf16[8,128,256]{2,1,0:T(8,128)(2,1)S(1)}, bf16[8,128,256]{2,1,0:T(8,128)(2,1)S(1)}, u32[]{:S(2)}, u32[]{:S(2)}) collective-permute-start(bf16[8,128,256]{2,1,0:T(8,128)(2,1)S(1)} %copy-done), channel_id=1, source_target_pairs={{0,1},{1,0},{2,3},{3,2},{4,5},{5,4},{6,7},{7,6},{8,9},{9,8},{10,11... | collective-permute-start | bytes 1572872 | tf_op jit(solution)/shard_map/ppermute | solution.py:247
  28.1 4.4 %collective-permute-start.5 = (bf16[8,128,256]{2,1,0:T(8,128)(2,1)S(1)}, bf16[8,128,256]{2,1,0:T(8,128)(2,1)S(1)}, u32[]{:S(2)}, u32[]{:S(2)}) collective-permute-start(bf16[8,128,256]{2,1,0:T(8,128)(2,1)S(1)} %collective-permute-done.refs_6_), channel_id=1, source_target_pairs={{0,1},{1,0},{2,3},{3,2},{4,5},{5,4},{6,7},{7,6},{8,9},{9,8},{10,11... | collective-permute-start | bytes 1572872 | tf_op jit(solution)/shard_map/ppermute | solution.py:247
  28.6 3.9 %copy-start.1 = (bf16[8,4096]{1,0:T(8,128)(2,1)S(1)}, bf16[8,4096]{1,0:T(8,128)(2,1)}, u32[]{:S(2)}) copy-start(bf16[8,4096]{1,0:T(8,128)(2,1)} %get-tuple-element.31.refs_0_) | copy-start | bytes 196612
  28.6 19.5 %all-to-all-start.1 = ((bf16[16,8,8,128]{3,2,1,0:T(8,128)(2,1)}), bf16[16,8,8,128]{3,2,1,0:T(8,128)(2,1)S(1)}, u32[]{:S(2)}, u32[]{:S(2)}) async-start(bf16[16,8,8,128]{3,2,1,0:T(8,128)(2,1)} %bitcast.4), calls=%async_computation.1 | async-start | bytes 524288 | tf_op jit(solution)/shard_map/all_to_all | solution.py:276
  34.0 6.9 %collective-permute-start.6 = (bf16[8,4224]{1,0:T(8,128)(2,1)S(1)}, bf16[8,4224]{1,0:T(8,128)(2,1)S(1)}, u32[]{:S(2)}, u32[]{:S(2)}) collective-permute-start(bf16[8,4224]{1,0:T(8,128)(2,1)S(1)} %get-tuple-element.43), channel_id=1, source_target_pairs={{0,4},{1,5},{2,6},{3,7},{4,0},{5,1},{6,2},{7,3},{8,12},{9,13},{10,... | collective-permute-start | bytes 202760 | tf_op jit(solution)/shard_map/ppermute | solution.py:247
  36.0 11.0 %collective-permute-start.7 = (bf16[8,4224]{1,0:T(8,128)(2,1)S(1)}, bf16[8,4224]{1,0:T(8,128)(2,1)S(1)}, u32[]{:S(2)}, u32[]{:S(2)}) collective-permute-start(bf16[8,4224]{1,0:T(8,128)(2,1)S(1)} %get-tuple-element.44), channel_id=1, source_target_pairs={{0,8},{1,9},{2,10},{3,11},{4,12},{5,13},{6,14},{7,15},{8,0},{9,1},... | collective-permute-start | bytes 202760 | tf_op jit(solution)/shard_map/ppermute | solution.py:247
  38.4 8.6 %collective-permute-start.8 = (bf16[8,4224]{1,0:T(8,128)(2,1)S(1)}, bf16[8,4224]{1,0:T(8,128)(2,1)S(1)}, u32[]{:S(2)}, u32[]{:S(2)}) collective-permute-start(bf16[8,4224]{1,0:T(8,128)(2,1)S(1)} %get-tuple-element.45), channel_id=1, source_target_pairs={{0,12},{1,13},{2,14},{3,15},{4,8},{5,9},{6,10},{7,11},{8,4},{9,5},... | collective-permute-start | bytes 202760 | tf_op jit(solution)/shard_map/ppermute | solution.py:247

commit v10 on v9

--- a/solution.py
+++ b/solution.py
@@ -301,7 +301,8 @@
         in_specs=[VMEM] * 3,
         out_specs=VMEM,
     )(keys, k_gain.reshape(1, width), tables)
-    key_got = lax.all_to_all(key, "patch", split_axis=0, concat_axis=0, tiled=True)
+    key_sent, value_got = lax.optimization_barrier((key, value_got))
+    key_got = lax.all_to_all(key_sent, "patch", split_axis=0, concat_axis=0, tiled=True)
     pieces, query_got = lax.optimization_barrier((pieces, query_got))
     while bit > 1:
         bit //= 2
@@ -327,6 +328,15 @@
         in_specs=[VMEM] * (videos + 2),
         out_specs=(VMEM, VMEM),
     )(*query, key_late, values)
+    next_cache = kernel(
+        cache_kernel,
+        "cache",
+        16,
+        out_shape=jax.ShapeDtypeStruct((pairs_here, patches, tok_rows, 2 * DH), BF16),
+        in_specs=[VMEM, VMEM],
+        out_specs=HBM,
+        scratch_shapes=[pltpu.SemaphoreType.DMA((2, pairs_here))],
+    )(key_got, value_got)
     attended = kernel(
         functools.partial(join_kernel, groups, videos),
         "join",
@@ -339,16 +349,6 @@
             pltpu.SemaphoreType.DMA((videos,)),
         ],
     )(*back, fresh_sum, fresh_log)
-    attended, key_got, value_got = lax.optimization_barrier((attended, key_got, value_got))
-    next_cache = kernel(
-        cache_kernel,
-        "cache",
-        16,
-        out_shape=jax.ShapeDtypeStruct((pairs_here, patches, tok_rows, 2 * DH), BF16),
-        in_specs=[VMEM, VMEM],
-        out_specs=HBM,
-        scratch_shapes=[pltpu.SemaphoreType.DMA((2, pairs_here))],
-    )(key_got, value_got)
     return (attended, next_cache.reshape(stale_cache.shape))
 
 

time: 49.5 us -> 45.8 us (0.925)
  waiting for transfers between devices: 16.2 us -> 12.3 us
    ppermute x9, waiting for transfers between devices: 16.2 us -> 7.85 us  [permuted(): lax.ppermute(array, 'patch', [(i, i ^ offset) for i in range(patches)])]
    all_to_all x1, waiting for transfers between devices: 0.01 us -> 4.48 us  [local(): lax.all_to_all(key_sent, 'patch', split_axis=0, concat_axis=0, tiled=True)]
    all_to_all x1, starting transfers between devices: 3.84 us -> 4.98 us  [local(): lax.all_to_all(value_sent.reshape(patches, pairs_here, tok_rows, DH), 'pa...]
    all_to_all x1, starting transfers between devices: 5.11 us -> 4.1 us  [local(): lax.all_to_all(key_sent, 'patch', split_axis=0, concat_axis=0, tiled=True)]
  transfers between devices with their start and end apart: 11 -> 11, of which waited for: 4 -> 4; matrix products, arithmetic and copies ran while one was open for 0% -> 0% of each run, Pallas kernels for 18% -> 19%
where the time goes in v10:
time: 45.8 us; the launch traced here: 45.3 us
  starting transfers between devices  21.6 us (47%)
  waiting for transfers between devices  12.3 us (27%)
  Pallas kernels  9.89 us (22%)
  between operations  0.8 us (2%)
  local copies, waits for them, and re-layouts  0.74 us (2%)
    ppermute x9, starting transfers between devices, permuted(): lax.ppermute(array, 'patch', [(i, i ^ offset) for i in range(patches)])  12.5 us
    ppermute x9, waiting for transfers between devices, permuted(): lax.ppermute(array, 'patch', [(i, i ^ offset) for i in range(patches)])  7.85 us
    all_to_all x1, starting transfers between devices, local(): lax.all_to_all(value_sent.reshape(patches, pairs_here, tok_rows, DH), 'pa...  4.98 us
    all_to_all x1, waiting for transfers between devices, local(): lax.all_to_all(key_sent, 'patch', split_axis=0, concat_axis=0, tiled=True)  4.48 us
    all_to_all x1, starting transfers between devices, local(): lax.all_to_all(key_sent, 'patch', split_axis=0, concat_axis=0, tiled=True)  4.1 us
    pallas_call x1, Pallas kernels, local(): kernel(functools.partial(query_kernel, groups), 'query', 56, out_shape=[r...  2.92 us
    pallas_call x1, Pallas kernels, local(): kernel(functools.partial(fresh_kernel, groups, videos), 'fresh', 16, out_...  2.06 us
    pallas_call x1, Pallas kernels, local(): kernel(functools.partial(stale_kernel, groups, videos), 'stale', 32, out_...  1.52 us
  transfers between devices with their start and end apart: 11, of which 4 were waited for; matrix products, arithmetic and copies ran while one was open for 0% of the time, Pallas kernels for 19%

profile of v10, /device:TPU:0, one launch (start us, length us, event | category | flops | bytes accessed | tf_op | source)
XLA Modules:
  0.0 45.3 jit_solution(17657433710313824230)
XLA Ops:
  0.6 0.0 copy-start.1
  0.6 3.0 %collective-permute-start = (bf16[8,128,256]{2,1,0:T(8,128)(2,1)}, bf16[8,128,256]{2,1,0:T(8,128)(2,1)S(1)}, u32[]{:S(2)}, u32[]{:S(2)}) collective-permute-start(bf16[8,128,256]{2,1,0:T(8,128)(2,1)} %refs_4_), channel_id=1, source_target_pairs={{0,2},{1,3},{2,0},{3,1},{4,6},{5,7},{6,4},{7,5},{8,10},{9,11},{10,... | collective-permute-start | bytes 1572872 | tf_op jit(solution)/shard_map/ppermute | solution.py:247
  3.6 5.0 %all-to-all-start = ((bf16[16,8,8,128]{3,2,1,0:T(8,128)(2,1)}), bf16[16,8,8,128]{3,2,1,0:T(8,128)(2,1)S(1)}, u32[]{:S(2)}, u32[]{:S(2)}) async-start(bf16[16,8,8,128]{3,2,1,0:T(8,128)(2,1)} %bitcast.8), calls=%async_computation | async-start | bytes 524288 | tf_op jit(solution)/shard_map/all_to_all | solution.py:276
  8.6 0.0 copy-start.3
  8.6 0.0 copy-start.7
  8.7 2.9 %query.1 = (bf16[8,4096]{1,0:T(8,128)(2,1)}, bf16[8,4096]{1,0:T(8,128)(2,1)}, bf16[8,4096]{1,0:T(8,128)(2,1)}, bf16[8,4096]{1,0:T(8,128)(2,1)}, f32[3,8,128]{2,1,0:T(8,128)}) custom-call(bf16[4,8,4096]{2,1,0:T(8,128)(2,1)} %q_hbm.1, f32[1,4096]{1,0:T(1,128)} %bitcast.11, s32[3,8]{1,0:T(4,128)} %coords_hbm.1), custom_call_target="tpu_custom_call" | custom-call | tf_op jit(solution)/shard_map/query/pallas_call | solution.py:279
  11.6 2.0 %collective-permute-start.1 = (bf16[8,4096]{1,0:T(8,128)(2,1)}, bf16[8,4096]{1,0:T(8,128)(2,1)S(1)}, u32[]{:S(2)}, u32[]{:S(2)}) collective-permute-start(bf16[8,4096]{1,0:T(8,128)(2,1)} %get-tuple-element.27.refs_1_), channel_id=1, source_target_pairs={{0,4},{1,5},{2,6},{3,7},{4,0},{5,1},{6,2},{7,3},{8,12},{9,13},{10,... | collective-permute-start | bytes 196616 | tf_op jit(solution)/shard_map/ppermute | solution.py:247
  13.6 2.4 %collective-permute-start.2 = (bf16[8,4096]{1,0:T(8,128)(2,1)}, bf16[8,4096]{1,0:T(8,128)(2,1)S(1)}, u32[]{:S(2)}, u32[]{:S(2)}) collective-permute-start(bf16[8,4096]{1,0:T(8,128)(2,1)} %get-tuple-element.28.refs_2_), channel_id=1, source_target_pairs={{0,8},{1,9},{2,10},{3,11},{4,12},{5,13},{6,14},{7,15},{8,0},{9,1},... | collective-permute-start | bytes 196616 | tf_op jit(solution)/shard_map/ppermute | solution.py:247
  15.9 0.1 collective-permute-start.3
  16.0 1.3 %collective-permute-done.1.refs_1_ = bf16[8,4096]{1,0:T(8,128)(2,1)S(1)} collective-permute-done((bf16[8,4096]{1,0:T(8,128)(2,1)}, bf16[8,4096]{1,0:T(8,128)(2,1)S(1)}, u32[]{:S(2)}, u32[]{:S(2)}) %collective-permute-start.1) | collective-permute-done | bytes 65568 | tf_op jit(solution)/shard_map/ppermute | solution.py:247
  17.3 5.6 %collective-permute-done.2.refs_2_ = bf16[8,4096]{1,0:T(8,128)(2,1)S(1)} collective-permute-done((bf16[8,4096]{1,0:T(8,128)(2,1)}, bf16[8,4096]{1,0:T(8,128)(2,1)S(1)}, u32[]{:S(2)}, u32[]{:S(2)}) %collective-permute-start.2) | collective-permute-done | bytes 65568 | tf_op jit(solution)/shard_map/ppermute | solution.py:247
  23.0 0.0 collective-permute-done.3.refs_3_
  23.0 0.0 collective-permute-done.refs_6_
  23.0 0.0 copy-done.1
  23.0 0.1 collective-permute-start.4
  23.1 0.5 %collective-permute-start.5 = (bf16[8,128,256]{2,1,0:T(8,128)(2,1)S(1)}, bf16[8,128,256]{2,1,0:T(8,128)(2,1)S(1)}, u32[]{:S(2)}, u32[]{:S(2)}) collective-permute-start(bf16[8,128,256]{2,1,0:T(8,128)(2,1)S(1)} %collective-permute-done.refs_6_), channel_id=1, source_target_pairs={{0,1},{1,0},{2,3},{3,2},{4,5},{5,4},{6,7},{7,6},{8,9},{9,8},{10,11... | collective-permute-start | bytes 1572872 | tf_op jit(solution)/shard_map/ppermute | solution.py:247
  23.6 0.0 copy-done.3
  23.6 0.0 copy-done.7
  23.6 0.0 copy-start.8
  23.6 0.7 %copy-done.8 = f32[3,8,128]{2,1,0:T(8,128)S(1)} copy-done((f32[3,8,128]{2,1,0:T(8,128)S(1)}, f32[3,8,128]{2,1,0:T(8,128)}, u32[]{:S(2)}) %copy-start.8) | copy-done | bytes 12312
  24.3 1.3 %key.1.refs_4_ = bf16[16,8,1024]{2,1,0:T(8,128)(2,1)} custom-call(bf16[4,8,4096]{2,1,0:T(8,128)(2,1)S(1)} %copy-done.3, f32[1,4096]{1,0:T(1,128)S(1)} %bitcast.9, f32[3,8,128]{2,1,0:T(8,128)S(1)} %copy-done.8), custom_call_target="tpu_custom_call" | custom-call | tf_op jit(solution)/shard_map/key/pallas_call | solution.py:296
  25.6 0.0 copy-start.2
  25.6 0.0 all-to-all-done.value_ref
  25.6 4.1 %all-to-all-start.1 = ((bf16[16,8,1024]{2,1,0:T(8,128)(2,1)}), bf16[16,8,1024]{2,1,0:T(8,128)(2,1)S(1)}, u32[]{:S(2)}, u32[]{:S(2)}) async-start(bf16[16,8,1024]{2,1,0:T(8,128)(2,1)} %key.1.refs_4_), calls=%async_computation.1 | async-start | bytes 524288 | tf_op jit(solution)/shard_map/all_to_all | solution.py:305
  29.7 0.0 collective-permute-done.4.refs_5_
  29.7 0.0 collective-permute-done.5.refs_7_
  29.7 0.0 copy-done.2
  29.7 1.5 %stale.1 = (bf16[8,4224]{1,0:T(8,128)(2,1)S(1)}, bf16[8,4224]{1,0:T(8,128)(2,1)S(1)}, bf16[8,4224]{1,0:T(8,128)(2,1)S(1)}, bf16[8,4224]{1,0:T(8,128)(2,1)S(1)}) custom-call(bf16[8,4096]{1,0:T(8,128)(2,1)S(1)} %copy-done.2, bf16[8,4096]{1,0:T(8,128)(2,1)S(1)} %collective-permute-done.1.refs_1_, bf16[8,4096]{1,0:T(8,128)(2,1)S(1)} %collective-permute-done.2.refs_2_, ...), custom_call_target="tpu_custom_call" | custom-call | tf_op jit(solution)/shard_map/stale/pallas_call | solution.py:310
  31.3 0.0 copy-start
  31.3 0.0 copy-start.4
  31.3 0.0 copy-start.5
  31.3 0.0 copy-start.6
  31.3 2.0 %collective-permute-start.6 = (bf16[8,4224]{1,0:T(8,128)(2,1)S(1)}, bf16[8,4224]{1,0:T(8,128)(2,1)S(1)}, u32[]{:S(2)}, u32[]{:S(2)}) collective-permute-start(bf16[8,4224]{1,0:T(8,128)(2,1)S(1)} %get-tuple-element.42), channel_id=1, source_target_pairs={{0,4},{1,5},{2,6},{3,7},{4,0},{5,1},{6,2},{7,3},{8,12},{9,13},{10,... | collective-permute-start | bytes 202760 | tf_op jit(solution)/shard_map/ppermute | solution.py:247
  33.3 2.4 %collective-permute-start.7 = (bf16[8,4224]{1,0:T(8,128)(2,1)S(1)}, bf16[8,4224]{1,0:T(8,128)(2,1)S(1)}, u32[]{:S(2)}, u32[]{:S(2)}) collective-permute-start(bf16[8,4224]{1,0:T(8,128)(2,1)S(1)} %get-tuple-element.43), channel_id=1, source_target_pairs={{0,8},{1,9},{2,10},{3,11},{4,12},{5,13},{6,14},{7,15},{8,0},{9,1},... | collective-permute-start | bytes 202760 | tf_op jit(solution)/shard_map/ppermute | solution.py:247
  35.6 0.1 collective-permute-start.8
  35.7 4.5 %all-to-all-done.1.key_ref = bf16[16,8,1024]{2,1,0:T(8,128)(2,1)S(1)} async-done(((bf16[16,8,1024]{2,1,0:T(8,128)(2,1)}), bf16[16,8,1024]{2,1,0:T(8,128)(2,1)S(1)}, u32[]{:S(2)}, u32[]{:S(2)}) %all-to-all-start.1) | async-done | bytes 262176 | tf_op jit(solution)/shard_map/all_to_all | solution.py:305
  40.2 0.9 %cache.1 = bf16[8,16,8,256]{3,2,1,0:T(8,128)(2,1)} custom-call(bf16[16,8,1024]{2,1,0:T(8,128)(2,1)S(1)} %all-to-all-done.1.key_ref, bf16[16,8,8,128]{3,2,1,0:T(8,128)(2,1)S(1)} %all-to-all-done.value_ref), custom_call_target="tpu_custom_call" | custom-call | tf_op jit(solution)/shard_map/cache/pallas_call | solution.py:331
  41.1 0.0 copy-done
  41.2 0.0 copy-done.4
  41.2 0.0 copy-done.5
  41.2 0.0 copy-done.6
  41.2 2.1 %fresh.1 = (f32[4,8,4096]{2,1,0:T(8,128)S(1)}, f32[4,8,128]{2,1,0:T(8,128)S(1)}) custom-call(bf16[8,4096]{1,0:T(8,128)(2,1)S(1)} %copy-done.2, bf16[8,4096]{1,0:T(8,128)(2,1)S(1)} %copy-done.4, bf16[8,4096]{1,0:T(8,128)(2,1)S(1)} %copy-done.5, bf16[8,4096]{1,0:T(8,128)(2,1)S(1)} %copy-done.6, bf16[16,8,1024]{2,1,0:T(8,128)(2,1)} %key.1.refs_4_, ...), custom_call_target="tpu_custom_call" | custom-call | tf_op jit(solution)/shard_map/fresh/pallas_call | solution.py:320
  43.3 0.0 collective-permute-done.6.refs_1_
  43.3 0.9 %collective-permute-done.7.refs_2_ = bf16[8,4224]{1,0:T(8,128)(2,1)S(1)} collective-permute-done((bf16[8,4224]{1,0:T(8,128)(2,1)S(1)}, bf16[8,4224]{1,0:T(8,128)(2,1)S(1)}, u32[]{:S(2)}, u32[]{:S(2)}) %collective-permute-start.7) | collective-permute-done | bytes 67616 | tf_op jit(solution)/shard_map/ppermute | solution.py:247
  44.2 0.0 collective-permute-done.8.refs_3_
  44.2 1.2 %join.1 = bf16[4,8,4096]{2,1,0:T(8,128)(2,1)} custom-call(bf16[8,4224]{1,0:T(8,128)(2,1)S(1)} %get-tuple-element.41.refs_0_, bf16[8,4224]{1,0:T(8,128)(2,1)S(1)} %collective-permute-done.6.refs_1_, bf16[8,4224]{1,0:T(8,128)(2,1)S(1)} %collective-permute-done.7.refs_2_, bf16[8,4224]{1,0:T(8,128)(2,1)S(1)} %collective-permute-done.8.refs_3_, ...), custom_call_target="tpu_custom_call" | custom-call | tf_op jit(solution)/shard_map/join/pallas_call | solution.py:340
Async XLA Ops:
  0.6 22.3 %copy-start.1 = (bf16[8,128,256]{2,1,0:T(8,128)(2,1)S(1)}, bf16[8,128,256]{2,1,0:T(8,128)(2,1)}, u32[]{:S(2)}) copy-start(bf16[8,128,256]{2,1,0:T(8,128)(2,1)} %refs_4_) | copy-start | bytes 1572868
  0.6 22.3 %collective-permute-start = (bf16[8,128,256]{2,1,0:T(8,128)(2,1)}, bf16[8,128,256]{2,1,0:T(8,128)(2,1)S(1)}, u32[]{:S(2)}, u32[]{:S(2)}) collective-permute-start(bf16[8,128,256]{2,1,0:T(8,128)(2,1)} %refs_4_), channel_id=1, source_target_pairs={{0,2},{1,3},{2,0},{3,1},{4,6},{5,7},{6,4},{7,5},{8,10},{9,11},{10,... | collective-permute-start | bytes 1572872 | tf_op jit(solution)/shard_map/ppermute | solution.py:247
  3.6 22.0 %all-to-all-start = ((bf16[16,8,8,128]{3,2,1,0:T(8,128)(2,1)}), bf16[16,8,8,128]{3,2,1,0:T(8,128)(2,1)S(1)}, u32[]{:S(2)}, u32[]{:S(2)}) async-start(bf16[16,8,8,128]{3,2,1,0:T(8,128)(2,1)} %bitcast.8), calls=%async_computation | async-start | bytes 524288 | tf_op jit(solution)/shard_map/all_to_all | solution.py:276
  8.6 14.9 %copy-start.3 = (bf16[4,8,4096]{2,1,0:T(8,128)(2,1)S(1)}, bf16[4,8,4096]{2,1,0:T(8,128)(2,1)}, u32[]{:S(2)}) copy-start(bf16[4,8,4096]{2,1,0:T(8,128)(2,1)} %k_ref.1) | copy-start | bytes 786436
  8.6 14.9 %copy-start.7 = (f32[4096]{0:T(1024)S(1)}, f32[4096]{0:T(1024)}, u32[]{:S(2)}) copy-start(f32[4096]{0:T(1024)} %param.11) | copy-start | bytes 49156
  11.6 5.8 %collective-permute-start.1 = (bf16[8,4096]{1,0:T(8,128)(2,1)}, bf16[8,4096]{1,0:T(8,128)(2,1)S(1)}, u32[]{:S(2)}, u32[]{:S(2)}) collective-permute-start(bf16[8,4096]{1,0:T(8,128)(2,1)} %get-tuple-element.27.refs_1_), channel_id=1, source_target_pairs={{0,4},{1,5},{2,6},{3,7},{4,0},{5,1},{6,2},{7,3},{8,12},{9,13},{10,... | collective-permute-start | bytes 196616 | tf_op jit(solution)/shard_map/ppermute | solution.py:247
  13.6 9.4 %collective-permute-start.2 = (bf16[8,4096]{1,0:T(8,128)(2,1)}, bf16[8,4096]{1,0:T(8,128)(2,1)S(1)}, u32[]{:S(2)}, u32[]{:S(2)}) collective-permute-start(bf16[8,4096]{1,0:T(8,128)(2,1)} %get-tuple-element.28.refs_2_), channel_id=1, source_target_pairs={{0,8},{1,9},{2,10},{3,11},{4,12},{5,13},{6,14},{7,15},{8,0},{9,1},... | collective-permute-start | bytes 196616 | tf_op jit(solution)/shard_map/ppermute | solution.py:247
  15.9 7.0 %collective-permute-start.3 = (bf16[8,4096]{1,0:T(8,128)(2,1)}, bf16[8,4096]{1,0:T(8,128)(2,1)S(1)}, u32[]{:S(2)}, u32[]{:S(2)}) collective-permute-start(bf16[8,4096]{1,0:T(8,128)(2,1)} %get-tuple-element.29.refs_3_), channel_id=1, source_target_pairs={{0,12},{1,13},{2,14},{3,15},{4,8},{5,9},{6,10},{7,11},{8,4},{9,5},... | collective-permute-start | bytes 196616 | tf_op jit(solution)/shard_map/ppermute | solution.py:247
  23.0 6.7 %collective-permute-start.4 = (bf16[8,128,256]{2,1,0:T(8,128)(2,1)S(1)}, bf16[8,128,256]{2,1,0:T(8,128)(2,1)S(1)}, u32[]{:S(2)}, u32[]{:S(2)}) collective-permute-start(bf16[8,128,256]{2,1,0:T(8,128)(2,1)S(1)} %copy-done.1), channel_id=1, source_target_pairs={{0,1},{1,0},{2,3},{3,2},{4,5},{5,4},{6,7},{7,6},{8,9},{9,8},{10,11... | collective-permute-start | bytes 1572872 | tf_op jit(solution)/shard_map/ppermute | solution.py:247
  23.1 6.7 %collective-permute-start.5 = (bf16[8,128,256]{2,1,0:T(8,128)(2,1)S(1)}, bf16[8,128,256]{2,1,0:T(8,128)(2,1)S(1)}, u32[]{:S(2)}, u32[]{:S(2)}) collective-permute-start(bf16[8,128,256]{2,1,0:T(8,128)(2,1)S(1)} %collective-permute-done.refs_6_), channel_id=1, source_target_pairs={{0,1},{1,0},{2,3},{3,2},{4,5},{5,4},{6,7},{7,6},{8,9},{9,8},{10,11... | collective-permute-start | bytes 1572872 | tf_op jit(solution)/shard_map/ppermute | solution.py:247
  23.6 0.7 %copy-start.8 = (f32[3,8,128]{2,1,0:T(8,128)S(1)}, f32[3,8,128]{2,1,0:T(8,128)}, u32[]{:S(2)}) copy-start(f32[3,8,128]{2,1,0:T(8,128)} %get-tuple-element.40.tables_ref) | copy-start | bytes 36868
  25.6 4.1 %copy-start.2 = (bf16[8,4096]{1,0:T(8,128)(2,1)S(1)}, bf16[8,4096]{1,0:T(8,128)(2,1)}, u32[]{:S(2)}) copy-start(bf16[8,4096]{1,0:T(8,128)(2,1)} %get-tuple-element.30.refs_0_) | copy-start | bytes 196612
  25.6 14.6 %all-to-all-start.1 = ((bf16[16,8,1024]{2,1,0:T(8,128)(2,1)}), bf16[16,8,1024]{2,1,0:T(8,128)(2,1)S(1)}, u32[]{:S(2)}, u32[]{:S(2)}) async-start(bf16[16,8,1024]{2,1,0:T(8,128)(2,1)} %key.1.refs_4_), calls=%async_computation.1 | async-start | bytes 524288 | tf_op jit(solution)/shard_map/all_to_all | solution.py:305
  31.3 9.9 %copy-start = (bf16[4,8,4096]{2,1,0:T(8,128)(2,1)S(1)}, bf16[4,8,4096]{2,1,0:T(8,128)(2,1)}, u32[]{:S(2)}) copy-start(bf16[4,8,4096]{2,1,0:T(8,128)(2,1)} %refs_5_.1) | copy-start | bytes 786436
  31.3 9.9 %copy-start.4 = (bf16[8,4096]{1,0:T(8,128)(2,1)S(1)}, bf16[8,4096]{1,0:T(8,128)(2,1)}, u32[]{:S(2)}) copy-start(bf16[8,4096]{1,0:T(8,128)(2,1)} %get-tuple-element.27.refs_1_) | copy-start | bytes 196612
  31.3 9.9 %copy-start.5 = (bf16[8,4096]{1,0:T(8,128)(2,1)S(1)}, bf16[8,4096]{1,0:T(8,128)(2,1)}, u32[]{:S(2)}) copy-start(bf16[8,4096]{1,0:T(8,128)(2,1)} %get-tuple-element.28.refs_2_) | copy-start | bytes 196612
  31.3 9.9 %copy-start.6 = (bf16[8,4096]{1,0:T(8,128)(2,1)S(1)}, bf16[8,4096]{1,0:T(8,128)(2,1)}, u32[]{:S(2)}) copy-start(bf16[8,4096]{1,0:T(8,128)(2,1)} %get-tuple-element.29.refs_3_) | copy-start | bytes 196612
  31.3 12.0 %collective-permute-start.6 = (bf16[8,4224]{1,0:T(8,128)(2,1)S(1)}, bf16[8,4224]{1,0:T(8,128)(2,1)S(1)}, u32[]{:S(2)}, u32[]{:S(2)}) collective-permute-start(bf16[8,4224]{1,0:T(8,128)(2,1)S(1)} %get-tuple-element.42), channel_id=1, source_target_pairs={{0,4},{1,5},{2,6},{3,7},{4,0},{5,1},{6,2},{7,3},{8,12},{9,13},{10,... | collective-permute-start | bytes 202760 | tf_op jit(solution)/shard_map/ppermute | solution.py:247
  33.3 10.9 %collective-permute-start.7 = (bf16[8,4224]{1,0:T(8,128)(2,1)S(1)}, bf16[8,4224]{1,0:T(8,128)(2,1)S(1)}, u32[]{:S(2)}, u32[]{:S(2)}) collective-permute-start(bf16[8,4224]{1,0:T(8,128)(2,1)S(1)} %get-tuple-element.43), channel_id=1, source_target_pairs={{0,8},{1,9},{2,10},{3,11},{4,12},{5,13},{6,14},{7,15},{8,0},{9,1},... | collective-permute-start | bytes 202760 | tf_op jit(solution)/shard_map/ppermute | solution.py:247
  35.6 8.5 %collective-permute-start.8 = (bf16[8,4224]{1,0:T(8,128)(2,1)S(1)}, bf16[8,4224]{1,0:T(8,128)(2,1)S(1)}, u32[]{:S(2)}, u32[]{:S(2)}) collective-permute-start(bf16[8,4224]{1,0:T(8,128)(2,1)S(1)} %get-tuple-element.44), channel_id=1, source_target_pairs={{0,12},{1,13},{2,14},{3,15},{4,8},{5,9},{6,10},{7,11},{8,4},{9,5},... | collective-permute-start | bytes 202760 | tf_op jit(solution)/shard_map/ppermute | solution.py:247

commit v11 on v9

--- a/solution.py
+++ b/solution.py
@@ -81,15 +81,19 @@
         send.wait()
 
 
-def key_kernel(k_ref, gain_ref, tables_ref, out_ref):
-    videos = k_ref.shape[0]
+def key_kernel(k_ref, v_ref, gain_ref, tables_ref, out_ref):
+    videos, tok_rows, width = k_ref.shape
     tables = [tables_ref[i] for i in range(3)]
+    span = out_ref.shape[2]
     groups = out_ref.shape[0] // videos
-    pairs = out_ref.shape[2] // DH
+    pairs = span // (2 * DH)
     for video in range(videos):
         for head, y in normed_heads(k_ref[video].astype(F32), gain_ref, tables):
-            start = head % pairs * DH
-            out_ref[video * groups + head // pairs, :, start : start + DH] = y
+            target, start = video * groups + head // pairs, head % pairs * 2 * DH
+            out_ref[target, :, start : start + DH] = y
+            out_ref[target, :, start + DH : start + 2 * DH] = v_ref[
+                video, :, head * DH : (head + 1) * DH
+            ]
 
 
 def softmax_parts(scores):
@@ -106,9 +110,9 @@
 
 def fresh_kernel(groups, videos, *refs):
     queries = refs[:videos]
-    key_ref, value_ref, out_ref, log_ref = refs[videos:]
+    fresh_ref, out_ref, log_ref = refs[videos:]
     me = lax.axis_index("patch")
-    own, mine = me // groups, me % groups
+    mine = me % groups
     _, tok_rows, width = out_ref.shape
     span = width // groups
     pairs = span // DH
@@ -123,13 +127,12 @@
     for t in range(groups):
         lanes = pl.ds(pl.multiple_of((mine ^ t) * span, DH), span)
         query = stacked(queries, lanes)
-        key = stacked([key_ref.at[me ^ (s * groups) ^ t] for s in range(videos)], slice(None))
-        value = stacked([value_ref.at[own ^ s] for s in range(videos)], lanes)
+        fresh = stacked([fresh_ref.at[me ^ (s * groups) ^ t] for s in range(videos)], slice(None))
         scores = jnp.concatenate(
             [
                 lax.dot_general(
                     query[:, pair * DH : (pair + 1) * DH],
-                    key[:, pair * DH : (pair + 1) * DH],
+                    fresh[:, 2 * pair * DH : (2 * pair + 1) * DH],
                     TRANSPOSED,
                     preferred_element_type=F32,
                 )
@@ -143,7 +146,7 @@
             head = t * pairs + pair
             result = inverse[here] * jnp.dot(
                 weights[here],
-                value[:, pair * DH : (pair + 1) * DH],
+                fresh[:, (2 * pair + 1) * DH : (2 * pair + 2) * DH],
                 preferred_element_type=F32,
             )
             logs = jnp.where(lane == head, log[here], logs)
@@ -232,13 +235,14 @@
         copy.wait()
 
 
-def cache_kernel(key_ref, value_ref, out_ref, sems):
+def cache_kernel(got_ref, out_ref, sems):
     copies = []
     for pair in range(out_ref.shape[0]):
-        for part, source in enumerate((key_ref.at[:, :, pl.ds(pair * DH, DH)], value_ref.at[:, pair])):
-            target = out_ref.at[pair, :, :, pl.ds(part * DH, DH)]
-            copies.append(pltpu.make_async_copy(source, target, sems.at[part, pair]))
-            copies[-1].start()
+        lanes = pl.ds(2 * pair * DH, 2 * DH)
+        copies.append(
+            pltpu.make_async_copy(got_ref.at[:, :, lanes], out_ref.at[pair], sems.at[pair])
+        )
+        copies[-1].start()
     for copy in copies:
         copy.wait()
 
@@ -272,10 +276,6 @@
     pieces = {0: stale_cache}
     bit = groups // 2
     pieces[bit] = permuted(stale_cache, bit, patches)
-    value_sent = jnp.transpose(values.reshape(videos, tok_rows, width // DH, DH), (0, 2, 1, 3))
-    value_got = lax.all_to_all(
-        value_sent.reshape(patches, pairs_here, tok_rows, DH), "patch", split_axis=0, concat_axis=0, tiled=True
-    )
     *query, tables = kernel(
         functools.partial(query_kernel, groups),
         "query",
@@ -293,15 +293,15 @@
         ],
     )(queries, q_gain.reshape(1, width), coords)
     query_got = exchange(query, groups, patches)
-    key = kernel(
+    fresh = kernel(
         key_kernel,
         "key",
         16,
-        out_shape=jax.ShapeDtypeStruct((patches, tok_rows, pairs_here * DH), BF16),
-        in_specs=[VMEM] * 3,
+        out_shape=jax.ShapeDtypeStruct((patches, tok_rows, 2 * pairs_here * DH), BF16),
+        in_specs=[VMEM] * 4,
         out_specs=VMEM,
-    )(keys, k_gain.reshape(1, width), tables)
-    key_got = lax.all_to_all(key, "patch", split_axis=0, concat_axis=0, tiled=True)
+    )(keys, values, k_gain.reshape(1, width), tables)
+    cached = lax.all_to_all(fresh, "patch", split_axis=0, concat_axis=0, tiled=True)
     pieces, query_got = lax.optimization_barrier((pieces, query_got))
     while bit > 1:
         bit //= 2
@@ -314,7 +314,7 @@
         in_specs=[VMEM] * (videos + groups),
         out_specs=[VMEM] * videos,
     )(*query_got, *[pieces[t] for t in range(groups)])
-    result, key_late = lax.optimization_barrier((result, key))
+    result, fresh_late = lax.optimization_barrier((result, fresh))
     back = exchange(result, groups, patches)
     fresh_sum, fresh_log = kernel(
         functools.partial(fresh_kernel, groups, videos),
@@ -324,9 +324,9 @@
             jax.ShapeDtypeStruct((videos, tok_rows, width), F32),
             jax.ShapeDtypeStruct((videos, tok_rows, DH), F32),
         ),
-        in_specs=[VMEM] * (videos + 2),
+        in_specs=[VMEM] * (videos + 1),
         out_specs=(VMEM, VMEM),
-    )(*query, key_late, values)
+    )(*query, fresh_late)
     attended = kernel(
         functools.partial(join_kernel, groups, videos),
         "join",
@@ -339,16 +339,16 @@
             pltpu.SemaphoreType.DMA((videos,)),
         ],
     )(*back, fresh_sum, fresh_log)
-    attended, key_got, value_got = lax.optimization_barrier((attended, key_got, value_got))
+    attended, cached = lax.optimization_barrier((attended, cached))
     next_cache = kernel(
         cache_kernel,
         "cache",
         16,
         out_shape=jax.ShapeDtypeStruct((pairs_here, patches, tok_rows, 2 * DH), BF16),
-        in_specs=[VMEM, VMEM],
+        in_specs=[VMEM],
         out_specs=HBM,
-        scratch_shapes=[pltpu.SemaphoreType.DMA((2, pairs_here))],
-    )(key_got, value_got)
+        scratch_shapes=[pltpu.SemaphoreType.DMA((pairs_here,))],
+    )(cached)
     return (attended, next_cache.reshape(stale_cache.shape))
 
 

time: 49.5 us -> 51 us (1.030)
  waiting for transfers between devices: 16.2 us -> 20.6 us
  starting transfers between devices: 21.4 us -> 17.6 us
  local copies, waits for them, and re-layouts: 0.73 us -> 1.68 us
    ppermute x9, waiting for transfers between devices: 16.2 us -> 20.6 us  [permuted(): lax.ppermute(array, 'patch', [(i, i ^ offset) for i in range(patches)])]
    all_to_all x2 -> x1, starting transfers between devices: 8.95 us -> 5.13 us  [local(): lax.all_to_all(fresh, 'patch', split_axis=0, concat_axis=0, tiled=True)]
    unnamed x16 -> x18, local copies, waits for them, and re-layouts: 0.73 us -> 1.68 us
  transfers between devices with their start and end apart: 11 -> 10, of which waited for: 4 -> 5; matrix products, arithmetic and copies ran while one was open for 0% -> 0% of each run, Pallas kernels for 18% -> 18%
where the time goes in v11:
time: 51 us; the launch traced here: 50.6 us
  waiting for transfers between devices  20.6 us (40%)
  starting transfers between devices  17.6 us (35%)
  Pallas kernels  9.97 us (20%)
  local copies, waits for them, and re-layouts  1.68 us (3%)
  between operations  0.75 us (1%)
    ppermute x9, waiting for transfers between devices, permuted(): lax.ppermute(array, 'patch', [(i, i ^ offset) for i in range(patches)])  20.6 us
    ppermute x9, starting transfers between devices, permuted(): lax.ppermute(array, 'patch', [(i, i ^ offset) for i in range(patches)])  12.4 us
    all_to_all x1, starting transfers between devices, local(): lax.all_to_all(fresh, 'patch', split_axis=0, concat_axis=0, tiled=True)  5.13 us
    pallas_call x1, Pallas kernels, local(): kernel(functools.partial(query_kernel, groups), 'query', 56, out_shape=[r...  2.87 us
    pallas_call x1, Pallas kernels, local(): kernel(functools.partial(fresh_kernel, groups, videos), 'fresh', 16, out_...  2.15 us
    unnamed x18, local copies, waits for them, and re-layouts  1.68 us
    pallas_call x1, Pallas kernels, local(): kernel(functools.partial(stale_kernel, groups, videos), 'stale', 32, out_...  1.52 us
    pallas_call x1, Pallas kernels, local(): kernel(key_kernel, 'key', 16, out_shape=jax.ShapeDtypeStruct((patches, to...  1.42 us
  transfers between devices with their start and end apart: 10, of which 5 were waited for; matrix products, arithmetic and copies ran while one was open for 0% of the time, Pallas kernels for 18%

profile of v11, /device:TPU:0, one launch (start us, length us, event | category | flops | bytes accessed | tf_op | source)
XLA Modules:
  0.0 50.6 jit_solution(3381930019360969796)
XLA Ops:
  0.6 0.0 copy-start.2
  0.6 3.0 %collective-permute-start = (bf16[8,128,256]{2,1,0:T(8,128)(2,1)}, bf16[8,128,256]{2,1,0:T(8,128)(2,1)S(1)}, u32[]{:S(2)}, u32[]{:S(2)}) collective-permute-start(bf16[8,128,256]{2,1,0:T(8,128)(2,1)} %refs_4_), channel_id=1, source_target_pairs={{0,2},{1,3},{2,0},{3,1},{4,6},{5,7},{6,4},{7,5},{8,10},{9,11},{10,... | collective-permute-start | bytes 1572872 | tf_op jit(solution)/shard_map/ppermute | solution.py:251
  3.6 0.0 copy-start.7
  3.6 2.9 %query.1 = (bf16[8,4096]{1,0:T(8,128)(2,1)}, bf16[8,4096]{1,0:T(8,128)(2,1)}, bf16[8,4096]{1,0:T(8,128)(2,1)}, bf16[8,4096]{1,0:T(8,128)(2,1)}, f32[3,8,128]{2,1,0:T(8,128)}) custom-call(bf16[4,8,4096]{2,1,0:T(8,128)(2,1)} %q_hbm.1, f32[1,4096]{1,0:T(1,128)} %bitcast.5, s32[3,8]{1,0:T(4,128)} %coords_hbm.1), custom_call_target="tpu_custom_call" | custom-call | tf_op jit(solution)/shard_map/query/pallas_call | solution.py:279
  6.5 0.0 copy-done.2
  6.5 0.0 copy-done.7
  6.5 0.0 copy-start.3
  6.6 0.9 %copy-done.3 = bf16[4,8,4096]{2,1,0:T(8,128)(2,1)S(1)} copy-done((bf16[4,8,4096]{2,1,0:T(8,128)(2,1)S(1)}, bf16[4,8,4096]{2,1,0:T(8,128)(2,1)}, u32[]{:S(2)}) %copy-start.3) | copy-done | bytes 262168
  7.5 0.0 copy-start.8
  7.5 0.7 %copy-done.8 = f32[3,8,128]{2,1,0:T(8,128)S(1)} copy-done((f32[3,8,128]{2,1,0:T(8,128)S(1)}, f32[3,8,128]{2,1,0:T(8,128)}, u32[]{:S(2)}) %copy-start.8) | copy-done | bytes 12312
  8.2 1.4 %key.1.refs_4_ = bf16[16,8,2048]{2,1,0:T(8,128)(2,1)} custom-call(bf16[4,8,4096]{2,1,0:T(8,128)(2,1)S(1)} %copy-done.2, bf16[4,8,4096]{2,1,0:T(8,128)(2,1)S(1)} %copy-done.3, f32[1,4096]{1,0:T(1,128)S(1)} %bitcast.3, f32[3,8,128]{2,1,0:T(8,128)S(1)} %copy-done.8), custom_call_target="tpu_custom_call" | custom-call | tf_op jit(solution)/shard_map/key/pallas_call | solution.py:296
  9.6 0.0 copy-start.4
  9.6 0.0 copy-start.5
  9.6 0.0 copy-start.6
  9.6 0.0 copy-start
  9.6 0.0 copy-start.1
  9.7 5.1 %all-to-all-start = ((bf16[16,8,2048]{2,1,0:T(8,128)(2,1)}), bf16[16,8,2048]{2,1,0:T(8,128)(2,1)S(1)}, u32[]{:S(2)}, u32[]{:S(2)}) async-start(bf16[16,8,2048]{2,1,0:T(8,128)(2,1)} %key.1.refs_4_), calls=%async_computation | async-start | bytes 1048576 | tf_op jit(solution)/shard_map/all_to_all | solution.py:304
  14.8 0.0 copy-done.4
  14.8 2.0 %collective-permute-start.1 = (bf16[8,4096]{1,0:T(8,128)(2,1)S(1)}, bf16[8,4096]{1,0:T(8,128)(2,1)S(1)}, u32[]{:S(2)}, u32[]{:S(2)}) collective-permute-start(bf16[8,4096]{1,0:T(8,128)(2,1)S(1)} %copy-done.4), channel_id=1, source_target_pairs={{0,4},{1,5},{2,6},{3,7},{4,0},{5,1},{6,2},{7,3},{8,12},{9,13},{10,... | collective-permute-start | bytes 196616 | tf_op jit(solution)/shard_map/ppermute | solution.py:251
  16.8 0.0 copy-done.5
  16.8 2.4 %collective-permute-start.2 = (bf16[8,4096]{1,0:T(8,128)(2,1)S(1)}, bf16[8,4096]{1,0:T(8,128)(2,1)S(1)}, u32[]{:S(2)}, u32[]{:S(2)}) collective-permute-start(bf16[8,4096]{1,0:T(8,128)(2,1)S(1)} %copy-done.5), channel_id=1, source_target_pairs={{0,8},{1,9},{2,10},{3,11},{4,12},{5,13},{6,14},{7,15},{8,0},{9,1},... | collective-permute-start | bytes 196616 | tf_op jit(solution)/shard_map/ppermute | solution.py:251
  19.2 0.0 copy-done.6
  19.2 0.1 collective-permute-start.3
  19.3 7.1 %collective-permute-done.1.refs_1_ = bf16[8,4096]{1,0:T(8,128)(2,1)S(1)} collective-permute-done((bf16[8,4096]{1,0:T(8,128)(2,1)S(1)}, bf16[8,4096]{1,0:T(8,128)(2,1)S(1)}, u32[]{:S(2)}, u32[]{:S(2)}) %collective-permute-start.1) | collective-permute-done | bytes 65568 | tf_op jit(solution)/shard_map/ppermute | solution.py:251
  26.4 8.4 %collective-permute-done.2.refs_2_ = bf16[8,4096]{1,0:T(8,128)(2,1)S(1)} collective-permute-done((bf16[8,4096]{1,0:T(8,128)(2,1)S(1)}, bf16[8,4096]{1,0:T(8,128)(2,1)S(1)}, u32[]{:S(2)}, u32[]{:S(2)}) %collective-permute-start.2) | collective-permute-done | bytes 65568 | tf_op jit(solution)/shard_map/ppermute | solution.py:251
  34.8 0.0 collective-permute-done.3.refs_3_
  34.8 0.0 collective-permute-done.refs_6_
  34.8 0.0 copy-done
  34.8 0.1 collective-permute-start.4
  34.8 0.5 collective-permute-start.5
  35.3 1.4 %collective-permute-done.4.refs_5_ = bf16[8,128,256]{2,1,0:T(8,128)(2,1)S(1)} collective-permute-done((bf16[8,128,256]{2,1,0:T(8,128)(2,1)S(1)}, bf16[8,128,256]{2,1,0:T(8,128)(2,1)S(1)}, u32[]{:S(2)}, u32[]{:S(2)}) %collective-permute-start.4) | collective-permute-done | bytes 524320 | tf_op jit(solution)/shard_map/ppermute | solution.py:251
  36.7 0.7 %collective-permute-done.5.refs_7_ = bf16[8,128,256]{2,1,0:T(8,128)(2,1)S(1)} collective-permute-done((bf16[8,128,256]{2,1,0:T(8,128)(2,1)S(1)}, bf16[8,128,256]{2,1,0:T(8,128)(2,1)S(1)}, u32[]{:S(2)}, u32[]{:S(2)}) %collective-permute-start.5) | collective-permute-done | bytes 524320 | tf_op jit(solution)/shard_map/ppermute | solution.py:251
  37.5 0.0 copy-done.1
  37.5 1.5 %stale.1 = (bf16[8,4224]{1,0:T(8,128)(2,1)S(1)}, bf16[8,4224]{1,0:T(8,128)(2,1)S(1)}, bf16[8,4224]{1,0:T(8,128)(2,1)S(1)}, bf16[8,4224]{1,0:T(8,128)(2,1)S(1)}) custom-call(bf16[8,4096]{1,0:T(8,128)(2,1)S(1)} %copy-done.1, bf16[8,4096]{1,0:T(8,128)(2,1)S(1)} %collective-permute-done.1.refs_1_, bf16[8,4096]{1,0:T(8,128)(2,1)S(1)} %collective-permute-done.2.refs_2_, ...), custom_call_target="tpu_custom_call" | custom-call | tf_op jit(solution)/shard_map/stale/pallas_call | solution.py:309
  39.0 1.5 %collective-permute-start.6 = (bf16[8,4224]{1,0:T(8,128)(2,1)S(1)}, bf16[8,4224]{1,0:T(8,128)(2,1)S(1)}, u32[]{:S(2)}, u32[]{:S(2)}) collective-permute-start(bf16[8,4224]{1,0:T(8,128)(2,1)S(1)} %get-tuple-element.42), channel_id=1, source_target_pairs={{0,4},{1,5},{2,6},{3,7},{4,0},{5,1},{6,2},{7,3},{8,12},{9,13},{10,... | collective-permute-start | bytes 202760 | tf_op jit(solution)/shard_map/ppermute | solution.py:251
  40.5 0.6 %collective-permute-start.7 = (bf16[8,4224]{1,0:T(8,128)(2,1)S(1)}, bf16[8,4224]{1,0:T(8,128)(2,1)S(1)}, u32[]{:S(2)}, u32[]{:S(2)}) collective-permute-start(bf16[8,4224]{1,0:T(8,128)(2,1)S(1)} %get-tuple-element.43), channel_id=1, source_target_pairs={{0,8},{1,9},{2,10},{3,11},{4,12},{5,13},{6,14},{7,15},{8,0},{9,1},... | collective-permute-start | bytes 202760 | tf_op jit(solution)/shard_map/ppermute | solution.py:251
  41.1 2.3 %collective-permute-start.8 = (bf16[8,4224]{1,0:T(8,128)(2,1)S(1)}, bf16[8,4224]{1,0:T(8,128)(2,1)S(1)}, u32[]{:S(2)}, u32[]{:S(2)}) collective-permute-start(bf16[8,4224]{1,0:T(8,128)(2,1)S(1)} %get-tuple-element.44), channel_id=1, source_target_pairs={{0,12},{1,13},{2,14},{3,15},{4,8},{5,9},{6,10},{7,11},{8,4},{9,5},... | collective-permute-start | bytes 202760 | tf_op jit(solution)/shard_map/ppermute | solution.py:251
  43.4 2.1 %fresh.1 = (f32[4,8,4096]{2,1,0:T(8,128)S(1)}, f32[4,8,128]{2,1,0:T(8,128)S(1)}) custom-call(bf16[8,4096]{1,0:T(8,128)(2,1)S(1)} %copy-done.1, bf16[8,4096]{1,0:T(8,128)(2,1)S(1)} %copy-done.4, bf16[8,4096]{1,0:T(8,128)(2,1)S(1)} %copy-done.5, bf16[8,4096]{1,0:T(8,128)(2,1)S(1)} %copy-done.6, bf16[16,8,2048]{2,1,0:T(8,128)(2,1)} %key.1.refs_4_), custom_call_target="tpu_custom_call" | custom-call | tf_op jit(solution)/shard_map/fresh/pallas_call | solution.py:319
  45.6 0.0 collective-permute-done.6.refs_1_
  45.6 3.0 %collective-permute-done.7.refs_2_ = bf16[8,4224]{1,0:T(8,128)(2,1)S(1)} collective-permute-done((bf16[8,4224]{1,0:T(8,128)(2,1)S(1)}, bf16[8,4224]{1,0:T(8,128)(2,1)S(1)}, u32[]{:S(2)}, u32[]{:S(2)}) %collective-permute-start.7) | collective-permute-done | bytes 67616 | tf_op jit(solution)/shard_map/ppermute | solution.py:251
  48.6 0.0 collective-permute-done.8.refs_3_
  48.6 1.2 %join.1 = bf16[4,8,4096]{2,1,0:T(8,128)(2,1)} custom-call(bf16[8,4224]{1,0:T(8,128)(2,1)S(1)} %get-tuple-element.41.refs_0_, bf16[8,4224]{1,0:T(8,128)(2,1)S(1)} %collective-permute-done.6.refs_1_, bf16[8,4224]{1,0:T(8,128)(2,1)S(1)} %collective-permute-done.7.refs_2_, bf16[8,4224]{1,0:T(8,128)(2,1)S(1)} %collective-permute-done.8.refs_3_, ...), custom_call_target="tpu_custom_call" | custom-call | tf_op jit(solution)/shard_map/join/pallas_call | solution.py:330
  49.7 0.0 all-to-all-done.got_ref
  49.8 0.9 %cache.1 = bf16[8,16,8,256]{3,2,1,0:T(8,128)(2,1)} custom-call(bf16[16,8,2048]{2,1,0:T(8,128)(2,1)S(1)} %all-to-all-done.got_ref), custom_call_target="tpu_custom_call" | custom-call | tf_op jit(solution)/shard_map/cache/pallas_call | solution.py:343
Async XLA Ops:
  0.6 5.9 %copy-start.2 = (bf16[4,8,4096]{2,1,0:T(8,128)(2,1)S(1)}, bf16[4,8,4096]{2,1,0:T(8,128)(2,1)}, u32[]{:S(2)}) copy-start(bf16[4,8,4096]{2,1,0:T(8,128)(2,1)} %k_ref.1) | copy-start | bytes 786436
  0.6 34.1 %collective-permute-start = (bf16[8,128,256]{2,1,0:T(8,128)(2,1)}, bf16[8,128,256]{2,1,0:T(8,128)(2,1)S(1)}, u32[]{:S(2)}, u32[]{:S(2)}) collective-permute-start(bf16[8,128,256]{2,1,0:T(8,128)(2,1)} %refs_4_), channel_id=1, source_target_pairs={{0,2},{1,3},{2,0},{3,1},{4,6},{5,7},{6,4},{7,5},{8,10},{9,11},{10,... | collective-permute-start | bytes 1572872 | tf_op jit(solution)/shard_map/ppermute | solution.py:251
  3.6 2.9 %copy-start.7 = (f32[4096]{0:T(1024)S(1)}, f32[4096]{0:T(1024)}, u32[]{:S(2)}) copy-start(f32[4096]{0:T(1024)} %param.11) | copy-start | bytes 49156
  6.5 1.0 %copy-start.3 = (bf16[4,8,4096]{2,1,0:T(8,128)(2,1)S(1)}, bf16[4,8,4096]{2,1,0:T(8,128)(2,1)}, u32[]{:S(2)}) copy-start(bf16[4,8,4096]{2,1,0:T(8,128)(2,1)} %v_ref.1) | copy-start | bytes 786436
  7.5 0.7 %copy-start.8 = (f32[3,8,128]{2,1,0:T(8,128)S(1)}, f32[3,8,128]{2,1,0:T(8,128)}, u32[]{:S(2)}) copy-start(f32[3,8,128]{2,1,0:T(8,128)} %get-tuple-element.40.tables_ref) | copy-start | bytes 36868
  9.6 5.2 %copy-start.4 = (bf16[8,4096]{1,0:T(8,128)(2,1)S(1)}, bf16[8,4096]{1,0:T(8,128)(2,1)}, u32[]{:S(2)}) copy-start(bf16[8,4096]{1,0:T(8,128)(2,1)} %get-tuple-element.27.refs_1_) | copy-start | bytes 196612
  9.6 7.2 %copy-start.5 = (bf16[8,4096]{1,0:T(8,128)(2,1)S(1)}, bf16[8,4096]{1,0:T(8,128)(2,1)}, u32[]{:S(2)}) copy-start(bf16[8,4096]{1,0:T(8,128)(2,1)} %get-tuple-element.28.refs_2_) | copy-start | bytes 196612
  9.6 9.5 %copy-start.6 = (bf16[8,4096]{1,0:T(8,128)(2,1)S(1)}, bf16[8,4096]{1,0:T(8,128)(2,1)}, u32[]{:S(2)}) copy-start(bf16[8,4096]{1,0:T(8,128)(2,1)} %get-tuple-element.29.refs_3_) | copy-start | bytes 196612
  9.6 25.1 %copy-start = (bf16[8,128,256]{2,1,0:T(8,128)(2,1)S(1)}, bf16[8,128,256]{2,1,0:T(8,128)(2,1)}, u32[]{:S(2)}) copy-start(bf16[8,128,256]{2,1,0:T(8,128)(2,1)} %refs_4_) | copy-start | bytes 1572868
  9.6 27.9 %copy-start.1 = (bf16[8,4096]{1,0:T(8,128)(2,1)S(1)}, bf16[8,4096]{1,0:T(8,128)(2,1)}, u32[]{:S(2)}) copy-start(bf16[8,4096]{1,0:T(8,128)(2,1)} %get-tuple-element.30.refs_0_) | copy-start | bytes 196612
  9.7 40.1 %all-to-all-start = ((bf16[16,8,2048]{2,1,0:T(8,128)(2,1)}), bf16[16,8,2048]{2,1,0:T(8,128)(2,1)S(1)}, u32[]{:S(2)}, u32[]{:S(2)}) async-start(bf16[16,8,2048]{2,1,0:T(8,128)(2,1)} %key.1.refs_4_), calls=%async_computation | async-start | bytes 1048576 | tf_op jit(solution)/shard_map/all_to_all | solution.py:304
  14.8 11.6 %collective-permute-start.1 = (bf16[8,4096]{1,0:T(8,128)(2,1)S(1)}, bf16[8,4096]{1,0:T(8,128)(2,1)S(1)}, u32[]{:S(2)}, u32[]{:S(2)}) collective-permute-start(bf16[8,4096]{1,0:T(8,128)(2,1)S(1)} %copy-done.4), channel_id=1, source_target_pairs={{0,4},{1,5},{2,6},{3,7},{4,0},{5,1},{6,2},{7,3},{8,12},{9,13},{10,... | collective-permute-start | bytes 196616 | tf_op jit(solution)/shard_map/ppermute | solution.py:251
  16.8 18.0 %collective-permute-start.2 = (bf16[8,4096]{1,0:T(8,128)(2,1)S(1)}, bf16[8,4096]{1,0:T(8,128)(2,1)S(1)}, u32[]{:S(2)}, u32[]{:S(2)}) collective-permute-start(bf16[8,4096]{1,0:T(8,128)(2,1)S(1)} %copy-done.5), channel_id=1, source_target_pairs={{0,8},{1,9},{2,10},{3,11},{4,12},{5,13},{6,14},{7,15},{8,0},{9,1},... | collective-permute-start | bytes 196616 | tf_op jit(solution)/shard_map/ppermute | solution.py:251
  19.2 15.6 %collective-permute-start.3 = (bf16[8,4096]{1,0:T(8,128)(2,1)S(1)}, bf16[8,4096]{1,0:T(8,128)(2,1)S(1)}, u32[]{:S(2)}, u32[]{:S(2)}) collective-permute-start(bf16[8,4096]{1,0:T(8,128)(2,1)S(1)} %copy-done.6), channel_id=1, source_target_pairs={{0,12},{1,13},{2,14},{3,15},{4,8},{5,9},{6,10},{7,11},{8,4},{9,5},... | collective-permute-start | bytes 196616 | tf_op jit(solution)/shard_map/ppermute | solution.py:251
  34.8 2.0 %collective-permute-start.4 = (bf16[8,128,256]{2,1,0:T(8,128)(2,1)S(1)}, bf16[8,128,256]{2,1,0:T(8,128)(2,1)S(1)}, u32[]{:S(2)}, u32[]{:S(2)}) collective-permute-start(bf16[8,128,256]{2,1,0:T(8,128)(2,1)S(1)} %copy-done), channel_id=1, source_target_pairs={{0,1},{1,0},{2,3},{3,2},{4,5},{5,4},{6,7},{7,6},{8,9},{9,8},{10,11... | collective-permute-start | bytes 1572872 | tf_op jit(solution)/shard_map/ppermute | solution.py:251
  34.8 2.6 %collective-permute-start.5 = (bf16[8,128,256]{2,1,0:T(8,128)(2,1)S(1)}, bf16[8,128,256]{2,1,0:T(8,128)(2,1)S(1)}, u32[]{:S(2)}, u32[]{:S(2)}) collective-permute-start(bf16[8,128,256]{2,1,0:T(8,128)(2,1)S(1)} %collective-permute-done.refs_6_), channel_id=1, source_target_pairs={{0,1},{1,0},{2,3},{3,2},{4,5},{5,4},{6,7},{7,6},{8,9},{9,8},{10,11... | collective-permute-start | bytes 1572872 | tf_op jit(solution)/shard_map/ppermute | solution.py:251
  39.0 6.6 %collective-permute-start.6 = (bf16[8,4224]{1,0:T(8,128)(2,1)S(1)}, bf16[8,4224]{1,0:T(8,128)(2,1)S(1)}, u32[]{:S(2)}, u32[]{:S(2)}) collective-permute-start(bf16[8,4224]{1,0:T(8,128)(2,1)S(1)} %get-tuple-element.42), channel_id=1, source_target_pairs={{0,4},{1,5},{2,6},{3,7},{4,0},{5,1},{6,2},{7,3},{8,12},{9,13},{10,... | collective-permute-start | bytes 202760 | tf_op jit(solution)/shard_map/ppermute | solution.py:251
  40.5 8.1 %collective-permute-start.7 = (bf16[8,4224]{1,0:T(8,128)(2,1)S(1)}, bf16[8,4224]{1,0:T(8,128)(2,1)S(1)}, u32[]{:S(2)}, u32[]{:S(2)}) collective-permute-start(bf16[8,4224]{1,0:T(8,128)(2,1)S(1)} %get-tuple-element.43), channel_id=1, source_target_pairs={{0,8},{1,9},{2,10},{3,11},{4,12},{5,13},{6,14},{7,15},{8,0},{9,1},... | collective-permute-start | bytes 202760 | tf_op jit(solution)/shard_map/ppermute | solution.py:251
  41.1 7.5 %collective-permute-start.8 = (bf16[8,4224]{1,0:T(8,128)(2,1)S(1)}, bf16[8,4224]{1,0:T(8,128)(2,1)S(1)}, u32[]{:S(2)}, u32[]{:S(2)}) collective-permute-start(bf16[8,4224]{1,0:T(8,128)(2,1)S(1)} %get-tuple-element.44), channel_id=1, source_target_pairs={{0,12},{1,13},{2,14},{3,15},{4,8},{5,9},{6,10},{7,11},{8,4},{9,5},... | collective-permute-start | bytes 202760 | tf_op jit(solution)/shard_map/ppermute | solution.py:251

commit v12 on v11

--- a/solution.py
+++ b/solution.py
@@ -273,9 +273,6 @@
             **kwargs,
         )
 
-    pieces = {0: stale_cache}
-    bit = groups // 2
-    pieces[bit] = permuted(stale_cache, bit, patches)
     *query, tables = kernel(
         functools.partial(query_kernel, groups),
         "query",
@@ -293,6 +290,10 @@
         ],
     )(queries, q_gain.reshape(1, width), coords)
     query_got = exchange(query, groups, patches)
+    stale_sent, tables = lax.optimization_barrier((stale_cache, tables))
+    pieces = {0: stale_cache}
+    bit = groups // 2
+    pieces[bit] = permuted(stale_sent, bit, patches)
     fresh = kernel(
         key_kernel,
         "key",
@@ -301,7 +302,8 @@
         in_specs=[VMEM] * 4,
         out_specs=VMEM,
     )(keys, values, k_gain.reshape(1, width), tables)
-    cached = lax.all_to_all(fresh, "patch", split_axis=0, concat_axis=0, tiled=True)
+    fresh_sent, query_got = lax.optimization_barrier((fresh, query_got))
+    cached = lax.all_to_all(fresh_sent, "patch", split_axis=0, concat_axis=0, tiled=True)
     pieces, query_got = lax.optimization_barrier((pieces, query_got))
     while bit > 1:
         bit //= 2
@@ -327,6 +329,15 @@
         in_specs=[VMEM] * (videos + 1),
         out_specs=(VMEM, VMEM),
     )(*query, fresh_late)
+    next_cache = kernel(
+        cache_kernel,
+        "cache",
+        16,
+        out_shape=jax.ShapeDtypeStruct((pairs_here, patches, tok_rows, 2 * DH), BF16),
+        in_specs=[VMEM],
+        out_specs=HBM,
+        scratch_shapes=[pltpu.SemaphoreType.DMA((pairs_here,))],
+    )(cached)
     attended = kernel(
         functools.partial(join_kernel, groups, videos),
         "join",
@@ -339,16 +350,6 @@
             pltpu.SemaphoreType.DMA((videos,)),
         ],
     )(*back, fresh_sum, fresh_log)
-    attended, cached = lax.optimization_barrier((attended, cached))
-    next_cache = kernel(
-        cache_kernel,
-        "cache",
-        16,
-        out_shape=jax.ShapeDtypeStruct((pairs_here, patches, tok_rows, 2 * DH), BF16),
-        in_specs=[VMEM],
-        out_specs=HBM,
-        scratch_shapes=[pltpu.SemaphoreType.DMA((pairs_here,))],
-    )(cached)
     return (attended, next_cache.reshape(stale_cache.shape))
 
 

time: 51 us -> 42.3 us (0.83)
  waiting for transfers between devices: 20.6 us -> 13.4 us
  starting transfers between devices: 17.6 us -> 16.1 us
    ppermute x9, waiting for transfers between devices: 20.6 us -> 9.48 us  [permuted(): lax.ppermute(array, 'patch', [(i, i ^ offset) for i in range(patches)])]
    all_to_all x1, waiting for transfers between devices: 0.01 us -> 3.91 us  [local(): lax.all_to_all(fresh_sent, 'patch', split_axis=0, concat_axis=0, tiled=True)]
    all_to_all x1, starting transfers between devices: 5.13 us -> 3.71 us  [local(): lax.all_to_all(fresh_sent, 'patch', split_axis=0, concat_axis=0, tiled=True)]
  transfers between devices with their start and end apart: 10 -> 10, of which waited for: 5 -> 6; matrix products, arithmetic and copies ran while one was open for 0% -> 0% of each run, Pallas kernels for 18% -> 14%
where the time goes in v12:
time: 42.3 us; the launch traced here: 41.9 us
  starting transfers between devices  16.1 us (38%)
  waiting for transfers between devices  13.4 us (32%)
  Pallas kernels  10 us (24%)
  local copies, waits for them, and re-layouts  1.69 us (4%)
  between operations  0.74 us (2%)
    ppermute x9, starting transfers between devices, permuted(): lax.ppermute(array, 'patch', [(i, i ^ offset) for i in range(patches)])  12.4 us
    ppermute x9, waiting for transfers between devices, permuted(): lax.ppermute(array, 'patch', [(i, i ^ offset) for i in range(patches)])  9.48 us
    all_to_all x1, waiting for transfers between devices, local(): lax.all_to_all(fresh_sent, 'patch', split_axis=0, concat_axis=0, tiled=True)  3.91 us
    all_to_all x1, starting transfers between devices, local(): lax.all_to_all(fresh_sent, 'patch', split_axis=0, concat_axis=0, tiled=True)  3.71 us
    pallas_call x1, Pallas kernels, local(): kernel(functools.partial(query_kernel, groups), 'query', 56, out_shape=[r...  2.9 us
    pallas_call x1, Pallas kernels, local(): kernel(functools.partial(fresh_kernel, groups, videos), 'fresh', 16, out_...  2.15 us
    unnamed x18, local copies, waits for them, and re-layouts  1.69 us
    pallas_call x1, Pallas kernels, local(): kernel(functools.partial(stale_kernel, groups, videos), 'stale', 32, out_...  1.52 us
  transfers between devices with their start and end apart: 10, of which 6 were waited for; matrix products, arithmetic and copies ran while one was open for 0% of the time, Pallas kernels for 14%

profile of v12, /device:TPU:0, one launch (start us, length us, event | category | flops | bytes accessed | tf_op | source)
XLA Modules:
  0.0 41.9 jit_solution(5462164096572276163)
XLA Ops:
  0.6 0.0 copy-start.2
  0.6 0.0 copy-start.7
  0.7 2.9 %query.1 = (bf16[8,4096]{1,0:T(8,128)(2,1)}, bf16[8,4096]{1,0:T(8,128)(2,1)}, bf16[8,4096]{1,0:T(8,128)(2,1)}, bf16[8,4096]{1,0:T(8,128)(2,1)}, f32[3,8,128]{2,1,0:T(8,128)}) custom-call(bf16[4,8,4096]{2,1,0:T(8,128)(2,1)} %q_hbm.1, f32[1,4096]{1,0:T(1,128)} %bitcast.5, s32[3,8]{1,0:T(4,128)} %coords_hbm.1), custom_call_target="tpu_custom_call" | custom-call | tf_op jit(solution)/shard_map/query/pallas_call | solution.py:276
  3.6 3.0 %collective-permute-start = (bf16[8,128,256]{2,1,0:T(8,128)(2,1)}, bf16[8,128,256]{2,1,0:T(8,128)(2,1)S(1)}, u32[]{:S(2)}, u32[]{:S(2)}) collective-permute-start(bf16[8,128,256]{2,1,0:T(8,128)(2,1)} %refs_4_), channel_id=1, source_target_pairs={{0,2},{1,3},{2,0},{3,1},{4,6},{5,7},{6,4},{7,5},{8,10},{9,11},{10,... | collective-permute-start | bytes 1572872 | tf_op jit(solution)/shard_map/ppermute | solution.py:251
  6.6 1.6 %collective-permute-start.1 = (bf16[8,4096]{1,0:T(8,128)(2,1)}, bf16[8,4096]{1,0:T(8,128)(2,1)S(1)}, u32[]{:S(2)}, u32[]{:S(2)}) collective-permute-start(bf16[8,4096]{1,0:T(8,128)(2,1)} %get-tuple-element.35.refs_1_), channel_id=1, source_target_pairs={{0,4},{1,5},{2,6},{3,7},{4,0},{5,1},{6,2},{7,3},{8,12},{9,13},{10,... | collective-permute-start | bytes 196616 | tf_op jit(solution)/shard_map/ppermute | solution.py:251
  8.1 2.6 %collective-permute-start.2 = (bf16[8,4096]{1,0:T(8,128)(2,1)}, bf16[8,4096]{1,0:T(8,128)(2,1)S(1)}, u32[]{:S(2)}, u32[]{:S(2)}) collective-permute-start(bf16[8,4096]{1,0:T(8,128)(2,1)} %get-tuple-element.36.refs_2_), channel_id=1, source_target_pairs={{0,8},{1,9},{2,10},{3,11},{4,12},{5,13},{6,14},{7,15},{8,0},{9,1},... | collective-permute-start | bytes 196616 | tf_op jit(solution)/shard_map/ppermute | solution.py:251
  10.7 0.2 collective-permute-start.3
  11.0 0.0 copy-done.2
  11.0 0.0 copy-done.7
  11.0 0.0 copy-start.3
  11.0 0.9 %copy-done.3 = bf16[4,8,4096]{2,1,0:T(8,128)(2,1)S(1)} copy-done((bf16[4,8,4096]{2,1,0:T(8,128)(2,1)S(1)}, bf16[4,8,4096]{2,1,0:T(8,128)(2,1)}, u32[]{:S(2)}) %copy-start.3) | copy-done | bytes 262168
  11.9 0.0 copy-start.8
  11.9 0.7 %copy-done.8 = f32[3,8,128]{2,1,0:T(8,128)S(1)} copy-done((f32[3,8,128]{2,1,0:T(8,128)S(1)}, f32[3,8,128]{2,1,0:T(8,128)}, u32[]{:S(2)}) %copy-start.8) | copy-done | bytes 12312
  12.6 1.4 %key.1.refs_4_ = bf16[16,8,2048]{2,1,0:T(8,128)(2,1)} custom-call(bf16[4,8,4096]{2,1,0:T(8,128)(2,1)S(1)} %copy-done.2, bf16[4,8,4096]{2,1,0:T(8,128)(2,1)S(1)} %copy-done.3, f32[1,4096]{1,0:T(1,128)S(1)} %bitcast.3, f32[3,8,128]{2,1,0:T(8,128)S(1)} %copy-done.8), custom_call_target="tpu_custom_call" | custom-call | tf_op jit(solution)/shard_map/key/pallas_call | solution.py:297
  14.0 0.0 collective-permute-done.1.refs_1_
  14.0 1.3 %collective-permute-done.2.refs_2_ = bf16[8,4096]{1,0:T(8,128)(2,1)S(1)} collective-permute-done((bf16[8,4096]{1,0:T(8,128)(2,1)}, bf16[8,4096]{1,0:T(8,128)(2,1)S(1)}, u32[]{:S(2)}, u32[]{:S(2)}) %collective-permute-start.2) | collective-permute-done | bytes 65568 | tf_op jit(solution)/shard_map/ppermute | solution.py:251
  15.3 1.7 %collective-permute-done.3.refs_3_ = bf16[8,4096]{1,0:T(8,128)(2,1)S(1)} collective-permute-done((bf16[8,4096]{1,0:T(8,128)(2,1)}, bf16[8,4096]{1,0:T(8,128)(2,1)S(1)}, u32[]{:S(2)}, u32[]{:S(2)}) %collective-permute-start.3) | collective-permute-done | bytes 65568 | tf_op jit(solution)/shard_map/ppermute | solution.py:251
  17.0 0.0 copy-start
  17.0 0.0 copy-start.1
  17.0 3.7 %all-to-all-start = ((bf16[16,8,2048]{2,1,0:T(8,128)(2,1)}), bf16[16,8,2048]{2,1,0:T(8,128)(2,1)S(1)}, u32[]{:S(2)}, u32[]{:S(2)}) async-start(bf16[16,8,2048]{2,1,0:T(8,128)(2,1)} %key.1.refs_4_), calls=%async_computation | async-start | bytes 1048576 | tf_op jit(solution)/shard_map/all_to_all | solution.py:306
  20.7 0.0 copy-start.4
  20.7 0.0 copy-start.5
  20.7 0.0 copy-start.6
  20.8 0.0 collective-permute-done.refs_6_
  20.8 0.0 copy-done
  20.8 0.4 collective-permute-start.4
  21.1 0.2 collective-permute-start.5
  21.3 1.4 %collective-permute-done.4.refs_5_ = bf16[8,128,256]{2,1,0:T(8,128)(2,1)S(1)} collective-permute-done((bf16[8,128,256]{2,1,0:T(8,128)(2,1)S(1)}, bf16[8,128,256]{2,1,0:T(8,128)(2,1)S(1)}, u32[]{:S(2)}, u32[]{:S(2)}) %collective-permute-start.4) | collective-permute-done | bytes 524320 | tf_op jit(solution)/shard_map/ppermute | solution.py:251
  22.7 0.7 %collective-permute-done.5.refs_7_ = bf16[8,128,256]{2,1,0:T(8,128)(2,1)S(1)} collective-permute-done((bf16[8,128,256]{2,1,0:T(8,128)(2,1)S(1)}, bf16[8,128,256]{2,1,0:T(8,128)(2,1)S(1)}, u32[]{:S(2)}, u32[]{:S(2)}) %collective-permute-start.5) | collective-permute-done | bytes 524320 | tf_op jit(solution)/shard_map/ppermute | solution.py:251
  23.5 0.0 copy-done.1
  23.5 1.5 %stale.1 = (bf16[8,4224]{1,0:T(8,128)(2,1)S(1)}, bf16[8,4224]{1,0:T(8,128)(2,1)S(1)}, bf16[8,4224]{1,0:T(8,128)(2,1)S(1)}, bf16[8,4224]{1,0:T(8,128)(2,1)S(1)}) custom-call(bf16[8,4096]{1,0:T(8,128)(2,1)S(1)} %copy-done.1, bf16[8,4096]{1,0:T(8,128)(2,1)S(1)} %collective-permute-done.1.refs_1_, bf16[8,4096]{1,0:T(8,128)(2,1)S(1)} %collective-permute-done.2.refs_2_, ...), custom_call_target="tpu_custom_call" | custom-call | tf_op jit(solution)/shard_map/stale/pallas_call | solution.py:311
  25.0 1.9 %collective-permute-start.6 = (bf16[8,4224]{1,0:T(8,128)(2,1)S(1)}, bf16[8,4224]{1,0:T(8,128)(2,1)S(1)}, u32[]{:S(2)}, u32[]{:S(2)}) collective-permute-start(bf16[8,4224]{1,0:T(8,128)(2,1)S(1)} %get-tuple-element.53), channel_id=1, source_target_pairs={{0,4},{1,5},{2,6},{3,7},{4,0},{5,1},{6,2},{7,3},{8,12},{9,13},{10,... | collective-permute-start | bytes 202760 | tf_op jit(solution)/shard_map/ppermute | solution.py:251
  26.9 2.4 %collective-permute-start.7 = (bf16[8,4224]{1,0:T(8,128)(2,1)S(1)}, bf16[8,4224]{1,0:T(8,128)(2,1)S(1)}, u32[]{:S(2)}, u32[]{:S(2)}) collective-permute-start(bf16[8,4224]{1,0:T(8,128)(2,1)S(1)} %get-tuple-element.54), channel_id=1, source_target_pairs={{0,8},{1,9},{2,10},{3,11},{4,12},{5,13},{6,14},{7,15},{8,0},{9,1},... | collective-permute-start | bytes 202760 | tf_op jit(solution)/shard_map/ppermute | solution.py:251
  29.3 0.1 collective-permute-start.8
  29.4 0.0 copy-done.4
  29.4 0.0 copy-done.5
  29.4 0.0 copy-done.6
  29.5 2.1 %fresh.1 = (f32[4,8,4096]{2,1,0:T(8,128)S(1)}, f32[4,8,128]{2,1,0:T(8,128)S(1)}) custom-call(bf16[8,4096]{1,0:T(8,128)(2,1)S(1)} %copy-done.1, bf16[8,4096]{1,0:T(8,128)(2,1)S(1)} %copy-done.4, bf16[8,4096]{1,0:T(8,128)(2,1)S(1)} %copy-done.5, bf16[8,4096]{1,0:T(8,128)(2,1)S(1)} %copy-done.6, bf16[16,8,2048]{2,1,0:T(8,128)(2,1)} %key.1.refs_4_), custom_call_target="tpu_custom_call" | custom-call | tf_op jit(solution)/shard_map/fresh/pallas_call | solution.py:321
  31.6 3.9 %all-to-all-done.got_ref = bf16[16,8,2048]{2,1,0:T(8,128)(2,1)S(1)} async-done(((bf16[16,8,2048]{2,1,0:T(8,128)(2,1)}), bf16[16,8,2048]{2,1,0:T(8,128)(2,1)S(1)}, u32[]{:S(2)}, u32[]{:S(2)}) %all-to-all-start) | async-done | bytes 524320 | tf_op jit(solution)/shard_map/all_to_all | solution.py:306
  35.5 0.8 %cache.1 = bf16[8,16,8,256]{3,2,1,0:T(8,128)(2,1)} custom-call(bf16[16,8,2048]{2,1,0:T(8,128)(2,1)S(1)} %all-to-all-done.got_ref), custom_call_target="tpu_custom_call" | custom-call | tf_op jit(solution)/shard_map/cache/pallas_call | solution.py:332
  36.4 0.0 collective-permute-done.6.refs_1_
  36.4 4.4 %collective-permute-done.7.refs_2_ = bf16[8,4224]{1,0:T(8,128)(2,1)S(1)} collective-permute-done((bf16[8,4224]{1,0:T(8,128)(2,1)S(1)}, bf16[8,4224]{1,0:T(8,128)(2,1)S(1)}, u32[]{:S(2)}, u32[]{:S(2)}) %collective-permute-start.7) | collective-permute-done | bytes 67616 | tf_op jit(solution)/shard_map/ppermute | solution.py:251
  40.7 0.0 collective-permute-done.8.refs_3_
  40.7 1.2 %join.1 = bf16[4,8,4096]{2,1,0:T(8,128)(2,1)} custom-call(bf16[8,4224]{1,0:T(8,128)(2,1)S(1)} %get-tuple-element.52.refs_0_, bf16[8,4224]{1,0:T(8,128)(2,1)S(1)} %collective-permute-done.6.refs_1_, bf16[8,4224]{1,0:T(8,128)(2,1)S(1)} %collective-permute-done.7.refs_2_, bf16[8,4224]{1,0:T(8,128)(2,1)S(1)} %collective-permute-done.8.refs_3_, ...), custom_call_target="tpu_custom_call" | custom-call | tf_op jit(solution)/shard_map/join/pallas_call | solution.py:341
Async XLA Ops:
  0.6 10.3 %copy-start.2 = (bf16[4,8,4096]{2,1,0:T(8,128)(2,1)S(1)}, bf16[4,8,4096]{2,1,0:T(8,128)(2,1)}, u32[]{:S(2)}) copy-start(bf16[4,8,4096]{2,1,0:T(8,128)(2,1)} %k_ref.1) | copy-start | bytes 786436
  0.6 10.3 %copy-start.7 = (f32[4096]{0:T(1024)S(1)}, f32[4096]{0:T(1024)}, u32[]{:S(2)}) copy-start(f32[4096]{0:T(1024)} %param.11) | copy-start | bytes 49156
  3.6 17.2 %collective-permute-start = (bf16[8,128,256]{2,1,0:T(8,128)(2,1)}, bf16[8,128,256]{2,1,0:T(8,128)(2,1)S(1)}, u32[]{:S(2)}, u32[]{:S(2)}) collective-permute-start(bf16[8,128,256]{2,1,0:T(8,128)(2,1)} %refs_4_), channel_id=1, source_target_pairs={{0,2},{1,3},{2,0},{3,1},{4,6},{5,7},{6,4},{7,5},{8,10},{9,11},{10,... | collective-permute-start | bytes 1572872 | tf_op jit(solution)/shard_map/ppermute | solution.py:251
  6.6 7.5 %collective-permute-start.1 = (bf16[8,4096]{1,0:T(8,128)(2,1)}, bf16[8,4096]{1,0:T(8,128)(2,1)S(1)}, u32[]{:S(2)}, u32[]{:S(2)}) collective-permute-start(bf16[8,4096]{1,0:T(8,128)(2,1)} %get-tuple-element.35.refs_1_), channel_id=1, source_target_pairs={{0,4},{1,5},{2,6},{3,7},{4,0},{5,1},{6,2},{7,3},{8,12},{9,13},{10,... | collective-permute-start | bytes 196616 | tf_op jit(solution)/shard_map/ppermute | solution.py:251
  8.1 7.2 %collective-permute-start.2 = (bf16[8,4096]{1,0:T(8,128)(2,1)}, bf16[8,4096]{1,0:T(8,128)(2,1)S(1)}, u32[]{:S(2)}, u32[]{:S(2)}) collective-permute-start(bf16[8,4096]{1,0:T(8,128)(2,1)} %get-tuple-element.36.refs_2_), channel_id=1, source_target_pairs={{0,8},{1,9},{2,10},{3,11},{4,12},{5,13},{6,14},{7,15},{8,0},{9,1},... | collective-permute-start | bytes 196616 | tf_op jit(solution)/shard_map/ppermute | solution.py:251
  10.7 6.3 %collective-permute-start.3 = (bf16[8,4096]{1,0:T(8,128)(2,1)}, bf16[8,4096]{1,0:T(8,128)(2,1)S(1)}, u32[]{:S(2)}, u32[]{:S(2)}) collective-permute-start(bf16[8,4096]{1,0:T(8,128)(2,1)} %get-tuple-element.37.refs_3_), channel_id=1, source_target_pairs={{0,12},{1,13},{2,14},{3,15},{4,8},{5,9},{6,10},{7,11},{8,4},{9,5},... | collective-permute-start | bytes 196616 | tf_op jit(solution)/shard_map/ppermute | solution.py:251
  11.0 1.0 %copy-start.3 = (bf16[4,8,4096]{2,1,0:T(8,128)(2,1)S(1)}, bf16[4,8,4096]{2,1,0:T(8,128)(2,1)}, u32[]{:S(2)}) copy-start(bf16[4,8,4096]{2,1,0:T(8,128)(2,1)} %v_ref.1) | copy-start | bytes 786436
  11.9 0.7 %copy-start.8 = (f32[3,8,128]{2,1,0:T(8,128)S(1)}, f32[3,8,128]{2,1,0:T(8,128)}, u32[]{:S(2)}) copy-start(f32[3,8,128]{2,1,0:T(8,128)} %get-tuple-element.33.tables_ref) | copy-start | bytes 36868
  17.0 3.8 %copy-start = (bf16[8,128,256]{2,1,0:T(8,128)(2,1)S(1)}, bf16[8,128,256]{2,1,0:T(8,128)(2,1)}, u32[]{:S(2)}) copy-start(bf16[8,128,256]{2,1,0:T(8,128)(2,1)} %refs_4_) | copy-start | bytes 1572868
  17.0 6.5 %copy-start.1 = (bf16[8,4096]{1,0:T(8,128)(2,1)S(1)}, bf16[8,4096]{1,0:T(8,128)(2,1)}, u32[]{:S(2)}) copy-start(bf16[8,4096]{1,0:T(8,128)(2,1)} %get-tuple-element.42.refs_0_) | copy-start | bytes 196612
  17.0 18.5 %all-to-all-start = ((bf16[16,8,2048]{2,1,0:T(8,128)(2,1)}), bf16[16,8,2048]{2,1,0:T(8,128)(2,1)S(1)}, u32[]{:S(2)}, u32[]{:S(2)}) async-start(bf16[16,8,2048]{2,1,0:T(8,128)(2,1)} %key.1.refs_4_), calls=%async_computation | async-start | bytes 1048576 | tf_op jit(solution)/shard_map/all_to_all | solution.py:306
  20.7 8.7 %copy-start.4 = (bf16[8,4096]{1,0:T(8,128)(2,1)S(1)}, bf16[8,4096]{1,0:T(8,128)(2,1)}, u32[]{:S(2)}) copy-start(bf16[8,4096]{1,0:T(8,128)(2,1)} %get-tuple-element.35.refs_1_) | copy-start | bytes 196612
  20.7 8.7 %copy-start.5 = (bf16[8,4096]{1,0:T(8,128)(2,1)S(1)}, bf16[8,4096]{1,0:T(8,128)(2,1)}, u32[]{:S(2)}) copy-start(bf16[8,4096]{1,0:T(8,128)(2,1)} %get-tuple-element.36.refs_2_) | copy-start | bytes 196612
  20.7 8.7 %copy-start.6 = (bf16[8,4096]{1,0:T(8,128)(2,1)S(1)}, bf16[8,4096]{1,0:T(8,128)(2,1)}, u32[]{:S(2)}) copy-start(bf16[8,4096]{1,0:T(8,128)(2,1)} %get-tuple-element.37.refs_3_) | copy-start | bytes 196612
  20.8 2.0 %collective-permute-start.4 = (bf16[8,128,256]{2,1,0:T(8,128)(2,1)S(1)}, bf16[8,128,256]{2,1,0:T(8,128)(2,1)S(1)}, u32[]{:S(2)}, u32[]{:S(2)}) collective-permute-start(bf16[8,128,256]{2,1,0:T(8,128)(2,1)S(1)} %copy-done), channel_id=1, source_target_pairs={{0,1},{1,0},{2,3},{3,2},{4,5},{5,4},{6,7},{7,6},{8,9},{9,8},{10,11... | collective-permute-start | bytes 1572872 | tf_op jit(solution)/shard_map/ppermute | solution.py:251
  21.1 2.4 %collective-permute-start.5 = (bf16[8,128,256]{2,1,0:T(8,128)(2,1)S(1)}, bf16[8,128,256]{2,1,0:T(8,128)(2,1)S(1)}, u32[]{:S(2)}, u32[]{:S(2)}) collective-permute-start(bf16[8,128,256]{2,1,0:T(8,128)(2,1)S(1)} %collective-permute-done.refs_6_), channel_id=1, source_target_pairs={{0,1},{1,0},{2,3},{3,2},{4,5},{5,4},{6,7},{7,6},{8,9},{9,8},{10,11... | collective-permute-start | bytes 1572872 | tf_op jit(solution)/shard_map/ppermute | solution.py:251
  25.0 11.4 %collective-permute-start.6 = (bf16[8,4224]{1,0:T(8,128)(2,1)S(1)}, bf16[8,4224]{1,0:T(8,128)(2,1)S(1)}, u32[]{:S(2)}, u32[]{:S(2)}) collective-permute-start(bf16[8,4224]{1,0:T(8,128)(2,1)S(1)} %get-tuple-element.53), channel_id=1, source_target_pairs={{0,4},{1,5},{2,6},{3,7},{4,0},{5,1},{6,2},{7,3},{8,12},{9,13},{10,... | collective-permute-start | bytes 202760 | tf_op jit(solution)/shard_map/ppermute | solution.py:251
  26.9 13.9 %collective-permute-start.7 = (bf16[8,4224]{1,0:T(8,128)(2,1)S(1)}, bf16[8,4224]{1,0:T(8,128)(2,1)S(1)}, u32[]{:S(2)}, u32[]{:S(2)}) collective-permute-start(bf16[8,4224]{1,0:T(8,128)(2,1)S(1)} %get-tuple-element.54), channel_id=1, source_target_pairs={{0,8},{1,9},{2,10},{3,11},{4,12},{5,13},{6,14},{7,15},{8,0},{9,1},... | collective-permute-start | bytes 202760 | tf_op jit(solution)/shard_map/ppermute | solution.py:251
  29.3 11.5 %collective-permute-start.8 = (bf16[8,4224]{1,0:T(8,128)(2,1)S(1)}, bf16[8,4224]{1,0:T(8,128)(2,1)S(1)}, u32[]{:S(2)}, u32[]{:S(2)}) collective-permute-start(bf16[8,4224]{1,0:T(8,128)(2,1)S(1)} %get-tuple-element.55), channel_id=1, source_target_pairs={{0,12},{1,13},{2,14},{3,15},{4,8},{5,9},{6,10},{7,11},{8,4},{9,5},... | collective-permute-start | bytes 202760 | tf_op jit(solution)/shard_map/ppermute | solution.py:251

commit v13 on v12

--- a/solution.py
+++ b/solution.py
@@ -54,8 +54,8 @@
 
 def query_kernel(groups, q_hbm, gain_hbm, coords_hbm, *refs):
     videos, tok_rows, width = q_hbm.shape
-    outs, tables_ref, refs = refs[:videos], refs[videos], refs[videos + 1 :]
-    q_ref, gain_ref, coords_ref, done_ref, sems, out_sems = refs
+    near_hbm, far_hbm, tables_ref, q_ref, gain_ref, coords_ref, done_ref, sems, out_sems = refs
+    half = videos // 2
     own = lax.axis_index("patch") // groups
     copies = [
         pltpu.make_async_copy(source, place, sems.at[i])
@@ -72,10 +72,11 @@
     copies[1].wait()
     copies[2].wait()
     sends = []
-    for s in range(videos):
+    for s in (*range(half, videos), *range(half)):
         for head, y in normed_heads(q_ref[own ^ s].astype(F32), gain_ref, tables):
             done_ref[s, :, head * DH : (head + 1) * DH] = y
-        sends.append(pltpu.make_async_copy(done_ref.at[s], outs[s], out_sems.at[s]))
+        out = far_hbm.at[s - half] if s >= half else near_hbm.at[s]
+        sends.append(pltpu.make_async_copy(done_ref.at[s], out, out_sems.at[s]))
         sends[-1].start()
     for send in sends:
         send.wait()
@@ -108,9 +109,8 @@
     return jnp.concatenate(rows, axis=0).astype(BF16)
 
 
-def fresh_kernel(groups, videos, *refs):
-    queries = refs[:videos]
-    fresh_ref, out_ref, log_ref = refs[videos:]
+def fresh_kernel(groups, videos, near_ref, far_ref, fresh_ref, out_ref, log_ref):
+    queries = [ref.at[i] for ref in (near_ref, far_ref) for i in range(videos // 2)]
     me = lax.axis_index("patch")
     mine = me % groups
     _, tok_rows, width = out_ref.shape
@@ -156,8 +156,14 @@
         log_ref[s] = logs[s * tok_rows : (s + 1) * tok_rows]
 
 
-def stale_kernel(groups, videos, *refs):
-    queries, pieces, outs = refs[:videos], refs[videos : videos + groups], refs[videos + groups :]
+def forward_kernel(near_ref, far_ref, out_ref):
+    out_ref[0] = near_ref[1]
+    out_ref[1] = far_ref[1]
+
+
+def stale_kernel(groups, videos, near_ref, far_ref, forward_ref, *refs):
+    queries = [near_ref.at[0], forward_ref.at[0], far_ref.at[0], forward_ref.at[1]]
+    pieces, outs = refs[:groups], refs[groups:]
     me = lax.axis_index("patch")
     mine = me % groups
     pairs, total_rows, _ = pieces[0].shape
@@ -262,7 +268,6 @@
     pairs_here, total_rows, _ = stale_cache.shape
     patches = total_rows // tok_rows
     groups = patches // videos
-    rows = jax.ShapeDtypeStruct((tok_rows, width), BF16)
 
     def kernel(body, name, limit, cost=0, **kwargs):
         return pl.pallas_call(
@@ -273,13 +278,15 @@
             **kwargs,
         )
 
-    *query, tables = kernel(
+    half = videos // 2
+    block = jax.ShapeDtypeStruct((half, tok_rows, width), BF16)
+    near, far, tables = kernel(
         functools.partial(query_kernel, groups),
         "query",
         56,
-        out_shape=[rows] * videos + [jax.ShapeDtypeStruct((3, tok_rows, DH), F32)],
+        out_shape=(block, block, jax.ShapeDtypeStruct((3, tok_rows, DH), F32)),
         in_specs=[HBM] * 3,
-        out_specs=[HBM] * videos + [VMEM],
+        out_specs=(HBM, HBM, VMEM),
         scratch_shapes=[
             pltpu.VMEM(queries.shape, BF16),
             pltpu.VMEM((1, width), F32),
@@ -289,7 +296,7 @@
             pltpu.SemaphoreType.DMA((videos,)),
         ],
     )(queries, q_gain.reshape(1, width), coords)
-    query_got = exchange(query, groups, patches)
+    far_got = permuted(far, half * groups, patches)
     stale_sent, tables = lax.optimization_barrier((stale_cache, tables))
     pieces = {0: stale_cache}
     bit = groups // 2
@@ -302,9 +309,18 @@
         in_specs=[VMEM] * 4,
         out_specs=VMEM,
     )(keys, values, k_gain.reshape(1, width), tables)
-    fresh_sent, query_got = lax.optimization_barrier((fresh, query_got))
+    fresh_sent, far_got = lax.optimization_barrier((fresh, far_got))
     cached = lax.all_to_all(fresh_sent, "patch", split_axis=0, concat_axis=0, tiled=True)
-    pieces, query_got = lax.optimization_barrier((pieces, query_got))
+    forward = kernel(
+        forward_kernel,
+        "forward",
+        16,
+        out_shape=jax.ShapeDtypeStruct((2, tok_rows, width), BF16),
+        in_specs=[VMEM] * 2,
+        out_specs=VMEM,
+    )(near, far_got)
+    forward_got = permuted(forward, groups, patches)
+    pieces, forward_got = lax.optimization_barrier((pieces, forward_got))
     while bit > 1:
         bit //= 2
         pieces.update({t | bit: permuted(piece, bit, patches) for t, piece in list(pieces.items())})
@@ -313,9 +329,9 @@
         "stale",
         32,
         out_shape=[jax.ShapeDtypeStruct((tok_rows, width + DH), BF16)] * videos,
-        in_specs=[VMEM] * (videos + groups),
+        in_specs=[VMEM] * (3 + groups),
         out_specs=[VMEM] * videos,
-    )(*query_got, *[pieces[t] for t in range(groups)])
+    )(near, far_got, forward_got, *[pieces[t] for t in range(groups)])
     result, fresh_late = lax.optimization_barrier((result, fresh))
     back = exchange(result, groups, patches)
     fresh_sum, fresh_log = kernel(
@@ -326,9 +342,9 @@
             jax.ShapeDtypeStruct((videos, tok_rows, width), F32),
             jax.ShapeDtypeStruct((videos, tok_rows, DH), F32),
         ),
-        in_specs=[VMEM] * (videos + 1),
+        in_specs=[VMEM] * 3,
         out_specs=(VMEM, VMEM),
-    )(*query, fresh_late)
+    )(near, far, fresh_late)
     next_cache = kernel(
         cache_kernel,
         "cache",

time: 42.3 us -> 49.5 us (1.17)
  waiting for transfers between devices: 13.4 us -> 19.3 us
  starting transfers between devices: 16.1 us -> 17.4 us
    ppermute x9 -> x8, waiting for transfers between devices: 9.48 us -> 19.3 us  [permuted(): lax.ppermute(array, 'patch', [(i, i ^ offset) for i in range(patches)])]
    all_to_all x1, waiting for transfers between devices: 3.91 us -> 0.01 us  [local(): lax.all_to_all(fresh_sent, 'patch', split_axis=0, concat_axis=0, tiled=True)]
    all_to_all x1, starting transfers between devices: 3.71 us -> 4.87 us  [local(): lax.all_to_all(fresh_sent, 'patch', split_axis=0, concat_axis=0, tiled=True)]
    ppermute x9 -> x8, starting transfers between devices: 12.4 us -> 12.5 us  [permuted(): lax.ppermute(array, 'patch', [(i, i ^ offset) for i in range(patches)])]
    pallas_call x1 -> x2, Pallas kernels: 2.9 us -> 2.92 us  [the longest x1 2.91 us: local(): kernel(functools.partial(query_kernel, groups), 'query', 56, out_shape=(b...]
    unnamed x18 -> x14, local copies, waits for them, and re-layouts: 1.69 us -> 1.68 us
  transfers between devices with their start and end apart: 10 -> 9, of which waited for: 6 -> 5; matrix products, arithmetic and copies ran while one was open for 0% -> 0% of each run, Pallas kernels for 14% -> 12%
where the time goes in v13:
time: 49.5 us; the launch traced here: 49.1 us
  waiting for transfers between devices  19.3 us (39%)
  starting transfers between devices  17.4 us (35%)
  Pallas kernels  10 us (20%)
  local copies, waits for them, and re-layouts  1.68 us (3%)
  between operations  0.74 us (1%)
    ppermute x8, waiting for transfers between devices, permuted(): lax.ppermute(array, 'patch', [(i, i ^ offset) for i in range(patches)])  19.3 us
    ppermute x8, starting transfers between devices, permuted(): lax.ppermute(array, 'patch', [(i, i ^ offset) for i in range(patches)])  12.5 us
    all_to_all x1, starting transfers between devices, local(): lax.all_to_all(fresh_sent, 'patch', split_axis=0, concat_axis=0, tiled=True)  4.87 us
    pallas_call x1, Pallas kernels, local(): kernel(functools.partial(query_kernel, groups), 'query', 56, out_shape=(b...  2.91 us
    pallas_call x1, Pallas kernels, local(): kernel(functools.partial(fresh_kernel, groups, videos), 'fresh', 16, out_...  2.15 us
    unnamed x14, local copies, waits for them, and re-layouts  1.68 us
    pallas_call x1, Pallas kernels, local(): kernel(functools.partial(stale_kernel, groups, videos), 'stale', 32, out_...  1.52 us
    pallas_call x1, Pallas kernels, local(): kernel(key_kernel, 'key', 16, out_shape=jax.ShapeDtypeStruct((patches, to...  1.42 us
  transfers between devices with their start and end apart: 9, of which 5 were waited for; matrix products, arithmetic and copies ran while one was open for 0% of the time, Pallas kernels for 12%

profile of v13, /device:TPU:0, one launch (start us, length us, event | category | flops | bytes accessed | tf_op | source)
XLA Modules:
  0.0 49.1 jit_solution(14468858765483525358)
XLA Ops:
  0.6 0.0 copy-start.2
  0.6 0.0 copy-start.5
  0.7 2.9 %query.1 = (bf16[2,8,4096]{2,1,0:T(8,128)(2,1)}, bf16[2,8,4096]{2,1,0:T(8,128)(2,1)}, f32[3,8,128]{2,1,0:T(8,128)}) custom-call(bf16[4,8,4096]{2,1,0:T(8,128)(2,1)} %q_hbm.1, f32[1,4096]{1,0:T(1,128)} %bitcast.5, s32[3,8]{1,0:T(4,128)} %coords_hbm.1), custom_call_target="tpu_custom_call" | custom-call | tf_op jit(solution)/shard_map/query/pallas_call | solution.py:283
  3.6 3.0 %collective-permute-start.1 = (bf16[8,128,256]{2,1,0:T(8,128)(2,1)}, bf16[8,128,256]{2,1,0:T(8,128)(2,1)S(1)}, u32[]{:S(2)}, u32[]{:S(2)}) collective-permute-start(bf16[8,128,256]{2,1,0:T(8,128)(2,1)} %refs_0_), channel_id=1, source_target_pairs={{0,2},{1,3},{2,0},{3,1},{4,6},{5,7},{6,4},{7,5},{8,10},{9,11},{10,... | collective-permute-start | bytes 1572872 | tf_op jit(solution)/shard_map/ppermute | solution.py:257
  6.6 2.6 %collective-permute-start = (bf16[2,8,4096]{2,1,0:T(8,128)(2,1)}, bf16[2,8,4096]{2,1,0:T(8,128)(2,1)S(1)}, u32[]{:S(2)}, u32[]{:S(2)}) collective-permute-start(bf16[2,8,4096]{2,1,0:T(8,128)(2,1)} %get-tuple-element.26.far_ref), channel_id=1, source_target_pairs={{0,8},{1,9},{2,10},{3,11},{4,12},{5,13},{6,14},{7,15},{8,0},{9,1},... | collective-permute-start | bytes 393224 | tf_op jit(solution)/shard_map/ppermute | solution.py:257
  9.2 0.0 copy-done.2
  9.2 0.0 copy-done.5
  9.2 0.0 copy-start.3
  9.2 0.9 %copy-done.3 = bf16[4,8,4096]{2,1,0:T(8,128)(2,1)S(1)} copy-done((bf16[4,8,4096]{2,1,0:T(8,128)(2,1)S(1)}, bf16[4,8,4096]{2,1,0:T(8,128)(2,1)}, u32[]{:S(2)}) %copy-start.3) | copy-done | bytes 262168
  10.1 0.0 copy-start.6
  10.1 0.7 %copy-done.6 = f32[3,8,128]{2,1,0:T(8,128)S(1)} copy-done((f32[3,8,128]{2,1,0:T(8,128)S(1)}, f32[3,8,128]{2,1,0:T(8,128)}, u32[]{:S(2)}) %copy-start.6) | copy-done | bytes 12312
  10.8 1.4 %key.1.fresh_ref = bf16[16,8,2048]{2,1,0:T(8,128)(2,1)} custom-call(bf16[4,8,4096]{2,1,0:T(8,128)(2,1)S(1)} %copy-done.2, bf16[4,8,4096]{2,1,0:T(8,128)(2,1)S(1)} %copy-done.3, f32[1,4096]{1,0:T(1,128)S(1)} %bitcast.3, f32[3,8,128]{2,1,0:T(8,128)S(1)} %copy-done.6), custom_call_target="tpu_custom_call" | custom-call | tf_op jit(solution)/shard_map/key/pallas_call | solution.py:304
  12.2 0.0 copy-start
  12.2 0.0 copy-start.1
  12.2 3.2 %collective-permute-done.far_ref = bf16[2,8,4096]{2,1,0:T(8,128)(2,1)S(1)} collective-permute-done((bf16[2,8,4096]{2,1,0:T(8,128)(2,1)}, bf16[2,8,4096]{2,1,0:T(8,128)(2,1)S(1)}, u32[]{:S(2)}, u32[]{:S(2)}) %collective-permute-start) | collective-permute-done | bytes 131104 | tf_op jit(solution)/shard_map/ppermute | solution.py:257
  15.4 4.9 %all-to-all-start = ((bf16[16,8,2048]{2,1,0:T(8,128)(2,1)}), bf16[16,8,2048]{2,1,0:T(8,128)(2,1)S(1)}, u32[]{:S(2)}, u32[]{:S(2)}) async-start(bf16[16,8,2048]{2,1,0:T(8,128)(2,1)} %key.1.fresh_ref), calls=%async_computation | async-start | bytes 1048576 | tf_op jit(solution)/shard_map/all_to_all | solution.py:313
  20.3 0.0 copy-done
  20.4 0.0 copy-start.4
  20.4 2.0 %collective-permute-start.2 = (bf16[2,8,4096]{2,1,0:T(8,128)(2,1)S(1)}, bf16[2,8,4096]{2,1,0:T(8,128)(2,1)S(1)}, u32[]{:S(2)}, u32[]{:S(2)}) collective-permute-start(bf16[2,8,4096]{2,1,0:T(8,128)(2,1)S(1)} %forward.1), channel_id=1, source_target_pairs={{0,4},{1,5},{2,6},{3,7},{4,0},{5,1},{6,2},{7,3},{8,12},{9,13},{10,... | collective-permute-start | bytes 393224 | tf_op jit(solution)/shard_map/ppermute | solution.py:257
  22.3 12.3 %collective-permute-done.2.forward_ref = bf16[2,8,4096]{2,1,0:T(8,128)(2,1)S(1)} collective-permute-done((bf16[2,8,4096]{2,1,0:T(8,128)(2,1)S(1)}, bf16[2,8,4096]{2,1,0:T(8,128)(2,1)S(1)}, u32[]{:S(2)}, u32[]{:S(2)}) %collective-permute-start.2) | collective-permute-done | bytes 131104 | tf_op jit(solution)/shard_map/ppermute | solution.py:257
  34.7 0.0 collective-permute-done.1.refs_2_
  34.7 0.0 copy-done.1
  34.7 0.0 collective-permute-start.3
  34.7 0.5 %collective-permute-start.4 = (bf16[8,128,256]{2,1,0:T(8,128)(2,1)S(1)}, bf16[8,128,256]{2,1,0:T(8,128)(2,1)S(1)}, u32[]{:S(2)}, u32[]{:S(2)}) collective-permute-start(bf16[8,128,256]{2,1,0:T(8,128)(2,1)S(1)} %collective-permute-done.1.refs_2_), channel_id=1, source_target_pairs={{0,1},{1,0},{2,3},{3,2},{4,5},{5,4},{6,7},{7,6},{8,9},{9,8},{10,11... | collective-permute-start | bytes 1572872 | tf_op jit(solution)/shard_map/ppermute | solution.py:257
  35.2 1.4 %collective-permute-done.3.refs_1_ = bf16[8,128,256]{2,1,0:T(8,128)(2,1)S(1)} collective-permute-done((bf16[8,128,256]{2,1,0:T(8,128)(2,1)S(1)}, bf16[8,128,256]{2,1,0:T(8,128)(2,1)S(1)}, u32[]{:S(2)}, u32[]{:S(2)}) %collective-permute-start.3) | collective-permute-done | bytes 524320 | tf_op jit(solution)/shard_map/ppermute | solution.py:257
  36.6 0.7 %collective-permute-done.4.refs_3_ = bf16[8,128,256]{2,1,0:T(8,128)(2,1)S(1)} collective-permute-done((bf16[8,128,256]{2,1,0:T(8,128)(2,1)S(1)}, bf16[8,128,256]{2,1,0:T(8,128)(2,1)S(1)}, u32[]{:S(2)}, u32[]{:S(2)}) %collective-permute-start.4) | collective-permute-done | bytes 524320 | tf_op jit(solution)/shard_map/ppermute | solution.py:257
  37.4 1.5 %stale.1 = (bf16[8,4224]{1,0:T(8,128)(2,1)S(1)}, bf16[8,4224]{1,0:T(8,128)(2,1)S(1)}, bf16[8,4224]{1,0:T(8,128)(2,1)S(1)}, bf16[8,4224]{1,0:T(8,128)(2,1)S(1)}) custom-call(bf16[2,8,4096]{2,1,0:T(8,128)(2,1)S(1)} %copy-done, bf16[2,8,4096]{2,1,0:T(8,128)(2,1)S(1)} %collective-permute-done.far_ref, ...), custom_call_target="tpu_custom_call" | custom-call | tf_op jit(solution)/shard_map/stale/pallas_call | solution.py:327
  38.9 0.5 collective-permute-start.5
  39.4 2.1 %collective-permute-start.6 = (bf16[8,4224]{1,0:T(8,128)(2,1)S(1)}, bf16[8,4224]{1,0:T(8,128)(2,1)S(1)}, u32[]{:S(2)}, u32[]{:S(2)}) collective-permute-start(bf16[8,4224]{1,0:T(8,128)(2,1)S(1)} %get-tuple-element.38), channel_id=1, source_target_pairs={{0,8},{1,9},{2,10},{3,11},{4,12},{5,13},{6,14},{7,15},{8,0},{9,1},... | collective-permute-start | bytes 202760 | tf_op jit(solution)/shard_map/ppermute | solution.py:257
  41.5 1.8 %collective-permute-start.7 = (bf16[8,4224]{1,0:T(8,128)(2,1)S(1)}, bf16[8,4224]{1,0:T(8,128)(2,1)S(1)}, u32[]{:S(2)}, u32[]{:S(2)}) collective-permute-start(bf16[8,4224]{1,0:T(8,128)(2,1)S(1)} %get-tuple-element.39), channel_id=1, source_target_pairs={{0,12},{1,13},{2,14},{3,15},{4,8},{5,9},{6,10},{7,11},{8,4},{9,5},... | collective-permute-start | bytes 202760 | tf_op jit(solution)/shard_map/ppermute | solution.py:257
  43.3 0.0 copy-done.4
  43.3 2.1 %fresh.1 = (f32[4,8,4096]{2,1,0:T(8,128)S(1)}, f32[4,8,128]{2,1,0:T(8,128)S(1)}) custom-call(bf16[2,8,4096]{2,1,0:T(8,128)(2,1)S(1)} %copy-done, bf16[2,8,4096]{2,1,0:T(8,128)(2,1)S(1)} %copy-done.4, bf16[16,8,2048]{2,1,0:T(8,128)(2,1)} %key.1.fresh_ref), custom_call_target="tpu_custom_call" | custom-call | tf_op jit(solution)/shard_map/fresh/pallas_call | solution.py:337
  45.4 0.0 all-to-all-done.got_ref
  45.5 0.9 %cache.1 = bf16[8,16,8,256]{3,2,1,0:T(8,128)(2,1)} custom-call(bf16[16,8,2048]{2,1,0:T(8,128)(2,1)S(1)} %all-to-all-done.got_ref), custom_call_target="tpu_custom_call" | custom-call | tf_op jit(solution)/shard_map/cache/pallas_call | solution.py:348
  46.3 0.0 collective-permute-done.5.refs_1_
  46.3 0.0 collective-permute-done.6.refs_2_
  46.3 1.6 %collective-permute-done.7.refs_3_ = bf16[8,4224]{1,0:T(8,128)(2,1)S(1)} collective-permute-done((bf16[8,4224]{1,0:T(8,128)(2,1)S(1)}, bf16[8,4224]{1,0:T(8,128)(2,1)S(1)}, u32[]{:S(2)}, u32[]{:S(2)}) %collective-permute-start.7) | collective-permute-done | bytes 67616 | tf_op jit(solution)/shard_map/ppermute | solution.py:257
  48.0 1.2 %join.1 = bf16[4,8,4096]{2,1,0:T(8,128)(2,1)} custom-call(bf16[8,4224]{1,0:T(8,128)(2,1)S(1)} %get-tuple-element.36.refs_0_, bf16[8,4224]{1,0:T(8,128)(2,1)S(1)} %collective-permute-done.5.refs_1_, bf16[8,4224]{1,0:T(8,128)(2,1)S(1)} %collective-permute-done.6.refs_2_, bf16[8,4224]{1,0:T(8,128)(2,1)S(1)} %collective-permute-done.7.refs_3_, ...), custom_call_target="tpu_custom_call" | custom-call | tf_op jit(solution)/shard_map/join/pallas_call | solution.py:357
  (1 shorter events, 0.0 us)
Async XLA Ops:
  0.6 8.5 %copy-start.2 = (bf16[4,8,4096]{2,1,0:T(8,128)(2,1)S(1)}, bf16[4,8,4096]{2,1,0:T(8,128)(2,1)}, u32[]{:S(2)}) copy-start(bf16[4,8,4096]{2,1,0:T(8,128)(2,1)} %k_ref.1) | copy-start | bytes 786436
  0.6 8.5 %copy-start.5 = (f32[4096]{0:T(1024)S(1)}, f32[4096]{0:T(1024)}, u32[]{:S(2)}) copy-start(f32[4096]{0:T(1024)} %param.11) | copy-start | bytes 49156
  3.6 31.1 %collective-permute-start.1 = (bf16[8,128,256]{2,1,0:T(8,128)(2,1)}, bf16[8,128,256]{2,1,0:T(8,128)(2,1)S(1)}, u32[]{:S(2)}, u32[]{:S(2)}) collective-permute-start(bf16[8,128,256]{2,1,0:T(8,128)(2,1)} %refs_0_), channel_id=1, source_target_pairs={{0,2},{1,3},{2,0},{3,1},{4,6},{5,7},{6,4},{7,5},{8,10},{9,11},{10,... | collective-permute-start | bytes 1572872 | tf_op jit(solution)/shard_map/ppermute | solution.py:257
  6.6 8.9 %collective-permute-start = (bf16[2,8,4096]{2,1,0:T(8,128)(2,1)}, bf16[2,8,4096]{2,1,0:T(8,128)(2,1)S(1)}, u32[]{:S(2)}, u32[]{:S(2)}) collective-permute-start(bf16[2,8,4096]{2,1,0:T(8,128)(2,1)} %get-tuple-element.26.far_ref), channel_id=1, source_target_pairs={{0,8},{1,9},{2,10},{3,11},{4,12},{5,13},{6,14},{7,15},{8,0},{9,1},... | collective-permute-start | bytes 393224 | tf_op jit(solution)/shard_map/ppermute | solution.py:257
  9.2 1.0 %copy-start.3 = (bf16[4,8,4096]{2,1,0:T(8,128)(2,1)S(1)}, bf16[4,8,4096]{2,1,0:T(8,128)(2,1)}, u32[]{:S(2)}) copy-start(bf16[4,8,4096]{2,1,0:T(8,128)(2,1)} %v_ref.1) | copy-start | bytes 786436
  10.1 0.7 %copy-start.6 = (f32[3,8,128]{2,1,0:T(8,128)S(1)}, f32[3,8,128]{2,1,0:T(8,128)}, u32[]{:S(2)}) copy-start(f32[3,8,128]{2,1,0:T(8,128)} %get-tuple-element.25.tables_ref) | copy-start | bytes 36868
  12.2 8.1 %copy-start = (bf16[2,8,4096]{2,1,0:T(8,128)(2,1)S(1)}, bf16[2,8,4096]{2,1,0:T(8,128)(2,1)}, u32[]{:S(2)}) copy-start(bf16[2,8,4096]{2,1,0:T(8,128)(2,1)} %get-tuple-element.23.near_ref) | copy-start | bytes 393220
  12.2 22.4 %copy-start.1 = (bf16[8,128,256]{2,1,0:T(8,128)(2,1)S(1)}, bf16[8,128,256]{2,1,0:T(8,128)(2,1)}, u32[]{:S(2)}) copy-start(bf16[8,128,256]{2,1,0:T(8,128)(2,1)} %refs_0_) | copy-start | bytes 1572868
  15.4 30.0 %all-to-all-start = ((bf16[16,8,2048]{2,1,0:T(8,128)(2,1)}), bf16[16,8,2048]{2,1,0:T(8,128)(2,1)S(1)}, u32[]{:S(2)}, u32[]{:S(2)}) async-start(bf16[16,8,2048]{2,1,0:T(8,128)(2,1)} %key.1.fresh_ref), calls=%async_computation | async-start | bytes 1048576 | tf_op jit(solution)/shard_map/all_to_all | solution.py:313
  20.4 22.9 %copy-start.4 = (bf16[2,8,4096]{2,1,0:T(8,128)(2,1)S(1)}, bf16[2,8,4096]{2,1,0:T(8,128)(2,1)}, u32[]{:S(2)}) copy-start(bf16[2,8,4096]{2,1,0:T(8,128)(2,1)} %get-tuple-element.26.far_ref) | copy-start | bytes 393220
  20.4 14.3 %collective-permute-start.2 = (bf16[2,8,4096]{2,1,0:T(8,128)(2,1)S(1)}, bf16[2,8,4096]{2,1,0:T(8,128)(2,1)S(1)}, u32[]{:S(2)}, u32[]{:S(2)}) collective-permute-start(bf16[2,8,4096]{2,1,0:T(8,128)(2,1)S(1)} %forward.1), channel_id=1, source_target_pairs={{0,4},{1,5},{2,6},{3,7},{4,0},{5,1},{6,2},{7,3},{8,12},{9,13},{10,... | collective-permute-start | bytes 393224 | tf_op jit(solution)/shard_map/ppermute | solution.py:257
  34.7 1.9 %collective-permute-start.3 = (bf16[8,128,256]{2,1,0:T(8,128)(2,1)S(1)}, bf16[8,128,256]{2,1,0:T(8,128)(2,1)S(1)}, u32[]{:S(2)}, u32[]{:S(2)}) collective-permute-start(bf16[8,128,256]{2,1,0:T(8,128)(2,1)S(1)} %copy-done.1), channel_id=1, source_target_pairs={{0,1},{1,0},{2,3},{3,2},{4,5},{5,4},{6,7},{7,6},{8,9},{9,8},{10,11... | collective-permute-start | bytes 1572872 | tf_op jit(solution)/shard_map/ppermute | solution.py:257
  34.7 2.7 %collective-permute-start.4 = (bf16[8,128,256]{2,1,0:T(8,128)(2,1)S(1)}, bf16[8,128,256]{2,1,0:T(8,128)(2,1)S(1)}, u32[]{:S(2)}, u32[]{:S(2)}) collective-permute-start(bf16[8,128,256]{2,1,0:T(8,128)(2,1)S(1)} %collective-permute-done.1.refs_2_), channel_id=1, source_target_pairs={{0,1},{1,0},{2,3},{3,2},{4,5},{5,4},{6,7},{7,6},{8,9},{9,8},{10,11... | collective-permute-start | bytes 1572872 | tf_op jit(solution)/shard_map/ppermute | solution.py:257
  38.9 7.4 %collective-permute-start.5 = (bf16[8,4224]{1,0:T(8,128)(2,1)S(1)}, bf16[8,4224]{1,0:T(8,128)(2,1)S(1)}, u32[]{:S(2)}, u32[]{:S(2)}) collective-permute-start(bf16[8,4224]{1,0:T(8,128)(2,1)S(1)} %get-tuple-element.37), channel_id=1, source_target_pairs={{0,4},{1,5},{2,6},{3,7},{4,0},{5,1},{6,2},{7,3},{8,12},{9,13},{10,... | collective-permute-start | bytes 202760 | tf_op jit(solution)/shard_map/ppermute | solution.py:257
  39.4 7.0 %collective-permute-start.6 = (bf16[8,4224]{1,0:T(8,128)(2,1)S(1)}, bf16[8,4224]{1,0:T(8,128)(2,1)S(1)}, u32[]{:S(2)}, u32[]{:S(2)}) collective-permute-start(bf16[8,4224]{1,0:T(8,128)(2,1)S(1)} %get-tuple-element.38), channel_id=1, source_target_pairs={{0,8},{1,9},{2,10},{3,11},{4,12},{5,13},{6,14},{7,15},{8,0},{9,1},... | collective-permute-start | bytes 202760 | tf_op jit(solution)/shard_map/ppermute | solution.py:257
  41.5 6.5 %collective-permute-start.7 = (bf16[8,4224]{1,0:T(8,128)(2,1)S(1)}, bf16[8,4224]{1,0:T(8,128)(2,1)S(1)}, u32[]{:S(2)}, u32[]{:S(2)}) collective-permute-start(bf16[8,4224]{1,0:T(8,128)(2,1)S(1)} %get-tuple-element.39), channel_id=1, source_target_pairs={{0,12},{1,13},{2,14},{3,15},{4,8},{5,9},{6,10},{7,11},{8,4},{9,5},... | collective-permute-start | bytes 202760 | tf_op jit(solution)/shard_map/ppermute | solution.py:257

commit v14 on v12

--- a/solution.py
+++ b/solution.py
@@ -252,9 +252,11 @@
 
 
 def exchange(arrays, stride, patches):
-    return [arrays[0]] + [
-        permuted(arrays[s], s * stride, patches) for s in range(1, len(arrays))
-    ]
+    half = len(arrays) // 2
+    got = {0: arrays[0]}
+    for s in (*range(half, 2 * half), *range(1, half)):
+        got[s] = permuted(arrays[s], s * stride, patches)
+    return [got[s] for s in range(2 * half)]
 
 
 def local(queries, keys, values, q_gain, k_gain, stale_cache, coords):

time: 42.3 us -> 42.3 us (level)
  no operation moved by 1% of the time
where the time goes in v14:
time: 42.3 us; the launch traced here: 41.9 us
  starting transfers between devices  16.1 us (38%)
  waiting for transfers between devices  13.4 us (32%)
  Pallas kernels  10 us (24%)
  local copies, waits for them, and re-layouts  1.69 us (4%)
  between operations  0.74 us (2%)
    ppermute x9, starting transfers between devices, permuted(): lax.ppermute(array, 'patch', [(i, i ^ offset) for i in range(patches)])  12.4 us
    ppermute x9, waiting for transfers between devices, permuted(): lax.ppermute(array, 'patch', [(i, i ^ offset) for i in range(patches)])  9.48 us
    all_to_all x1, waiting for transfers between devices, local(): lax.all_to_all(fresh_sent, 'patch', split_axis=0, concat_axis=0, tiled=True)  3.91 us
    all_to_all x1, starting transfers between devices, local(): lax.all_to_all(fresh_sent, 'patch', split_axis=0, concat_axis=0, tiled=True)  3.71 us
    pallas_call x1, Pallas kernels, local(): kernel(functools.partial(query_kernel, groups), 'query', 56, out_shape=[r...  2.9 us
    pallas_call x1, Pallas kernels, local(): kernel(functools.partial(fresh_kernel, groups, videos), 'fresh', 16, out_...  2.15 us
    unnamed x18, local copies, waits for them, and re-layouts  1.69 us
    pallas_call x1, Pallas kernels, local(): kernel(functools.partial(stale_kernel, groups, videos), 'stale', 32, out_...  1.52 us
  transfers between devices with their start and end apart: 10, of which 6 were waited for; matrix products, arithmetic and copies ran while one was open for 0% of the time, Pallas kernels for 14%

profile of v14, /device:TPU:0, one launch (start us, length us, event | category | flops | bytes accessed | tf_op | source)
XLA Modules:
  0.0 41.9 jit_solution(5462164096572276163)
XLA Ops:
  0.6 0.0 copy-start.2
  0.6 0.0 copy-start.7
  0.7 2.9 %query.1 = (bf16[8,4096]{1,0:T(8,128)(2,1)}, bf16[8,4096]{1,0:T(8,128)(2,1)}, bf16[8,4096]{1,0:T(8,128)(2,1)}, bf16[8,4096]{1,0:T(8,128)(2,1)}, f32[3,8,128]{2,1,0:T(8,128)}) custom-call(bf16[4,8,4096]{2,1,0:T(8,128)(2,1)} %q_hbm.1, f32[1,4096]{1,0:T(1,128)} %bitcast.5, s32[3,8]{1,0:T(4,128)} %coords_hbm.1), custom_call_target="tpu_custom_call" | custom-call | tf_op jit(solution)/shard_map/query/pallas_call | solution.py:278
  3.6 3.0 %collective-permute-start = (bf16[8,128,256]{2,1,0:T(8,128)(2,1)}, bf16[8,128,256]{2,1,0:T(8,128)(2,1)S(1)}, u32[]{:S(2)}, u32[]{:S(2)}) collective-permute-start(bf16[8,128,256]{2,1,0:T(8,128)(2,1)} %refs_4_), channel_id=1, source_target_pairs={{0,2},{1,3},{2,0},{3,1},{4,6},{5,7},{6,4},{7,5},{8,10},{9,11},{10,... | collective-permute-start | bytes 1572872 | tf_op jit(solution)/shard_map/ppermute | solution.py:251
  6.6 1.6 %collective-permute-start.1 = (bf16[8,4096]{1,0:T(8,128)(2,1)}, bf16[8,4096]{1,0:T(8,128)(2,1)S(1)}, u32[]{:S(2)}, u32[]{:S(2)}) collective-permute-start(bf16[8,4096]{1,0:T(8,128)(2,1)} %get-tuple-element.35.refs_1_), channel_id=1, source_target_pairs={{0,4},{1,5},{2,6},{3,7},{4,0},{5,1},{6,2},{7,3},{8,12},{9,13},{10,... | collective-permute-start | bytes 196616 | tf_op jit(solution)/shard_map/ppermute | solution.py:251
  8.1 2.6 %collective-permute-start.2 = (bf16[8,4096]{1,0:T(8,128)(2,1)}, bf16[8,4096]{1,0:T(8,128)(2,1)S(1)}, u32[]{:S(2)}, u32[]{:S(2)}) collective-permute-start(bf16[8,4096]{1,0:T(8,128)(2,1)} %get-tuple-element.36.refs_2_), channel_id=1, source_target_pairs={{0,8},{1,9},{2,10},{3,11},{4,12},{5,13},{6,14},{7,15},{8,0},{9,1},... | collective-permute-start | bytes 196616 | tf_op jit(solution)/shard_map/ppermute | solution.py:251
  10.7 0.2 collective-permute-start.3
  11.0 0.0 copy-done.2
  11.0 0.0 copy-done.7
  11.0 0.0 copy-start.3
  11.0 0.9 %copy-done.3 = bf16[4,8,4096]{2,1,0:T(8,128)(2,1)S(1)} copy-done((bf16[4,8,4096]{2,1,0:T(8,128)(2,1)S(1)}, bf16[4,8,4096]{2,1,0:T(8,128)(2,1)}, u32[]{:S(2)}) %copy-start.3) | copy-done | bytes 262168
  11.9 0.0 copy-start.8
  11.9 0.7 %copy-done.8 = f32[3,8,128]{2,1,0:T(8,128)S(1)} copy-done((f32[3,8,128]{2,1,0:T(8,128)S(1)}, f32[3,8,128]{2,1,0:T(8,128)}, u32[]{:S(2)}) %copy-start.8) | copy-done | bytes 12312
  12.6 1.4 %key.1.refs_4_ = bf16[16,8,2048]{2,1,0:T(8,128)(2,1)} custom-call(bf16[4,8,4096]{2,1,0:T(8,128)(2,1)S(1)} %copy-done.2, bf16[4,8,4096]{2,1,0:T(8,128)(2,1)S(1)} %copy-done.3, f32[1,4096]{1,0:T(1,128)S(1)} %bitcast.3, f32[3,8,128]{2,1,0:T(8,128)S(1)} %copy-done.8), custom_call_target="tpu_custom_call" | custom-call | tf_op jit(solution)/shard_map/key/pallas_call | solution.py:299
  14.0 0.0 collective-permute-done.1.refs_1_
  14.0 1.3 %collective-permute-done.2.refs_2_ = bf16[8,4096]{1,0:T(8,128)(2,1)S(1)} collective-permute-done((bf16[8,4096]{1,0:T(8,128)(2,1)}, bf16[8,4096]{1,0:T(8,128)(2,1)S(1)}, u32[]{:S(2)}, u32[]{:S(2)}) %collective-permute-start.2) | collective-permute-done | bytes 65568 | tf_op jit(solution)/shard_map/ppermute | solution.py:251
  15.3 1.7 %collective-permute-done.3.refs_3_ = bf16[8,4096]{1,0:T(8,128)(2,1)S(1)} collective-permute-done((bf16[8,4096]{1,0:T(8,128)(2,1)}, bf16[8,4096]{1,0:T(8,128)(2,1)S(1)}, u32[]{:S(2)}, u32[]{:S(2)}) %collective-permute-start.3) | collective-permute-done | bytes 65568 | tf_op jit(solution)/shard_map/ppermute | solution.py:251
  17.0 0.0 copy-start
  17.0 0.0 copy-start.1
  17.0 3.7 %all-to-all-start = ((bf16[16,8,2048]{2,1,0:T(8,128)(2,1)}), bf16[16,8,2048]{2,1,0:T(8,128)(2,1)S(1)}, u32[]{:S(2)}, u32[]{:S(2)}) async-start(bf16[16,8,2048]{2,1,0:T(8,128)(2,1)} %key.1.refs_4_), calls=%async_computation | async-start | bytes 1048576 | tf_op jit(solution)/shard_map/all_to_all | solution.py:308
  20.7 0.0 copy-start.4
  20.7 0.0 copy-start.5
  20.7 0.0 copy-start.6
  20.8 0.0 collective-permute-done.refs_6_
  20.8 0.0 copy-done
  20.8 0.4 collective-permute-start.4
  21.1 0.2 collective-permute-start.5
  21.3 1.4 %collective-permute-done.4.refs_5_ = bf16[8,128,256]{2,1,0:T(8,128)(2,1)S(1)} collective-permute-done((bf16[8,128,256]{2,1,0:T(8,128)(2,1)S(1)}, bf16[8,128,256]{2,1,0:T(8,128)(2,1)S(1)}, u32[]{:S(2)}, u32[]{:S(2)}) %collective-permute-start.4) | collective-permute-done | bytes 524320 | tf_op jit(solution)/shard_map/ppermute | solution.py:251
  22.7 0.7 %collective-permute-done.5.refs_7_ = bf16[8,128,256]{2,1,0:T(8,128)(2,1)S(1)} collective-permute-done((bf16[8,128,256]{2,1,0:T(8,128)(2,1)S(1)}, bf16[8,128,256]{2,1,0:T(8,128)(2,1)S(1)}, u32[]{:S(2)}, u32[]{:S(2)}) %collective-permute-start.5) | collective-permute-done | bytes 524320 | tf_op jit(solution)/shard_map/ppermute | solution.py:251
  23.5 0.0 copy-done.1
  23.5 1.5 %stale.1 = (bf16[8,4224]{1,0:T(8,128)(2,1)S(1)}, bf16[8,4224]{1,0:T(8,128)(2,1)S(1)}, bf16[8,4224]{1,0:T(8,128)(2,1)S(1)}, bf16[8,4224]{1,0:T(8,128)(2,1)S(1)}) custom-call(bf16[8,4096]{1,0:T(8,128)(2,1)S(1)} %copy-done.1, bf16[8,4096]{1,0:T(8,128)(2,1)S(1)} %collective-permute-done.1.refs_1_, bf16[8,4096]{1,0:T(8,128)(2,1)S(1)} %collective-permute-done.2.refs_2_, ...), custom_call_target="tpu_custom_call" | custom-call | tf_op jit(solution)/shard_map/stale/pallas_call | solution.py:313
  25.0 1.9 %collective-permute-start.6 = (bf16[8,4224]{1,0:T(8,128)(2,1)S(1)}, bf16[8,4224]{1,0:T(8,128)(2,1)S(1)}, u32[]{:S(2)}, u32[]{:S(2)}) collective-permute-start(bf16[8,4224]{1,0:T(8,128)(2,1)S(1)} %get-tuple-element.53), channel_id=1, source_target_pairs={{0,4},{1,5},{2,6},{3,7},{4,0},{5,1},{6,2},{7,3},{8,12},{9,13},{10,... | collective-permute-start | bytes 202760 | tf_op jit(solution)/shard_map/ppermute | solution.py:251
  26.9 2.4 %collective-permute-start.7 = (bf16[8,4224]{1,0:T(8,128)(2,1)S(1)}, bf16[8,4224]{1,0:T(8,128)(2,1)S(1)}, u32[]{:S(2)}, u32[]{:S(2)}) collective-permute-start(bf16[8,4224]{1,0:T(8,128)(2,1)S(1)} %get-tuple-element.54), channel_id=1, source_target_pairs={{0,8},{1,9},{2,10},{3,11},{4,12},{5,13},{6,14},{7,15},{8,0},{9,1},... | collective-permute-start | bytes 202760 | tf_op jit(solution)/shard_map/ppermute | solution.py:251
  29.3 0.1 collective-permute-start.8
  29.4 0.0 copy-done.4
  29.4 0.0 copy-done.5
  29.4 0.0 copy-done.6
  29.5 2.1 %fresh.1 = (f32[4,8,4096]{2,1,0:T(8,128)S(1)}, f32[4,8,128]{2,1,0:T(8,128)S(1)}) custom-call(bf16[8,4096]{1,0:T(8,128)(2,1)S(1)} %copy-done.1, bf16[8,4096]{1,0:T(8,128)(2,1)S(1)} %copy-done.4, bf16[8,4096]{1,0:T(8,128)(2,1)S(1)} %copy-done.5, bf16[8,4096]{1,0:T(8,128)(2,1)S(1)} %copy-done.6, bf16[16,8,2048]{2,1,0:T(8,128)(2,1)} %key.1.refs_4_), custom_call_target="tpu_custom_call" | custom-call | tf_op jit(solution)/shard_map/fresh/pallas_call | solution.py:323
  31.6 3.9 %all-to-all-done.got_ref = bf16[16,8,2048]{2,1,0:T(8,128)(2,1)S(1)} async-done(((bf16[16,8,2048]{2,1,0:T(8,128)(2,1)}), bf16[16,8,2048]{2,1,0:T(8,128)(2,1)S(1)}, u32[]{:S(2)}, u32[]{:S(2)}) %all-to-all-start) | async-done | bytes 524320 | tf_op jit(solution)/shard_map/all_to_all | solution.py:308
  35.5 0.8 %cache.1 = bf16[8,16,8,256]{3,2,1,0:T(8,128)(2,1)} custom-call(bf16[16,8,2048]{2,1,0:T(8,128)(2,1)S(1)} %all-to-all-done.got_ref), custom_call_target="tpu_custom_call" | custom-call | tf_op jit(solution)/shard_map/cache/pallas_call | solution.py:334
  36.4 0.0 collective-permute-done.6.refs_1_
  36.4 4.4 %collective-permute-done.7.refs_2_ = bf16[8,4224]{1,0:T(8,128)(2,1)S(1)} collective-permute-done((bf16[8,4224]{1,0:T(8,128)(2,1)S(1)}, bf16[8,4224]{1,0:T(8,128)(2,1)S(1)}, u32[]{:S(2)}, u32[]{:S(2)}) %collective-permute-start.7) | collective-permute-done | bytes 67616 | tf_op jit(solution)/shard_map/ppermute | solution.py:251
  40.7 0.0 collective-permute-done.8.refs_3_
  40.7 1.2 %join.1 = bf16[4,8,4096]{2,1,0:T(8,128)(2,1)} custom-call(bf16[8,4224]{1,0:T(8,128)(2,1)S(1)} %get-tuple-element.52.refs_0_, bf16[8,4224]{1,0:T(8,128)(2,1)S(1)} %collective-permute-done.6.refs_1_, bf16[8,4224]{1,0:T(8,128)(2,1)S(1)} %collective-permute-done.7.refs_2_, bf16[8,4224]{1,0:T(8,128)(2,1)S(1)} %collective-permute-done.8.refs_3_, ...), custom_call_target="tpu_custom_call" | custom-call | tf_op jit(solution)/shard_map/join/pallas_call | solution.py:343
Async XLA Ops:
  0.6 10.3 %copy-start.2 = (bf16[4,8,4096]{2,1,0:T(8,128)(2,1)S(1)}, bf16[4,8,4096]{2,1,0:T(8,128)(2,1)}, u32[]{:S(2)}) copy-start(bf16[4,8,4096]{2,1,0:T(8,128)(2,1)} %k_ref.1) | copy-start | bytes 786436
  0.6 10.3 %copy-start.7 = (f32[4096]{0:T(1024)S(1)}, f32[4096]{0:T(1024)}, u32[]{:S(2)}) copy-start(f32[4096]{0:T(1024)} %param.11) | copy-start | bytes 49156
  3.6 17.2 %collective-permute-start = (bf16[8,128,256]{2,1,0:T(8,128)(2,1)}, bf16[8,128,256]{2,1,0:T(8,128)(2,1)S(1)}, u32[]{:S(2)}, u32[]{:S(2)}) collective-permute-start(bf16[8,128,256]{2,1,0:T(8,128)(2,1)} %refs_4_), channel_id=1, source_target_pairs={{0,2},{1,3},{2,0},{3,1},{4,6},{5,7},{6,4},{7,5},{8,10},{9,11},{10,... | collective-permute-start | bytes 1572872 | tf_op jit(solution)/shard_map/ppermute | solution.py:251
  6.6 7.5 %collective-permute-start.1 = (bf16[8,4096]{1,0:T(8,128)(2,1)}, bf16[8,4096]{1,0:T(8,128)(2,1)S(1)}, u32[]{:S(2)}, u32[]{:S(2)}) collective-permute-start(bf16[8,4096]{1,0:T(8,128)(2,1)} %get-tuple-element.35.refs_1_), channel_id=1, source_target_pairs={{0,4},{1,5},{2,6},{3,7},{4,0},{5,1},{6,2},{7,3},{8,12},{9,13},{10,... | collective-permute-start | bytes 196616 | tf_op jit(solution)/shard_map/ppermute | solution.py:251
  8.1 7.2 %collective-permute-start.2 = (bf16[8,4096]{1,0:T(8,128)(2,1)}, bf16[8,4096]{1,0:T(8,128)(2,1)S(1)}, u32[]{:S(2)}, u32[]{:S(2)}) collective-permute-start(bf16[8,4096]{1,0:T(8,128)(2,1)} %get-tuple-element.36.refs_2_), channel_id=1, source_target_pairs={{0,8},{1,9},{2,10},{3,11},{4,12},{5,13},{6,14},{7,15},{8,0},{9,1},... | collective-permute-start | bytes 196616 | tf_op jit(solution)/shard_map/ppermute | solution.py:251
  10.7 6.3 %collective-permute-start.3 = (bf16[8,4096]{1,0:T(8,128)(2,1)}, bf16[8,4096]{1,0:T(8,128)(2,1)S(1)}, u32[]{:S(2)}, u32[]{:S(2)}) collective-permute-start(bf16[8,4096]{1,0:T(8,128)(2,1)} %get-tuple-element.37.refs_3_), channel_id=1, source_target_pairs={{0,12},{1,13},{2,14},{3,15},{4,8},{5,9},{6,10},{7,11},{8,4},{9,5},... | collective-permute-start | bytes 196616 | tf_op jit(solution)/shard_map/ppermute | solution.py:251
  11.0 1.0 %copy-start.3 = (bf16[4,8,4096]{2,1,0:T(8,128)(2,1)S(1)}, bf16[4,8,4096]{2,1,0:T(8,128)(2,1)}, u32[]{:S(2)}) copy-start(bf16[4,8,4096]{2,1,0:T(8,128)(2,1)} %v_ref.1) | copy-start | bytes 786436
  11.9 0.7 %copy-start.8 = (f32[3,8,128]{2,1,0:T(8,128)S(1)}, f32[3,8,128]{2,1,0:T(8,128)}, u32[]{:S(2)}) copy-start(f32[3,8,128]{2,1,0:T(8,128)} %get-tuple-element.33.tables_ref) | copy-start | bytes 36868
  17.0 3.8 %copy-start = (bf16[8,128,256]{2,1,0:T(8,128)(2,1)S(1)}, bf16[8,128,256]{2,1,0:T(8,128)(2,1)}, u32[]{:S(2)}) copy-start(bf16[8,128,256]{2,1,0:T(8,128)(2,1)} %refs_4_) | copy-start | bytes 1572868
  17.0 6.5 %copy-start.1 = (bf16[8,4096]{1,0:T(8,128)(2,1)S(1)}, bf16[8,4096]{1,0:T(8,128)(2,1)}, u32[]{:S(2)}) copy-start(bf16[8,4096]{1,0:T(8,128)(2,1)} %get-tuple-element.42.refs_0_) | copy-start | bytes 196612
  17.0 18.5 %all-to-all-start = ((bf16[16,8,2048]{2,1,0:T(8,128)(2,1)}), bf16[16,8,2048]{2,1,0:T(8,128)(2,1)S(1)}, u32[]{:S(2)}, u32[]{:S(2)}) async-start(bf16[16,8,2048]{2,1,0:T(8,128)(2,1)} %key.1.refs_4_), calls=%async_computation | async-start | bytes 1048576 | tf_op jit(solution)/shard_map/all_to_all | solution.py:308
  20.7 8.7 %copy-start.4 = (bf16[8,4096]{1,0:T(8,128)(2,1)S(1)}, bf16[8,4096]{1,0:T(8,128)(2,1)}, u32[]{:S(2)}) copy-start(bf16[8,4096]{1,0:T(8,128)(2,1)} %get-tuple-element.35.refs_1_) | copy-start | bytes 196612
  20.7 8.7 %copy-start.5 = (bf16[8,4096]{1,0:T(8,128)(2,1)S(1)}, bf16[8,4096]{1,0:T(8,128)(2,1)}, u32[]{:S(2)}) copy-start(bf16[8,4096]{1,0:T(8,128)(2,1)} %get-tuple-element.36.refs_2_) | copy-start | bytes 196612
  20.7 8.7 %copy-start.6 = (bf16[8,4096]{1,0:T(8,128)(2,1)S(1)}, bf16[8,4096]{1,0:T(8,128)(2,1)}, u32[]{:S(2)}) copy-start(bf16[8,4096]{1,0:T(8,128)(2,1)} %get-tuple-element.37.refs_3_) | copy-start | bytes 196612
  20.8 2.0 %collective-permute-start.4 = (bf16[8,128,256]{2,1,0:T(8,128)(2,1)S(1)}, bf16[8,128,256]{2,1,0:T(8,128)(2,1)S(1)}, u32[]{:S(2)}, u32[]{:S(2)}) collective-permute-start(bf16[8,128,256]{2,1,0:T(8,128)(2,1)S(1)} %copy-done), channel_id=1, source_target_pairs={{0,1},{1,0},{2,3},{3,2},{4,5},{5,4},{6,7},{7,6},{8,9},{9,8},{10,11... | collective-permute-start | bytes 1572872 | tf_op jit(solution)/shard_map/ppermute | solution.py:251
  21.1 2.4 %collective-permute-start.5 = (bf16[8,128,256]{2,1,0:T(8,128)(2,1)S(1)}, bf16[8,128,256]{2,1,0:T(8,128)(2,1)S(1)}, u32[]{:S(2)}, u32[]{:S(2)}) collective-permute-start(bf16[8,128,256]{2,1,0:T(8,128)(2,1)S(1)} %collective-permute-done.refs_6_), channel_id=1, source_target_pairs={{0,1},{1,0},{2,3},{3,2},{4,5},{5,4},{6,7},{7,6},{8,9},{9,8},{10,11... | collective-permute-start | bytes 1572872 | tf_op jit(solution)/shard_map/ppermute | solution.py:251
  25.0 11.4 %collective-permute-start.6 = (bf16[8,4224]{1,0:T(8,128)(2,1)S(1)}, bf16[8,4224]{1,0:T(8,128)(2,1)S(1)}, u32[]{:S(2)}, u32[]{:S(2)}) collective-permute-start(bf16[8,4224]{1,0:T(8,128)(2,1)S(1)} %get-tuple-element.53), channel_id=1, source_target_pairs={{0,4},{1,5},{2,6},{3,7},{4,0},{5,1},{6,2},{7,3},{8,12},{9,13},{10,... | collective-permute-start | bytes 202760 | tf_op jit(solution)/shard_map/ppermute | solution.py:251
  26.9 13.9 %collective-permute-start.7 = (bf16[8,4224]{1,0:T(8,128)(2,1)S(1)}, bf16[8,4224]{1,0:T(8,128)(2,1)S(1)}, u32[]{:S(2)}, u32[]{:S(2)}) collective-permute-start(bf16[8,4224]{1,0:T(8,128)(2,1)S(1)} %get-tuple-element.54), channel_id=1, source_target_pairs={{0,8},{1,9},{2,10},{3,11},{4,12},{5,13},{6,14},{7,15},{8,0},{9,1},... | collective-permute-start | bytes 202760 | tf_op jit(solution)/shard_map/ppermute | solution.py:251
  29.3 11.5 %collective-permute-start.8 = (bf16[8,4224]{1,0:T(8,128)(2,1)S(1)}, bf16[8,4224]{1,0:T(8,128)(2,1)S(1)}, u32[]{:S(2)}, u32[]{:S(2)}) collective-permute-start(bf16[8,4224]{1,0:T(8,128)(2,1)S(1)} %get-tuple-element.55), channel_id=1, source_target_pairs={{0,12},{1,13},{2,14},{3,15},{4,8},{5,9},{6,10},{7,11},{8,4},{9,5},... | collective-permute-start | bytes 202760 | tf_op jit(solution)/shard_map/ppermute | solution.py:251

commit v15 on v12

--- a/solution.py
+++ b/solution.py
@@ -157,7 +157,7 @@
 
 
 def stale_kernel(groups, videos, *refs):
-    queries, pieces, outs = refs[:videos], refs[videos : videos + groups], refs[videos + groups :]
+    queries, pieces, outs = in_order(refs[:videos]), refs[videos : videos + groups], refs[videos + groups :]
     me = lax.axis_index("patch")
     mine = me % groups
     pairs, total_rows, _ = pieces[0].shape
@@ -207,7 +207,7 @@
 
 
 def join_kernel(groups, videos, *refs):
-    back = refs[:videos]
+    back = in_order(refs[:videos])
     fresh_ref, log_ref, out_ref, done_ref, sems = refs[videos:]
     me = lax.axis_index("patch")
     own, mine = me // groups, me % groups
@@ -251,6 +251,16 @@
     return lax.ppermute(array, "patch", [(i, i ^ offset) for i in range(patches)])
 
 
+def far_first(arrays):
+    half = len(arrays) // 2
+    return [*arrays[half:], *arrays[1:half], arrays[0]]
+
+
+def in_order(arrays):
+    half = len(arrays) // 2
+    return [arrays[-1], *arrays[half:-1], *arrays[:half]]
+
+
 def exchange(arrays, stride, patches):
     return [arrays[0]] + [
         permuted(arrays[s], s * stride, patches) for s in range(1, len(arrays))
@@ -289,7 +299,7 @@
             pltpu.SemaphoreType.DMA((videos,)),
         ],
     )(queries, q_gain.reshape(1, width), coords)
-    query_got = exchange(query, groups, patches)
+    query_got = far_first(exchange(query, groups, patches))
     stale_sent, tables = lax.optimization_barrier((stale_cache, tables))
     pieces = {0: stale_cache}
     bit = groups // 2
@@ -317,7 +327,7 @@
         out_specs=[VMEM] * videos,
     )(*query_got, *[pieces[t] for t in range(groups)])
     result, fresh_late = lax.optimization_barrier((result, fresh))
-    back = exchange(result, groups, patches)
+    back = far_first(exchange(result, groups, patches))
     fresh_sum, fresh_log = kernel(
         functools.partial(fresh_kernel, groups, videos),
         "fresh",

time: 42.3 us -> 41.4 us (0.979)
  waiting for transfers between devices: 13.4 us -> 12.5 us
    ppermute x9, waiting for transfers between devices: 9.48 us -> 8.36 us  [permuted(): lax.ppermute(array, 'patch', [(i, i ^ offset) for i in range(patches)])]
where the time goes in v15:
time: 41.4 us; the launch traced here: 41.1 us
  starting transfers between devices  16.1 us (39%)
  waiting for transfers between devices  12.5 us (30%)
  Pallas kernels  10 us (24%)
  local copies, waits for them, and re-layouts  1.69 us (4%)
  between operations  0.74 us (2%)
    ppermute x9, starting transfers between devices, permuted(): lax.ppermute(array, 'patch', [(i, i ^ offset) for i in range(patches)])  12 us
    ppermute x9, waiting for transfers between devices, permuted(): lax.ppermute(array, 'patch', [(i, i ^ offset) for i in range(patches)])  8.36 us
    all_to_all x1, waiting for transfers between devices, local(): lax.all_to_all(fresh_sent, 'patch', split_axis=0, concat_axis=0, tiled=True)  4.14 us
    all_to_all x1, starting transfers between devices, local(): lax.all_to_all(fresh_sent, 'patch', split_axis=0, concat_axis=0, tiled=True)  4.1 us
    pallas_call x1, Pallas kernels, local(): kernel(functools.partial(query_kernel, groups), 'query', 56, out_shape=[r...  2.9 us
    pallas_call x1, Pallas kernels, local(): kernel(functools.partial(fresh_kernel, groups, videos), 'fresh', 16, out_...  2.15 us
    unnamed x18, local copies, waits for them, and re-layouts  1.69 us
    pallas_call x1, Pallas kernels, local(): kernel(functools.partial(stale_kernel, groups, videos), 'stale', 32, out_...  1.52 us
  transfers between devices with their start and end apart: 10, of which 6 were waited for; matrix products, arithmetic and copies ran while one was open for 0% of the time, Pallas kernels for 14%

profile of v15, /device:TPU:0, one launch (start us, length us, event | category | flops | bytes accessed | tf_op | source)
XLA Modules:
  0.0 41.1 jit_solution(10925926988416079930)
XLA Ops:
  0.6 0.0 copy-start.2
  0.6 0.0 copy-start.7
  0.7 2.9 %query.1 = (bf16[8,4096]{1,0:T(8,128)(2,1)}, bf16[8,4096]{1,0:T(8,128)(2,1)}, bf16[8,4096]{1,0:T(8,128)(2,1)}, bf16[8,4096]{1,0:T(8,128)(2,1)}, f32[3,8,128]{2,1,0:T(8,128)}) custom-call(bf16[4,8,4096]{2,1,0:T(8,128)(2,1)} %q_hbm.1, f32[1,4096]{1,0:T(1,128)} %bitcast.5, s32[3,8]{1,0:T(4,128)} %coords_hbm.1), custom_call_target="tpu_custom_call" | custom-call | tf_op jit(solution)/shard_map/query/pallas_call | solution.py:286
  3.6 3.0 %collective-permute-start = (bf16[8,128,256]{2,1,0:T(8,128)(2,1)}, bf16[8,128,256]{2,1,0:T(8,128)(2,1)S(1)}, u32[]{:S(2)}, u32[]{:S(2)}) collective-permute-start(bf16[8,128,256]{2,1,0:T(8,128)(2,1)} %refs_4_), channel_id=1, source_target_pairs={{0,2},{1,3},{2,0},{3,1},{4,6},{5,7},{6,4},{7,5},{8,10},{9,11},{10,... | collective-permute-start | bytes 1572872 | tf_op jit(solution)/shard_map/ppermute | solution.py:251
  6.6 2.6 %collective-permute-start.1 = (bf16[8,4096]{1,0:T(8,128)(2,1)}, bf16[8,4096]{1,0:T(8,128)(2,1)S(1)}, u32[]{:S(2)}, u32[]{:S(2)}) collective-permute-start(bf16[8,4096]{1,0:T(8,128)(2,1)} %get-tuple-element.34.refs_2_), channel_id=1, source_target_pairs={{0,8},{1,9},{2,10},{3,11},{4,12},{5,13},{6,14},{7,15},{8,0},{9,1},... | collective-permute-start | bytes 196616 | tf_op jit(solution)/shard_map/ppermute | solution.py:251
  9.2 1.3 %collective-permute-start.2 = (bf16[8,4096]{1,0:T(8,128)(2,1)}, bf16[8,4096]{1,0:T(8,128)(2,1)S(1)}, u32[]{:S(2)}, u32[]{:S(2)}) collective-permute-start(bf16[8,4096]{1,0:T(8,128)(2,1)} %get-tuple-element.35.refs_3_), channel_id=1, source_target_pairs={{0,12},{1,13},{2,14},{3,15},{4,8},{5,9},{6,10},{7,11},{8,4},{9,5},... | collective-permute-start | bytes 196616 | tf_op jit(solution)/shard_map/ppermute | solution.py:251
  10.5 0.2 collective-permute-start.3
  10.7 0.0 copy-done.2
  10.7 0.0 copy-done.7
  10.7 0.0 copy-start.3
  10.7 0.9 %copy-done.3 = bf16[4,8,4096]{2,1,0:T(8,128)(2,1)S(1)} copy-done((bf16[4,8,4096]{2,1,0:T(8,128)(2,1)S(1)}, bf16[4,8,4096]{2,1,0:T(8,128)(2,1)}, u32[]{:S(2)}) %copy-start.3) | copy-done | bytes 262168
  11.7 0.0 copy-start.8
  11.7 0.7 %copy-done.8 = f32[3,8,128]{2,1,0:T(8,128)S(1)} copy-done((f32[3,8,128]{2,1,0:T(8,128)S(1)}, f32[3,8,128]{2,1,0:T(8,128)}, u32[]{:S(2)}) %copy-start.8) | copy-done | bytes 12312
  12.4 1.4 %key.1.refs_4_ = bf16[16,8,2048]{2,1,0:T(8,128)(2,1)} custom-call(bf16[4,8,4096]{2,1,0:T(8,128)(2,1)S(1)} %copy-done.2, bf16[4,8,4096]{2,1,0:T(8,128)(2,1)S(1)} %copy-done.3, f32[1,4096]{1,0:T(1,128)S(1)} %bitcast.3, f32[3,8,128]{2,1,0:T(8,128)S(1)} %copy-done.8), custom_call_target="tpu_custom_call" | custom-call | tf_op jit(solution)/shard_map/key/pallas_call | solution.py:307
  13.8 0.0 collective-permute-done.1.refs_0_
  13.8 1.8 %collective-permute-done.2.refs_1_ = bf16[8,4096]{1,0:T(8,128)(2,1)S(1)} collective-permute-done((bf16[8,4096]{1,0:T(8,128)(2,1)}, bf16[8,4096]{1,0:T(8,128)(2,1)S(1)}, u32[]{:S(2)}, u32[]{:S(2)}) %collective-permute-start.2) | collective-permute-done | bytes 65568 | tf_op jit(solution)/shard_map/ppermute | solution.py:251
  15.6 0.1 collective-permute-done.3.refs_2_
  15.7 0.0 copy-start
  15.7 0.0 copy-start.1
  15.7 4.1 %all-to-all-start = ((bf16[16,8,2048]{2,1,0:T(8,128)(2,1)}), bf16[16,8,2048]{2,1,0:T(8,128)(2,1)S(1)}, u32[]{:S(2)}, u32[]{:S(2)}) async-start(bf16[16,8,2048]{2,1,0:T(8,128)(2,1)} %key.1.refs_4_), calls=%async_computation | async-start | bytes 1048576 | tf_op jit(solution)/shard_map/all_to_all | solution.py:316
  19.8 0.0 copy-start.4
  19.8 0.0 copy-start.5
  19.8 0.0 copy-start.6
  19.8 0.0 collective-permute-done.refs_6_
  19.8 0.0 copy-done
  19.8 0.5 %collective-permute-start.4 = (bf16[8,128,256]{2,1,0:T(8,128)(2,1)S(1)}, bf16[8,128,256]{2,1,0:T(8,128)(2,1)S(1)}, u32[]{:S(2)}, u32[]{:S(2)}) collective-permute-start(bf16[8,128,256]{2,1,0:T(8,128)(2,1)S(1)} %copy-done), channel_id=1, source_target_pairs={{0,1},{1,0},{2,3},{3,2},{4,5},{5,4},{6,7},{7,6},{8,9},{9,8},{10,11... | collective-permute-start | bytes 1572872 | tf_op jit(solution)/shard_map/ppermute | solution.py:251
  20.3 0.1 collective-permute-start.5
  20.4 1.4 %collective-permute-done.4.refs_5_ = bf16[8,128,256]{2,1,0:T(8,128)(2,1)S(1)} collective-permute-done((bf16[8,128,256]{2,1,0:T(8,128)(2,1)S(1)}, bf16[8,128,256]{2,1,0:T(8,128)(2,1)S(1)}, u32[]{:S(2)}, u32[]{:S(2)}) %collective-permute-start.4) | collective-permute-done | bytes 524320 | tf_op jit(solution)/shard_map/ppermute | solution.py:251
  21.9 0.7 %collective-permute-done.5.refs_7_ = bf16[8,128,256]{2,1,0:T(8,128)(2,1)S(1)} collective-permute-done((bf16[8,128,256]{2,1,0:T(8,128)(2,1)S(1)}, bf16[8,128,256]{2,1,0:T(8,128)(2,1)S(1)}, u32[]{:S(2)}, u32[]{:S(2)}) %collective-permute-start.5) | collective-permute-done | bytes 524320 | tf_op jit(solution)/shard_map/ppermute | solution.py:251
  22.6 0.0 copy-done.1
  22.6 1.5 %stale.1 = (bf16[8,4224]{1,0:T(8,128)(2,1)S(1)}, bf16[8,4224]{1,0:T(8,128)(2,1)S(1)}, bf16[8,4224]{1,0:T(8,128)(2,1)S(1)}, bf16[8,4224]{1,0:T(8,128)(2,1)S(1)}) custom-call(bf16[8,4096]{1,0:T(8,128)(2,1)S(1)} %collective-permute-done.1.refs_0_, bf16[8,4096]{1,0:T(8,128)(2,1)S(1)} %collective-permute-done.2.refs_1_, ...), custom_call_target="tpu_custom_call" | custom-call | tf_op jit(solution)/shard_map/stale/pallas_call | solution.py:321
  24.1 2.8 %collective-permute-start.6 = (bf16[8,4224]{1,0:T(8,128)(2,1)S(1)}, bf16[8,4224]{1,0:T(8,128)(2,1)S(1)}, u32[]{:S(2)}, u32[]{:S(2)}) collective-permute-start(bf16[8,4224]{1,0:T(8,128)(2,1)S(1)} %get-tuple-element.52), channel_id=1, source_target_pairs={{0,8},{1,9},{2,10},{3,11},{4,12},{5,13},{6,14},{7,15},{8,0},{9,1},... | collective-permute-start | bytes 202760 | tf_op jit(solution)/shard_map/ppermute | solution.py:251
  27.0 1.5 %collective-permute-start.7 = (bf16[8,4224]{1,0:T(8,128)(2,1)S(1)}, bf16[8,4224]{1,0:T(8,128)(2,1)S(1)}, u32[]{:S(2)}, u32[]{:S(2)}) collective-permute-start(bf16[8,4224]{1,0:T(8,128)(2,1)S(1)} %get-tuple-element.53), channel_id=1, source_target_pairs={{0,12},{1,13},{2,14},{3,15},{4,8},{5,9},{6,10},{7,11},{8,4},{9,5},... | collective-permute-start | bytes 202760 | tf_op jit(solution)/shard_map/ppermute | solution.py:251
  28.4 0.0 collective-permute-start.8
  28.4 0.0 copy-done.4
  28.4 0.0 copy-done.5
  28.4 0.0 copy-done.6
  28.4 2.2 %fresh.1 = (f32[4,8,4096]{2,1,0:T(8,128)S(1)}, f32[4,8,128]{2,1,0:T(8,128)S(1)}) custom-call(bf16[8,4096]{1,0:T(8,128)(2,1)S(1)} %copy-done.1, bf16[8,4096]{1,0:T(8,128)(2,1)S(1)} %copy-done.4, bf16[8,4096]{1,0:T(8,128)(2,1)S(1)} %copy-done.5, bf16[8,4096]{1,0:T(8,128)(2,1)S(1)} %copy-done.6, bf16[16,8,2048]{2,1,0:T(8,128)(2,1)} %key.1.refs_4_), custom_call_target="tpu_custom_call" | custom-call | tf_op jit(solution)/shard_map/fresh/pallas_call | solution.py:331
  30.6 4.1 %all-to-all-done.got_ref = bf16[16,8,2048]{2,1,0:T(8,128)(2,1)S(1)} async-done(((bf16[16,8,2048]{2,1,0:T(8,128)(2,1)}), bf16[16,8,2048]{2,1,0:T(8,128)(2,1)S(1)}, u32[]{:S(2)}, u32[]{:S(2)}) %all-to-all-start) | async-done | bytes 524320 | tf_op jit(solution)/shard_map/all_to_all | solution.py:316
  34.7 0.8 %cache.1 = bf16[8,16,8,256]{3,2,1,0:T(8,128)(2,1)} custom-call(bf16[16,8,2048]{2,1,0:T(8,128)(2,1)S(1)} %all-to-all-done.got_ref), custom_call_target="tpu_custom_call" | custom-call | tf_op jit(solution)/shard_map/cache/pallas_call | solution.py:342
  35.6 4.3 %collective-permute-done.6.refs_0_ = bf16[8,4224]{1,0:T(8,128)(2,1)S(1)} collective-permute-done((bf16[8,4224]{1,0:T(8,128)(2,1)S(1)}, bf16[8,4224]{1,0:T(8,128)(2,1)S(1)}, u32[]{:S(2)}, u32[]{:S(2)}) %collective-permute-start.6) | collective-permute-done | bytes 67616 | tf_op jit(solution)/shard_map/ppermute | solution.py:251
  39.9 0.0 collective-permute-done.7.refs_1_
  39.9 0.0 collective-permute-done.8.refs_2_
  39.9 1.2 %join.1 = bf16[4,8,4096]{2,1,0:T(8,128)(2,1)} custom-call(bf16[8,4224]{1,0:T(8,128)(2,1)S(1)} %collective-permute-done.6.refs_0_, bf16[8,4224]{1,0:T(8,128)(2,1)S(1)} %collective-permute-done.7.refs_1_, bf16[8,4224]{1,0:T(8,128)(2,1)S(1)} %collective-permute-done.8.refs_2_, bf16[8,4224]{1,0:T(8,128)(2,1)S(1)} %get-tuple-element.55.refs_3_, ...), custom_call_target="tpu_custom_call" | custom-call | tf_op jit(solution)/shard_map/join/pallas_call | solution.py:351
Async XLA Ops:
  0.6 10.1 %copy-start.2 = (bf16[4,8,4096]{2,1,0:T(8,128)(2,1)S(1)}, bf16[4,8,4096]{2,1,0:T(8,128)(2,1)}, u32[]{:S(2)}) copy-start(bf16[4,8,4096]{2,1,0:T(8,128)(2,1)} %k_ref.1) | copy-start | bytes 786436
  0.6 10.1 %copy-start.7 = (f32[4096]{0:T(1024)S(1)}, f32[4096]{0:T(1024)}, u32[]{:S(2)}) copy-start(f32[4096]{0:T(1024)} %param.11) | copy-start | bytes 49156
  3.6 16.3 %collective-permute-start = (bf16[8,128,256]{2,1,0:T(8,128)(2,1)}, bf16[8,128,256]{2,1,0:T(8,128)(2,1)S(1)}, u32[]{:S(2)}, u32[]{:S(2)}) collective-permute-start(bf16[8,128,256]{2,1,0:T(8,128)(2,1)} %refs_4_), channel_id=1, source_target_pairs={{0,2},{1,3},{2,0},{3,1},{4,6},{5,7},{6,4},{7,5},{8,10},{9,11},{10,... | collective-permute-start | bytes 1572872 | tf_op jit(solution)/shard_map/ppermute | solution.py:251
  6.6 7.3 %collective-permute-start.1 = (bf16[8,4096]{1,0:T(8,128)(2,1)}, bf16[8,4096]{1,0:T(8,128)(2,1)S(1)}, u32[]{:S(2)}, u32[]{:S(2)}) collective-permute-start(bf16[8,4096]{1,0:T(8,128)(2,1)} %get-tuple-element.34.refs_2_), channel_id=1, source_target_pairs={{0,8},{1,9},{2,10},{3,11},{4,12},{5,13},{6,14},{7,15},{8,0},{9,1},... | collective-permute-start | bytes 196616 | tf_op jit(solution)/shard_map/ppermute | solution.py:251
  9.2 6.4 %collective-permute-start.2 = (bf16[8,4096]{1,0:T(8,128)(2,1)}, bf16[8,4096]{1,0:T(8,128)(2,1)S(1)}, u32[]{:S(2)}, u32[]{:S(2)}) collective-permute-start(bf16[8,4096]{1,0:T(8,128)(2,1)} %get-tuple-element.35.refs_3_), channel_id=1, source_target_pairs={{0,12},{1,13},{2,14},{3,15},{4,8},{5,9},{6,10},{7,11},{8,4},{9,5},... | collective-permute-start | bytes 196616 | tf_op jit(solution)/shard_map/ppermute | solution.py:251
  10.5 5.2 %collective-permute-start.3 = (bf16[8,4096]{1,0:T(8,128)(2,1)}, bf16[8,4096]{1,0:T(8,128)(2,1)S(1)}, u32[]{:S(2)}, u32[]{:S(2)}) collective-permute-start(bf16[8,4096]{1,0:T(8,128)(2,1)} %get-tuple-element.36.refs_1_), channel_id=1, source_target_pairs={{0,4},{1,5},{2,6},{3,7},{4,0},{5,1},{6,2},{7,3},{8,12},{9,13},{10,... | collective-permute-start | bytes 196616 | tf_op jit(solution)/shard_map/ppermute | solution.py:251
  10.7 1.0 %copy-start.3 = (bf16[4,8,4096]{2,1,0:T(8,128)(2,1)S(1)}, bf16[4,8,4096]{2,1,0:T(8,128)(2,1)}, u32[]{:S(2)}) copy-start(bf16[4,8,4096]{2,1,0:T(8,128)(2,1)} %v_ref.1) | copy-start | bytes 786436
  11.7 0.7 %copy-start.8 = (f32[3,8,128]{2,1,0:T(8,128)S(1)}, f32[3,8,128]{2,1,0:T(8,128)}, u32[]{:S(2)}) copy-start(f32[3,8,128]{2,1,0:T(8,128)} %get-tuple-element.33.tables_ref) | copy-start | bytes 36868
  15.7 4.2 %copy-start = (bf16[8,128,256]{2,1,0:T(8,128)(2,1)S(1)}, bf16[8,128,256]{2,1,0:T(8,128)(2,1)}, u32[]{:S(2)}) copy-start(bf16[8,128,256]{2,1,0:T(8,128)(2,1)} %refs_4_) | copy-start | bytes 1572868
  15.7 6.9 %copy-start.1 = (bf16[8,4096]{1,0:T(8,128)(2,1)S(1)}, bf16[8,4096]{1,0:T(8,128)(2,1)}, u32[]{:S(2)}) copy-start(bf16[8,4096]{1,0:T(8,128)(2,1)} %get-tuple-element.45.refs_3_.refs_0_) | copy-start | bytes 196612
  15.7 19.0 %all-to-all-start = ((bf16[16,8,2048]{2,1,0:T(8,128)(2,1)}), bf16[16,8,2048]{2,1,0:T(8,128)(2,1)S(1)}, u32[]{:S(2)}, u32[]{:S(2)}) async-start(bf16[16,8,2048]{2,1,0:T(8,128)(2,1)} %key.1.refs_4_), calls=%async_computation | async-start | bytes 1048576 | tf_op jit(solution)/shard_map/all_to_all | solution.py:316
  19.8 8.6 %copy-start.4 = (bf16[8,4096]{1,0:T(8,128)(2,1)S(1)}, bf16[8,4096]{1,0:T(8,128)(2,1)}, u32[]{:S(2)}) copy-start(bf16[8,4096]{1,0:T(8,128)(2,1)} %get-tuple-element.36.refs_1_) | copy-start | bytes 196612
  19.8 8.6 %copy-start.5 = (bf16[8,4096]{1,0:T(8,128)(2,1)S(1)}, bf16[8,4096]{1,0:T(8,128)(2,1)}, u32[]{:S(2)}) copy-start(bf16[8,4096]{1,0:T(8,128)(2,1)} %get-tuple-element.34.refs_2_) | copy-start | bytes 196612
  19.8 8.6 %copy-start.6 = (bf16[8,4096]{1,0:T(8,128)(2,1)S(1)}, bf16[8,4096]{1,0:T(8,128)(2,1)}, u32[]{:S(2)}) copy-start(bf16[8,4096]{1,0:T(8,128)(2,1)} %get-tuple-element.35.refs_3_) | copy-start | bytes 196612
  19.8 2.0 %collective-permute-start.4 = (bf16[8,128,256]{2,1,0:T(8,128)(2,1)S(1)}, bf16[8,128,256]{2,1,0:T(8,128)(2,1)S(1)}, u32[]{:S(2)}, u32[]{:S(2)}) collective-permute-start(bf16[8,128,256]{2,1,0:T(8,128)(2,1)S(1)} %copy-done), channel_id=1, source_target_pairs={{0,1},{1,0},{2,3},{3,2},{4,5},{5,4},{6,7},{7,6},{8,9},{9,8},{10,11... | collective-permute-start | bytes 1572872 | tf_op jit(solution)/shard_map/ppermute | solution.py:251
  20.3 2.3 %collective-permute-start.5 = (bf16[8,128,256]{2,1,0:T(8,128)(2,1)S(1)}, bf16[8,128,256]{2,1,0:T(8,128)(2,1)S(1)}, u32[]{:S(2)}, u32[]{:S(2)}) collective-permute-start(bf16[8,128,256]{2,1,0:T(8,128)(2,1)S(1)} %collective-permute-done.refs_6_), channel_id=1, source_target_pairs={{0,1},{1,0},{2,3},{3,2},{4,5},{5,4},{6,7},{7,6},{8,9},{9,8},{10,11... | collective-permute-start | bytes 1572872 | tf_op jit(solution)/shard_map/ppermute | solution.py:251
  24.1 15.8 %collective-permute-start.6 = (bf16[8,4224]{1,0:T(8,128)(2,1)S(1)}, bf16[8,4224]{1,0:T(8,128)(2,1)S(1)}, u32[]{:S(2)}, u32[]{:S(2)}) collective-permute-start(bf16[8,4224]{1,0:T(8,128)(2,1)S(1)} %get-tuple-element.52), channel_id=1, source_target_pairs={{0,8},{1,9},{2,10},{3,11},{4,12},{5,13},{6,14},{7,15},{8,0},{9,1},... | collective-permute-start | bytes 202760 | tf_op jit(solution)/shard_map/ppermute | solution.py:251
  27.0 12.9 %collective-permute-start.7 = (bf16[8,4224]{1,0:T(8,128)(2,1)S(1)}, bf16[8,4224]{1,0:T(8,128)(2,1)S(1)}, u32[]{:S(2)}, u32[]{:S(2)}) collective-permute-start(bf16[8,4224]{1,0:T(8,128)(2,1)S(1)} %get-tuple-element.53), channel_id=1, source_target_pairs={{0,12},{1,13},{2,14},{3,15},{4,8},{5,9},{6,10},{7,11},{8,4},{9,5},... | collective-permute-start | bytes 202760 | tf_op jit(solution)/shard_map/ppermute | solution.py:251
  28.4 11.5 %collective-permute-start.8 = (bf16[8,4224]{1,0:T(8,128)(2,1)S(1)}, bf16[8,4224]{1,0:T(8,128)(2,1)S(1)}, u32[]{:S(2)}, u32[]{:S(2)}) collective-permute-start(bf16[8,4224]{1,0:T(8,128)(2,1)S(1)} %get-tuple-element.54), channel_id=1, source_target_pairs={{0,4},{1,5},{2,6},{3,7},{4,0},{5,1},{6,2},{7,3},{8,12},{9,13},{10,... | collective-permute-start | bytes 202760 | tf_op jit(solution)/shard_map/ppermute | solution.py:251

commit v16 on v15

--- a/solution.py
+++ b/solution.py
@@ -18,19 +18,24 @@
 TRANSPOSED = (((1,), (1,)), ((), ()))
 
 
-def rope_tables(coords_ref, tok_rows):
+def rope_tables(coords, tok_rows):
     half = DH // 2
     side = DH // 6
     first = half - 2 * side
-    shape = (tok_rows, DH)
+    shape = (len(coords) * tok_rows, DH)
     row = lax.broadcasted_iota(jnp.int32, shape, 0)
     lane = lax.broadcasted_iota(jnp.int32, shape, 1)
     pair = lane // 2
     axis = (pair >= first).astype(jnp.int32) + (pair >= first + side).astype(jnp.int32)
-    place = jnp.zeros(shape, jnp.int32)
-    for which in range(3):
-        for token in range(tok_rows):
-            place = jnp.where((axis == which) & (row == token), coords_ref[which, token], place)
+    places = []
+    for ref in coords:
+        place = jnp.zeros((tok_rows, DH), jnp.int32)
+        for which in range(3):
+            for token in range(tok_rows):
+                here = (axis[:tok_rows] == which) & (row[:tok_rows] == token)
+                place = jnp.where(here, ref[which, token], place)
+        places.append(place)
+    place = jnp.concatenate(places, axis=0)
     step = jnp.where(axis == 0, pair, jnp.where(axis == 1, pair - first, pair - first - side))
     count = jnp.where(axis == 0, float(first), float(side))
     freq = jnp.exp(step.astype(F32) / count * (-math.log(10000.0)))
@@ -52,48 +57,33 @@
         yield head, y.astype(BF16)
 
 
-def query_kernel(groups, q_hbm, gain_hbm, coords_hbm, *refs):
-    videos, tok_rows, width = q_hbm.shape
-    outs, tables_ref, refs = refs[:videos], refs[videos], refs[videos + 1 :]
-    q_ref, gain_ref, coords_ref, done_ref, sems, out_sems = refs
-    own = lax.axis_index("patch") // groups
-    copies = [
-        pltpu.make_async_copy(source, place, sems.at[i])
-        for i, (source, place) in enumerate(
-            ((coords_hbm, coords_ref), (q_hbm, q_ref), (gain_hbm, gain_ref))
-        )
-    ]
-    for copy in copies:
-        copy.start()
-    copies[0].wait()
-    tables = rope_tables(coords_ref, tok_rows)
-    for i in range(3):
-        tables_ref[i] = tables[i]
-    copies[1].wait()
-    copies[2].wait()
-    sends = []
-    for s in range(videos):
-        for head, y in normed_heads(q_ref[own ^ s].astype(F32), gain_ref, tables):
-            done_ref[s, :, head * DH : (head + 1) * DH] = y
-        sends.append(pltpu.make_async_copy(done_ref.at[s], outs[s], out_sems.at[s]))
-        sends[-1].start()
-    for send in sends:
-        send.wait()
-
-
-def key_kernel(k_ref, v_ref, gain_ref, tables_ref, out_ref):
+def own_kernel(q_ref, k_ref, v_ref, q_gain_ref, k_gain_ref, coords_ref, query_ref, fresh_ref):
     videos, tok_rows, width = k_ref.shape
-    tables = [tables_ref[i] for i in range(3)]
-    span = out_ref.shape[2]
-    groups = out_ref.shape[0] // videos
+    tables = rope_tables([coords_ref], tok_rows)
+    span = fresh_ref.shape[2]
+    groups = fresh_ref.shape[0] // videos
     pairs = span // (2 * DH)
     for video in range(videos):
-        for head, y in normed_heads(k_ref[video].astype(F32), gain_ref, tables):
+        for head, y in normed_heads(k_ref[video].astype(F32), k_gain_ref, tables):
             target, start = video * groups + head // pairs, head % pairs * 2 * DH
-            out_ref[target, :, start : start + DH] = y
-            out_ref[target, :, start + DH : start + 2 * DH] = v_ref[
+            fresh_ref[target, :, start : start + DH] = y
+            fresh_ref[target, :, start + DH : start + 2 * DH] = v_ref[
                 video, :, head * DH : (head + 1) * DH
             ]
+    for video in range(videos):
+        for head, y in normed_heads(q_ref[video].astype(F32), q_gain_ref, tables):
+            query_ref[video, :, head * DH : (head + 1) * DH] = y
+
+
+def turn_kernel(groups, q_ref, gain_ref, *refs):
+    coords, out_ref = refs[:-1], refs[-1]
+    videos, tok_rows, _ = q_ref.shape
+    own = lax.axis_index("patch") // groups
+    tables = rope_tables(coords, tok_rows)
+    for s in range(videos):
+        mine = [table[s * tok_rows : (s + 1) * tok_rows] for table in tables]
+        for head, y in normed_heads(q_ref[own ^ s].astype(F32), gain_ref, mine):
+            out_ref[s, :, head * DH : (head + 1) * DH] = y
 
 
 def softmax_parts(scores):
@@ -108,11 +98,10 @@
     return jnp.concatenate(rows, axis=0).astype(BF16)
 
 
-def fresh_kernel(groups, videos, *refs):
-    queries = refs[:videos]
-    fresh_ref, out_ref, log_ref = refs[videos:]
+def fresh_kernel(groups, videos, query_ref, fresh_ref, out_ref, log_ref):
     me = lax.axis_index("patch")
-    mine = me % groups
+    own, mine = me // groups, me % groups
+    queries = [query_ref.at[own ^ s] for s in range(videos)]
     _, tok_rows, width = out_ref.shape
     span = width // groups
     pairs = span // DH
@@ -156,8 +145,9 @@
         log_ref[s] = logs[s * tok_rows : (s + 1) * tok_rows]
 
 
-def stale_kernel(groups, videos, *refs):
-    queries, pieces, outs = in_order(refs[:videos]), refs[videos : videos + groups], refs[videos + groups :]
+def stale_kernel(groups, videos, query_ref, *refs):
+    queries = [query_ref.at[s] for s in range(videos)]
+    pieces, outs = refs[:groups], refs[groups:]
     me = lax.axis_index("patch")
     mine = me % groups
     pairs, total_rows, _ = pieces[0].shape
@@ -272,7 +262,6 @@
     pairs_here, total_rows, _ = stale_cache.shape
     patches = total_rows // tok_rows
     groups = patches // videos
-    rows = jax.ShapeDtypeStruct((tok_rows, width), BF16)
 
     def kernel(body, name, limit, cost=0, **kwargs):
         return pl.pallas_call(
@@ -283,37 +272,36 @@
             **kwargs,
         )
 
-    *query, tables = kernel(
-        functools.partial(query_kernel, groups),
-        "query",
-        56,
-        out_shape=[rows] * videos + [jax.ShapeDtypeStruct((3, tok_rows, DH), F32)],
-        in_specs=[HBM] * 3,
-        out_specs=[HBM] * videos + [VMEM],
-        scratch_shapes=[
-            pltpu.VMEM(queries.shape, BF16),
-            pltpu.VMEM((1, width), F32),
-            pltpu.SMEM(coords.shape, jnp.int32),
-            pltpu.VMEM(queries.shape, BF16),
-            pltpu.SemaphoreType.DMA((3,)),
-            pltpu.SemaphoreType.DMA((videos,)),
-        ],
-    )(queries, q_gain.reshape(1, width), coords)
-    query_got = far_first(exchange(query, groups, patches))
-    stale_sent, tables = lax.optimization_barrier((stale_cache, tables))
+    columns = [[v * groups + g for v in range(videos)] for g in range(groups)]
+    query_raw = lax.all_to_all(
+        queries, "patch", split_axis=0, concat_axis=0, axis_index_groups=columns, tiled=True
+    )
+    coords_got = exchange([coords] * videos, groups, patches)
     pieces = {0: stale_cache}
     bit = groups // 2
-    pieces[bit] = permuted(stale_sent, bit, patches)
-    fresh = kernel(
-        key_kernel,
-        "key",
-        16,
-        out_shape=jax.ShapeDtypeStruct((patches, tok_rows, 2 * pairs_here * DH), BF16),
-        in_specs=[VMEM] * 4,
+    pieces[bit] = permuted(stale_cache, bit, patches)
+    gains = q_gain.reshape(1, width), k_gain.reshape(1, width)
+    query, fresh = kernel(
+        own_kernel,
+        "own",
+        16,
+        out_shape=(
+            jax.ShapeDtypeStruct(queries.shape, BF16),
+            jax.ShapeDtypeStruct((patches, tok_rows, 2 * pairs_here * DH), BF16),
+        ),
+        in_specs=[VMEM] * 5 + [SMEM],
+        out_specs=(VMEM, VMEM),
+    )(queries, keys, values, *gains, coords)
+    fresh_sent, query_raw, coords_got = lax.optimization_barrier((fresh, query_raw, coords_got))
+    cached = lax.all_to_all(fresh_sent, "patch", split_axis=0, concat_axis=0, tiled=True)
+    query_got = kernel(
+        functools.partial(turn_kernel, groups),
+        "turn",
+        16,
+        out_shape=jax.ShapeDtypeStruct(queries.shape, BF16),
+        in_specs=[VMEM] * 2 + [SMEM] * videos,
         out_specs=VMEM,
-    )(keys, values, k_gain.reshape(1, width), tables)
-    fresh_sent, query_got = lax.optimization_barrier((fresh, query_got))
-    cached = lax.all_to_all(fresh_sent, "patch", split_axis=0, concat_axis=0, tiled=True)
+    )(query_raw, gains[0], *coords_got)
     pieces, query_got = lax.optimization_barrier((pieces, query_got))
     while bit > 1:
         bit //= 2
@@ -323,9 +311,9 @@
         "stale",
         32,
         out_shape=[jax.ShapeDtypeStruct((tok_rows, width + DH), BF16)] * videos,
-        in_specs=[VMEM] * (videos + groups),
+        in_specs=[VMEM] * (1 + groups),
         out_specs=[VMEM] * videos,
-    )(*query_got, *[pieces[t] for t in range(groups)])
+    )(query_got, *[pieces[t] for t in range(groups)])
     result, fresh_late = lax.optimization_barrier((result, fresh))
     back = far_first(exchange(result, groups, patches))
     fresh_sum, fresh_log = kernel(
@@ -336,9 +324,9 @@
             jax.ShapeDtypeStruct((videos, tok_rows, width), F32),
             jax.ShapeDtypeStruct((videos, tok_rows, DH), F32),
         ),
-        in_specs=[VMEM] * (videos + 1),
+        in_specs=[VMEM] * 2,
         out_specs=(VMEM, VMEM),
-    )(*query, fresh_late)
+    )(query, fresh_late)
     next_cache = kernel(
         cache_kernel,
         "cache",

time: 41.4 us -> 46 us (1.11)
  starting transfers between devices: 16.1 us -> 22.1 us
  waiting for transfers between devices: 12.5 us -> 10.5 us
  local copies, waits for them, and re-layouts: 1.69 us -> 2.4 us
    all_to_all x0 -> x1, starting transfers between devices: none -> 6.46 us  [local(): lax.all_to_all(queries, 'patch', split_axis=0, concat_axis=0, axis_index_...]
    all_to_all x1, waiting for transfers between devices: 4.14 us -> 0.01 us  [local(): lax.all_to_all(fresh_sent, 'patch', split_axis=0, concat_axis=0, tiled=True)]
    ppermute x9, waiting for transfers between devices: 8.36 us -> 10.5 us  [permuted(): lax.ppermute(array, 'patch', [(i, i ^ offset) for i in range(patches)])]
    ppermute x9, starting transfers between devices: 12 us -> 10.7 us  [permuted(): lax.ppermute(array, 'patch', [(i, i ^ offset) for i in range(patches)])]
    all_to_all x1, starting transfers between devices: 4.1 us -> 4.9 us  [local(): lax.all_to_all(fresh_sent, 'patch', split_axis=0, concat_axis=0, tiled=True)]
    unnamed x18 -> x16, local copies, waits for them, and re-layouts: 1.69 us -> 2.4 us
  transfers between devices with their start and end apart: 10 -> 11, of which waited for: 6 -> 4; matrix products, arithmetic and copies ran while one was open for 0% -> 0% of each run, Pallas kernels for 14% -> 19%
where the time goes in v16:
time: 46 us; the launch traced here: 45.4 us
  starting transfers between devices  22.1 us (48%)
  waiting for transfers between devices  10.5 us (23%)
  Pallas kernels  9.65 us (21%)
  local copies, waits for them, and re-layouts  2.4 us (5%)
  between operations  0.75 us (2%)
    ppermute x9, starting transfers between devices, permuted(): lax.ppermute(array, 'patch', [(i, i ^ offset) for i in range(patches)])  10.7 us
    ppermute x9, waiting for transfers between devices, permuted(): lax.ppermute(array, 'patch', [(i, i ^ offset) for i in range(patches)])  10.5 us
    all_to_all x1, starting transfers between devices, local(): lax.all_to_all(queries, 'patch', split_axis=0, concat_axis=0, axis_index_...  6.46 us
    all_to_all x1, starting transfers between devices, local(): lax.all_to_all(fresh_sent, 'patch', split_axis=0, concat_axis=0, tiled=True)  4.9 us
    pallas_call x1, Pallas kernels, local(): kernel(own_kernel, 'own', 16, out_shape=(jax.ShapeDtypeStruct(queries.sha...  2.64 us
    unnamed x16, local copies, waits for them, and re-layouts  2.4 us
    pallas_call x1, Pallas kernels, local(): kernel(functools.partial(fresh_kernel, groups, videos), 'fresh', 16, out_...  2.15 us
    pallas_call x1, Pallas kernels, local(): kernel(functools.partial(stale_kernel, groups, videos), 'stale', 32, out_...  1.52 us
  transfers between devices with their start and end apart: 11, of which 4 were waited for; matrix products, arithmetic and copies ran while one was open for 0% of the time, Pallas kernels for 19%

profile of v16, /device:TPU:0, one launch (start us, length us, event | category | flops | bytes accessed | tf_op | source)
XLA Modules:
  0.0 45.4 jit_solution(5858209618697519016)
XLA Ops:
  0.6 0.0 copy-start
  0.6 0.0 copy-start.7
  0.7 0.0 copy-start.2
  0.7 6.5 %all-to-all-start = ((bf16[4,8,4096]{2,1,0:T(8,128)(2,1)}), bf16[4,8,4096]{2,1,0:T(8,128)(2,1)S(1)}, u32[]{:S(2)}, u32[]{:S(2)}) async-start(bf16[4,8,4096]{2,1,0:T(8,128)(2,1)} %q_ref.1), calls=%async_computation | async-start | bytes 524288 | tf_op jit(solution)/shard_map/all_to_all | solution.py:276
  7.1 1.5 %collective-permute-start = (bf16[8,128,256]{2,1,0:T(8,128)(2,1)}, bf16[8,128,256]{2,1,0:T(8,128)(2,1)S(1)}, u32[]{:S(2)}, u32[]{:S(2)}) collective-permute-start(bf16[8,128,256]{2,1,0:T(8,128)(2,1)} %refs_0_.1), channel_id=1, source_target_pairs={{0,2},{1,3},{2,0},{3,1},{4,6},{5,7},{6,4},{7,5},{8,10},{9,11},{10,... | collective-permute-start | bytes 1572872 | tf_op jit(solution)/shard_map/ppermute | solution.py:241
  8.6 0.0 copy-done.7
  8.6 2.0 %collective-permute-start.1 = (s32[3,8]{1,0:T(4,128)S(1)}, s32[3,8]{1,0:T(4,128)S(1)}, u32[]{:S(2)}, u32[]{:S(2)}) collective-permute-start(s32[3,8]{1,0:T(4,128)S(1)} %copy-done.7), channel_id=1, source_target_pairs={{0,4},{1,5},{2,6},{3,7},{4,0},{5,1},{6,2},{7,3},{8,12},{9,13},{10,... | collective-permute-start | bytes 296 | tf_op jit(solution)/shard_map/ppermute | solution.py:241
  10.6 2.4 %collective-permute-start.2 = (s32[3,8]{1,0:T(4,128)S(1)}, s32[3,8]{1,0:T(4,128)S(1)}, u32[]{:S(2)}, u32[]{:S(2)}) collective-permute-start(s32[3,8]{1,0:T(4,128)S(1)} %copy-done.7), channel_id=1, source_target_pairs={{0,8},{1,9},{2,10},{3,11},{4,12},{5,13},{6,14},{7,15},{8,0},{9,1},... | collective-permute-start | bytes 296 | tf_op jit(solution)/shard_map/ppermute | solution.py:241
  13.0 0.0 collective-permute-start.3
  13.0 0.0 copy-done
  13.0 0.0 copy-done.2
  13.0 0.0 copy-start.3
  13.0 0.9 %copy-done.3 = bf16[4,8,4096]{2,1,0:T(8,128)(2,1)S(1)} copy-done((bf16[4,8,4096]{2,1,0:T(8,128)(2,1)S(1)}, bf16[4,8,4096]{2,1,0:T(8,128)(2,1)}, u32[]{:S(2)}) %copy-start.3) | copy-done | bytes 262168
  14.0 0.0 copy-start.4
  14.0 0.7 %copy-done.4 = f32[4096]{0:T(1024)S(1)} copy-done((f32[4096]{0:T(1024)S(1)}, f32[4096]{0:T(1024)}, u32[]{:S(2)}) %copy-start.4) | copy-done | bytes 16408
  14.7 0.0 copy-start.6
  14.7 0.7 %copy-done.6 = f32[4096]{0:T(1024)S(1)} copy-done((f32[4096]{0:T(1024)S(1)}, f32[4096]{0:T(1024)}, u32[]{:S(2)}) %copy-start.6) | copy-done | bytes 16408
  15.4 2.6 %own.1 = (bf16[4,8,4096]{2,1,0:T(8,128)(2,1)S(1)}, bf16[16,8,2048]{2,1,0:T(8,128)(2,1)}) custom-call(bf16[4,8,4096]{2,1,0:T(8,128)(2,1)S(1)} %copy-done, bf16[4,8,4096]{2,1,0:T(8,128)(2,1)S(1)} %copy-done.2, bf16[4,8,4096]{2,1,0:T(8,128)(2,1)S(1)} %copy-done.3, f32[1,4096]{1,0:T(1,128)S(1)} %bitcast.3, f32[1,4096]{1,0:T(1,128)S(1)} %bitcast.5, ...), custom_call_target="tpu_custom_call" | custom-call | tf_op jit(solution)/shard_map/own/pallas_call | solution.py:284
  18.0 0.0 collective-permute-done.1.refs_1_
  18.0 0.0 collective-permute-done.2.refs_2_
  18.1 0.3 collective-permute-done.3.refs_3_
  18.4 0.0 all-to-all-done.q_ref
  18.4 0.0 copy-start.5
  18.4 4.9 %all-to-all-start.1 = ((bf16[16,8,2048]{2,1,0:T(8,128)(2,1)}), bf16[16,8,2048]{2,1,0:T(8,128)(2,1)S(1)}, u32[]{:S(2)}, u32[]{:S(2)}) async-start(bf16[16,8,2048]{2,1,0:T(8,128)(2,1)} %get-tuple-element.45.fresh_ref), calls=%async_computation.1 | async-start | bytes 1048576 | tf_op jit(solution)/shard_map/all_to_all | solution.py:296
  23.3 0.0 copy-done.5
  23.3 0.0 copy-start.1
  23.3 1.3 %turn.1.query_ref = bf16[4,8,4096]{2,1,0:T(8,128)(2,1)S(1)} custom-call(bf16[4,8,4096]{2,1,0:T(8,128)(2,1)S(1)} %all-to-all-done.q_ref, f32[1,4096]{1,0:T(1,128)S(1)} %bitcast.4, s32[3,8]{1,0:T(4,128)S(1)} %copy-done.7, s32[3,8]{1,0:T(4,128)S(1)} %collective-permute-done.1.refs_1_, s32[3,8]{1,0:T(4,128)S(1)} %collective-permute-done.2.refs_2_, ...), custom_call_target="tpu_custom_call" | custom-call | tf_op jit(solution)/shard_map/turn/pallas_call | solution.py:297
  24.7 0.0 collective-permute-done.refs_2_
  24.7 0.0 copy-done.1
  24.7 0.5 %collective-permute-start.4 = (bf16[8,128,256]{2,1,0:T(8,128)(2,1)S(1)}, bf16[8,128,256]{2,1,0:T(8,128)(2,1)S(1)}, u32[]{:S(2)}, u32[]{:S(2)}) collective-permute-start(bf16[8,128,256]{2,1,0:T(8,128)(2,1)S(1)} %copy-done.1), channel_id=1, source_target_pairs={{0,1},{1,0},{2,3},{3,2},{4,5},{5,4},{6,7},{7,6},{8,9},{9,8},{10,11... | collective-permute-start | bytes 1572872 | tf_op jit(solution)/shard_map/ppermute | solution.py:241
  25.1 0.1 collective-permute-start.5
  25.3 1.4 %collective-permute-done.4.refs_1_ = bf16[8,128,256]{2,1,0:T(8,128)(2,1)S(1)} collective-permute-done((bf16[8,128,256]{2,1,0:T(8,128)(2,1)S(1)}, bf16[8,128,256]{2,1,0:T(8,128)(2,1)S(1)}, u32[]{:S(2)}, u32[]{:S(2)}) %collective-permute-start.4) | collective-permute-done | bytes 524320 | tf_op jit(solution)/shard_map/ppermute | solution.py:241
  26.7 0.7 %collective-permute-done.5.refs_3_ = bf16[8,128,256]{2,1,0:T(8,128)(2,1)S(1)} collective-permute-done((bf16[8,128,256]{2,1,0:T(8,128)(2,1)S(1)}, bf16[8,128,256]{2,1,0:T(8,128)(2,1)S(1)}, u32[]{:S(2)}, u32[]{:S(2)}) %collective-permute-start.5) | collective-permute-done | bytes 524320 | tf_op jit(solution)/shard_map/ppermute | solution.py:241
  27.4 1.5 %stale.1 = (bf16[8,4224]{1,0:T(8,128)(2,1)S(1)}, bf16[8,4224]{1,0:T(8,128)(2,1)S(1)}, bf16[8,4224]{1,0:T(8,128)(2,1)S(1)}, bf16[8,4224]{1,0:T(8,128)(2,1)S(1)}) custom-call(bf16[4,8,4096]{2,1,0:T(8,128)(2,1)S(1)} %turn.1.query_ref, bf16[8,128,256]{2,1,0:T(8,128)(2,1)S(1)} %copy-done.1, bf16[8,128,256]{2,1,0:T(8,128)(2,1)S(1)} %collective-permute-done.4.refs_1_, ...), custom_call_target="tpu_custom_call" | custom-call | tf_op jit(solution)/shard_map/stale/pallas_call | solution.py:309
  29.0 2.8 %collective-permute-start.6 = (bf16[8,4224]{1,0:T(8,128)(2,1)S(1)}, bf16[8,4224]{1,0:T(8,128)(2,1)S(1)}, u32[]{:S(2)}, u32[]{:S(2)}) collective-permute-start(bf16[8,4224]{1,0:T(8,128)(2,1)S(1)} %get-tuple-element.37), channel_id=1, source_target_pairs={{0,8},{1,9},{2,10},{3,11},{4,12},{5,13},{6,14},{7,15},{8,0},{9,1},... | collective-permute-start | bytes 202760 | tf_op jit(solution)/shard_map/ppermute | solution.py:241
  31.8 1.5 %collective-permute-start.7 = (bf16[8,4224]{1,0:T(8,128)(2,1)S(1)}, bf16[8,4224]{1,0:T(8,128)(2,1)S(1)}, u32[]{:S(2)}, u32[]{:S(2)}) collective-permute-start(bf16[8,4224]{1,0:T(8,128)(2,1)S(1)} %get-tuple-element.38), channel_id=1, source_target_pairs={{0,12},{1,13},{2,14},{3,15},{4,8},{5,9},{6,10},{7,11},{8,4},{9,5},... | collective-permute-start | bytes 202760 | tf_op jit(solution)/shard_map/ppermute | solution.py:241
  33.2 0.0 collective-permute-start.8
  33.2 2.1 %fresh.1 = (f32[4,8,4096]{2,1,0:T(8,128)S(1)}, f32[4,8,128]{2,1,0:T(8,128)S(1)}) custom-call(bf16[4,8,4096]{2,1,0:T(8,128)(2,1)S(1)} %get-tuple-element.41.query_ref, bf16[16,8,2048]{2,1,0:T(8,128)(2,1)} %get-tuple-element.45.fresh_ref), custom_call_target="tpu_custom_call" | custom-call | tf_op jit(solution)/shard_map/fresh/pallas_call | solution.py:319
  35.4 8.0 %collective-permute-done.6.refs_0_ = bf16[8,4224]{1,0:T(8,128)(2,1)S(1)} collective-permute-done((bf16[8,4224]{1,0:T(8,128)(2,1)S(1)}, bf16[8,4224]{1,0:T(8,128)(2,1)S(1)}, u32[]{:S(2)}, u32[]{:S(2)}) %collective-permute-start.6) | collective-permute-done | bytes 67616 | tf_op jit(solution)/shard_map/ppermute | solution.py:241
  43.4 0.0 collective-permute-done.7.refs_1_
  43.4 0.0 collective-permute-done.8.refs_2_
  43.4 1.2 %join.1 = bf16[4,8,4096]{2,1,0:T(8,128)(2,1)} custom-call(bf16[8,4224]{1,0:T(8,128)(2,1)S(1)} %collective-permute-done.6.refs_0_, bf16[8,4224]{1,0:T(8,128)(2,1)S(1)} %collective-permute-done.7.refs_1_, bf16[8,4224]{1,0:T(8,128)(2,1)S(1)} %collective-permute-done.8.refs_2_, bf16[8,4224]{1,0:T(8,128)(2,1)S(1)} %get-tuple-element.40.refs_3_, ...), custom_call_target="tpu_custom_call" | custom-call | tf_op jit(solution)/shard_map/join/pallas_call | solution.py:339
  44.6 0.0 all-to-all-done.1.got_ref
  44.6 0.9 %cache.1 = bf16[8,16,8,256]{3,2,1,0:T(8,128)(2,1)} custom-call(bf16[16,8,2048]{2,1,0:T(8,128)(2,1)S(1)} %all-to-all-done.1.got_ref), custom_call_target="tpu_custom_call" | custom-call | tf_op jit(solution)/shard_map/cache/pallas_call | solution.py:330
Async XLA Ops:
  0.6 12.4 %copy-start = (bf16[4,8,4096]{2,1,0:T(8,128)(2,1)S(1)}, bf16[4,8,4096]{2,1,0:T(8,128)(2,1)}, u32[]{:S(2)}) copy-start(bf16[4,8,4096]{2,1,0:T(8,128)(2,1)} %q_ref.1) | copy-start | bytes 786436
  0.6 8.0 %copy-start.7 = (s32[3,8]{1,0:T(4,128)S(1)}, s32[3,8]{1,0:T(4,128)}, u32[]{:S(2)}) copy-start(s32[3,8]{1,0:T(4,128)} %refs_0_) | copy-start | bytes 292
  0.7 12.4 %copy-start.2 = (bf16[4,8,4096]{2,1,0:T(8,128)(2,1)S(1)}, bf16[4,8,4096]{2,1,0:T(8,128)(2,1)}, u32[]{:S(2)}) copy-start(bf16[4,8,4096]{2,1,0:T(8,128)(2,1)} %k_ref.1) | copy-start | bytes 786436
  0.7 17.7 %all-to-all-start = ((bf16[4,8,4096]{2,1,0:T(8,128)(2,1)}), bf16[4,8,4096]{2,1,0:T(8,128)(2,1)S(1)}, u32[]{:S(2)}, u32[]{:S(2)}) async-start(bf16[4,8,4096]{2,1,0:T(8,128)(2,1)} %q_ref.1), calls=%async_computation | async-start | bytes 524288 | tf_op jit(solution)/shard_map/all_to_all | solution.py:276
  7.1 17.5 %collective-permute-start = (bf16[8,128,256]{2,1,0:T(8,128)(2,1)}, bf16[8,128,256]{2,1,0:T(8,128)(2,1)S(1)}, u32[]{:S(2)}, u32[]{:S(2)}) collective-permute-start(bf16[8,128,256]{2,1,0:T(8,128)(2,1)} %refs_0_.1), channel_id=1, source_target_pairs={{0,2},{1,3},{2,0},{3,1},{4,6},{5,7},{6,4},{7,5},{8,10},{9,11},{10,... | collective-permute-start | bytes 1572872 | tf_op jit(solution)/shard_map/ppermute | solution.py:241
  8.6 9.4 %collective-permute-start.1 = (s32[3,8]{1,0:T(4,128)S(1)}, s32[3,8]{1,0:T(4,128)S(1)}, u32[]{:S(2)}, u32[]{:S(2)}) collective-permute-start(s32[3,8]{1,0:T(4,128)S(1)} %copy-done.7), channel_id=1, source_target_pairs={{0,4},{1,5},{2,6},{3,7},{4,0},{5,1},{6,2},{7,3},{8,12},{9,13},{10,... | collective-permute-start | bytes 296 | tf_op jit(solution)/shard_map/ppermute | solution.py:241
  10.6 7.4 %collective-permute-start.2 = (s32[3,8]{1,0:T(4,128)S(1)}, s32[3,8]{1,0:T(4,128)S(1)}, u32[]{:S(2)}, u32[]{:S(2)}) collective-permute-start(s32[3,8]{1,0:T(4,128)S(1)} %copy-done.7), channel_id=1, source_target_pairs={{0,8},{1,9},{2,10},{3,11},{4,12},{5,13},{6,14},{7,15},{8,0},{9,1},... | collective-permute-start | bytes 296 | tf_op jit(solution)/shard_map/ppermute | solution.py:241
  13.0 5.4 %collective-permute-start.3 = (s32[3,8]{1,0:T(4,128)S(1)}, s32[3,8]{1,0:T(4,128)S(1)}, u32[]{:S(2)}, u32[]{:S(2)}) collective-permute-start(s32[3,8]{1,0:T(4,128)S(1)} %copy-done.7), channel_id=1, source_target_pairs={{0,12},{1,13},{2,14},{3,15},{4,8},{5,9},{6,10},{7,11},{8,4},{9,5},... | collective-permute-start | bytes 296 | tf_op jit(solution)/shard_map/ppermute | solution.py:241
  13.0 1.0 %copy-start.3 = (bf16[4,8,4096]{2,1,0:T(8,128)(2,1)S(1)}, bf16[4,8,4096]{2,1,0:T(8,128)(2,1)}, u32[]{:S(2)}) copy-start(bf16[4,8,4096]{2,1,0:T(8,128)(2,1)} %v_ref.1) | copy-start | bytes 786436
  14.0 0.7 %copy-start.4 = (f32[4096]{0:T(1024)S(1)}, f32[4096]{0:T(1024)}, u32[]{:S(2)}) copy-start(f32[4096]{0:T(1024)} %param.10) | copy-start | bytes 49156
  14.7 0.7 %copy-start.6 = (f32[4096]{0:T(1024)S(1)}, f32[4096]{0:T(1024)}, u32[]{:S(2)}) copy-start(f32[4096]{0:T(1024)} %param.11) | copy-start | bytes 49156
  18.4 4.9 %copy-start.5 = (f32[4096]{0:T(1024)S(1)}, f32[4096]{0:T(1024)}, u32[]{:S(2)}) copy-start(f32[4096]{0:T(1024)} %param.10) | copy-start | bytes 49156
  18.4 26.2 %all-to-all-start.1 = ((bf16[16,8,2048]{2,1,0:T(8,128)(2,1)}), bf16[16,8,2048]{2,1,0:T(8,128)(2,1)S(1)}, u32[]{:S(2)}, u32[]{:S(2)}) async-start(bf16[16,8,2048]{2,1,0:T(8,128)(2,1)} %get-tuple-element.45.fresh_ref), calls=%async_computation.1 | async-start | bytes 1048576 | tf_op jit(solution)/shard_map/all_to_all | solution.py:296
  23.3 1.4 %copy-start.1 = (bf16[8,128,256]{2,1,0:T(8,128)(2,1)S(1)}, bf16[8,128,256]{2,1,0:T(8,128)(2,1)}, u32[]{:S(2)}) copy-start(bf16[8,128,256]{2,1,0:T(8,128)(2,1)} %refs_0_.1) | copy-start | bytes 1572868
  24.7 2.0 %collective-permute-start.4 = (bf16[8,128,256]{2,1,0:T(8,128)(2,1)S(1)}, bf16[8,128,256]{2,1,0:T(8,128)(2,1)S(1)}, u32[]{:S(2)}, u32[]{:S(2)}) collective-permute-start(bf16[8,128,256]{2,1,0:T(8,128)(2,1)S(1)} %copy-done.1), channel_id=1, source_target_pairs={{0,1},{1,0},{2,3},{3,2},{4,5},{5,4},{6,7},{7,6},{8,9},{9,8},{10,11... | collective-permute-start | bytes 1572872 | tf_op jit(solution)/shard_map/ppermute | solution.py:241
  25.1 2.3 %collective-permute-start.5 = (bf16[8,128,256]{2,1,0:T(8,128)(2,1)S(1)}, bf16[8,128,256]{2,1,0:T(8,128)(2,1)S(1)}, u32[]{:S(2)}, u32[]{:S(2)}) collective-permute-start(bf16[8,128,256]{2,1,0:T(8,128)(2,1)S(1)} %collective-permute-done.refs_2_), channel_id=1, source_target_pairs={{0,1},{1,0},{2,3},{3,2},{4,5},{5,4},{6,7},{7,6},{8,9},{9,8},{10,11... | collective-permute-start | bytes 1572872 | tf_op jit(solution)/shard_map/ppermute | solution.py:241
  29.0 14.4 %collective-permute-start.6 = (bf16[8,4224]{1,0:T(8,128)(2,1)S(1)}, bf16[8,4224]{1,0:T(8,128)(2,1)S(1)}, u32[]{:S(2)}, u32[]{:S(2)}) collective-permute-start(bf16[8,4224]{1,0:T(8,128)(2,1)S(1)} %get-tuple-element.37), channel_id=1, source_target_pairs={{0,8},{1,9},{2,10},{3,11},{4,12},{5,13},{6,14},{7,15},{8,0},{9,1},... | collective-permute-start | bytes 202760 | tf_op jit(solution)/shard_map/ppermute | solution.py:241
  31.8 11.6 %collective-permute-start.7 = (bf16[8,4224]{1,0:T(8,128)(2,1)S(1)}, bf16[8,4224]{1,0:T(8,128)(2,1)S(1)}, u32[]{:S(2)}, u32[]{:S(2)}) collective-permute-start(bf16[8,4224]{1,0:T(8,128)(2,1)S(1)} %get-tuple-element.38), channel_id=1, source_target_pairs={{0,12},{1,13},{2,14},{3,15},{4,8},{5,9},{6,10},{7,11},{8,4},{9,5},... | collective-permute-start | bytes 202760 | tf_op jit(solution)/shard_map/ppermute | solution.py:241
  33.2 10.2 %collective-permute-start.8 = (bf16[8,4224]{1,0:T(8,128)(2,1)S(1)}, bf16[8,4224]{1,0:T(8,128)(2,1)S(1)}, u32[]{:S(2)}, u32[]{:S(2)}) collective-permute-start(bf16[8,4224]{1,0:T(8,128)(2,1)S(1)} %get-tuple-element.39), channel_id=1, source_target_pairs={{0,4},{1,5},{2,6},{3,7},{4,0},{5,1},{6,2},{7,3},{8,12},{9,13},{10,... | collective-permute-start | bytes 202760 | tf_op jit(solution)/shard_map/ppermute | solution.py:241

commit v17 on v16

--- a/solution.py
+++ b/solution.py
@@ -18,30 +18,33 @@
 TRANSPOSED = (((1,), (1,)), ((), ()))
 
 
-def rope_tables(coords, tok_rows):
-    half = DH // 2
+def lane_axis(shape):
     side = DH // 6
-    first = half - 2 * side
-    shape = (len(coords) * tok_rows, DH)
+    first = DH // 2 - 2 * side
+    pair = lax.broadcasted_iota(jnp.int32, shape, 1) // 2
+    return pair, (pair >= first).astype(jnp.int32) + (pair >= first + side).astype(jnp.int32)
+
+
+def lane_places(coords_ref, tok_rows):
+    shape = (tok_rows, DH)
     row = lax.broadcasted_iota(jnp.int32, shape, 0)
-    lane = lax.broadcasted_iota(jnp.int32, shape, 1)
-    pair = lane // 2
-    axis = (pair >= first).astype(jnp.int32) + (pair >= first + side).astype(jnp.int32)
-    places = []
-    for ref in coords:
-        place = jnp.zeros((tok_rows, DH), jnp.int32)
-        for which in range(3):
-            for token in range(tok_rows):
-                here = (axis[:tok_rows] == which) & (row[:tok_rows] == token)
-                place = jnp.where(here, ref[which, token], place)
-        places.append(place)
-    place = jnp.concatenate(places, axis=0)
+    _, axis = lane_axis(shape)
+    place = jnp.zeros(shape, jnp.int32)
+    for which in range(3):
+        for token in range(tok_rows):
+            place = jnp.where((axis == which) & (row == token), coords_ref[which, token], place)
+    return place.astype(F32)
+
+
+def rope_tables(place):
+    side = DH // 6
+    first = DH // 2 - 2 * side
+    pair, axis = lane_axis(place.shape)
     step = jnp.where(axis == 0, pair, jnp.where(axis == 1, pair - first, pair - first - side))
     count = jnp.where(axis == 0, float(first), float(side))
-    freq = jnp.exp(step.astype(F32) / count * (-math.log(10000.0)))
-    angle = place.astype(F32) * freq
+    angle = place * jnp.exp(step.astype(F32) / count * (-math.log(10000.0)))
     sine = jnp.sin(angle)
-    even = lane % 2 == 0
+    even = lax.broadcasted_iota(jnp.int32, place.shape, 1) % 2 == 0
     return jnp.cos(angle), jnp.where(even, -sine, 0.0), jnp.where(even, 0.0, sine)
 
 
@@ -57,33 +60,76 @@
         yield head, y.astype(BF16)
 
 
-def own_kernel(q_ref, k_ref, v_ref, q_gain_ref, k_gain_ref, coords_ref, query_ref, fresh_ref):
-    videos, tok_rows, width = k_ref.shape
-    tables = rope_tables([coords_ref], tok_rows)
-    span = fresh_ref.shape[2]
-    groups = fresh_ref.shape[0] // videos
-    pairs = span // (2 * DH)
+def lay_kernel(groups, q_hbm, coords_hbm, *refs):
+    videos, tok_rows, width = q_hbm.shape
+    outs, (held, coords_ref, sems, coords_sem) = refs[:videos], refs[videos:]
+    own = lax.axis_index("patch") // groups
+    first = pltpu.make_async_copy(coords_hbm, coords_ref, coords_sem)
+    first.start()
+    reads = [
+        pltpu.make_async_copy(q_hbm.at[own ^ s], held.at[s, :, pl.ds(0, width)], sems.at[0, s])
+        for s in range(videos)
+    ]
+    writes = [pltpu.make_async_copy(held.at[s], outs[s], sems.at[1, s]) for s in range(videos)]
+    for read in reads:
+        read.start()
+    first.wait()
+    place = lane_places(coords_ref, tok_rows).astype(BF16)
+    for s in range(videos):
+        held[s, :, width:] = place
+    for read, write in zip(reads, writes):
+        read.wait()
+        write.start()
+    for write in writes:
+        write.wait()
+
+
+def key_kernel(k_hbm, v_hbm, gain_hbm, coords_hbm, out_hbm, k_ref, v_ref, gain_ref, coords_ref, done_ref, sems):
+    videos, tok_rows, width = k_hbm.shape
+    pairs = out_hbm.shape[2] // (2 * DH)
+    groups = out_hbm.shape[0] // videos
+    sources, places = (coords_hbm, k_hbm, gain_hbm, v_hbm), (coords_ref, k_ref, gain_ref, v_ref)
+    reads = [
+        pltpu.make_async_copy(source, place, sems.at[i])
+        for i, (source, place) in enumerate(zip(sources, places))
+    ]
+    for read in reads:
+        read.start()
+    for read in reads:
+        read.wait()
+    tables = rope_tables(lane_places(coords_ref, tok_rows))
+    writes = []
     for video in range(videos):
-        for head, y in normed_heads(k_ref[video].astype(F32), k_gain_ref, tables):
+        for head, y in normed_heads(k_ref[video].astype(F32), gain_ref, tables):
             target, start = video * groups + head // pairs, head % pairs * 2 * DH
-            fresh_ref[target, :, start : start + DH] = y
-            fresh_ref[target, :, start + DH : start + 2 * DH] = v_ref[
+            done_ref[target, :, start : start + DH] = y
+            done_ref[target, :, start + DH : start + 2 * DH] = v_ref[
                 video, :, head * DH : (head + 1) * DH
             ]
-    for video in range(videos):
-        for head, y in normed_heads(q_ref[video].astype(F32), q_gain_ref, tables):
-            query_ref[video, :, head * DH : (head + 1) * DH] = y
-
-
-def turn_kernel(groups, q_ref, gain_ref, *refs):
-    coords, out_ref = refs[:-1], refs[-1]
-    videos, tok_rows, _ = q_ref.shape
-    own = lax.axis_index("patch") // groups
-    tables = rope_tables(coords, tok_rows)
+        part = pl.ds(video * groups, groups)
+        writes.append(pltpu.make_async_copy(done_ref.at[part], out_hbm.at[part], sems.at[4 + video]))
+        writes[-1].start()
+    for write in writes:
+        write.wait()
+
+
+def turn_kernel(gain_ref, *refs):
+    got, out_ref = in_order(refs[:-1]), refs[-1]
+    videos, tok_rows, width = out_ref.shape
+    place = jnp.concatenate([ref[:, width:].astype(F32) for ref in got], axis=0)
+    tables = rope_tables(place)
     for s in range(videos):
         mine = [table[s * tok_rows : (s + 1) * tok_rows] for table in tables]
-        for head, y in normed_heads(q_ref[own ^ s].astype(F32), gain_ref, mine):
+        for head, y in normed_heads(got[s][:, :width].astype(F32), gain_ref, mine):
             out_ref[s, :, head * DH : (head + 1) * DH] = y
+
+
+def query_kernel(q_ref, gain_ref, coords_ref, out_ref):
+    videos, tok_rows, _ = q_ref.shape
+    tables = rope_tables(lane_places(coords_ref, tok_rows))
+    for video in range(videos):
+        for head, y in normed_heads(q_ref[video].astype(F32), gain_ref, tables):
+            out_ref[video, :, head * DH : (head + 1) * DH] = y
 
 
 def softmax_parts(scores):
@@ -272,36 +318,52 @@
             **kwargs,
         )
 
-    columns = [[v * groups + g for v in range(videos)] for g in range(groups)]
-    query_raw = lax.all_to_all(
-        queries, "patch", split_axis=0, concat_axis=0, axis_index_groups=columns, tiled=True
-    )
-    coords_got = exchange([coords] * videos, groups, patches)
+    gains = q_gain.reshape(1, width), k_gain.reshape(1, width)
+    sent = kernel(
+        functools.partial(lay_kernel, groups),
+        "lay",
+        56,
+        out_shape=[jax.ShapeDtypeStruct((tok_rows, width + DH), BF16)] * videos,
+        in_specs=[HBM] * 2,
+        out_specs=[HBM] * videos,
+        scratch_shapes=[
+            pltpu.VMEM((videos, tok_rows, width + DH), BF16),
+            pltpu.SMEM(coords.shape, jnp.int32),
+            pltpu.SemaphoreType.DMA((2, videos)),
+            pltpu.SemaphoreType.DMA,
+        ],
+    )(queries, coords)
+    stale_sent, kept = lax.optimization_barrier((stale_cache, sent[0]))
     pieces = {0: stale_cache}
     bit = groups // 2
-    pieces[bit] = permuted(stale_cache, bit, patches)
-    gains = q_gain.reshape(1, width), k_gain.reshape(1, width)
-    query, fresh = kernel(
-        own_kernel,
-        "own",
-        16,
-        out_shape=(
-            jax.ShapeDtypeStruct(queries.shape, BF16),
-            jax.ShapeDtypeStruct((patches, tok_rows, 2 * pairs_here * DH), BF16),
-        ),
-        in_specs=[VMEM] * 5 + [SMEM],
-        out_specs=(VMEM, VMEM),
-    )(queries, keys, values, *gains, coords)
-    fresh_sent, query_raw, coords_got = lax.optimization_barrier((fresh, query_raw, coords_got))
+    pieces[bit] = permuted(stale_sent, bit, patches)
+    query_raw = far_first(exchange([kept, *sent[1:]], groups, patches))
+    fresh = kernel(
+        key_kernel,
+        "key",
+        56,
+        out_shape=jax.ShapeDtypeStruct((patches, tok_rows, 2 * pairs_here * DH), BF16),
+        in_specs=[HBM] * 4,
+        out_specs=HBM,
+        scratch_shapes=[
+            pltpu.VMEM(keys.shape, BF16),
+            pltpu.VMEM(keys.shape, BF16),
+            pltpu.VMEM((1, width), F32),
+            pltpu.SMEM(coords.shape, jnp.int32),
+            pltpu.VMEM((patches, tok_rows, 2 * pairs_here * DH), BF16),
+            pltpu.SemaphoreType.DMA((4 + videos,)),
+        ],
+    )(keys, values, gains[1], coords)
+    fresh_sent, query_raw = lax.optimization_barrier((fresh, query_raw))
     cached = lax.all_to_all(fresh_sent, "patch", split_axis=0, concat_axis=0, tiled=True)
     query_got = kernel(
-        functools.partial(turn_kernel, groups),
+        turn_kernel,
         "turn",
         16,
         out_shape=jax.ShapeDtypeStruct(queries.shape, BF16),
-        in_specs=[VMEM] * 2 + [SMEM] * videos,
+        in_specs=[VMEM] * (1 + videos),
         out_specs=VMEM,
-    )(query_raw, gains[0], *coords_got)
+    )(gains[0], *query_raw)
     pieces, query_got = lax.optimization_barrier((pieces, query_got))
     while bit > 1:
         bit //= 2
@@ -314,7 +376,15 @@
         in_specs=[VMEM] * (1 + groups),
         out_specs=[VMEM] * videos,
     )(query_got, *[pieces[t] for t in range(groups)])
-    result, fresh_late = lax.optimization_barrier((result, fresh))
+    result, fresh_late, queries_late = lax.optimization_barrier((result, fresh, queries))
+    query = kernel(
+        query_kernel,
+        "query",
+        16,
+        out_shape=jax.ShapeDtypeStruct(queries.shape, BF16),
+        in_specs=[VMEM] * 2 + [SMEM],
+        out_specs=VMEM,
+    )(queries_late, gains[0], coords)
     back = far_first(exchange(result, groups, patches))
     fresh_sum, fresh_log = kernel(
         functools.partial(fresh_kernel, groups, videos),

time: 46 us -> 40.1 us (0.87)
  starting transfers between devices: 22.1 us -> 16.1 us
  local copies, waits for them, and re-layouts: 2.4 us -> 0.36 us
  waiting for transfers between devices: 10.5 us -> 12.1 us
  Pallas kernels: 9.65 us -> 10.6 us
    all_to_all x1 -> x0, starting transfers between devices: 6.46 us -> none  [local(): lax.all_to_all(queries, 'patch', split_axis=0, concat_axis=0, axis_index_...]
    all_to_all x1, waiting for transfers between devices: 0.01 us -> 3.01 us  [local(): lax.all_to_all(fresh_sent, 'patch', split_axis=0, concat_axis=0, tiled=True)]
    unnamed x16 -> x12, local copies, waits for them, and re-layouts: 2.4 us -> 0.36 us
    pallas_call x2 -> x4, Pallas kernels: 3.97 us -> 5.91 us  [the longest x1 2.4 us: local(): kernel(key_kernel, 'key', 56, out_shape=jax.ShapeDtypeStruct((patches, to...]
    ppermute x9, waiting for transfers between devices: 10.5 us -> 9.04 us  [permuted(): lax.ppermute(array, 'patch', [(i, i ^ offset) for i in range(patches)])]
    ppermute x9, starting transfers between devices: 10.7 us -> 12 us  [permuted(): lax.ppermute(array, 'patch', [(i, i ^ offset) for i in range(patches)])]
    pallas_call x1, Pallas kernels: 2.15 us -> 1.12 us  [local(): kernel(functools.partial(fresh_kernel, groups, videos), 'fresh', 16, out_...]
    all_to_all x1, starting transfers between devices: 4.9 us -> 4.08 us  [local(): lax.all_to_all(fresh_sent, 'patch', split_axis=0, concat_axis=0, tiled=True)]
  transfers between devices with their start and end apart: 11 -> 10, of which waited for: 4 -> 6; matrix products, arithmetic and copies ran while one was open for 0% -> 0% of each run, Pallas kernels for 19% -> 19%
where the time goes in v17:
time: 40.1 us; the launch traced here: 39.8 us
  starting transfers between devices  16.1 us (40%)
  waiting for transfers between devices  12.1 us (30%)
  Pallas kernels  10.6 us (26%)
  between operations  0.76 us (2%)
    ppermute x9, starting transfers between devices, permuted(): lax.ppermute(array, 'patch', [(i, i ^ offset) for i in range(patches)])  12 us
    ppermute x9, waiting for transfers between devices, permuted(): lax.ppermute(array, 'patch', [(i, i ^ offset) for i in range(patches)])  9.04 us
    all_to_all x1, starting transfers between devices, local(): lax.all_to_all(fresh_sent, 'patch', split_axis=0, concat_axis=0, tiled=True)  4.08 us
    all_to_all x1, waiting for transfers between devices, local(): lax.all_to_all(fresh_sent, 'patch', split_axis=0, concat_axis=0, tiled=True)  3.01 us
    pallas_call x1, Pallas kernels, local(): kernel(key_kernel, 'key', 56, out_shape=jax.ShapeDtypeStruct((patches, to...  2.4 us
    pallas_call x1, Pallas kernels, local(): kernel(functools.partial(lay_kernel, groups), 'lay', 56, out_shape=[jax.S...  1.64 us
    pallas_call x1, Pallas kernels, local(): kernel(functools.partial(stale_kernel, groups, videos), 'stale', 32, out_...  1.52 us
    pallas_call x1, Pallas kernels, local(): kernel(query_kernel, 'query', 16, out_shape=jax.ShapeDtypeStruct(queries....  1.21 us
  transfers between devices with their start and end apart: 10, of which 6 were waited for; matrix products, arithmetic and copies ran while one was open for 0% of the time, Pallas kernels for 19%

profile of v17, /device:TPU:0, one launch (start us, length us, event | category | flops | bytes accessed | tf_op | source)
XLA Modules:
  0.0 39.8 jit_solution(1704391900066581349)
XLA Ops:
  0.6 1.6 %lay.1 = (bf16[8,4224]{1,0:T(8,128)(2,1)}, bf16[8,4224]{1,0:T(8,128)(2,1)}, bf16[8,4224]{1,0:T(8,128)(2,1)}, bf16[8,4224]{1,0:T(8,128)(2,1)}) custom-call(bf16[4,8,4096]{2,1,0:T(8,128)(2,1)} %q_ref, s32[3,8]{1,0:T(4,128)} %coords_ref.1), custom_call_target="tpu_custom_call" | custom-call | tf_op jit(solution)/shard_map/lay/pallas_call | solution.py:322
  2.3 3.0 %collective-permute-start = (bf16[8,128,256]{2,1,0:T(8,128)(2,1)}, bf16[8,128,256]{2,1,0:T(8,128)(2,1)S(1)}, u32[]{:S(2)}, u32[]{:S(2)}) collective-permute-start(bf16[8,128,256]{2,1,0:T(8,128)(2,1)} %refs_0_), channel_id=1, source_target_pairs={{0,2},{1,3},{2,0},{3,1},{4,6},{5,7},{6,4},{7,5},{8,10},{9,11},{10,... | collective-permute-start | bytes 1572872 | tf_op jit(solution)/shard_map/ppermute | solution.py:287
  5.3 2.6 %collective-permute-start.1 = (bf16[8,4224]{1,0:T(8,128)(2,1)}, bf16[8,4224]{1,0:T(8,128)(2,1)S(1)}, u32[]{:S(2)}, u32[]{:S(2)}) collective-permute-start(bf16[8,4224]{1,0:T(8,128)(2,1)} %get-tuple-element.30), channel_id=1, source_target_pairs={{0,8},{1,9},{2,10},{3,11},{4,12},{5,13},{6,14},{7,15},{8,0},{9,1},... | collective-permute-start | bytes 202760 | tf_op jit(solution)/shard_map/ppermute | solution.py:287
  7.9 1.3 %collective-permute-start.2 = (bf16[8,4224]{1,0:T(8,128)(2,1)}, bf16[8,4224]{1,0:T(8,128)(2,1)S(1)}, u32[]{:S(2)}, u32[]{:S(2)}) collective-permute-start(bf16[8,4224]{1,0:T(8,128)(2,1)} %get-tuple-element.31), channel_id=1, source_target_pairs={{0,12},{1,13},{2,14},{3,15},{4,8},{5,9},{6,10},{7,11},{8,4},{9,5},... | collective-permute-start | bytes 202760 | tf_op jit(solution)/shard_map/ppermute | solution.py:287
  9.2 0.2 collective-permute-start.3
  9.4 2.4 %key.1.fresh_ref = bf16[16,8,2048]{2,1,0:T(8,128)(2,1)} custom-call(bf16[4,8,4096]{2,1,0:T(8,128)(2,1)} %k_hbm.1, bf16[4,8,4096]{2,1,0:T(8,128)(2,1)} %v_hbm.1, f32[1,4096]{1,0:T(1,128)} %bitcast.6, s32[3,8]{1,0:T(4,128)} %coords_ref.1), custom_call_target="tpu_custom_call" | custom-call | tf_op jit(solution)/shard_map/key/pallas_call | solution.py:341
  11.9 0.0 copy-start.3
  11.9 0.0 copy-start.4
  11.9 0.0 collective-permute-done.1.refs_0_
  11.9 2.4 %collective-permute-done.2.refs_1_ = bf16[8,4224]{1,0:T(8,128)(2,1)S(1)} collective-permute-done((bf16[8,4224]{1,0:T(8,128)(2,1)}, bf16[8,4224]{1,0:T(8,128)(2,1)S(1)}, u32[]{:S(2)}, u32[]{:S(2)}) %collective-permute-start.2) | collective-permute-done | bytes 67616 | tf_op jit(solution)/shard_map/ppermute | solution.py:287
  14.3 0.1 collective-permute-done.3.refs_2_
  14.4 4.1 %all-to-all-start = ((bf16[16,8,2048]{2,1,0:T(8,128)(2,1)}), bf16[16,8,2048]{2,1,0:T(8,128)(2,1)S(1)}, u32[]{:S(2)}, u32[]{:S(2)}) async-start(bf16[16,8,2048]{2,1,0:T(8,128)(2,1)} %key.1.fresh_ref), calls=%async_computation | async-start | bytes 1048576 | tf_op jit(solution)/shard_map/all_to_all | solution.py:358
  18.5 0.0 copy-start.2
  18.5 0.0 copy-done.3
  18.6 0.0 copy-done.4
  18.6 0.7 %turn.1.query_ref = bf16[4,8,4096]{2,1,0:T(8,128)(2,1)S(1)} custom-call(f32[1,4096]{1,0:T(1,128)S(1)} %bitcast.3, bf16[8,4224]{1,0:T(8,128)(2,1)S(1)} %collective-permute-done.1.refs_0_, bf16[8,4224]{1,0:T(8,128)(2,1)S(1)} %collective-permute-done.2.refs_1_, bf16[8,4224]{1,0:T(8,128)(2,1)S(1)} %collective-permute-done.3.refs_2_, bf16[8,4224]{1,0:T(8,128)(2,1)S(1)} %copy-done.3), custom_call_target="tpu_custom_call" | custom-call | tf_op jit(solution)/shard_map/turn/pallas_call | solution.py:359
  19.2 0.0 copy-start.1
  19.2 0.0 collective-permute-done.refs_2_
  19.2 0.3 copy-done.2
  19.6 0.4 %collective-permute-start.4 = (bf16[8,128,256]{2,1,0:T(8,128)(2,1)S(1)}, bf16[8,128,256]{2,1,0:T(8,128)(2,1)S(1)}, u32[]{:S(2)}, u32[]{:S(2)}) collective-permute-start(bf16[8,128,256]{2,1,0:T(8,128)(2,1)S(1)} %copy-done.2), channel_id=1, source_target_pairs={{0,1},{1,0},{2,3},{3,2},{4,5},{5,4},{6,7},{7,6},{8,9},{9,8},{10,11... | collective-permute-start | bytes 1572872 | tf_op jit(solution)/shard_map/ppermute | solution.py:287
  20.0 0.1 collective-permute-start.5
  20.1 1.4 %collective-permute-done.4.refs_1_ = bf16[8,128,256]{2,1,0:T(8,128)(2,1)S(1)} collective-permute-done((bf16[8,128,256]{2,1,0:T(8,128)(2,1)S(1)}, bf16[8,128,256]{2,1,0:T(8,128)(2,1)S(1)}, u32[]{:S(2)}, u32[]{:S(2)}) %collective-permute-start.4) | collective-permute-done | bytes 524320 | tf_op jit(solution)/shard_map/ppermute | solution.py:287
  21.5 0.7 %collective-permute-done.5.refs_3_ = bf16[8,128,256]{2,1,0:T(8,128)(2,1)S(1)} collective-permute-done((bf16[8,128,256]{2,1,0:T(8,128)(2,1)S(1)}, bf16[8,128,256]{2,1,0:T(8,128)(2,1)S(1)}, u32[]{:S(2)}, u32[]{:S(2)}) %collective-permute-start.5) | collective-permute-done | bytes 524320 | tf_op jit(solution)/shard_map/ppermute | solution.py:287
  22.3 0.0 copy-start.5
  22.3 1.5 %stale.1 = (bf16[8,4224]{1,0:T(8,128)(2,1)S(1)}, bf16[8,4224]{1,0:T(8,128)(2,1)S(1)}, bf16[8,4224]{1,0:T(8,128)(2,1)S(1)}, bf16[8,4224]{1,0:T(8,128)(2,1)S(1)}) custom-call(bf16[4,8,4096]{2,1,0:T(8,128)(2,1)S(1)} %turn.1.query_ref, bf16[8,128,256]{2,1,0:T(8,128)(2,1)S(1)} %copy-done.2, bf16[8,128,256]{2,1,0:T(8,128)(2,1)S(1)} %collective-permute-done.4.refs_1_, ...), custom_call_target="tpu_custom_call" | custom-call | tf_op jit(solution)/shard_map/stale/pallas_call | solution.py:371
  23.8 0.0 copy-start
  23.8 2.8 %collective-permute-start.6 = (bf16[8,4224]{1,0:T(8,128)(2,1)S(1)}, bf16[8,4224]{1,0:T(8,128)(2,1)S(1)}, u32[]{:S(2)}, u32[]{:S(2)}) collective-permute-start(bf16[8,4224]{1,0:T(8,128)(2,1)S(1)} %get-tuple-element.45), channel_id=1, source_target_pairs={{0,8},{1,9},{2,10},{3,11},{4,12},{5,13},{6,14},{7,15},{8,0},{9,1},... | collective-permute-start | bytes 202760 | tf_op jit(solution)/shard_map/ppermute | solution.py:287
  26.6 1.5 %collective-permute-start.7 = (bf16[8,4224]{1,0:T(8,128)(2,1)S(1)}, bf16[8,4224]{1,0:T(8,128)(2,1)S(1)}, u32[]{:S(2)}, u32[]{:S(2)}) collective-permute-start(bf16[8,4224]{1,0:T(8,128)(2,1)S(1)} %get-tuple-element.46), channel_id=1, source_target_pairs={{0,12},{1,13},{2,14},{3,15},{4,8},{5,9},{6,10},{7,11},{8,4},{9,5},... | collective-permute-start | bytes 202760 | tf_op jit(solution)/shard_map/ppermute | solution.py:287
  28.1 0.0 collective-permute-start.8
  28.1 0.0 copy-done.1
  28.1 0.0 copy-done.5
  28.1 1.2 %query.1.query_ref = bf16[4,8,4096]{2,1,0:T(8,128)(2,1)S(1)} custom-call(bf16[4,8,4096]{2,1,0:T(8,128)(2,1)S(1)} %copy-done.1, f32[1,4096]{1,0:T(1,128)S(1)} %bitcast.4, s32[3,8]{1,0:T(4,128)S(1)} %copy-done.5), custom_call_target="tpu_custom_call" | custom-call | tf_op jit(solution)/shard_map/query/pallas_call | solution.py:380
  29.3 0.0 copy-done
  29.3 1.1 %fresh.1 = (f32[4,8,4096]{2,1,0:T(8,128)S(1)}, f32[4,8,128]{2,1,0:T(8,128)S(1)}) custom-call(bf16[4,8,4096]{2,1,0:T(8,128)(2,1)S(1)} %query.1.query_ref, bf16[16,8,2048]{2,1,0:T(8,128)(2,1)S(1)} %copy-done), custom_call_target="tpu_custom_call" | custom-call | tf_op jit(solution)/shard_map/fresh/pallas_call | solution.py:389
  30.5 3.0 %all-to-all-done.got_ref = bf16[16,8,2048]{2,1,0:T(8,128)(2,1)S(1)} async-done(((bf16[16,8,2048]{2,1,0:T(8,128)(2,1)}), bf16[16,8,2048]{2,1,0:T(8,128)(2,1)S(1)}, u32[]{:S(2)}, u32[]{:S(2)}) %all-to-all-start) | async-done | bytes 524320 | tf_op jit(solution)/shard_map/all_to_all | solution.py:358
  33.5 0.8 %cache.1 = bf16[8,16,8,256]{3,2,1,0:T(8,128)(2,1)} custom-call(bf16[16,8,2048]{2,1,0:T(8,128)(2,1)S(1)} %all-to-all-done.got_ref), custom_call_target="tpu_custom_call" | custom-call | tf_op jit(solution)/shard_map/cache/pallas_call | solution.py:400
  34.3 4.3 %collective-permute-done.6.refs_0_ = bf16[8,4224]{1,0:T(8,128)(2,1)S(1)} collective-permute-done((bf16[8,4224]{1,0:T(8,128)(2,1)S(1)}, bf16[8,4224]{1,0:T(8,128)(2,1)S(1)}, u32[]{:S(2)}, u32[]{:S(2)}) %collective-permute-start.6) | collective-permute-done | bytes 67616 | tf_op jit(solution)/shard_map/ppermute | solution.py:287
  38.6 0.0 collective-permute-done.7.refs_1_
  38.6 0.0 collective-permute-done.8.refs_2_
  38.6 1.2 %join.1 = bf16[4,8,4096]{2,1,0:T(8,128)(2,1)} custom-call(bf16[8,4224]{1,0:T(8,128)(2,1)S(1)} %collective-permute-done.6.refs_0_, bf16[8,4224]{1,0:T(8,128)(2,1)S(1)} %collective-permute-done.7.refs_1_, bf16[8,4224]{1,0:T(8,128)(2,1)S(1)} %collective-permute-done.8.refs_2_, bf16[8,4224]{1,0:T(8,128)(2,1)S(1)} %get-tuple-element.48.refs_3_, ...), custom_call_target="tpu_custom_call" | custom-call | tf_op jit(solution)/shard_map/join/pallas_call | solution.py:409
Async XLA Ops:
  2.3 17.0 %collective-permute-start = (bf16[8,128,256]{2,1,0:T(8,128)(2,1)}, bf16[8,128,256]{2,1,0:T(8,128)(2,1)S(1)}, u32[]{:S(2)}, u32[]{:S(2)}) collective-permute-start(bf16[8,128,256]{2,1,0:T(8,128)(2,1)} %refs_0_), channel_id=1, source_target_pairs={{0,2},{1,3},{2,0},{3,1},{4,6},{5,7},{6,4},{7,5},{8,10},{9,11},{10,... | collective-permute-start | bytes 1572872 | tf_op jit(solution)/shard_map/ppermute | solution.py:287
  5.3 6.6 %collective-permute-start.1 = (bf16[8,4224]{1,0:T(8,128)(2,1)}, bf16[8,4224]{1,0:T(8,128)(2,1)S(1)}, u32[]{:S(2)}, u32[]{:S(2)}) collective-permute-start(bf16[8,4224]{1,0:T(8,128)(2,1)} %get-tuple-element.30), channel_id=1, source_target_pairs={{0,8},{1,9},{2,10},{3,11},{4,12},{5,13},{6,14},{7,15},{8,0},{9,1},... | collective-permute-start | bytes 202760 | tf_op jit(solution)/shard_map/ppermute | solution.py:287
  7.9 6.5 %collective-permute-start.2 = (bf16[8,4224]{1,0:T(8,128)(2,1)}, bf16[8,4224]{1,0:T(8,128)(2,1)S(1)}, u32[]{:S(2)}, u32[]{:S(2)}) collective-permute-start(bf16[8,4224]{1,0:T(8,128)(2,1)} %get-tuple-element.31), channel_id=1, source_target_pairs={{0,12},{1,13},{2,14},{3,15},{4,8},{5,9},{6,10},{7,11},{8,4},{9,5},... | collective-permute-start | bytes 202760 | tf_op jit(solution)/shard_map/ppermute | solution.py:287
  9.2 5.2 %collective-permute-start.3 = (bf16[8,4224]{1,0:T(8,128)(2,1)}, bf16[8,4224]{1,0:T(8,128)(2,1)S(1)}, u32[]{:S(2)}, u32[]{:S(2)}) collective-permute-start(bf16[8,4224]{1,0:T(8,128)(2,1)} %get-tuple-element.32), channel_id=1, source_target_pairs={{0,4},{1,5},{2,6},{3,7},{4,0},{5,1},{6,2},{7,3},{8,12},{9,13},{10,... | collective-permute-start | bytes 202760 | tf_op jit(solution)/shard_map/ppermute | solution.py:287
  11.9 6.7 %copy-start.3 = (bf16[8,4224]{1,0:T(8,128)(2,1)S(1)}, bf16[8,4224]{1,0:T(8,128)(2,1)}, u32[]{:S(2)}) copy-start(bf16[8,4224]{1,0:T(8,128)(2,1)} %get-tuple-element.37.refs_3_) | copy-start | bytes 202756
  11.9 6.7 %copy-start.4 = (f32[4096]{0:T(1024)S(1)}, f32[4096]{0:T(1024)}, u32[]{:S(2)}) copy-start(f32[4096]{0:T(1024)} %param.10) | copy-start | bytes 49156
  14.4 19.0 %all-to-all-start = ((bf16[16,8,2048]{2,1,0:T(8,128)(2,1)}), bf16[16,8,2048]{2,1,0:T(8,128)(2,1)S(1)}, u32[]{:S(2)}, u32[]{:S(2)}) async-start(bf16[16,8,2048]{2,1,0:T(8,128)(2,1)} %key.1.fresh_ref), calls=%async_computation | async-start | bytes 1048576 | tf_op jit(solution)/shard_map/all_to_all | solution.py:358
  18.5 1.0 %copy-start.2 = (bf16[8,128,256]{2,1,0:T(8,128)(2,1)S(1)}, bf16[8,128,256]{2,1,0:T(8,128)(2,1)}, u32[]{:S(2)}) copy-start(bf16[8,128,256]{2,1,0:T(8,128)(2,1)} %refs_0_) | copy-start | bytes 1572868
  19.2 8.9 %copy-start.1 = (bf16[4,8,4096]{2,1,0:T(8,128)(2,1)S(1)}, bf16[4,8,4096]{2,1,0:T(8,128)(2,1)}, u32[]{:S(2)}) copy-start(bf16[4,8,4096]{2,1,0:T(8,128)(2,1)} %q_ref) | copy-start | bytes 786436
  19.6 1.9 %collective-permute-start.4 = (bf16[8,128,256]{2,1,0:T(8,128)(2,1)S(1)}, bf16[8,128,256]{2,1,0:T(8,128)(2,1)S(1)}, u32[]{:S(2)}, u32[]{:S(2)}) collective-permute-start(bf16[8,128,256]{2,1,0:T(8,128)(2,1)S(1)} %copy-done.2), channel_id=1, source_target_pairs={{0,1},{1,0},{2,3},{3,2},{4,5},{5,4},{6,7},{7,6},{8,9},{9,8},{10,11... | collective-permute-start | bytes 1572872 | tf_op jit(solution)/shard_map/ppermute | solution.py:287
  20.0 2.3 %collective-permute-start.5 = (bf16[8,128,256]{2,1,0:T(8,128)(2,1)S(1)}, bf16[8,128,256]{2,1,0:T(8,128)(2,1)S(1)}, u32[]{:S(2)}, u32[]{:S(2)}) collective-permute-start(bf16[8,128,256]{2,1,0:T(8,128)(2,1)S(1)} %collective-permute-done.refs_2_), channel_id=1, source_target_pairs={{0,1},{1,0},{2,3},{3,2},{4,5},{5,4},{6,7},{7,6},{8,9},{9,8},{10,11... | collective-permute-start | bytes 1572872 | tf_op jit(solution)/shard_map/ppermute | solution.py:287
  22.3 5.8 %copy-start.5 = (s32[3,8]{1,0:T(4,128)S(1)}, s32[3,8]{1,0:T(4,128)}, u32[]{:S(2)}) copy-start(s32[3,8]{1,0:T(4,128)} %coords_ref.1) | copy-start | bytes 292
  23.8 5.5 %copy-start = (bf16[16,8,2048]{2,1,0:T(8,128)(2,1)S(1)}, bf16[16,8,2048]{2,1,0:T(8,128)(2,1)}, u32[]{:S(2)}) copy-start(bf16[16,8,2048]{2,1,0:T(8,128)(2,1)} %key.1.fresh_ref) | copy-start | bytes 1572868
  23.8 14.8 %collective-permute-start.6 = (bf16[8,4224]{1,0:T(8,128)(2,1)S(1)}, bf16[8,4224]{1,0:T(8,128)(2,1)S(1)}, u32[]{:S(2)}, u32[]{:S(2)}) collective-permute-start(bf16[8,4224]{1,0:T(8,128)(2,1)S(1)} %get-tuple-element.45), channel_id=1, source_target_pairs={{0,8},{1,9},{2,10},{3,11},{4,12},{5,13},{6,14},{7,15},{8,0},{9,1},... | collective-permute-start | bytes 202760 | tf_op jit(solution)/shard_map/ppermute | solution.py:287
  26.6 12.0 %collective-permute-start.7 = (bf16[8,4224]{1,0:T(8,128)(2,1)S(1)}, bf16[8,4224]{1,0:T(8,128)(2,1)S(1)}, u32[]{:S(2)}, u32[]{:S(2)}) collective-permute-start(bf16[8,4224]{1,0:T(8,128)(2,1)S(1)} %get-tuple-element.46), channel_id=1, source_target_pairs={{0,12},{1,13},{2,14},{3,15},{4,8},{5,9},{6,10},{7,11},{8,4},{9,5},... | collective-permute-start | bytes 202760 | tf_op jit(solution)/shard_map/ppermute | solution.py:287
  28.1 10.5 %collective-permute-start.8 = (bf16[8,4224]{1,0:T(8,128)(2,1)S(1)}, bf16[8,4224]{1,0:T(8,128)(2,1)S(1)}, u32[]{:S(2)}, u32[]{:S(2)}) collective-permute-start(bf16[8,4224]{1,0:T(8,128)(2,1)S(1)} %get-tuple-element.47), channel_id=1, source_target_pairs={{0,4},{1,5},{2,6},{3,7},{4,0},{5,1},{6,2},{7,3},{8,12},{9,13},{10,... | collective-permute-start | bytes 202760 | tf_op jit(solution)/shard_map/ppermute | solution.py:287

commit v18 on v17

--- a/solution.py
+++ b/solution.py
@@ -314,7 +314,7 @@
             body,
             name=name,
             compiler_params=pltpu.CompilerParams(vmem_limit_bytes=limit * MIB),
-            cost_estimate=pl.CostEstimate(flops=0, bytes_accessed=cost, transcendentals=0),
+            cost_estimate=pl.CostEstimate(flops=cost, bytes_accessed=0, transcendentals=0),
             **kwargs,
         )
 
@@ -354,12 +354,13 @@
             pltpu.SemaphoreType.DMA((4 + videos,)),
         ],
     )(keys, values, gains[1], coords)
-    fresh_sent, query_raw = lax.optimization_barrier((fresh, query_raw))
-    cached = lax.all_to_all(fresh_sent, "patch", split_axis=0, concat_axis=0, tiled=True)
+    cached = lax.all_to_all(fresh, "patch", split_axis=0, concat_axis=0, tiled=True)
+    query_raw, pieces, fresh = lax.optimization_barrier((query_raw, pieces, fresh))
     query_got = kernel(
         turn_kernel,
         "turn",
         16,
+        cost=10**12,
         out_shape=jax.ShapeDtypeStruct(queries.shape, BF16),
         in_specs=[VMEM] * (1 + videos),
         out_specs=VMEM,

time: 40.1 us -> 38.8 us (0.968)
  the two profiles are of different devices: /device:TPU:0 before, /device:TPU:9 now
where the time goes in v18:
time: 38.8 us; the launch traced here: 38.3 us
  starting transfers between devices  15.8 us (41%)
  Pallas kernels  11.6 us (30%)
  waiting for transfers between devices  8.48 us (22%)
  local copies, waits for them, and re-layouts  1.62 us (4%)
  between operations  0.82 us (2%)
    ppermute x9, starting transfers between devices, permuted(): lax.ppermute(array, 'patch', [(i, i ^ offset) for i in range(patches)])  9.76 us
    all_to_all x1, starting transfers between devices, local(): lax.all_to_all(fresh, 'patch', split_axis=0, concat_axis=0, tiled=True)  6.02 us
    all_to_all x1, waiting for transfers between devices, local(): lax.all_to_all(fresh, 'patch', split_axis=0, concat_axis=0, tiled=True)  5.97 us
    ppermute x9, waiting for transfers between devices, permuted(): lax.ppermute(array, 'patch', [(i, i ^ offset) for i in range(patches)])  2.51 us
    pallas_call x1, Pallas kernels, local(): kernel(key_kernel, 'key', 56, out_shape=jax.ShapeDtypeStruct((patches, to...  2.39 us
    pallas_call x1, Pallas kernels, local(): kernel(cache_kernel, 'cache', 16, out_shape=jax.ShapeDtypeStruct((pairs_h...  1.89 us
    pallas_call x1, Pallas kernels, local(): kernel(functools.partial(lay_kernel, groups), 'lay', 56, out_shape=[jax.S...  1.66 us
    unnamed x16, local copies, waits for them, and re-layouts  1.62 us
  transfers between devices with their start and end apart: 10, of which 3 were waited for; matrix products, arithmetic and copies ran while one was open for 0% of the time, Pallas kernels for 23%

profile of v18, /device:TPU:9, one launch (start us, length us, event | category | flops | bytes accessed | tf_op | source)
XLA Modules:
  0.0 38.3 jit_solution(16323890173291405359)
XLA Ops:
  0.6 1.7 %lay.1 = (bf16[8,4224]{1,0:T(8,128)(2,1)}, bf16[8,4224]{1,0:T(8,128)(2,1)}, bf16[8,4224]{1,0:T(8,128)(2,1)}, bf16[8,4224]{1,0:T(8,128)(2,1)}) custom-call(bf16[4,8,4096]{2,1,0:T(8,128)(2,1)} %q_ref, s32[3,8]{1,0:T(4,128)} %coords_ref.1), custom_call_target="tpu_custom_call" | custom-call | tf_op jit(solution)/shard_map/lay/pallas_call | solution.py:322
  2.3 1.3 %collective-permute-start.3 = (bf16[8,128,256]{2,1,0:T(8,128)(2,1)}, bf16[8,128,256]{2,1,0:T(8,128)(2,1)S(1)}, u32[]{:S(2)}, u32[]{:S(2)}) collective-permute-start(bf16[8,128,256]{2,1,0:T(8,128)(2,1)} %refs_0_), channel_id=1, source_target_pairs={{0,2},{1,3},{2,0},{3,1},{4,6},{5,7},{6,4},{7,5},{8,10},{9,11},{10,... | collective-permute-start | bytes 1572872 | tf_op jit(solution)/shard_map/ppermute | solution.py:287
  3.6 2.3 %collective-permute-start = (bf16[8,4224]{1,0:T(8,128)(2,1)}, bf16[8,4224]{1,0:T(8,128)(2,1)S(1)}, u32[]{:S(2)}, u32[]{:S(2)}) collective-permute-start(bf16[8,4224]{1,0:T(8,128)(2,1)} %get-tuple-element.30), channel_id=1, source_target_pairs={{0,8},{1,9},{2,10},{3,11},{4,12},{5,13},{6,14},{7,15},{8,0},{9,1},... | collective-permute-start | bytes 202760 | tf_op jit(solution)/shard_map/ppermute | solution.py:287
  5.9 0.0 collective-permute-start.1
  5.9 1.2 %collective-permute-start.2 = (bf16[8,4224]{1,0:T(8,128)(2,1)}, bf16[8,4224]{1,0:T(8,128)(2,1)S(1)}, u32[]{:S(2)}, u32[]{:S(2)}) collective-permute-start(bf16[8,4224]{1,0:T(8,128)(2,1)} %get-tuple-element.32), channel_id=1, source_target_pairs={{0,4},{1,5},{2,6},{3,7},{4,0},{5,1},{6,2},{7,3},{8,12},{9,13},{10,... | collective-permute-start | bytes 202760 | tf_op jit(solution)/shard_map/ppermute | solution.py:287
  7.1 2.4 %key.1.fresh_ref = bf16[16,8,2048]{2,1,0:T(8,128)(2,1)} custom-call(bf16[4,8,4096]{2,1,0:T(8,128)(2,1)} %k_hbm.1, bf16[4,8,4096]{2,1,0:T(8,128)(2,1)} %v_hbm.1, f32[1,4096]{1,0:T(1,128)} %bitcast.6, s32[3,8]{1,0:T(4,128)} %coords_ref.1), custom_call_target="tpu_custom_call" | custom-call | tf_op jit(solution)/shard_map/key/pallas_call | solution.py:341
  9.5 0.0 copy-start.6
  9.5 0.0 copy-start.7
  9.5 6.0 %all-to-all-start = ((bf16[16,8,2048]{2,1,0:T(8,128)(2,1)}), bf16[16,8,2048]{2,1,0:T(8,128)(2,1)}, u32[]{:S(2)}, u32[]{:S(2)}) async-start(bf16[16,8,2048]{2,1,0:T(8,128)(2,1)} %key.1.fresh_ref), calls=%async_computation | async-start | bytes 1048576 | tf_op jit(solution)/shard_map/all_to_all | solution.py:357
  15.6 0.0 collective-permute-done.refs_0_
  15.6 0.0 collective-permute-done.1.refs_1_
  15.6 0.0 collective-permute-done.2.refs_2_
  15.6 0.0 collective-permute-done.3.refs_2_
  15.6 0.0 copy-start.3
  15.6 0.0 copy-done.6
  15.6 0.0 copy-done.7
  15.6 0.0 copy-start.2
  15.6 0.7 %turn.1.query_ref = bf16[4,8,4096]{2,1,0:T(8,128)(2,1)S(1)} custom-call(f32[1,4096]{1,0:T(1,128)S(1)} %bitcast.3, bf16[8,4224]{1,0:T(8,128)(2,1)S(1)} %collective-permute-done.refs_0_, bf16[8,4224]{1,0:T(8,128)(2,1)S(1)} %collective-permute-done.1.refs_1_, bf16[8,4224]{1,0:T(8,128)(2,1)S(1)} %collective-permute-done.2.refs_2_, bf16[8,4224]{1,0:T(8,128)(2,1)S(1)} %copy-done.7), custom_call_target="tpu_custom_call" | custom-call | flops 999999995904 | tf_op jit(solution)/shard_map/turn/pallas_call | solution.py:359
  16.3 0.1 copy-done.3
  16.4 0.5 %copy-done.2 = bf16[8,128,256]{2,1,0:T(8,128)(2,1)S(1)} copy-done((bf16[8,128,256]{2,1,0:T(8,128)(2,1)S(1)}, bf16[8,128,256]{2,1,0:T(8,128)(2,1)}, u32[]{:S(2)}) %copy-start.2) | copy-done | bytes 524312
  16.9 1.3 %collective-permute-start.4 = (bf16[8,128,256]{2,1,0:T(8,128)(2,1)S(1)}, bf16[8,128,256]{2,1,0:T(8,128)(2,1)S(1)}, u32[]{:S(2)}, u32[]{:S(2)}) collective-permute-start(bf16[8,128,256]{2,1,0:T(8,128)(2,1)S(1)} %copy-done.2), channel_id=1, source_target_pairs={{0,1},{1,0},{2,3},{3,2},{4,5},{5,4},{6,7},{7,6},{8,9},{9,8},{10,11... | collective-permute-start | bytes 1572872 | tf_op jit(solution)/shard_map/ppermute | solution.py:287
  18.2 0.0 collective-permute-start.5
  18.2 2.3 %collective-permute-done.4.refs_1_ = bf16[8,128,256]{2,1,0:T(8,128)(2,1)S(1)} collective-permute-done((bf16[8,128,256]{2,1,0:T(8,128)(2,1)S(1)}, bf16[8,128,256]{2,1,0:T(8,128)(2,1)S(1)}, u32[]{:S(2)}, u32[]{:S(2)}) %collective-permute-start.4) | collective-permute-done | bytes 524320 | tf_op jit(solution)/shard_map/ppermute | solution.py:287
  20.4 0.2 collective-permute-done.5.refs_3_
  20.6 0.0 copy-start.4
  20.7 1.0 %copy-done.4 = bf16[8,128,256]{2,1,0:T(8,128)(2,1)S(1)} copy-done((bf16[8,128,256]{2,1,0:T(8,128)(2,1)S(1)}, bf16[8,128,256]{2,1,0:T(8,128)(2,1)}, u32[]{:S(2)}) %copy-start.4) | copy-done | bytes 524312
  21.7 1.5 %stale.1 = (bf16[8,4224]{1,0:T(8,128)(2,1)S(1)}, bf16[8,4224]{1,0:T(8,128)(2,1)S(1)}, bf16[8,4224]{1,0:T(8,128)(2,1)S(1)}, bf16[8,4224]{1,0:T(8,128)(2,1)S(1)}) custom-call(bf16[4,8,4096]{2,1,0:T(8,128)(2,1)S(1)} %turn.1.query_ref, bf16[8,128,256]{2,1,0:T(8,128)(2,1)S(1)} %copy-done.2, bf16[8,128,256]{2,1,0:T(8,128)(2,1)S(1)} %collective-permute-done.4.refs_1_, ...), custom_call_target="tpu_custom_call" | custom-call | tf_op jit(solution)/shard_map/stale/pallas_call | solution.py:372
  23.2 0.0 copy-start.1
  23.2 0.0 copy-start.5
  23.2 2.4 %collective-permute-start.6 = (bf16[8,4224]{1,0:T(8,128)(2,1)S(1)}, bf16[8,4224]{1,0:T(8,128)(2,1)S(1)}, u32[]{:S(2)}, u32[]{:S(2)}) collective-permute-start(bf16[8,4224]{1,0:T(8,128)(2,1)S(1)} %get-tuple-element.50), channel_id=1, source_target_pairs={{0,8},{1,9},{2,10},{3,11},{4,12},{5,13},{6,14},{7,15},{8,0},{9,1},... | collective-permute-start | bytes 202760 | tf_op jit(solution)/shard_map/ppermute | solution.py:287
  25.6 0.0 collective-permute-start.7
  25.6 1.3 %collective-permute-start.8 = (bf16[8,4224]{1,0:T(8,128)(2,1)S(1)}, bf16[8,4224]{1,0:T(8,128)(2,1)S(1)}, u32[]{:S(2)}, u32[]{:S(2)}) collective-permute-start(bf16[8,4224]{1,0:T(8,128)(2,1)S(1)} %get-tuple-element.52), channel_id=1, source_target_pairs={{0,4},{1,5},{2,6},{3,7},{4,0},{5,1},{6,2},{7,3},{8,12},{9,13},{10,... | collective-permute-start | bytes 202760 | tf_op jit(solution)/shard_map/ppermute | solution.py:287
  26.9 6.0 %all-to-all-done.got_ref = bf16[16,8,2048]{2,1,0:T(8,128)(2,1)} async-done(((bf16[16,8,2048]{2,1,0:T(8,128)(2,1)}), bf16[16,8,2048]{2,1,0:T(8,128)(2,1)}, u32[]{:S(2)}, u32[]{:S(2)}) %all-to-all-start) | async-done | bytes 524320 | tf_op jit(solution)/shard_map/all_to_all | solution.py:357
  32.8 1.9 %cache.1 = bf16[8,16,8,256]{3,2,1,0:T(8,128)(2,1)} custom-call(bf16[16,8,2048]{2,1,0:T(8,128)(2,1)} %all-to-all-done.got_ref), custom_call_target="tpu_custom_call" | custom-call | tf_op jit(solution)/shard_map/cache/pallas_call | solution.py:401
  34.7 0.0 copy-done.1
  34.7 0.0 copy-done.5
  34.7 0.0 copy-start
  34.8 1.2 %query.1.query_ref = bf16[4,8,4096]{2,1,0:T(8,128)(2,1)S(1)} custom-call(bf16[4,8,4096]{2,1,0:T(8,128)(2,1)S(1)} %copy-done.1, f32[1,4096]{1,0:T(1,128)S(1)} %bitcast.4, s32[3,8]{1,0:T(4,128)S(1)} %copy-done.5), custom_call_target="tpu_custom_call" | custom-call | tf_op jit(solution)/shard_map/query/pallas_call | solution.py:381
  36.0 0.0 copy-done
  36.0 1.1 %fresh.1 = (f32[4,8,4096]{2,1,0:T(8,128)S(1)}, f32[4,8,128]{2,1,0:T(8,128)S(1)}) custom-call(bf16[4,8,4096]{2,1,0:T(8,128)(2,1)S(1)} %query.1.query_ref, bf16[16,8,2048]{2,1,0:T(8,128)(2,1)S(1)} %copy-done), custom_call_target="tpu_custom_call" | custom-call | tf_op jit(solution)/shard_map/fresh/pallas_call | solution.py:390
  37.1 0.0 collective-permute-done.6.refs_0_
  37.1 0.0 collective-permute-done.7.refs_1_
  37.1 0.0 collective-permute-done.8.refs_2_
  37.1 1.2 %join.1 = bf16[4,8,4096]{2,1,0:T(8,128)(2,1)} custom-call(bf16[8,4224]{1,0:T(8,128)(2,1)S(1)} %collective-permute-done.6.refs_0_, bf16[8,4224]{1,0:T(8,128)(2,1)S(1)} %collective-permute-done.7.refs_1_, bf16[8,4224]{1,0:T(8,128)(2,1)S(1)} %collective-permute-done.8.refs_2_, bf16[8,4224]{1,0:T(8,128)(2,1)S(1)} %get-tuple-element.53.refs_3_, ...), custom_call_target="tpu_custom_call" | custom-call | tf_op jit(solution)/shard_map/join/pallas_call | solution.py:410
Async XLA Ops:
  2.3 13.3 %collective-permute-start.3 = (bf16[8,128,256]{2,1,0:T(8,128)(2,1)}, bf16[8,128,256]{2,1,0:T(8,128)(2,1)S(1)}, u32[]{:S(2)}, u32[]{:S(2)}) collective-permute-start(bf16[8,128,256]{2,1,0:T(8,128)(2,1)} %refs_0_), channel_id=1, source_target_pairs={{0,2},{1,3},{2,0},{3,1},{4,6},{5,7},{6,4},{7,5},{8,10},{9,11},{10,... | collective-permute-start | bytes 1572872 | tf_op jit(solution)/shard_map/ppermute | solution.py:287
  3.6 12.0 %collective-permute-start = (bf16[8,4224]{1,0:T(8,128)(2,1)}, bf16[8,4224]{1,0:T(8,128)(2,1)S(1)}, u32[]{:S(2)}, u32[]{:S(2)}) collective-permute-start(bf16[8,4224]{1,0:T(8,128)(2,1)} %get-tuple-element.30), channel_id=1, source_target_pairs={{0,8},{1,9},{2,10},{3,11},{4,12},{5,13},{6,14},{7,15},{8,0},{9,1},... | collective-permute-start | bytes 202760 | tf_op jit(solution)/shard_map/ppermute | solution.py:287
  5.9 9.7 %collective-permute-start.1 = (bf16[8,4224]{1,0:T(8,128)(2,1)}, bf16[8,4224]{1,0:T(8,128)(2,1)S(1)}, u32[]{:S(2)}, u32[]{:S(2)}) collective-permute-start(bf16[8,4224]{1,0:T(8,128)(2,1)} %get-tuple-element.31), channel_id=1, source_target_pairs={{0,12},{1,13},{2,14},{3,15},{4,8},{5,9},{6,10},{7,11},{8,4},{9,5},... | collective-permute-start | bytes 202760 | tf_op jit(solution)/shard_map/ppermute | solution.py:287
  5.9 9.7 %collective-permute-start.2 = (bf16[8,4224]{1,0:T(8,128)(2,1)}, bf16[8,4224]{1,0:T(8,128)(2,1)S(1)}, u32[]{:S(2)}, u32[]{:S(2)}) collective-permute-start(bf16[8,4224]{1,0:T(8,128)(2,1)} %get-tuple-element.32), channel_id=1, source_target_pairs={{0,4},{1,5},{2,6},{3,7},{4,0},{5,1},{6,2},{7,3},{8,12},{9,13},{10,... | collective-permute-start | bytes 202760 | tf_op jit(solution)/shard_map/ppermute | solution.py:287
  9.5 6.1 %copy-start.6 = (f32[4096]{0:T(1024)S(1)}, f32[4096]{0:T(1024)}, u32[]{:S(2)}) copy-start(f32[4096]{0:T(1024)} %param.10) | copy-start | bytes 49156
  9.5 6.1 %copy-start.7 = (bf16[8,4224]{1,0:T(8,128)(2,1)S(1)}, bf16[8,4224]{1,0:T(8,128)(2,1)}, u32[]{:S(2)}) copy-start(bf16[8,4224]{1,0:T(8,128)(2,1)} %get-tuple-element.41.refs_3_) | copy-start | bytes 202756
  9.5 23.3 %all-to-all-start = ((bf16[16,8,2048]{2,1,0:T(8,128)(2,1)}), bf16[16,8,2048]{2,1,0:T(8,128)(2,1)}, u32[]{:S(2)}, u32[]{:S(2)}) async-start(bf16[16,8,2048]{2,1,0:T(8,128)(2,1)} %key.1.fresh_ref), calls=%async_computation | async-start | bytes 1048576 | tf_op jit(solution)/shard_map/all_to_all | solution.py:357
  15.6 0.8 %copy-start.3 = (bf16[8,128,256]{2,1,0:T(8,128)(2,1)}, bf16[8,128,256]{2,1,0:T(8,128)(2,1)S(1)}, u32[]{:S(2)}) copy-start(bf16[8,128,256]{2,1,0:T(8,128)(2,1)S(1)} %collective-permute-done.3.refs_2_) | copy-start | bytes 1572868
  15.6 1.2 %copy-start.2 = (bf16[8,128,256]{2,1,0:T(8,128)(2,1)S(1)}, bf16[8,128,256]{2,1,0:T(8,128)(2,1)}, u32[]{:S(2)}) copy-start(bf16[8,128,256]{2,1,0:T(8,128)(2,1)} %refs_0_) | copy-start | bytes 1572868
  16.9 3.6 %collective-permute-start.4 = (bf16[8,128,256]{2,1,0:T(8,128)(2,1)S(1)}, bf16[8,128,256]{2,1,0:T(8,128)(2,1)S(1)}, u32[]{:S(2)}, u32[]{:S(2)}) collective-permute-start(bf16[8,128,256]{2,1,0:T(8,128)(2,1)S(1)} %copy-done.2), channel_id=1, source_target_pairs={{0,1},{1,0},{2,3},{3,2},{4,5},{5,4},{6,7},{7,6},{8,9},{9,8},{10,11... | collective-permute-start | bytes 1572872 | tf_op jit(solution)/shard_map/ppermute | solution.py:287
  18.2 2.5 %collective-permute-start.5 = (bf16[8,128,256]{2,1,0:T(8,128)(2,1)}, bf16[8,128,256]{2,1,0:T(8,128)(2,1)S(1)}, u32[]{:S(2)}, u32[]{:S(2)}) collective-permute-start(bf16[8,128,256]{2,1,0:T(8,128)(2,1)} %copy-done.3), channel_id=1, source_target_pairs={{0,1},{1,0},{2,3},{3,2},{4,5},{5,4},{6,7},{7,6},{8,9},{9,8},{10,11... | collective-permute-start | bytes 1572872 | tf_op jit(solution)/shard_map/ppermute | solution.py:287
  20.6 1.0 %copy-start.4 = (bf16[8,128,256]{2,1,0:T(8,128)(2,1)S(1)}, bf16[8,128,256]{2,1,0:T(8,128)(2,1)}, u32[]{:S(2)}) copy-start(bf16[8,128,256]{2,1,0:T(8,128)(2,1)} %copy-done.3) | copy-start | bytes 1572868
  23.2 11.5 %copy-start.1 = (bf16[4,8,4096]{2,1,0:T(8,128)(2,1)S(1)}, bf16[4,8,4096]{2,1,0:T(8,128)(2,1)}, u32[]{:S(2)}) copy-start(bf16[4,8,4096]{2,1,0:T(8,128)(2,1)} %q_ref) | copy-start | bytes 786436
  23.2 11.5 %copy-start.5 = (s32[3,8]{1,0:T(4,128)S(1)}, s32[3,8]{1,0:T(4,128)}, u32[]{:S(2)}) copy-start(s32[3,8]{1,0:T(4,128)} %coords_ref.1) | copy-start | bytes 292
  23.2 13.9 %collective-permute-start.6 = (bf16[8,4224]{1,0:T(8,128)(2,1)S(1)}, bf16[8,4224]{1,0:T(8,128)(2,1)S(1)}, u32[]{:S(2)}, u32[]{:S(2)}) collective-permute-start(bf16[8,4224]{1,0:T(8,128)(2,1)S(1)} %get-tuple-element.50), channel_id=1, source_target_pairs={{0,8},{1,9},{2,10},{3,11},{4,12},{5,13},{6,14},{7,15},{8,0},{9,1},... | collective-permute-start | bytes 202760 | tf_op jit(solution)/shard_map/ppermute | solution.py:287
  25.6 11.5 %collective-permute-start.7 = (bf16[8,4224]{1,0:T(8,128)(2,1)S(1)}, bf16[8,4224]{1,0:T(8,128)(2,1)S(1)}, u32[]{:S(2)}, u32[]{:S(2)}) collective-permute-start(bf16[8,4224]{1,0:T(8,128)(2,1)S(1)} %get-tuple-element.51), channel_id=1, source_target_pairs={{0,12},{1,13},{2,14},{3,15},{4,8},{5,9},{6,10},{7,11},{8,4},{9,5},... | collective-permute-start | bytes 202760 | tf_op jit(solution)/shard_map/ppermute | solution.py:287
  25.6 11.5 %collective-permute-start.8 = (bf16[8,4224]{1,0:T(8,128)(2,1)S(1)}, bf16[8,4224]{1,0:T(8,128)(2,1)S(1)}, u32[]{:S(2)}, u32[]{:S(2)}) collective-permute-start(bf16[8,4224]{1,0:T(8,128)(2,1)S(1)} %get-tuple-element.52), channel_id=1, source_target_pairs={{0,4},{1,5},{2,6},{3,7},{4,0},{5,1},{6,2},{7,3},{8,12},{9,13},{10,... | collective-permute-start | bytes 202760 | tf_op jit(solution)/shard_map/ppermute | solution.py:287
  34.7 1.2 %copy-start = (bf16[16,8,2048]{2,1,0:T(8,128)(2,1)S(1)}, bf16[16,8,2048]{2,1,0:T(8,128)(2,1)}, u32[]{:S(2)}) copy-start(bf16[16,8,2048]{2,1,0:T(8,128)(2,1)} %key.1.fresh_ref) | copy-start | bytes 1572868

commit v19 on v18

--- a/solution.py
+++ b/solution.py
@@ -84,14 +84,15 @@
         write.wait()
 
 
-def key_kernel(k_hbm, v_hbm, gain_hbm, coords_hbm, out_hbm, k_ref, v_ref, gain_ref, coords_ref, done_ref, sems):
+def key_kernel(k_hbm, gain_hbm, coords_hbm, out_hbm, k_ref, gain_ref, coords_ref, done_ref, sems):
     videos, tok_rows, width = k_hbm.shape
-    pairs = out_hbm.shape[2] // (2 * DH)
+    pairs = out_hbm.shape[2] // DH
     groups = out_hbm.shape[0] // videos
-    sources, places = (coords_hbm, k_hbm, gain_hbm, v_hbm), (coords_ref, k_ref, gain_ref, v_ref)
     reads = [
         pltpu.make_async_copy(source, place, sems.at[i])
-        for i, (source, place) in enumerate(zip(sources, places))
+        for i, (source, place) in enumerate(
+            ((coords_hbm, coords_ref), (k_hbm, k_ref), (gain_hbm, gain_ref))
+        )
     ]
     for read in reads:
         read.start()
@@ -101,13 +102,10 @@
     writes = []
     for video in range(videos):
         for head, y in normed_heads(k_ref[video].astype(F32), gain_ref, tables):
-            target, start = video * groups + head // pairs, head % pairs * 2 * DH
-            done_ref[target, :, start : start + DH] = y
-            done_ref[target, :, start + DH : start + 2 * DH] = v_ref[
-                video, :, head * DH : (head + 1) * DH
-            ]
+            start = head % pairs * DH
+            done_ref[video * groups + head // pairs, :, start : start + DH] = y
         part = pl.ds(video * groups, groups)
-        writes.append(pltpu.make_async_copy(done_ref.at[part], out_hbm.at[part], sems.at[4 + video]))
+        writes.append(pltpu.make_async_copy(done_ref.at[part], out_hbm.at[part], sems.at[3 + video]))
         writes[-1].start()
     for write in writes:
         write.wait()
@@ -144,7 +142,7 @@
     return jnp.concatenate(rows, axis=0).astype(BF16)
 
 
-def fresh_kernel(groups, videos, query_ref, fresh_ref, out_ref, log_ref):
+def fresh_kernel(groups, videos, query_ref, key_ref, value_ref, out_ref, log_ref):
     me = lax.axis_index("patch")
     own, mine = me // groups, me % groups
     queries = [query_ref.at[own ^ s] for s in range(videos)]
@@ -162,12 +160,13 @@
     for t in range(groups):
         lanes = pl.ds(pl.multiple_of((mine ^ t) * span, DH), span)
         query = stacked(queries, lanes)
-        fresh = stacked([fresh_ref.at[me ^ (s * groups) ^ t] for s in range(videos)], slice(None))
+        key = stacked([key_ref.at[me ^ (s * groups) ^ t] for s in range(videos)], slice(None))
+        value = stacked([value_ref.at[own ^ s] for s in range(videos)], lanes)
         scores = jnp.concatenate(
             [
                 lax.dot_general(
                     query[:, pair * DH : (pair + 1) * DH],
-                    fresh[:, 2 * pair * DH : (2 * pair + 1) * DH],
+                    key[:, pair * DH : (pair + 1) * DH],
                     TRANSPOSED,
                     preferred_element_type=F32,
                 )
@@ -181,7 +180,7 @@
             head = t * pairs + pair
             result = inverse[here] * jnp.dot(
                 weights[here],
-                fresh[:, (2 * pair + 1) * DH : (2 * pair + 2) * DH],
+                value[:, pair * DH : (pair + 1) * DH],
                 preferred_element_type=F32,
             )
             logs = jnp.where(lane == head, log[here], logs)
@@ -271,14 +270,13 @@
         copy.wait()
 
 
-def cache_kernel(got_ref, out_ref, sems):
+def cache_kernel(key_ref, value_ref, out_ref, sems):
     copies = []
     for pair in range(out_ref.shape[0]):
-        lanes = pl.ds(2 * pair * DH, 2 * DH)
-        copies.append(
-            pltpu.make_async_copy(got_ref.at[:, :, lanes], out_ref.at[pair], sems.at[pair])
-        )
-        copies[-1].start()
+        for part, source in enumerate((key_ref.at[:, :, pl.ds(pair * DH, DH)], value_ref.at[:, pair])):
+            target = out_ref.at[pair, :, :, pl.ds(part * DH, DH)]
+            copies.append(pltpu.make_async_copy(source, target, sems.at[part, pair]))
+            copies[-1].start()
     for copy in copies:
         copy.wait()
 
@@ -338,24 +336,28 @@
     bit = groups // 2
     pieces[bit] = permuted(stale_sent, bit, patches)
     query_raw = far_first(exchange([kept, *sent[1:]], groups, patches))
-    fresh = kernel(
+    value_sent = jnp.transpose(values.reshape(videos, tok_rows, width // DH, DH), (0, 2, 1, 3))
+    value_got = lax.all_to_all(
+        value_sent.reshape(patches, pairs_here, tok_rows, DH), "patch", split_axis=0, concat_axis=0, tiled=True
+    )
+    key = kernel(
         key_kernel,
         "key",
         56,
-        out_shape=jax.ShapeDtypeStruct((patches, tok_rows, 2 * pairs_here * DH), BF16),
-        in_specs=[HBM] * 4,
+        out_shape=jax.ShapeDtypeStruct((patches, tok_rows, pairs_here * DH), BF16),
+        in_specs=[HBM] * 3,
         out_specs=HBM,
         scratch_shapes=[
             pltpu.VMEM(keys.shape, BF16),
-            pltpu.VMEM(keys.shape, BF16),
             pltpu.VMEM((1, width), F32),
             pltpu.SMEM(coords.shape, jnp.int32),
-            pltpu.VMEM((patches, tok_rows, 2 * pairs_here * DH), BF16),
-            pltpu.SemaphoreType.DMA((4 + videos,)),
+            pltpu.VMEM((patches, tok_rows, pairs_here * DH), BF16),
+            pltpu.SemaphoreType.DMA((3 + videos,)),
         ],
-    )(keys, values, gains[1], coords)
-    cached = lax.all_to_all(fresh, "patch", split_axis=0, concat_axis=0, tiled=True)
-    query_raw, pieces, fresh = lax.optimization_barrier((query_raw, pieces, fresh))
+    )(keys, gains[1], coords)
+    key_sent, value_got = lax.optimization_barrier((key, value_got))
+    key_got = lax.all_to_all(key_sent, "patch", split_axis=0, concat_axis=0, tiled=True)
+    query_raw, pieces, key = lax.optimization_barrier((query_raw, pieces, key))
     query_got = kernel(
         turn_kernel,
         "turn",
@@ -377,7 +379,7 @@
         in_specs=[VMEM] * (1 + groups),
         out_specs=[VMEM] * videos,
     )(query_got, *[pieces[t] for t in range(groups)])
-    result, fresh_late, queries_late = lax.optimization_barrier((result, fresh, queries))
+    result, key_late, queries_late = lax.optimization_barrier((result, key, queries))
     query = kernel(
         query_kernel,
         "query",
@@ -395,18 +397,18 @@
             jax.ShapeDtypeStruct((videos, tok_rows, width), F32),
             jax.ShapeDtypeStruct((videos, tok_rows, DH), F32),
         ),
-        in_specs=[VMEM] * 2,
+        in_specs=[VMEM] * 3,
         out_specs=(VMEM, VMEM),
-    )(query, fresh_late)
+    )(query, key_late, values)
     next_cache = kernel(
         cache_kernel,
         "cache",
         16,
         out_shape=jax.ShapeDtypeStruct((pairs_here, patches, tok_rows, 2 * DH), BF16),
-        in_specs=[VMEM],
+        in_specs=[VMEM, VMEM],
         out_specs=HBM,
-        scratch_shapes=[pltpu.SemaphoreType.DMA((pairs_here,))],
-    )(cached)
+        scratch_shapes=[pltpu.SemaphoreType.DMA((2, pairs_here))],
+    )(key_got, value_got)
     attended = kernel(
         functools.partial(join_kernel, groups, videos),
         "join",

time: 38.8 us -> 45.6 us (1.18)
  starting transfers between devices: 15.8 us -> 21.6 us
  Pallas kernels: 11.6 us -> 12.5 us
  waiting for transfers between devices: 8.48 us -> 9.06 us
    all_to_all x1 -> x2, starting transfers between devices: 6.02 us -> 11 us  [the longest x1 5.88 us: local(): lax.all_to_all(value_sent.reshape(patches, pairs_here, tok_rows, DH), 'pa...]
    all_to_all x1 -> x2, waiting for transfers between devices: 5.97 us -> 9.03 us  [the longest x1 6.71 us: local(): lax.all_to_all(key_sent, 'patch', split_axis=0, concat_axis=0, tiled=True)]
    ppermute x9, waiting for transfers between devices: 2.51 us -> 0.03 us  [permuted(): lax.ppermute(array, 'patch', [(i, i ^ offset) for i in range(patches)])]
    pallas_call x1, Pallas kernels: 1.12 us -> 2.14 us  [local(): kernel(functools.partial(fresh_kernel, groups, videos), 'fresh', 16, out_...]
    ppermute x9, starting transfers between devices: 9.76 us -> 10.7 us  [permuted(): lax.ppermute(array, 'patch', [(i, i ^ offset) for i in range(patches)])]
    unnamed x16 -> x14, local copies, waits for them, and re-layouts: 1.62 us -> 1.18 us
  transfers between devices with their start and end apart: 10 -> 11, of which waited for: 3 -> 2; matrix products, arithmetic and copies ran while one was open for 0% -> 0% of each run, Pallas kernels for 23% -> 21%
where the time goes in v19:
time: 45.6 us; the launch traced here: 45.2 us
  starting transfers between devices  21.6 us (47%)
  Pallas kernels  12.5 us (27%)
  waiting for transfers between devices  9.06 us (20%)
  local copies, waits for them, and re-layouts  1.18 us (3%)
  between operations  0.79 us (2%)
    ppermute x9, starting transfers between devices, permuted(): lax.ppermute(array, 'patch', [(i, i ^ offset) for i in range(patches)])  10.7 us
    all_to_all x1, waiting for transfers between devices, local(): lax.all_to_all(key_sent, 'patch', split_axis=0, concat_axis=0, tiled=True)  6.71 us
    all_to_all x1, starting transfers between devices, local(): lax.all_to_all(value_sent.reshape(patches, pairs_here, tok_rows, DH), 'pa...  5.88 us
    all_to_all x1, starting transfers between devices, local(): lax.all_to_all(key_sent, 'patch', split_axis=0, concat_axis=0, tiled=True)  5.08 us
    all_to_all x1, waiting for transfers between devices, local(): lax.all_to_all(value_sent.reshape(patches, pairs_here, tok_rows, DH), 'pa...  2.32 us
    pallas_call x1, Pallas kernels, local(): kernel(key_kernel, 'key', 56, out_shape=jax.ShapeDtypeStruct((patches, to...  2.3 us
    pallas_call x1, Pallas kernels, local(): kernel(functools.partial(fresh_kernel, groups, videos), 'fresh', 16, out_...  2.14 us
    pallas_call x1, Pallas kernels, local(): kernel(cache_kernel, 'cache', 16, out_shape=jax.ShapeDtypeStruct((pairs_h...  1.86 us
  transfers between devices with their start and end apart: 11, of which 2 were waited for; matrix products, arithmetic and copies ran while one was open for 0% of the time, Pallas kernels for 21%

profile of v19, /device:TPU:9, one launch (start us, length us, event | category | flops | bytes accessed | tf_op | source)
XLA Modules:
  0.0 45.2 jit_solution(3488966034470558469)
XLA Ops:
  0.6 1.7 %lay.1 = (bf16[8,4224]{1,0:T(8,128)(2,1)}, bf16[8,4224]{1,0:T(8,128)(2,1)}, bf16[8,4224]{1,0:T(8,128)(2,1)}, bf16[8,4224]{1,0:T(8,128)(2,1)}) custom-call(bf16[4,8,4096]{2,1,0:T(8,128)(2,1)} %q_ref, s32[3,8]{1,0:T(4,128)} %coords_ref.1), custom_call_target="tpu_custom_call" | custom-call | tf_op jit(solution)/shard_map/lay/pallas_call | solution.py:320
  2.3 1.3 %collective-permute-start.3 = (bf16[8,128,256]{2,1,0:T(8,128)(2,1)}, bf16[8,128,256]{2,1,0:T(8,128)(2,1)S(1)}, u32[]{:S(2)}, u32[]{:S(2)}) collective-permute-start(bf16[8,128,256]{2,1,0:T(8,128)(2,1)} %refs_0_), channel_id=1, source_target_pairs={{0,2},{1,3},{2,0},{3,1},{4,6},{5,7},{6,4},{7,5},{8,10},{9,11},{10,... | collective-permute-start | bytes 1572872 | tf_op jit(solution)/shard_map/ppermute | solution.py:285
  3.6 2.3 %collective-permute-start = (bf16[8,4224]{1,0:T(8,128)(2,1)}, bf16[8,4224]{1,0:T(8,128)(2,1)S(1)}, u32[]{:S(2)}, u32[]{:S(2)}) collective-permute-start(bf16[8,4224]{1,0:T(8,128)(2,1)} %get-tuple-element.32), channel_id=1, source_target_pairs={{0,8},{1,9},{2,10},{3,11},{4,12},{5,13},{6,14},{7,15},{8,0},{9,1},... | collective-permute-start | bytes 202760 | tf_op jit(solution)/shard_map/ppermute | solution.py:285
  5.9 0.0 collective-permute-start.1
  5.9 1.2 %collective-permute-start.2 = (bf16[8,4224]{1,0:T(8,128)(2,1)}, bf16[8,4224]{1,0:T(8,128)(2,1)S(1)}, u32[]{:S(2)}, u32[]{:S(2)}) collective-permute-start(bf16[8,4224]{1,0:T(8,128)(2,1)} %get-tuple-element.34), channel_id=1, source_target_pairs={{0,4},{1,5},{2,6},{3,7},{4,0},{5,1},{6,2},{7,3},{8,12},{9,13},{10,... | collective-permute-start | bytes 202760 | tf_op jit(solution)/shard_map/ppermute | solution.py:285
  7.1 5.9 %all-to-all-start = ((bf16[16,8,8,128]{3,2,1,0:T(8,128)(2,1)}), bf16[16,8,8,128]{3,2,1,0:T(8,128)(2,1)}, u32[]{:S(2)}, u32[]{:S(2)}) async-start(bf16[16,8,8,128]{3,2,1,0:T(8,128)(2,1)} %bitcast.4), calls=%async_computation | async-start | bytes 524288 | tf_op jit(solution)/shard_map/all_to_all | solution.py:340
  13.0 0.0 copy-start.5
  13.0 0.0 copy-start.6
  13.0 2.3 %key.1.key_ref = bf16[16,8,1024]{2,1,0:T(8,128)(2,1)} custom-call(bf16[4,8,4096]{2,1,0:T(8,128)(2,1)} %k_hbm.1, f32[1,4096]{1,0:T(1,128)} %bitcast.11, s32[3,8]{1,0:T(4,128)} %coords_ref.1), custom_call_target="tpu_custom_call" | custom-call | tf_op jit(solution)/shard_map/key/pallas_call | solution.py:343
  15.3 0.0 collective-permute-done.refs_0_
  15.3 0.0 collective-permute-done.1.refs_1_
  15.3 0.0 collective-permute-done.2.refs_2_
  15.4 0.0 collective-permute-done.3.refs_2_
  15.4 0.0 copy-start.2
  15.4 0.8 %copy-done.2 = bf16[8,128,256]{2,1,0:T(8,128)(2,1)} copy-done((bf16[8,128,256]{2,1,0:T(8,128)(2,1)}, bf16[8,128,256]{2,1,0:T(8,128)(2,1)S(1)}, u32[]{:S(2)}) %copy-start.2) | copy-done | bytes 524312
  16.2 0.0 copy-done.5
  16.2 0.0 copy-done.6
  16.2 0.0 copy-start.1
  16.2 0.0 copy-start.3
  16.2 0.7 %turn.1.query_ref = bf16[4,8,4096]{2,1,0:T(8,128)(2,1)S(1)} custom-call(f32[1,4096]{1,0:T(1,128)S(1)} %bitcast.8, bf16[8,4224]{1,0:T(8,128)(2,1)S(1)} %collective-permute-done.refs_0_, bf16[8,4224]{1,0:T(8,128)(2,1)S(1)} %collective-permute-done.1.refs_1_, bf16[8,4224]{1,0:T(8,128)(2,1)S(1)} %collective-permute-done.2.refs_2_, bf16[8,4224]{1,0:T(8,128)(2,1)S(1)} %copy-done.6), custom_call_target="tpu_custom_call" | custom-call | flops 999999995904 | tf_op jit(solution)/shard_map/turn/pallas_call | solution.py:361
  16.8 0.4 copy-done.1
  17.2 2.1 %collective-permute-start.4 = (bf16[8,128,256]{2,1,0:T(8,128)(2,1)S(1)}, bf16[8,128,256]{2,1,0:T(8,128)(2,1)S(1)}, u32[]{:S(2)}, u32[]{:S(2)}) collective-permute-start(bf16[8,128,256]{2,1,0:T(8,128)(2,1)S(1)} %copy-done.1), channel_id=1, source_target_pairs={{0,1},{1,0},{2,3},{3,2},{4,5},{5,4},{6,7},{7,6},{8,9},{9,8},{10,11... | collective-permute-start | bytes 1572872 | tf_op jit(solution)/shard_map/ppermute | solution.py:285
  19.3 0.0 copy-done.3
  19.3 0.2 collective-permute-start.5
  19.5 2.3 %all-to-all-done.value_ref = bf16[16,8,8,128]{3,2,1,0:T(8,128)(2,1)} async-done(((bf16[16,8,8,128]{3,2,1,0:T(8,128)(2,1)}), bf16[16,8,8,128]{3,2,1,0:T(8,128)(2,1)}, u32[]{:S(2)}, u32[]{:S(2)}) %all-to-all-start) | async-done | bytes 262176 | tf_op jit(solution)/shard_map/all_to_all | solution.py:340
  21.8 5.1 %all-to-all-start.1 = ((bf16[16,8,1024]{2,1,0:T(8,128)(2,1)}), bf16[16,8,1024]{2,1,0:T(8,128)(2,1)S(1)}, u32[]{:S(2)}, u32[]{:S(2)}) async-start(bf16[16,8,1024]{2,1,0:T(8,128)(2,1)} %key.1.key_ref), calls=%async_computation.1 | async-start | bytes 524288 | tf_op jit(solution)/shard_map/all_to_all | solution.py:359
  26.9 0.0 collective-permute-done.4.refs_1_
  26.9 0.0 collective-permute-done.5.refs_3_
  26.9 1.5 %stale.1 = (bf16[8,4224]{1,0:T(8,128)(2,1)S(1)}, bf16[8,4224]{1,0:T(8,128)(2,1)S(1)}, bf16[8,4224]{1,0:T(8,128)(2,1)S(1)}, bf16[8,4224]{1,0:T(8,128)(2,1)S(1)}) custom-call(bf16[4,8,4096]{2,1,0:T(8,128)(2,1)S(1)} %turn.1.query_ref, bf16[8,128,256]{2,1,0:T(8,128)(2,1)S(1)} %copy-done.1, bf16[8,128,256]{2,1,0:T(8,128)(2,1)S(1)} %collective-permute-done.4.refs_1_, ...), custom_call_target="tpu_custom_call" | custom-call | tf_op jit(solution)/shard_map/stale/pallas_call | solution.py:374
  28.4 0.0 copy-start
  28.4 0.0 copy-start.4
  28.4 2.2 %collective-permute-start.6 = (bf16[8,4224]{1,0:T(8,128)(2,1)S(1)}, bf16[8,4224]{1,0:T(8,128)(2,1)S(1)}, u32[]{:S(2)}, u32[]{:S(2)}) collective-permute-start(bf16[8,4224]{1,0:T(8,128)(2,1)S(1)} %get-tuple-element.52), channel_id=1, source_target_pairs={{0,8},{1,9},{2,10},{3,11},{4,12},{5,13},{6,14},{7,15},{8,0},{9,1},... | collective-permute-start | bytes 202760 | tf_op jit(solution)/shard_map/ppermute | solution.py:285
  30.6 0.0 collective-permute-start.7
  30.6 1.5 %collective-permute-start.8 = (bf16[8,4224]{1,0:T(8,128)(2,1)S(1)}, bf16[8,4224]{1,0:T(8,128)(2,1)S(1)}, u32[]{:S(2)}, u32[]{:S(2)}) collective-permute-start(bf16[8,4224]{1,0:T(8,128)(2,1)S(1)} %get-tuple-element.54), channel_id=1, source_target_pairs={{0,4},{1,5},{2,6},{3,7},{4,0},{5,1},{6,2},{7,3},{8,12},{9,13},{10,... | collective-permute-start | bytes 202760 | tf_op jit(solution)/shard_map/ppermute | solution.py:285
  32.0 6.7 %all-to-all-done.1.key_ref = bf16[16,8,1024]{2,1,0:T(8,128)(2,1)S(1)} async-done(((bf16[16,8,1024]{2,1,0:T(8,128)(2,1)}), bf16[16,8,1024]{2,1,0:T(8,128)(2,1)S(1)}, u32[]{:S(2)}, u32[]{:S(2)}) %all-to-all-start.1) | async-done | bytes 262176 | tf_op jit(solution)/shard_map/all_to_all | solution.py:359
  38.7 1.9 %cache.1 = bf16[8,16,8,256]{3,2,1,0:T(8,128)(2,1)} custom-call(bf16[16,8,1024]{2,1,0:T(8,128)(2,1)S(1)} %all-to-all-done.1.key_ref, bf16[16,8,8,128]{3,2,1,0:T(8,128)(2,1)} %all-to-all-done.value_ref), custom_call_target="tpu_custom_call" | custom-call | tf_op jit(solution)/shard_map/cache/pallas_call | solution.py:403
  40.6 0.0 copy-done
  40.6 0.0 copy-done.4
  40.6 1.2 %query.1.query_ref = bf16[4,8,4096]{2,1,0:T(8,128)(2,1)S(1)} custom-call(bf16[4,8,4096]{2,1,0:T(8,128)(2,1)S(1)} %copy-done, f32[1,4096]{1,0:T(1,128)S(1)} %bitcast.9, s32[3,8]{1,0:T(4,128)S(1)} %copy-done.4), custom_call_target="tpu_custom_call" | custom-call | tf_op jit(solution)/shard_map/query/pallas_call | solution.py:383
  41.9 2.1 %fresh.1 = (f32[4,8,4096]{2,1,0:T(8,128)S(1)}, f32[4,8,128]{2,1,0:T(8,128)S(1)}) custom-call(bf16[4,8,4096]{2,1,0:T(8,128)(2,1)S(1)} %query.1.query_ref, bf16[16,8,1024]{2,1,0:T(8,128)(2,1)} %key.1.key_ref, bf16[4,8,4096]{2,1,0:T(8,128)(2,1)} %value_ref.1), custom_call_target="tpu_custom_call" | custom-call | tf_op jit(solution)/shard_map/fresh/pallas_call | solution.py:392
  44.0 0.0 collective-permute-done.6.refs_0_
  44.0 0.0 collective-permute-done.7.refs_1_
  44.0 0.0 collective-permute-done.8.refs_2_
  44.0 1.2 %join.1 = bf16[4,8,4096]{2,1,0:T(8,128)(2,1)} custom-call(bf16[8,4224]{1,0:T(8,128)(2,1)S(1)} %collective-permute-done.6.refs_0_, bf16[8,4224]{1,0:T(8,128)(2,1)S(1)} %collective-permute-done.7.refs_1_, bf16[8,4224]{1,0:T(8,128)(2,1)S(1)} %collective-permute-done.8.refs_2_, bf16[8,4224]{1,0:T(8,128)(2,1)S(1)} %get-tuple-element.55.refs_3_, ...), custom_call_target="tpu_custom_call" | custom-call | tf_op jit(solution)/shard_map/join/pallas_call | solution.py:412
Async XLA Ops:
  2.3 13.1 %collective-permute-start.3 = (bf16[8,128,256]{2,1,0:T(8,128)(2,1)}, bf16[8,128,256]{2,1,0:T(8,128)(2,1)S(1)}, u32[]{:S(2)}, u32[]{:S(2)}) collective-permute-start(bf16[8,128,256]{2,1,0:T(8,128)(2,1)} %refs_0_), channel_id=1, source_target_pairs={{0,2},{1,3},{2,0},{3,1},{4,6},{5,7},{6,4},{7,5},{8,10},{9,11},{10,... | collective-permute-start | bytes 1572872 | tf_op jit(solution)/shard_map/ppermute | solution.py:285
  3.6 11.8 %collective-permute-start = (bf16[8,4224]{1,0:T(8,128)(2,1)}, bf16[8,4224]{1,0:T(8,128)(2,1)S(1)}, u32[]{:S(2)}, u32[]{:S(2)}) collective-permute-start(bf16[8,4224]{1,0:T(8,128)(2,1)} %get-tuple-element.32), channel_id=1, source_target_pairs={{0,8},{1,9},{2,10},{3,11},{4,12},{5,13},{6,14},{7,15},{8,0},{9,1},... | collective-permute-start | bytes 202760 | tf_op jit(solution)/shard_map/ppermute | solution.py:285
  5.9 9.5 %collective-permute-start.1 = (bf16[8,4224]{1,0:T(8,128)(2,1)}, bf16[8,4224]{1,0:T(8,128)(2,1)S(1)}, u32[]{:S(2)}, u32[]{:S(2)}) collective-permute-start(bf16[8,4224]{1,0:T(8,128)(2,1)} %get-tuple-element.33), channel_id=1, source_target_pairs={{0,12},{1,13},{2,14},{3,15},{4,8},{5,9},{6,10},{7,11},{8,4},{9,5},... | collective-permute-start | bytes 202760 | tf_op jit(solution)/shard_map/ppermute | solution.py:285
  5.9 9.5 %collective-permute-start.2 = (bf16[8,4224]{1,0:T(8,128)(2,1)}, bf16[8,4224]{1,0:T(8,128)(2,1)S(1)}, u32[]{:S(2)}, u32[]{:S(2)}) collective-permute-start(bf16[8,4224]{1,0:T(8,128)(2,1)} %get-tuple-element.34), channel_id=1, source_target_pairs={{0,4},{1,5},{2,6},{3,7},{4,0},{5,1},{6,2},{7,3},{8,12},{9,13},{10,... | collective-permute-start | bytes 202760 | tf_op jit(solution)/shard_map/ppermute | solution.py:285
  7.1 14.7 %all-to-all-start = ((bf16[16,8,8,128]{3,2,1,0:T(8,128)(2,1)}), bf16[16,8,8,128]{3,2,1,0:T(8,128)(2,1)}, u32[]{:S(2)}, u32[]{:S(2)}) async-start(bf16[16,8,8,128]{3,2,1,0:T(8,128)(2,1)} %bitcast.4), calls=%async_computation | async-start | bytes 524288 | tf_op jit(solution)/shard_map/all_to_all | solution.py:340
  13.0 3.2 %copy-start.5 = (f32[4096]{0:T(1024)S(1)}, f32[4096]{0:T(1024)}, u32[]{:S(2)}) copy-start(f32[4096]{0:T(1024)} %param.10) | copy-start | bytes 49156
  13.0 3.2 %copy-start.6 = (bf16[8,4224]{1,0:T(8,128)(2,1)S(1)}, bf16[8,4224]{1,0:T(8,128)(2,1)}, u32[]{:S(2)}) copy-start(bf16[8,4224]{1,0:T(8,128)(2,1)} %get-tuple-element.43.refs_3_) | copy-start | bytes 202756
  15.4 0.8 %copy-start.2 = (bf16[8,128,256]{2,1,0:T(8,128)(2,1)}, bf16[8,128,256]{2,1,0:T(8,128)(2,1)S(1)}, u32[]{:S(2)}) copy-start(bf16[8,128,256]{2,1,0:T(8,128)(2,1)S(1)} %collective-permute-done.3.refs_2_) | copy-start | bytes 1572868
  16.2 1.0 %copy-start.1 = (bf16[8,128,256]{2,1,0:T(8,128)(2,1)S(1)}, bf16[8,128,256]{2,1,0:T(8,128)(2,1)}, u32[]{:S(2)}) copy-start(bf16[8,128,256]{2,1,0:T(8,128)(2,1)} %refs_0_) | copy-start | bytes 1572868
  16.2 3.1 %copy-start.3 = (bf16[8,128,256]{2,1,0:T(8,128)(2,1)S(1)}, bf16[8,128,256]{2,1,0:T(8,128)(2,1)}, u32[]{:S(2)}) copy-start(bf16[8,128,256]{2,1,0:T(8,128)(2,1)} %copy-done.2) | copy-start | bytes 1572868
  17.2 9.7 %collective-permute-start.4 = (bf16[8,128,256]{2,1,0:T(8,128)(2,1)S(1)}, bf16[8,128,256]{2,1,0:T(8,128)(2,1)S(1)}, u32[]{:S(2)}, u32[]{:S(2)}) collective-permute-start(bf16[8,128,256]{2,1,0:T(8,128)(2,1)S(1)} %copy-done.1), channel_id=1, source_target_pairs={{0,1},{1,0},{2,3},{3,2},{4,5},{5,4},{6,7},{7,6},{8,9},{9,8},{10,11... | collective-permute-start | bytes 1572872 | tf_op jit(solution)/shard_map/ppermute | solution.py:285
  19.3 7.6 %collective-permute-start.5 = (bf16[8,128,256]{2,1,0:T(8,128)(2,1)S(1)}, bf16[8,128,256]{2,1,0:T(8,128)(2,1)S(1)}, u32[]{:S(2)}, u32[]{:S(2)}) collective-permute-start(bf16[8,128,256]{2,1,0:T(8,128)(2,1)S(1)} %copy-done.3), channel_id=1, source_target_pairs={{0,1},{1,0},{2,3},{3,2},{4,5},{5,4},{6,7},{7,6},{8,9},{9,8},{10,11... | collective-permute-start | bytes 1572872 | tf_op jit(solution)/shard_map/ppermute | solution.py:285
  21.8 17.0 %all-to-all-start.1 = ((bf16[16,8,1024]{2,1,0:T(8,128)(2,1)}), bf16[16,8,1024]{2,1,0:T(8,128)(2,1)S(1)}, u32[]{:S(2)}, u32[]{:S(2)}) async-start(bf16[16,8,1024]{2,1,0:T(8,128)(2,1)} %key.1.key_ref), calls=%async_computation.1 | async-start | bytes 524288 | tf_op jit(solution)/shard_map/all_to_all | solution.py:359
  28.4 12.2 %copy-start = (bf16[4,8,4096]{2,1,0:T(8,128)(2,1)S(1)}, bf16[4,8,4096]{2,1,0:T(8,128)(2,1)}, u32[]{:S(2)}) copy-start(bf16[4,8,4096]{2,1,0:T(8,128)(2,1)} %q_ref) | copy-start | bytes 786436
  28.4 12.2 %copy-start.4 = (s32[3,8]{1,0:T(4,128)S(1)}, s32[3,8]{1,0:T(4,128)}, u32[]{:S(2)}) copy-start(s32[3,8]{1,0:T(4,128)} %coords_ref.1) | copy-start | bytes 292
  28.4 15.6 %collective-permute-start.6 = (bf16[8,4224]{1,0:T(8,128)(2,1)S(1)}, bf16[8,4224]{1,0:T(8,128)(2,1)S(1)}, u32[]{:S(2)}, u32[]{:S(2)}) collective-permute-start(bf16[8,4224]{1,0:T(8,128)(2,1)S(1)} %get-tuple-element.52), channel_id=1, source_target_pairs={{0,8},{1,9},{2,10},{3,11},{4,12},{5,13},{6,14},{7,15},{8,0},{9,1},... | collective-permute-start | bytes 202760 | tf_op jit(solution)/shard_map/ppermute | solution.py:285
  30.6 13.5 %collective-permute-start.7 = (bf16[8,4224]{1,0:T(8,128)(2,1)S(1)}, bf16[8,4224]{1,0:T(8,128)(2,1)S(1)}, u32[]{:S(2)}, u32[]{:S(2)}) collective-permute-start(bf16[8,4224]{1,0:T(8,128)(2,1)S(1)} %get-tuple-element.53), channel_id=1, source_target_pairs={{0,12},{1,13},{2,14},{3,15},{4,8},{5,9},{6,10},{7,11},{8,4},{9,5},... | collective-permute-start | bytes 202760 | tf_op jit(solution)/shard_map/ppermute | solution.py:285
  30.6 13.5 %collective-permute-start.8 = (bf16[8,4224]{1,0:T(8,128)(2,1)S(1)}, bf16[8,4224]{1,0:T(8,128)(2,1)S(1)}, u32[]{:S(2)}, u32[]{:S(2)}) collective-permute-start(bf16[8,4224]{1,0:T(8,128)(2,1)S(1)} %get-tuple-element.54), channel_id=1, source_target_pairs={{0,4},{1,5},{2,6},{3,7},{4,0},{5,1},{6,2},{7,3},{8,12},{9,13},{10,... | collective-permute-start | bytes 202760 | tf_op jit(solution)/shard_map/ppermute | solution.py:285

commit v20 on v18

--- a/solution.py
+++ b/solution.py
@@ -398,6 +398,7 @@
         in_specs=[VMEM] * 2,
         out_specs=(VMEM, VMEM),
     )(query, fresh_late)
+    fresh_sum, cached = lax.optimization_barrier((fresh_sum, cached))
     next_cache = kernel(
         cache_kernel,
         "cache",

time: 38.8 us -> 38.1 us (0.982)
  the two profiles are of different devices: /device:TPU:9 before, /device:TPU:0 now
where the time goes in v20:
time: 38.1 us; the launch traced here: 37.6 us
  starting transfers between devices  16.6 us (44%)
  Pallas kernels  11.6 us (30%)
  waiting for transfers between devices  7 us (18%)
  local copies, waits for them, and re-layouts  1.64 us (4%)
  between operations  0.74 us (2%)
    ppermute x9, starting transfers between devices, permuted(): lax.ppermute(array, 'patch', [(i, i ^ offset) for i in range(patches)])  12.1 us
    ppermute x9, waiting for transfers between devices, permuted(): lax.ppermute(array, 'patch', [(i, i ^ offset) for i in range(patches)])  6.54 us
    all_to_all x1, starting transfers between devices, local(): lax.all_to_all(fresh, 'patch', split_axis=0, concat_axis=0, tiled=True)  4.5 us
    pallas_call x1, Pallas kernels, local(): kernel(key_kernel, 'key', 56, out_shape=jax.ShapeDtypeStruct((patches, to...  2.39 us
    pallas_call x1, Pallas kernels, local(): kernel(cache_kernel, 'cache', 16, out_shape=jax.ShapeDtypeStruct((pairs_h...  1.89 us
    pallas_call x1, Pallas kernels, local(): kernel(functools.partial(lay_kernel, groups), 'lay', 56, out_shape=[jax.S...  1.66 us
    unnamed x16, local copies, waits for them, and re-layouts  1.64 us
    pallas_call x1, Pallas kernels, local(): kernel(functools.partial(stale_kernel, groups, videos), 'stale', 32, out_...  1.52 us
  transfers between devices with their start and end apart: 10, of which 5 were waited for; matrix products, arithmetic and copies ran while one was open for 0% of the time, Pallas kernels for 23%

profile of v20, /device:TPU:0, one launch (start us, length us, event | category | flops | bytes accessed | tf_op | source)
XLA Modules:
  0.0 37.6 jit_solution(11824021523437084339)
XLA Ops:
  0.6 1.7 %lay.1 = (bf16[8,4224]{1,0:T(8,128)(2,1)}, bf16[8,4224]{1,0:T(8,128)(2,1)}, bf16[8,4224]{1,0:T(8,128)(2,1)}, bf16[8,4224]{1,0:T(8,128)(2,1)}) custom-call(bf16[4,8,4096]{2,1,0:T(8,128)(2,1)} %q_ref, s32[3,8]{1,0:T(4,128)} %coords_ref.1), custom_call_target="tpu_custom_call" | custom-call | tf_op jit(solution)/shard_map/lay/pallas_call | solution.py:322
  2.3 3.0 %collective-permute-start.3 = (bf16[8,128,256]{2,1,0:T(8,128)(2,1)}, bf16[8,128,256]{2,1,0:T(8,128)(2,1)S(1)}, u32[]{:S(2)}, u32[]{:S(2)}) collective-permute-start(bf16[8,128,256]{2,1,0:T(8,128)(2,1)} %refs_0_), channel_id=1, source_target_pairs={{0,2},{1,3},{2,0},{3,1},{4,6},{5,7},{6,4},{7,5},{8,10},{9,11},{10,... | collective-permute-start | bytes 1572872 | tf_op jit(solution)/shard_map/ppermute | solution.py:287
  5.3 2.6 %collective-permute-start = (bf16[8,4224]{1,0:T(8,128)(2,1)}, bf16[8,4224]{1,0:T(8,128)(2,1)S(1)}, u32[]{:S(2)}, u32[]{:S(2)}) collective-permute-start(bf16[8,4224]{1,0:T(8,128)(2,1)} %get-tuple-element.32), channel_id=1, source_target_pairs={{0,8},{1,9},{2,10},{3,11},{4,12},{5,13},{6,14},{7,15},{8,0},{9,1},... | collective-permute-start | bytes 202760 | tf_op jit(solution)/shard_map/ppermute | solution.py:287
  7.9 1.3 %collective-permute-start.1 = (bf16[8,4224]{1,0:T(8,128)(2,1)}, bf16[8,4224]{1,0:T(8,128)(2,1)S(1)}, u32[]{:S(2)}, u32[]{:S(2)}) collective-permute-start(bf16[8,4224]{1,0:T(8,128)(2,1)} %get-tuple-element.33), channel_id=1, source_target_pairs={{0,12},{1,13},{2,14},{3,15},{4,8},{5,9},{6,10},{7,11},{8,4},{9,5},... | collective-permute-start | bytes 202760 | tf_op jit(solution)/shard_map/ppermute | solution.py:287
  9.2 0.2 collective-permute-start.2
  9.5 2.4 %key.1.fresh_ref = bf16[16,8,2048]{2,1,0:T(8,128)(2,1)} custom-call(bf16[4,8,4096]{2,1,0:T(8,128)(2,1)} %k_hbm.1, bf16[4,8,4096]{2,1,0:T(8,128)(2,1)} %v_hbm.1, f32[1,4096]{1,0:T(1,128)} %bitcast.6, s32[3,8]{1,0:T(4,128)} %coords_ref.1), custom_call_target="tpu_custom_call" | custom-call | tf_op jit(solution)/shard_map/key/pallas_call | solution.py:341
  11.9 0.0 copy-start.6
  11.9 0.0 copy-start.7
  11.9 4.5 %all-to-all-start = ((bf16[16,8,2048]{2,1,0:T(8,128)(2,1)}), bf16[16,8,2048]{2,1,0:T(8,128)(2,1)}, u32[]{:S(2)}, u32[]{:S(2)}) async-start(bf16[16,8,2048]{2,1,0:T(8,128)(2,1)} %key.1.fresh_ref), calls=%async_computation | async-start | bytes 1048576 | tf_op jit(solution)/shard_map/all_to_all | solution.py:357
  16.4 0.0 collective-permute-done.refs_0_
  16.4 0.0 collective-permute-done.1.refs_1_
  16.4 0.0 collective-permute-done.2.refs_2_
  16.4 1.0 %collective-permute-done.3.refs_2_ = bf16[8,128,256]{2,1,0:T(8,128)(2,1)S(1)} collective-permute-done((bf16[8,128,256]{2,1,0:T(8,128)(2,1)}, bf16[8,128,256]{2,1,0:T(8,128)(2,1)S(1)}, u32[]{:S(2)}, u32[]{:S(2)}) %collective-permute-start.3) | collective-permute-done | bytes 524320 | tf_op jit(solution)/shard_map/ppermute | solution.py:287
  17.4 0.0 copy-start.3
  17.4 0.0 copy-done.6
  17.4 0.0 copy-done.7
  17.4 0.0 copy-start.2
  17.5 0.7 %turn.1.query_ref = bf16[4,8,4096]{2,1,0:T(8,128)(2,1)S(1)} custom-call(f32[1,4096]{1,0:T(1,128)S(1)} %bitcast.3, bf16[8,4224]{1,0:T(8,128)(2,1)S(1)} %collective-permute-done.refs_0_, bf16[8,4224]{1,0:T(8,128)(2,1)S(1)} %collective-permute-done.1.refs_1_, bf16[8,4224]{1,0:T(8,128)(2,1)S(1)} %collective-permute-done.2.refs_2_, bf16[8,4224]{1,0:T(8,128)(2,1)S(1)} %copy-done.7), custom_call_target="tpu_custom_call" | custom-call | flops 999999995904 | tf_op jit(solution)/shard_map/turn/pallas_call | solution.py:359
  18.1 0.1 copy-done.3
  18.2 0.4 %copy-done.2 = bf16[8,128,256]{2,1,0:T(8,128)(2,1)S(1)} copy-done((bf16[8,128,256]{2,1,0:T(8,128)(2,1)S(1)}, bf16[8,128,256]{2,1,0:T(8,128)(2,1)}, u32[]{:S(2)}) %copy-start.2) | copy-done | bytes 524312
  18.7 0.0 copy-start.1
  18.7 0.0 collective-permute-start.4
  18.7 0.5 %collective-permute-start.5 = (bf16[8,128,256]{2,1,0:T(8,128)(2,1)}, bf16[8,128,256]{2,1,0:T(8,128)(2,1)S(1)}, u32[]{:S(2)}, u32[]{:S(2)}) collective-permute-start(bf16[8,128,256]{2,1,0:T(8,128)(2,1)} %copy-done.3), channel_id=1, source_target_pairs={{0,1},{1,0},{2,3},{3,2},{4,5},{5,4},{6,7},{7,6},{8,9},{9,8},{10,11... | collective-permute-start | bytes 1572872 | tf_op jit(solution)/shard_map/ppermute | solution.py:287
  19.2 2.1 %collective-permute-done.4.refs_1_ = bf16[8,128,256]{2,1,0:T(8,128)(2,1)S(1)} collective-permute-done((bf16[8,128,256]{2,1,0:T(8,128)(2,1)S(1)}, bf16[8,128,256]{2,1,0:T(8,128)(2,1)S(1)}, u32[]{:S(2)}, u32[]{:S(2)}) %collective-permute-start.4) | collective-permute-done | bytes 524320 | tf_op jit(solution)/shard_map/ppermute | solution.py:287
  21.3 0.2 collective-permute-done.5.refs_3_
  21.6 0.0 copy-start.4
  21.6 1.0 %copy-done.4 = bf16[8,128,256]{2,1,0:T(8,128)(2,1)S(1)} copy-done((bf16[8,128,256]{2,1,0:T(8,128)(2,1)S(1)}, bf16[8,128,256]{2,1,0:T(8,128)(2,1)}, u32[]{:S(2)}) %copy-start.4) | copy-done | bytes 524312
  22.6 0.0 copy-start.5
  22.6 1.5 %stale.1 = (bf16[8,4224]{1,0:T(8,128)(2,1)S(1)}, bf16[8,4224]{1,0:T(8,128)(2,1)S(1)}, bf16[8,4224]{1,0:T(8,128)(2,1)S(1)}, bf16[8,4224]{1,0:T(8,128)(2,1)S(1)}) custom-call(bf16[4,8,4096]{2,1,0:T(8,128)(2,1)S(1)} %turn.1.query_ref, bf16[8,128,256]{2,1,0:T(8,128)(2,1)S(1)} %copy-done.2, bf16[8,128,256]{2,1,0:T(8,128)(2,1)S(1)} %collective-permute-done.4.refs_1_, ...), custom_call_target="tpu_custom_call" | custom-call | tf_op jit(solution)/shard_map/stale/pallas_call | solution.py:372
  24.1 0.0 copy-start
  24.1 2.9 %collective-permute-start.6 = (bf16[8,4224]{1,0:T(8,128)(2,1)S(1)}, bf16[8,4224]{1,0:T(8,128)(2,1)S(1)}, u32[]{:S(2)}, u32[]{:S(2)}) collective-permute-start(bf16[8,4224]{1,0:T(8,128)(2,1)S(1)} %get-tuple-element.52), channel_id=1, source_target_pairs={{0,8},{1,9},{2,10},{3,11},{4,12},{5,13},{6,14},{7,15},{8,0},{9,1},... | collective-permute-start | bytes 202760 | tf_op jit(solution)/shard_map/ppermute | solution.py:287
  27.0 1.3 %collective-permute-start.7 = (bf16[8,4224]{1,0:T(8,128)(2,1)S(1)}, bf16[8,4224]{1,0:T(8,128)(2,1)S(1)}, u32[]{:S(2)}, u32[]{:S(2)}) collective-permute-start(bf16[8,4224]{1,0:T(8,128)(2,1)S(1)} %get-tuple-element.53), channel_id=1, source_target_pairs={{0,12},{1,13},{2,14},{3,15},{4,8},{5,9},{6,10},{7,11},{8,4},{9,5},... | collective-permute-start | bytes 202760 | tf_op jit(solution)/shard_map/ppermute | solution.py:287
  28.3 0.2 collective-permute-start.8
  28.6 0.0 copy-done.1
  28.6 0.0 copy-done.5
  28.6 1.2 %query.1.query_ref = bf16[4,8,4096]{2,1,0:T(8,128)(2,1)S(1)} custom-call(bf16[4,8,4096]{2,1,0:T(8,128)(2,1)S(1)} %copy-done.1, f32[1,4096]{1,0:T(1,128)S(1)} %bitcast.4, s32[3,8]{1,0:T(4,128)S(1)} %copy-done.5), custom_call_target="tpu_custom_call" | custom-call | tf_op jit(solution)/shard_map/query/pallas_call | solution.py:381
  29.8 0.0 copy-done
  29.8 1.1 %fresh.1 = (f32[4,8,4096]{2,1,0:T(8,128)S(1)}, f32[4,8,128]{2,1,0:T(8,128)S(1)}) custom-call(bf16[4,8,4096]{2,1,0:T(8,128)(2,1)S(1)} %query.1.query_ref, bf16[16,8,2048]{2,1,0:T(8,128)(2,1)S(1)} %copy-done), custom_call_target="tpu_custom_call" | custom-call | tf_op jit(solution)/shard_map/fresh/pallas_call | solution.py:390
  30.9 0.5 %all-to-all-done.got_ref = bf16[16,8,2048]{2,1,0:T(8,128)(2,1)} async-done(((bf16[16,8,2048]{2,1,0:T(8,128)(2,1)}), bf16[16,8,2048]{2,1,0:T(8,128)(2,1)}, u32[]{:S(2)}, u32[]{:S(2)}) %all-to-all-start) | async-done | bytes 524320 | tf_op jit(solution)/shard_map/all_to_all | solution.py:357
  31.4 1.9 %cache.1 = bf16[8,16,8,256]{3,2,1,0:T(8,128)(2,1)} custom-call(bf16[16,8,2048]{2,1,0:T(8,128)(2,1)} %all-to-all-done.got_ref), custom_call_target="tpu_custom_call" | custom-call | tf_op jit(solution)/shard_map/cache/pallas_call | solution.py:402
  33.3 3.2 %collective-permute-done.6.refs_0_ = bf16[8,4224]{1,0:T(8,128)(2,1)S(1)} collective-permute-done((bf16[8,4224]{1,0:T(8,128)(2,1)S(1)}, bf16[8,4224]{1,0:T(8,128)(2,1)S(1)}, u32[]{:S(2)}, u32[]{:S(2)}) %collective-permute-start.6) | collective-permute-done | bytes 67616 | tf_op jit(solution)/shard_map/ppermute | solution.py:287
  36.4 0.0 collective-permute-done.7.refs_1_
  36.5 0.0 collective-permute-done.8.refs_2_
  36.5 1.2 %join.1 = bf16[4,8,4096]{2,1,0:T(8,128)(2,1)} custom-call(bf16[8,4224]{1,0:T(8,128)(2,1)S(1)} %collective-permute-done.6.refs_0_, bf16[8,4224]{1,0:T(8,128)(2,1)S(1)} %collective-permute-done.7.refs_1_, bf16[8,4224]{1,0:T(8,128)(2,1)S(1)} %collective-permute-done.8.refs_2_, bf16[8,4224]{1,0:T(8,128)(2,1)S(1)} %get-tuple-element.55.refs_3_, ...), custom_call_target="tpu_custom_call" | custom-call | tf_op jit(solution)/shard_map/join/pallas_call | solution.py:411
Async XLA Ops:
  2.3 15.1 %collective-permute-start.3 = (bf16[8,128,256]{2,1,0:T(8,128)(2,1)}, bf16[8,128,256]{2,1,0:T(8,128)(2,1)S(1)}, u32[]{:S(2)}, u32[]{:S(2)}) collective-permute-start(bf16[8,128,256]{2,1,0:T(8,128)(2,1)} %refs_0_), channel_id=1, source_target_pairs={{0,2},{1,3},{2,0},{3,1},{4,6},{5,7},{6,4},{7,5},{8,10},{9,11},{10,... | collective-permute-start | bytes 1572872 | tf_op jit(solution)/shard_map/ppermute | solution.py:287
  5.3 11.1 %collective-permute-start = (bf16[8,4224]{1,0:T(8,128)(2,1)}, bf16[8,4224]{1,0:T(8,128)(2,1)S(1)}, u32[]{:S(2)}, u32[]{:S(2)}) collective-permute-start(bf16[8,4224]{1,0:T(8,128)(2,1)} %get-tuple-element.32), channel_id=1, source_target_pairs={{0,8},{1,9},{2,10},{3,11},{4,12},{5,13},{6,14},{7,15},{8,0},{9,1},... | collective-permute-start | bytes 202760 | tf_op jit(solution)/shard_map/ppermute | solution.py:287
  7.9 8.5 %collective-permute-start.1 = (bf16[8,4224]{1,0:T(8,128)(2,1)}, bf16[8,4224]{1,0:T(8,128)(2,1)S(1)}, u32[]{:S(2)}, u32[]{:S(2)}) collective-permute-start(bf16[8,4224]{1,0:T(8,128)(2,1)} %get-tuple-element.33), channel_id=1, source_target_pairs={{0,12},{1,13},{2,14},{3,15},{4,8},{5,9},{6,10},{7,11},{8,4},{9,5},... | collective-permute-start | bytes 202760 | tf_op jit(solution)/shard_map/ppermute | solution.py:287
  9.2 7.2 %collective-permute-start.2 = (bf16[8,4224]{1,0:T(8,128)(2,1)}, bf16[8,4224]{1,0:T(8,128)(2,1)S(1)}, u32[]{:S(2)}, u32[]{:S(2)}) collective-permute-start(bf16[8,4224]{1,0:T(8,128)(2,1)} %get-tuple-element.34), channel_id=1, source_target_pairs={{0,4},{1,5},{2,6},{3,7},{4,0},{5,1},{6,2},{7,3},{8,12},{9,13},{10,... | collective-permute-start | bytes 202760 | tf_op jit(solution)/shard_map/ppermute | solution.py:287
  11.9 5.6 %copy-start.6 = (f32[4096]{0:T(1024)S(1)}, f32[4096]{0:T(1024)}, u32[]{:S(2)}) copy-start(f32[4096]{0:T(1024)} %param.10) | copy-start | bytes 49156
  11.9 5.6 %copy-start.7 = (bf16[8,4224]{1,0:T(8,128)(2,1)S(1)}, bf16[8,4224]{1,0:T(8,128)(2,1)}, u32[]{:S(2)}) copy-start(bf16[8,4224]{1,0:T(8,128)(2,1)} %get-tuple-element.43.refs_3_) | copy-start | bytes 202756
  11.9 19.5 %all-to-all-start = ((bf16[16,8,2048]{2,1,0:T(8,128)(2,1)}), bf16[16,8,2048]{2,1,0:T(8,128)(2,1)}, u32[]{:S(2)}, u32[]{:S(2)}) async-start(bf16[16,8,2048]{2,1,0:T(8,128)(2,1)} %key.1.fresh_ref), calls=%async_computation | async-start | bytes 1048576 | tf_op jit(solution)/shard_map/all_to_all | solution.py:357
  17.4 0.8 %copy-start.3 = (bf16[8,128,256]{2,1,0:T(8,128)(2,1)}, bf16[8,128,256]{2,1,0:T(8,128)(2,1)S(1)}, u32[]{:S(2)}) copy-start(bf16[8,128,256]{2,1,0:T(8,128)(2,1)S(1)} %collective-permute-done.3.refs_2_) | copy-start | bytes 1572868
  17.4 1.2 %copy-start.2 = (bf16[8,128,256]{2,1,0:T(8,128)(2,1)S(1)}, bf16[8,128,256]{2,1,0:T(8,128)(2,1)}, u32[]{:S(2)}) copy-start(bf16[8,128,256]{2,1,0:T(8,128)(2,1)} %refs_0_) | copy-start | bytes 1572868
  18.7 9.9 %copy-start.1 = (bf16[4,8,4096]{2,1,0:T(8,128)(2,1)S(1)}, bf16[4,8,4096]{2,1,0:T(8,128)(2,1)}, u32[]{:S(2)}) copy-start(bf16[4,8,4096]{2,1,0:T(8,128)(2,1)} %q_ref) | copy-start | bytes 786436
  18.7 2.6 %collective-permute-start.4 = (bf16[8,128,256]{2,1,0:T(8,128)(2,1)S(1)}, bf16[8,128,256]{2,1,0:T(8,128)(2,1)S(1)}, u32[]{:S(2)}, u32[]{:S(2)}) collective-permute-start(bf16[8,128,256]{2,1,0:T(8,128)(2,1)S(1)} %copy-done.2), channel_id=1, source_target_pairs={{0,1},{1,0},{2,3},{3,2},{4,5},{5,4},{6,7},{7,6},{8,9},{9,8},{10,11... | collective-permute-start | bytes 1572872 | tf_op jit(solution)/shard_map/ppermute | solution.py:287
  18.7 2.9 %collective-permute-start.5 = (bf16[8,128,256]{2,1,0:T(8,128)(2,1)}, bf16[8,128,256]{2,1,0:T(8,128)(2,1)S(1)}, u32[]{:S(2)}, u32[]{:S(2)}) collective-permute-start(bf16[8,128,256]{2,1,0:T(8,128)(2,1)} %copy-done.3), channel_id=1, source_target_pairs={{0,1},{1,0},{2,3},{3,2},{4,5},{5,4},{6,7},{7,6},{8,9},{9,8},{10,11... | collective-permute-start | bytes 1572872 | tf_op jit(solution)/shard_map/ppermute | solution.py:287
  21.6 1.0 %copy-start.4 = (bf16[8,128,256]{2,1,0:T(8,128)(2,1)S(1)}, bf16[8,128,256]{2,1,0:T(8,128)(2,1)}, u32[]{:S(2)}) copy-start(bf16[8,128,256]{2,1,0:T(8,128)(2,1)} %copy-done.3) | copy-start | bytes 1572868
  22.6 6.0 %copy-start.5 = (s32[3,8]{1,0:T(4,128)S(1)}, s32[3,8]{1,0:T(4,128)}, u32[]{:S(2)}) copy-start(s32[3,8]{1,0:T(4,128)} %coords_ref.1) | copy-start | bytes 292
  24.1 5.7 %copy-start = (bf16[16,8,2048]{2,1,0:T(8,128)(2,1)S(1)}, bf16[16,8,2048]{2,1,0:T(8,128)(2,1)}, u32[]{:S(2)}) copy-start(bf16[16,8,2048]{2,1,0:T(8,128)(2,1)} %key.1.fresh_ref) | copy-start | bytes 1572868
  24.1 12.3 %collective-permute-start.6 = (bf16[8,4224]{1,0:T(8,128)(2,1)S(1)}, bf16[8,4224]{1,0:T(8,128)(2,1)S(1)}, u32[]{:S(2)}, u32[]{:S(2)}) collective-permute-start(bf16[8,4224]{1,0:T(8,128)(2,1)S(1)} %get-tuple-element.52), channel_id=1, source_target_pairs={{0,8},{1,9},{2,10},{3,11},{4,12},{5,13},{6,14},{7,15},{8,0},{9,1},... | collective-permute-start | bytes 202760 | tf_op jit(solution)/shard_map/ppermute | solution.py:287
  27.0 9.5 %collective-permute-start.7 = (bf16[8,4224]{1,0:T(8,128)(2,1)S(1)}, bf16[8,4224]{1,0:T(8,128)(2,1)S(1)}, u32[]{:S(2)}, u32[]{:S(2)}) collective-permute-start(bf16[8,4224]{1,0:T(8,128)(2,1)S(1)} %get-tuple-element.53), channel_id=1, source_target_pairs={{0,12},{1,13},{2,14},{3,15},{4,8},{5,9},{6,10},{7,11},{8,4},{9,5},... | collective-permute-start | bytes 202760 | tf_op jit(solution)/shard_map/ppermute | solution.py:287
  28.3 8.1 %collective-permute-start.8 = (bf16[8,4224]{1,0:T(8,128)(2,1)S(1)}, bf16[8,4224]{1,0:T(8,128)(2,1)S(1)}, u32[]{:S(2)}, u32[]{:S(2)}) collective-permute-start(bf16[8,4224]{1,0:T(8,128)(2,1)S(1)} %get-tuple-element.54), channel_id=1, source_target_pairs={{0,4},{1,5},{2,6},{3,7},{4,0},{5,1},{6,2},{7,3},{8,12},{9,13},{10,... | collective-permute-start | bytes 202760 | tf_op jit(solution)/shard_map/ppermute | solution.py:287

commit v21 on v20

--- a/solution.py
+++ b/solution.py
@@ -360,7 +360,7 @@
         turn_kernel,
         "turn",
         16,
-        cost=10**12,
+        cost=10**11,
         out_shape=jax.ShapeDtypeStruct(queries.shape, BF16),
         in_specs=[VMEM] * (1 + videos),
         out_specs=VMEM,

time: 38.1 us -> 38 us (level)
  waiting for transfers between devices: 7 us -> 9.31 us
  local copies, waits for them, and re-layouts: 1.64 us -> 0.4 us
  Pallas kernels: 11.6 us -> 10.6 us
    all_to_all x1, waiting for transfers between devices: 0.45 us -> 1.79 us  [local(): lax.all_to_all(fresh, 'patch', split_axis=0, concat_axis=0, tiled=True)]
    unnamed x16 -> x12, local copies, waits for them, and re-layouts: 1.64 us -> 0.4 us
    pallas_call x1, Pallas kernels: 1.89 us -> 0.85 us  [local(): kernel(cache_kernel, 'cache', 16, out_shape=jax.ShapeDtypeStruct((pairs_h...]
    ppermute x9, waiting for transfers between devices: 6.54 us -> 7.52 us  [permuted(): lax.ppermute(array, 'patch', [(i, i ^ offset) for i in range(patches)])]
  transfers between devices with their start and end apart: 10 -> 10, of which waited for: 5 -> 5; matrix products, arithmetic and copies ran while one was open for 0% -> 0% of each run, Pallas kernels for 23% -> 21%
where the time goes in v21:
time: 38 us; the launch traced here: 37.6 us
  starting transfers between devices  16.6 us (44%)
  Pallas kernels  10.6 us (28%)
  waiting for transfers between devices  9.31 us (24%)
  between operations  0.74 us (2%)
  local copies, waits for them, and re-layouts  0.4 us (1%)
    ppermute x9, starting transfers between devices, permuted(): lax.ppermute(array, 'patch', [(i, i ^ offset) for i in range(patches)])  12.1 us
    ppermute x9, waiting for transfers between devices, permuted(): lax.ppermute(array, 'patch', [(i, i ^ offset) for i in range(patches)])  7.52 us
    all_to_all x1, starting transfers between devices, local(): lax.all_to_all(fresh, 'patch', split_axis=0, concat_axis=0, tiled=True)  4.45 us
    pallas_call x1, Pallas kernels, local(): kernel(key_kernel, 'key', 56, out_shape=jax.ShapeDtypeStruct((patches, to...  2.4 us
    all_to_all x1, waiting for transfers between devices, local(): lax.all_to_all(fresh, 'patch', split_axis=0, concat_axis=0, tiled=True)  1.79 us
    pallas_call x1, Pallas kernels, local(): kernel(functools.partial(lay_kernel, groups), 'lay', 56, out_shape=[jax.S...  1.64 us
    pallas_call x1, Pallas kernels, local(): kernel(functools.partial(stale_kernel, groups, videos), 'stale', 32, out_...  1.52 us
    pallas_call x1, Pallas kernels, local(): kernel(query_kernel, 'query', 16, out_shape=jax.ShapeDtypeStruct(queries....  1.22 us
  transfers between devices with their start and end apart: 10, of which 5 were waited for; matrix products, arithmetic and copies ran while one was open for 0% of the time, Pallas kernels for 21%

profile of v21, /device:TPU:0, one launch (start us, length us, event | category | flops | bytes accessed | tf_op | source)
XLA Modules:
  0.0 37.6 jit_solution(3193758204152835352)
XLA Ops:
  0.6 1.6 %lay.1 = (bf16[8,4224]{1,0:T(8,128)(2,1)}, bf16[8,4224]{1,0:T(8,128)(2,1)}, bf16[8,4224]{1,0:T(8,128)(2,1)}, bf16[8,4224]{1,0:T(8,128)(2,1)}) custom-call(bf16[4,8,4096]{2,1,0:T(8,128)(2,1)} %q_ref, s32[3,8]{1,0:T(4,128)} %coords_ref.1), custom_call_target="tpu_custom_call" | custom-call | tf_op jit(solution)/shard_map/lay/pallas_call | solution.py:322
  2.3 3.0 %collective-permute-start.3 = (bf16[8,128,256]{2,1,0:T(8,128)(2,1)}, bf16[8,128,256]{2,1,0:T(8,128)(2,1)S(1)}, u32[]{:S(2)}, u32[]{:S(2)}) collective-permute-start(bf16[8,128,256]{2,1,0:T(8,128)(2,1)} %refs_0_), channel_id=1, source_target_pairs={{0,2},{1,3},{2,0},{3,1},{4,6},{5,7},{6,4},{7,5},{8,10},{9,11},{10,... | collective-permute-start | bytes 1572872 | tf_op jit(solution)/shard_map/ppermute | solution.py:287
  5.3 2.6 %collective-permute-start = (bf16[8,4224]{1,0:T(8,128)(2,1)}, bf16[8,4224]{1,0:T(8,128)(2,1)S(1)}, u32[]{:S(2)}, u32[]{:S(2)}) collective-permute-start(bf16[8,4224]{1,0:T(8,128)(2,1)} %get-tuple-element.32), channel_id=1, source_target_pairs={{0,8},{1,9},{2,10},{3,11},{4,12},{5,13},{6,14},{7,15},{8,0},{9,1},... | collective-permute-start | bytes 202760 | tf_op jit(solution)/shard_map/ppermute | solution.py:287
  7.9 1.3 %collective-permute-start.1 = (bf16[8,4224]{1,0:T(8,128)(2,1)}, bf16[8,4224]{1,0:T(8,128)(2,1)S(1)}, u32[]{:S(2)}, u32[]{:S(2)}) collective-permute-start(bf16[8,4224]{1,0:T(8,128)(2,1)} %get-tuple-element.33), channel_id=1, source_target_pairs={{0,12},{1,13},{2,14},{3,15},{4,8},{5,9},{6,10},{7,11},{8,4},{9,5},... | collective-permute-start | bytes 202760 | tf_op jit(solution)/shard_map/ppermute | solution.py:287
  9.2 0.2 collective-permute-start.2
  9.4 2.4 %key.1.fresh_ref = bf16[16,8,2048]{2,1,0:T(8,128)(2,1)} custom-call(bf16[4,8,4096]{2,1,0:T(8,128)(2,1)} %k_hbm.1, bf16[4,8,4096]{2,1,0:T(8,128)(2,1)} %v_hbm.1, f32[1,4096]{1,0:T(1,128)} %bitcast.6, s32[3,8]{1,0:T(4,128)} %coords_ref.1), custom_call_target="tpu_custom_call" | custom-call | tf_op jit(solution)/shard_map/key/pallas_call | solution.py:341
  11.9 0.0 copy-start.4
  11.9 0.0 copy-start.5
  11.9 4.4 %all-to-all-start = ((bf16[16,8,2048]{2,1,0:T(8,128)(2,1)}), bf16[16,8,2048]{2,1,0:T(8,128)(2,1)S(1)}, u32[]{:S(2)}, u32[]{:S(2)}) async-start(bf16[16,8,2048]{2,1,0:T(8,128)(2,1)} %key.1.fresh_ref), calls=%async_computation | async-start | bytes 1048576 | tf_op jit(solution)/shard_map/all_to_all | solution.py:357
  16.3 0.0 collective-permute-done.refs_0_
  16.3 0.0 collective-permute-done.1.refs_1_
  16.4 0.0 collective-permute-done.2.refs_2_
  16.4 1.0 %collective-permute-done.3.refs_2_ = bf16[8,128,256]{2,1,0:T(8,128)(2,1)S(1)} collective-permute-done((bf16[8,128,256]{2,1,0:T(8,128)(2,1)}, bf16[8,128,256]{2,1,0:T(8,128)(2,1)S(1)}, u32[]{:S(2)}, u32[]{:S(2)}) %collective-permute-start.3) | collective-permute-done | bytes 524320 | tf_op jit(solution)/shard_map/ppermute | solution.py:287
  17.4 0.0 copy-done.4
  17.4 0.0 copy-done.5
  17.4 0.0 copy-start.2
  17.4 0.0 copy-start.3
  17.4 0.7 %turn.1.query_ref = bf16[4,8,4096]{2,1,0:T(8,128)(2,1)S(1)} custom-call(f32[1,4096]{1,0:T(1,128)S(1)} %bitcast.3, bf16[8,4224]{1,0:T(8,128)(2,1)S(1)} %collective-permute-done.refs_0_, bf16[8,4224]{1,0:T(8,128)(2,1)S(1)} %collective-permute-done.1.refs_1_, bf16[8,4224]{1,0:T(8,128)(2,1)S(1)} %collective-permute-done.2.refs_2_, bf16[8,4224]{1,0:T(8,128)(2,1)S(1)} %copy-done.5), custom_call_target="tpu_custom_call" | custom-call | flops 99999997952 | tf_op jit(solution)/shard_map/turn/pallas_call | solution.py:359
  18.1 0.4 copy-done.2
  18.5 0.0 copy-start.1
  18.5 0.0 collective-permute-start.4
  18.5 0.5 %collective-permute-start.5 = (bf16[8,128,256]{2,1,0:T(8,128)(2,1)S(1)}, bf16[8,128,256]{2,1,0:T(8,128)(2,1)S(1)}, u32[]{:S(2)}, u32[]{:S(2)}) collective-permute-start(bf16[8,128,256]{2,1,0:T(8,128)(2,1)S(1)} %collective-permute-done.3.refs_2_), channel_id=1, source_target_pairs={{0,1},{1,0},{2,3},{3,2},{4,5},{5,4},{6,7},{7,6},{8,9},{9,8},{10,11... | collective-permute-start | bytes 1572872 | tf_op jit(solution)/shard_map/ppermute | solution.py:287
  19.0 1.4 %collective-permute-done.4.refs_1_ = bf16[8,128,256]{2,1,0:T(8,128)(2,1)S(1)} collective-permute-done((bf16[8,128,256]{2,1,0:T(8,128)(2,1)S(1)}, bf16[8,128,256]{2,1,0:T(8,128)(2,1)S(1)}, u32[]{:S(2)}, u32[]{:S(2)}) %collective-permute-start.4) | collective-permute-done | bytes 524320 | tf_op jit(solution)/shard_map/ppermute | solution.py:287
  20.4 0.7 %collective-permute-done.5.refs_3_ = bf16[8,128,256]{2,1,0:T(8,128)(2,1)S(1)} collective-permute-done((bf16[8,128,256]{2,1,0:T(8,128)(2,1)S(1)}, bf16[8,128,256]{2,1,0:T(8,128)(2,1)S(1)}, u32[]{:S(2)}, u32[]{:S(2)}) %collective-permute-start.5) | collective-permute-done | bytes 524320 | tf_op jit(solution)/shard_map/ppermute | solution.py:287
  21.1 1.5 %stale.1 = (bf16[8,4224]{1,0:T(8,128)(2,1)S(1)}, bf16[8,4224]{1,0:T(8,128)(2,1)S(1)}, bf16[8,4224]{1,0:T(8,128)(2,1)S(1)}, bf16[8,4224]{1,0:T(8,128)(2,1)S(1)}) custom-call(bf16[4,8,4096]{2,1,0:T(8,128)(2,1)S(1)} %turn.1.query_ref, bf16[8,128,256]{2,1,0:T(8,128)(2,1)S(1)} %copy-done.2, bf16[8,128,256]{2,1,0:T(8,128)(2,1)S(1)} %collective-permute-done.4.refs_1_, ...), custom_call_target="tpu_custom_call" | custom-call | tf_op jit(solution)/shard_map/stale/pallas_call | solution.py:372
  22.6 0.0 copy-start
  22.6 2.9 %collective-permute-start.6 = (bf16[8,4224]{1,0:T(8,128)(2,1)S(1)}, bf16[8,4224]{1,0:T(8,128)(2,1)S(1)}, u32[]{:S(2)}, u32[]{:S(2)}) collective-permute-start(bf16[8,4224]{1,0:T(8,128)(2,1)S(1)} %get-tuple-element.52), channel_id=1, source_target_pairs={{0,8},{1,9},{2,10},{3,11},{4,12},{5,13},{6,14},{7,15},{8,0},{9,1},... | collective-permute-start | bytes 202760 | tf_op jit(solution)/shard_map/ppermute | solution.py:287
  25.5 1.3 %collective-permute-start.7 = (bf16[8,4224]{1,0:T(8,128)(2,1)S(1)}, bf16[8,4224]{1,0:T(8,128)(2,1)S(1)}, u32[]{:S(2)}, u32[]{:S(2)}) collective-permute-start(bf16[8,4224]{1,0:T(8,128)(2,1)S(1)} %get-tuple-element.53), channel_id=1, source_target_pairs={{0,12},{1,13},{2,14},{3,15},{4,8},{5,9},{6,10},{7,11},{8,4},{9,5},... | collective-permute-start | bytes 202760 | tf_op jit(solution)/shard_map/ppermute | solution.py:287
  26.9 0.2 collective-permute-start.8
  27.1 0.0 copy-done.3
  27.1 0.0 copy-done.1
  27.1 1.2 %query.1.query_ref = bf16[4,8,4096]{2,1,0:T(8,128)(2,1)S(1)} custom-call(bf16[4,8,4096]{2,1,0:T(8,128)(2,1)S(1)} %copy-done.1, f32[1,4096]{1,0:T(1,128)S(1)} %bitcast.4, s32[3,8]{1,0:T(4,128)S(1)} %copy-done.3), custom_call_target="tpu_custom_call" | custom-call | tf_op jit(solution)/shard_map/query/pallas_call | solution.py:381
  28.3 0.0 copy-done
  28.4 1.1 %fresh.1 = (f32[4,8,4096]{2,1,0:T(8,128)S(1)}, f32[4,8,128]{2,1,0:T(8,128)S(1)}) custom-call(bf16[4,8,4096]{2,1,0:T(8,128)(2,1)S(1)} %query.1.query_ref, bf16[16,8,2048]{2,1,0:T(8,128)(2,1)S(1)} %copy-done), custom_call_target="tpu_custom_call" | custom-call | tf_op jit(solution)/shard_map/fresh/pallas_call | solution.py:390
  29.5 1.8 %all-to-all-done.got_ref = bf16[16,8,2048]{2,1,0:T(8,128)(2,1)S(1)} async-done(((bf16[16,8,2048]{2,1,0:T(8,128)(2,1)}), bf16[16,8,2048]{2,1,0:T(8,128)(2,1)S(1)}, u32[]{:S(2)}, u32[]{:S(2)}) %all-to-all-start) | async-done | bytes 524320 | tf_op jit(solution)/shard_map/all_to_all | solution.py:357
  31.3 0.8 %cache.1 = bf16[8,16,8,256]{3,2,1,0:T(8,128)(2,1)} custom-call(bf16[16,8,2048]{2,1,0:T(8,128)(2,1)S(1)} %all-to-all-done.got_ref), custom_call_target="tpu_custom_call" | custom-call | tf_op jit(solution)/shard_map/cache/pallas_call | solution.py:402
  32.1 4.3 %collective-permute-done.6.refs_0_ = bf16[8,4224]{1,0:T(8,128)(2,1)S(1)} collective-permute-done((bf16[8,4224]{1,0:T(8,128)(2,1)S(1)}, bf16[8,4224]{1,0:T(8,128)(2,1)S(1)}, u32[]{:S(2)}, u32[]{:S(2)}) %collective-permute-start.6) | collective-permute-done | bytes 67616 | tf_op jit(solution)/shard_map/ppermute | solution.py:287
  36.4 0.0 collective-permute-done.7.refs_1_
  36.4 0.0 collective-permute-done.8.refs_2_
  36.4 1.2 %join.1 = bf16[4,8,4096]{2,1,0:T(8,128)(2,1)} custom-call(bf16[8,4224]{1,0:T(8,128)(2,1)S(1)} %collective-permute-done.6.refs_0_, bf16[8,4224]{1,0:T(8,128)(2,1)S(1)} %collective-permute-done.7.refs_1_, bf16[8,4224]{1,0:T(8,128)(2,1)S(1)} %collective-permute-done.8.refs_2_, bf16[8,4224]{1,0:T(8,128)(2,1)S(1)} %get-tuple-element.55.refs_3_, ...), custom_call_target="tpu_custom_call" | custom-call | tf_op jit(solution)/shard_map/join/pallas_call | solution.py:411
Async XLA Ops:
  2.3 15.1 %collective-permute-start.3 = (bf16[8,128,256]{2,1,0:T(8,128)(2,1)}, bf16[8,128,256]{2,1,0:T(8,128)(2,1)S(1)}, u32[]{:S(2)}, u32[]{:S(2)}) collective-permute-start(bf16[8,128,256]{2,1,0:T(8,128)(2,1)} %refs_0_), channel_id=1, source_target_pairs={{0,2},{1,3},{2,0},{3,1},{4,6},{5,7},{6,4},{7,5},{8,10},{9,11},{10,... | collective-permute-start | bytes 1572872 | tf_op jit(solution)/shard_map/ppermute | solution.py:287
  5.3 11.1 %collective-permute-start = (bf16[8,4224]{1,0:T(8,128)(2,1)}, bf16[8,4224]{1,0:T(8,128)(2,1)S(1)}, u32[]{:S(2)}, u32[]{:S(2)}) collective-permute-start(bf16[8,4224]{1,0:T(8,128)(2,1)} %get-tuple-element.32), channel_id=1, source_target_pairs={{0,8},{1,9},{2,10},{3,11},{4,12},{5,13},{6,14},{7,15},{8,0},{9,1},... | collective-permute-start | bytes 202760 | tf_op jit(solution)/shard_map/ppermute | solution.py:287
  7.9 8.5 %collective-permute-start.1 = (bf16[8,4224]{1,0:T(8,128)(2,1)}, bf16[8,4224]{1,0:T(8,128)(2,1)S(1)}, u32[]{:S(2)}, u32[]{:S(2)}) collective-permute-start(bf16[8,4224]{1,0:T(8,128)(2,1)} %get-tuple-element.33), channel_id=1, source_target_pairs={{0,12},{1,13},{2,14},{3,15},{4,8},{5,9},{6,10},{7,11},{8,4},{9,5},... | collective-permute-start | bytes 202760 | tf_op jit(solution)/shard_map/ppermute | solution.py:287
  9.2 7.1 %collective-permute-start.2 = (bf16[8,4224]{1,0:T(8,128)(2,1)}, bf16[8,4224]{1,0:T(8,128)(2,1)S(1)}, u32[]{:S(2)}, u32[]{:S(2)}) collective-permute-start(bf16[8,4224]{1,0:T(8,128)(2,1)} %get-tuple-element.34), channel_id=1, source_target_pairs={{0,4},{1,5},{2,6},{3,7},{4,0},{5,1},{6,2},{7,3},{8,12},{9,13},{10,... | collective-permute-start | bytes 202760 | tf_op jit(solution)/shard_map/ppermute | solution.py:287
  11.9 5.6 %copy-start.4 = (f32[4096]{0:T(1024)S(1)}, f32[4096]{0:T(1024)}, u32[]{:S(2)}) copy-start(f32[4096]{0:T(1024)} %param.10) | copy-start | bytes 49156
  11.9 5.6 %copy-start.5 = (bf16[8,4224]{1,0:T(8,128)(2,1)S(1)}, bf16[8,4224]{1,0:T(8,128)(2,1)}, u32[]{:S(2)}) copy-start(bf16[8,4224]{1,0:T(8,128)(2,1)} %get-tuple-element.43.refs_3_) | copy-start | bytes 202756
  11.9 19.4 %all-to-all-start = ((bf16[16,8,2048]{2,1,0:T(8,128)(2,1)}), bf16[16,8,2048]{2,1,0:T(8,128)(2,1)S(1)}, u32[]{:S(2)}, u32[]{:S(2)}) async-start(bf16[16,8,2048]{2,1,0:T(8,128)(2,1)} %key.1.fresh_ref), calls=%async_computation | async-start | bytes 1048576 | tf_op jit(solution)/shard_map/all_to_all | solution.py:357
  17.4 1.0 %copy-start.2 = (bf16[8,128,256]{2,1,0:T(8,128)(2,1)S(1)}, bf16[8,128,256]{2,1,0:T(8,128)(2,1)}, u32[]{:S(2)}) copy-start(bf16[8,128,256]{2,1,0:T(8,128)(2,1)} %refs_0_) | copy-start | bytes 1572868
  17.4 9.7 %copy-start.3 = (s32[3,8]{1,0:T(4,128)S(1)}, s32[3,8]{1,0:T(4,128)}, u32[]{:S(2)}) copy-start(s32[3,8]{1,0:T(4,128)} %coords_ref.1) | copy-start | bytes 292
  18.5 8.7 %copy-start.1 = (bf16[4,8,4096]{2,1,0:T(8,128)(2,1)S(1)}, bf16[4,8,4096]{2,1,0:T(8,128)(2,1)}, u32[]{:S(2)}) copy-start(bf16[4,8,4096]{2,1,0:T(8,128)(2,1)} %q_ref) | copy-start | bytes 786436
  18.5 1.9 %collective-permute-start.4 = (bf16[8,128,256]{2,1,0:T(8,128)(2,1)S(1)}, bf16[8,128,256]{2,1,0:T(8,128)(2,1)S(1)}, u32[]{:S(2)}, u32[]{:S(2)}) collective-permute-start(bf16[8,128,256]{2,1,0:T(8,128)(2,1)S(1)} %copy-done.2), channel_id=1, source_target_pairs={{0,1},{1,0},{2,3},{3,2},{4,5},{5,4},{6,7},{7,6},{8,9},{9,8},{10,11... | collective-permute-start | bytes 1572872 | tf_op jit(solution)/shard_map/ppermute | solution.py:287
  18.5 2.7 %collective-permute-start.5 = (bf16[8,128,256]{2,1,0:T(8,128)(2,1)S(1)}, bf16[8,128,256]{2,1,0:T(8,128)(2,1)S(1)}, u32[]{:S(2)}, u32[]{:S(2)}) collective-permute-start(bf16[8,128,256]{2,1,0:T(8,128)(2,1)S(1)} %collective-permute-done.3.refs_2_), channel_id=1, source_target_pairs={{0,1},{1,0},{2,3},{3,2},{4,5},{5,4},{6,7},{7,6},{8,9},{9,8},{10,11... | collective-permute-start | bytes 1572872 | tf_op jit(solution)/shard_map/ppermute | solution.py:287
  22.6 5.7 %copy-start = (bf16[16,8,2048]{2,1,0:T(8,128)(2,1)S(1)}, bf16[16,8,2048]{2,1,0:T(8,128)(2,1)}, u32[]{:S(2)}) copy-start(bf16[16,8,2048]{2,1,0:T(8,128)(2,1)} %key.1.fresh_ref) | copy-start | bytes 1572868
  22.6 13.8 %collective-permute-start.6 = (bf16[8,4224]{1,0:T(8,128)(2,1)S(1)}, bf16[8,4224]{1,0:T(8,128)(2,1)S(1)}, u32[]{:S(2)}, u32[]{:S(2)}) collective-permute-start(bf16[8,4224]{1,0:T(8,128)(2,1)S(1)} %get-tuple-element.52), channel_id=1, source_target_pairs={{0,8},{1,9},{2,10},{3,11},{4,12},{5,13},{6,14},{7,15},{8,0},{9,1},... | collective-permute-start | bytes 202760 | tf_op jit(solution)/shard_map/ppermute | solution.py:287
  25.5 10.9 %collective-permute-start.7 = (bf16[8,4224]{1,0:T(8,128)(2,1)S(1)}, bf16[8,4224]{1,0:T(8,128)(2,1)S(1)}, u32[]{:S(2)}, u32[]{:S(2)}) collective-permute-start(bf16[8,4224]{1,0:T(8,128)(2,1)S(1)} %get-tuple-element.53), channel_id=1, source_target_pairs={{0,12},{1,13},{2,14},{3,15},{4,8},{5,9},{6,10},{7,11},{8,4},{9,5},... | collective-permute-start | bytes 202760 | tf_op jit(solution)/shard_map/ppermute | solution.py:287
  26.9 9.6 %collective-permute-start.8 = (bf16[8,4224]{1,0:T(8,128)(2,1)S(1)}, bf16[8,4224]{1,0:T(8,128)(2,1)S(1)}, u32[]{:S(2)}, u32[]{:S(2)}) collective-permute-start(bf16[8,4224]{1,0:T(8,128)(2,1)S(1)} %get-tuple-element.54), channel_id=1, source_target_pairs={{0,4},{1,5},{2,6},{3,7},{4,0},{5,1},{6,2},{7,3},{8,12},{9,13},{10,... | collective-permute-start | bytes 202760 | tf_op jit(solution)/shard_map/ppermute | solution.py:287

commit v22 on v21

--- a/solution.py
+++ b/solution.py
@@ -288,13 +288,11 @@
 
 
 def far_first(arrays):
-    half = len(arrays) // 2
-    return [*arrays[half:], *arrays[1:half], arrays[0]]
+    return [*arrays[:0:-1], arrays[0]]
 
 
 def in_order(arrays):
-    half = len(arrays) // 2
-    return [arrays[-1], *arrays[half:-1], *arrays[:half]]
+    return [arrays[-1], *arrays[-2::-1]]
 
 
 def exchange(arrays, stride, patches):

time: 38 us -> 39.8 us (1.047)
  starting transfers between devices: 16.6 us -> 17.6 us
  waiting for transfers between devices: 9.31 us -> 10.2 us
    all_to_all x1, waiting for transfers between devices: 1.79 us -> 2.68 us  [local(): lax.all_to_all(fresh, 'patch', split_axis=0, concat_axis=0, tiled=True)]
    all_to_all x1, starting transfers between devices: 4.45 us -> 5.13 us  [local(): lax.all_to_all(fresh, 'patch', split_axis=0, concat_axis=0, tiled=True)]
  transfers between devices with their start and end apart: 10 -> 10, of which waited for: 5 -> 5; matrix products, arithmetic and copies ran while one was open for 0% -> 0% of each run, Pallas kernels for 21% -> 20%
where the time goes in v22:
time: 39.8 us; the launch traced here: 39.5 us
  starting transfers between devices  17.6 us (44%)
  Pallas kernels  10.6 us (27%)
  waiting for transfers between devices  10.2 us (26%)
  between operations  0.75 us (2%)
  local copies, waits for them, and re-layouts  0.4 us (1%)
    ppermute x9, starting transfers between devices, permuted(): lax.ppermute(array, 'patch', [(i, i ^ offset) for i in range(patches)])  12.4 us
    ppermute x9, waiting for transfers between devices, permuted(): lax.ppermute(array, 'patch', [(i, i ^ offset) for i in range(patches)])  7.53 us
    all_to_all x1, starting transfers between devices, local(): lax.all_to_all(fresh, 'patch', split_axis=0, concat_axis=0, tiled=True)  5.13 us
    all_to_all x1, waiting for transfers between devices, local(): lax.all_to_all(fresh, 'patch', split_axis=0, concat_axis=0, tiled=True)  2.68 us
    pallas_call x1, Pallas kernels, local(): kernel(key_kernel, 'key', 56, out_shape=jax.ShapeDtypeStruct((patches, to...  2.4 us
    pallas_call x1, Pallas kernels, local(): kernel(functools.partial(lay_kernel, groups), 'lay', 56, out_shape=[jax.S...  1.64 us
    pallas_call x1, Pallas kernels, local(): kernel(functools.partial(stale_kernel, groups, videos), 'stale', 32, out_...  1.52 us
    pallas_call x1, Pallas kernels, local(): kernel(query_kernel, 'query', 16, out_shape=jax.ShapeDtypeStruct(queries....  1.22 us
  transfers between devices with their start and end apart: 10, of which 5 were waited for; matrix products, arithmetic and copies ran while one was open for 0% of the time, Pallas kernels for 20%

profile of v22, /device:TPU:0, one launch (start us, length us, event | category | flops | bytes accessed | tf_op | source)
XLA Modules:
  0.0 39.5 jit_solution(17024143218752324057)
XLA Ops:
  0.6 1.6 %lay.1 = (bf16[8,4224]{1,0:T(8,128)(2,1)}, bf16[8,4224]{1,0:T(8,128)(2,1)}, bf16[8,4224]{1,0:T(8,128)(2,1)}, bf16[8,4224]{1,0:T(8,128)(2,1)}) custom-call(bf16[4,8,4096]{2,1,0:T(8,128)(2,1)} %q_ref, s32[3,8]{1,0:T(4,128)} %coords_ref.1), custom_call_target="tpu_custom_call" | custom-call | tf_op jit(solution)/shard_map/lay/pallas_call | solution.py:320
  2.3 3.0 %collective-permute-start.3 = (bf16[8,128,256]{2,1,0:T(8,128)(2,1)}, bf16[8,128,256]{2,1,0:T(8,128)(2,1)S(1)}, u32[]{:S(2)}, u32[]{:S(2)}) collective-permute-start(bf16[8,128,256]{2,1,0:T(8,128)(2,1)} %refs_0_), channel_id=1, source_target_pairs={{0,2},{1,3},{2,0},{3,1},{4,6},{5,7},{6,4},{7,5},{8,10},{9,11},{10,... | collective-permute-start | bytes 1572872 | tf_op jit(solution)/shard_map/ppermute | solution.py:287
  5.3 3.6 %collective-permute-start = (bf16[8,4224]{1,0:T(8,128)(2,1)}, bf16[8,4224]{1,0:T(8,128)(2,1)S(1)}, u32[]{:S(2)}, u32[]{:S(2)}) collective-permute-start(bf16[8,4224]{1,0:T(8,128)(2,1)} %get-tuple-element.32), channel_id=1, source_target_pairs={{0,12},{1,13},{2,14},{3,15},{4,8},{5,9},{6,10},{7,11},{8,4},{9,5},... | collective-permute-start | bytes 202760 | tf_op jit(solution)/shard_map/ppermute | solution.py:287
  8.9 0.0 collective-permute-start.1
  8.9 0.8 %collective-permute-start.2 = (bf16[8,4224]{1,0:T(8,128)(2,1)}, bf16[8,4224]{1,0:T(8,128)(2,1)S(1)}, u32[]{:S(2)}, u32[]{:S(2)}) collective-permute-start(bf16[8,4224]{1,0:T(8,128)(2,1)} %get-tuple-element.34), channel_id=1, source_target_pairs={{0,4},{1,5},{2,6},{3,7},{4,0},{5,1},{6,2},{7,3},{8,12},{9,13},{10,... | collective-permute-start | bytes 202760 | tf_op jit(solution)/shard_map/ppermute | solution.py:287
  9.7 2.4 %key.1.fresh_ref = bf16[16,8,2048]{2,1,0:T(8,128)(2,1)} custom-call(bf16[4,8,4096]{2,1,0:T(8,128)(2,1)} %k_hbm.1, bf16[4,8,4096]{2,1,0:T(8,128)(2,1)} %v_hbm.1, f32[1,4096]{1,0:T(1,128)} %bitcast.6, s32[3,8]{1,0:T(4,128)} %coords_ref.1), custom_call_target="tpu_custom_call" | custom-call | tf_op jit(solution)/shard_map/key/pallas_call | solution.py:339
  12.1 0.0 copy-start.4
  12.1 0.0 copy-start.5
  12.1 5.1 %all-to-all-start = ((bf16[16,8,2048]{2,1,0:T(8,128)(2,1)}), bf16[16,8,2048]{2,1,0:T(8,128)(2,1)S(1)}, u32[]{:S(2)}, u32[]{:S(2)}) async-start(bf16[16,8,2048]{2,1,0:T(8,128)(2,1)} %key.1.fresh_ref), calls=%async_computation | async-start | bytes 1048576 | tf_op jit(solution)/shard_map/all_to_all | solution.py:355
  17.2 0.0 collective-permute-done.refs_0_
  17.2 0.0 collective-permute-done.1.refs_1_
  17.3 0.0 collective-permute-done.2.refs_2_
  17.3 0.1 collective-permute-done.3.refs_2_
  17.4 0.0 copy-done.4
  17.4 0.0 copy-done.5
  17.4 0.0 copy-start.2
  17.4 0.0 copy-start.3
  17.4 0.7 %turn.1.query_ref = bf16[4,8,4096]{2,1,0:T(8,128)(2,1)S(1)} custom-call(f32[1,4096]{1,0:T(1,128)S(1)} %bitcast.3, bf16[8,4224]{1,0:T(8,128)(2,1)S(1)} %collective-permute-done.refs_0_, bf16[8,4224]{1,0:T(8,128)(2,1)S(1)} %collective-permute-done.1.refs_1_, bf16[8,4224]{1,0:T(8,128)(2,1)S(1)} %collective-permute-done.2.refs_2_, bf16[8,4224]{1,0:T(8,128)(2,1)S(1)} %copy-done.5), custom_call_target="tpu_custom_call" | custom-call | flops 99999997952 | tf_op jit(solution)/shard_map/turn/pallas_call | solution.py:357
  18.1 0.4 copy-done.2
  18.5 0.0 copy-start.1
  18.5 0.3 collective-permute-start.4
  18.8 0.2 collective-permute-start.5
  19.0 1.4 %collective-permute-done.4.refs_1_ = bf16[8,128,256]{2,1,0:T(8,128)(2,1)S(1)} collective-permute-done((bf16[8,128,256]{2,1,0:T(8,128)(2,1)S(1)}, bf16[8,128,256]{2,1,0:T(8,128)(2,1)S(1)}, u32[]{:S(2)}, u32[]{:S(2)}) %collective-permute-start.4) | collective-permute-done | bytes 524320 | tf_op jit(solution)/shard_map/ppermute | solution.py:287
  20.4 0.7 %collective-permute-done.5.refs_3_ = bf16[8,128,256]{2,1,0:T(8,128)(2,1)S(1)} collective-permute-done((bf16[8,128,256]{2,1,0:T(8,128)(2,1)S(1)}, bf16[8,128,256]{2,1,0:T(8,128)(2,1)S(1)}, u32[]{:S(2)}, u32[]{:S(2)}) %collective-permute-start.5) | collective-permute-done | bytes 524320 | tf_op jit(solution)/shard_map/ppermute | solution.py:287
  21.1 1.5 %stale.1 = (bf16[8,4224]{1,0:T(8,128)(2,1)S(1)}, bf16[8,4224]{1,0:T(8,128)(2,1)S(1)}, bf16[8,4224]{1,0:T(8,128)(2,1)S(1)}, bf16[8,4224]{1,0:T(8,128)(2,1)S(1)}) custom-call(bf16[4,8,4096]{2,1,0:T(8,128)(2,1)S(1)} %turn.1.query_ref, bf16[8,128,256]{2,1,0:T(8,128)(2,1)S(1)} %copy-done.2, bf16[8,128,256]{2,1,0:T(8,128)(2,1)S(1)} %collective-permute-done.4.refs_1_, ...), custom_call_target="tpu_custom_call" | custom-call | tf_op jit(solution)/shard_map/stale/pallas_call | solution.py:370
  22.6 0.0 copy-start
  22.6 3.9 %collective-permute-start.6 = (bf16[8,4224]{1,0:T(8,128)(2,1)S(1)}, bf16[8,4224]{1,0:T(8,128)(2,1)S(1)}, u32[]{:S(2)}, u32[]{:S(2)}) collective-permute-start(bf16[8,4224]{1,0:T(8,128)(2,1)S(1)} %get-tuple-element.52), channel_id=1, source_target_pairs={{0,12},{1,13},{2,14},{3,15},{4,8},{5,9},{6,10},{7,11},{8,4},{9,5},... | collective-permute-start | bytes 202760 | tf_op jit(solution)/shard_map/ppermute | solution.py:287
  26.5 0.0 collective-permute-start.7
  26.5 0.6 %collective-permute-start.8 = (bf16[8,4224]{1,0:T(8,128)(2,1)S(1)}, bf16[8,4224]{1,0:T(8,128)(2,1)S(1)}, u32[]{:S(2)}, u32[]{:S(2)}) collective-permute-start(bf16[8,4224]{1,0:T(8,128)(2,1)S(1)} %get-tuple-element.54), channel_id=1, source_target_pairs={{0,4},{1,5},{2,6},{3,7},{4,0},{5,1},{6,2},{7,3},{8,12},{9,13},{10,... | collective-permute-start | bytes 202760 | tf_op jit(solution)/shard_map/ppermute | solution.py:287
  27.2 0.0 copy-done.3
  27.2 0.0 copy-done.1
  27.2 1.2 %query.1.query_ref = bf16[4,8,4096]{2,1,0:T(8,128)(2,1)S(1)} custom-call(bf16[4,8,4096]{2,1,0:T(8,128)(2,1)S(1)} %copy-done.1, f32[1,4096]{1,0:T(1,128)S(1)} %bitcast.4, s32[3,8]{1,0:T(4,128)S(1)} %copy-done.3), custom_call_target="tpu_custom_call" | custom-call | tf_op jit(solution)/shard_map/query/pallas_call | solution.py:379
  28.4 0.0 copy-done
  28.4 1.1 %fresh.1 = (f32[4,8,4096]{2,1,0:T(8,128)S(1)}, f32[4,8,128]{2,1,0:T(8,128)S(1)}) custom-call(bf16[4,8,4096]{2,1,0:T(8,128)(2,1)S(1)} %query.1.query_ref, bf16[16,8,2048]{2,1,0:T(8,128)(2,1)S(1)} %copy-done), custom_call_target="tpu_custom_call" | custom-call | tf_op jit(solution)/shard_map/fresh/pallas_call | solution.py:388
  29.6 2.7 %all-to-all-done.got_ref = bf16[16,8,2048]{2,1,0:T(8,128)(2,1)S(1)} async-done(((bf16[16,8,2048]{2,1,0:T(8,128)(2,1)}), bf16[16,8,2048]{2,1,0:T(8,128)(2,1)S(1)}, u32[]{:S(2)}, u32[]{:S(2)}) %all-to-all-start) | async-done | bytes 524320 | tf_op jit(solution)/shard_map/all_to_all | solution.py:355
  32.2 0.8 %cache.1 = bf16[8,16,8,256]{3,2,1,0:T(8,128)(2,1)} custom-call(bf16[16,8,2048]{2,1,0:T(8,128)(2,1)S(1)} %all-to-all-done.got_ref), custom_call_target="tpu_custom_call" | custom-call | tf_op jit(solution)/shard_map/cache/pallas_call | solution.py:400
  33.1 0.0 collective-permute-done.6.refs_0_
  33.1 5.2 %collective-permute-done.7.refs_1_ = bf16[8,4224]{1,0:T(8,128)(2,1)S(1)} collective-permute-done((bf16[8,4224]{1,0:T(8,128)(2,1)S(1)}, bf16[8,4224]{1,0:T(8,128)(2,1)S(1)}, u32[]{:S(2)}, u32[]{:S(2)}) %collective-permute-start.7) | collective-permute-done | bytes 67616 | tf_op jit(solution)/shard_map/ppermute | solution.py:287
  38.3 0.0 collective-permute-done.8.refs_2_
  38.3 1.2 %join.1 = bf16[4,8,4096]{2,1,0:T(8,128)(2,1)} custom-call(bf16[8,4224]{1,0:T(8,128)(2,1)S(1)} %collective-permute-done.6.refs_0_, bf16[8,4224]{1,0:T(8,128)(2,1)S(1)} %collective-permute-done.7.refs_1_, bf16[8,4224]{1,0:T(8,128)(2,1)S(1)} %collective-permute-done.8.refs_2_, bf16[8,4224]{1,0:T(8,128)(2,1)S(1)} %get-tuple-element.55.refs_3_, ...), custom_call_target="tpu_custom_call" | custom-call | tf_op jit(solution)/shard_map/join/pallas_call | solution.py:409
Async XLA Ops:
  2.3 15.1 %collective-permute-start.3 = (bf16[8,128,256]{2,1,0:T(8,128)(2,1)}, bf16[8,128,256]{2,1,0:T(8,128)(2,1)S(1)}, u32[]{:S(2)}, u32[]{:S(2)}) collective-permute-start(bf16[8,128,256]{2,1,0:T(8,128)(2,1)} %refs_0_), channel_id=1, source_target_pairs={{0,2},{1,3},{2,0},{3,1},{4,6},{5,7},{6,4},{7,5},{8,10},{9,11},{10,... | collective-permute-start | bytes 1572872 | tf_op jit(solution)/shard_map/ppermute | solution.py:287
  5.3 12.0 %collective-permute-start = (bf16[8,4224]{1,0:T(8,128)(2,1)}, bf16[8,4224]{1,0:T(8,128)(2,1)S(1)}, u32[]{:S(2)}, u32[]{:S(2)}) collective-permute-start(bf16[8,4224]{1,0:T(8,128)(2,1)} %get-tuple-element.32), channel_id=1, source_target_pairs={{0,12},{1,13},{2,14},{3,15},{4,8},{5,9},{6,10},{7,11},{8,4},{9,5},... | collective-permute-start | bytes 202760 | tf_op jit(solution)/shard_map/ppermute | solution.py:287
  8.9 8.4 %collective-permute-start.1 = (bf16[8,4224]{1,0:T(8,128)(2,1)}, bf16[8,4224]{1,0:T(8,128)(2,1)S(1)}, u32[]{:S(2)}, u32[]{:S(2)}) collective-permute-start(bf16[8,4224]{1,0:T(8,128)(2,1)} %get-tuple-element.33), channel_id=1, source_target_pairs={{0,8},{1,9},{2,10},{3,11},{4,12},{5,13},{6,14},{7,15},{8,0},{9,1},... | collective-permute-start | bytes 202760 | tf_op jit(solution)/shard_map/ppermute | solution.py:287
  8.9 8.4 %collective-permute-start.2 = (bf16[8,4224]{1,0:T(8,128)(2,1)}, bf16[8,4224]{1,0:T(8,128)(2,1)S(1)}, u32[]{:S(2)}, u32[]{:S(2)}) collective-permute-start(bf16[8,4224]{1,0:T(8,128)(2,1)} %get-tuple-element.34), channel_id=1, source_target_pairs={{0,4},{1,5},{2,6},{3,7},{4,0},{5,1},{6,2},{7,3},{8,12},{9,13},{10,... | collective-permute-start | bytes 202760 | tf_op jit(solution)/shard_map/ppermute | solution.py:287
  12.1 5.3 %copy-start.4 = (f32[4096]{0:T(1024)S(1)}, f32[4096]{0:T(1024)}, u32[]{:S(2)}) copy-start(f32[4096]{0:T(1024)} %param.10) | copy-start | bytes 49156
  12.1 5.3 %copy-start.5 = (bf16[8,4224]{1,0:T(8,128)(2,1)S(1)}, bf16[8,4224]{1,0:T(8,128)(2,1)}, u32[]{:S(2)}) copy-start(bf16[8,4224]{1,0:T(8,128)(2,1)} %get-tuple-element.43.refs_3_) | copy-start | bytes 202756
  12.1 20.1 %all-to-all-start = ((bf16[16,8,2048]{2,1,0:T(8,128)(2,1)}), bf16[16,8,2048]{2,1,0:T(8,128)(2,1)S(1)}, u32[]{:S(2)}, u32[]{:S(2)}) async-start(bf16[16,8,2048]{2,1,0:T(8,128)(2,1)} %key.1.fresh_ref), calls=%async_computation | async-start | bytes 1048576 | tf_op jit(solution)/shard_map/all_to_all | solution.py:355
  17.4 1.0 %copy-start.2 = (bf16[8,128,256]{2,1,0:T(8,128)(2,1)S(1)}, bf16[8,128,256]{2,1,0:T(8,128)(2,1)}, u32[]{:S(2)}) copy-start(bf16[8,128,256]{2,1,0:T(8,128)(2,1)} %refs_0_) | copy-start | bytes 1572868
  17.4 9.8 %copy-start.3 = (s32[3,8]{1,0:T(4,128)S(1)}, s32[3,8]{1,0:T(4,128)}, u32[]{:S(2)}) copy-start(s32[3,8]{1,0:T(4,128)} %coords_ref.1) | copy-start | bytes 292
  18.5 8.7 %copy-start.1 = (bf16[4,8,4096]{2,1,0:T(8,128)(2,1)S(1)}, bf16[4,8,4096]{2,1,0:T(8,128)(2,1)}, u32[]{:S(2)}) copy-start(bf16[4,8,4096]{2,1,0:T(8,128)(2,1)} %q_ref) | copy-start | bytes 786436
  18.5 1.9 %collective-permute-start.4 = (bf16[8,128,256]{2,1,0:T(8,128)(2,1)S(1)}, bf16[8,128,256]{2,1,0:T(8,128)(2,1)S(1)}, u32[]{:S(2)}, u32[]{:S(2)}) collective-permute-start(bf16[8,128,256]{2,1,0:T(8,128)(2,1)S(1)} %copy-done.2), channel_id=1, source_target_pairs={{0,1},{1,0},{2,3},{3,2},{4,5},{5,4},{6,7},{7,6},{8,9},{9,8},{10,11... | collective-permute-start | bytes 1572872 | tf_op jit(solution)/shard_map/ppermute | solution.py:287
  18.8 2.4 %collective-permute-start.5 = (bf16[8,128,256]{2,1,0:T(8,128)(2,1)S(1)}, bf16[8,128,256]{2,1,0:T(8,128)(2,1)S(1)}, u32[]{:S(2)}, u32[]{:S(2)}) collective-permute-start(bf16[8,128,256]{2,1,0:T(8,128)(2,1)S(1)} %collective-permute-done.3.refs_2_), channel_id=1, source_target_pairs={{0,1},{1,0},{2,3},{3,2},{4,5},{5,4},{6,7},{7,6},{8,9},{9,8},{10,11... | collective-permute-start | bytes 1572872 | tf_op jit(solution)/shard_map/ppermute | solution.py:287
  22.6 5.8 %copy-start = (bf16[16,8,2048]{2,1,0:T(8,128)(2,1)S(1)}, bf16[16,8,2048]{2,1,0:T(8,128)(2,1)}, u32[]{:S(2)}) copy-start(bf16[16,8,2048]{2,1,0:T(8,128)(2,1)} %key.1.fresh_ref) | copy-start | bytes 1572868
  22.6 10.4 %collective-permute-start.6 = (bf16[8,4224]{1,0:T(8,128)(2,1)S(1)}, bf16[8,4224]{1,0:T(8,128)(2,1)S(1)}, u32[]{:S(2)}, u32[]{:S(2)}) collective-permute-start(bf16[8,4224]{1,0:T(8,128)(2,1)S(1)} %get-tuple-element.52), channel_id=1, source_target_pairs={{0,12},{1,13},{2,14},{3,15},{4,8},{5,9},{6,10},{7,11},{8,4},{9,5},... | collective-permute-start | bytes 202760 | tf_op jit(solution)/shard_map/ppermute | solution.py:287
  26.5 11.8 %collective-permute-start.7 = (bf16[8,4224]{1,0:T(8,128)(2,1)S(1)}, bf16[8,4224]{1,0:T(8,128)(2,1)S(1)}, u32[]{:S(2)}, u32[]{:S(2)}) collective-permute-start(bf16[8,4224]{1,0:T(8,128)(2,1)S(1)} %get-tuple-element.53), channel_id=1, source_target_pairs={{0,8},{1,9},{2,10},{3,11},{4,12},{5,13},{6,14},{7,15},{8,0},{9,1},... | collective-permute-start | bytes 202760 | tf_op jit(solution)/shard_map/ppermute | solution.py:287
  26.5 11.8 %collective-permute-start.8 = (bf16[8,4224]{1,0:T(8,128)(2,1)S(1)}, bf16[8,4224]{1,0:T(8,128)(2,1)S(1)}, u32[]{:S(2)}, u32[]{:S(2)}) collective-permute-start(bf16[8,4224]{1,0:T(8,128)(2,1)S(1)} %get-tuple-element.54), channel_id=1, source_target_pairs={{0,4},{1,5},{2,6},{3,7},{4,0},{5,1},{6,2},{7,3},{8,12},{9,13},{10,... | collective-permute-start | bytes 202760 | tf_op jit(solution)/shard_map/ppermute | solution.py:287

commit v23 on v21

--- a/solution.py
+++ b/solution.py
@@ -84,30 +84,41 @@
         write.wait()
 
 
-def key_kernel(k_hbm, v_hbm, gain_hbm, coords_hbm, out_hbm, k_ref, v_ref, gain_ref, coords_ref, done_ref, sems):
+def key_kernel(k_hbm, v_hbm, gain_hbm, coords_hbm, out_hbm, k_ref, gain_ref, coords_ref, done_ref, sems, value_sems):
     videos, tok_rows, width = k_hbm.shape
-    pairs = out_hbm.shape[2] // (2 * DH)
+    span = out_hbm.shape[2] // 2
+    pairs = span // DH
     groups = out_hbm.shape[0] // videos
-    sources, places = (coords_hbm, k_hbm, gain_hbm, v_hbm), (coords_ref, k_ref, gain_ref, v_ref)
     reads = [
         pltpu.make_async_copy(source, place, sems.at[i])
-        for i, (source, place) in enumerate(zip(sources, places))
+        for i, (source, place) in enumerate(
+            ((coords_hbm, coords_ref), (k_hbm, k_ref), (gain_hbm, gain_ref))
+        )
     ]
     for read in reads:
         read.start()
+    values = [
+        pltpu.make_async_copy(
+            v_hbm.at[target // groups, :, pl.ds(target % groups * span, span)],
+            done_ref.at[target, :, pl.ds(span, span)],
+            value_sems.at[target],
+        )
+        for target in range(videos * groups)
+    ]
+    for value in values:
+        value.start()
     for read in reads:
         read.wait()
     tables = rope_tables(lane_places(coords_ref, tok_rows))
     writes = []
     for video in range(videos):
         for head, y in normed_heads(k_ref[video].astype(F32), gain_ref, tables):
-            target, start = video * groups + head // pairs, head % pairs * 2 * DH
-            done_ref[target, :, start : start + DH] = y
-            done_ref[target, :, start + DH : start + 2 * DH] = v_ref[
-                video, :, head * DH : (head + 1) * DH
-            ]
+            start = head % pairs * DH
+            done_ref[video * groups + head // pairs, :, start : start + DH] = y
+        for value in values[video * groups : (video + 1) * groups]:
+            value.wait()
         part = pl.ds(video * groups, groups)
-        writes.append(pltpu.make_async_copy(done_ref.at[part], out_hbm.at[part], sems.at[4 + video]))
+        writes.append(pltpu.make_async_copy(done_ref.at[part], out_hbm.at[part], sems.at[3 + video]))
         writes[-1].start()
     for write in writes:
         write.wait()
@@ -167,7 +178,7 @@
             [
                 lax.dot_general(
                     query[:, pair * DH : (pair + 1) * DH],
-                    fresh[:, 2 * pair * DH : (2 * pair + 1) * DH],
+                    fresh[:, pair * DH : (pair + 1) * DH],
                     TRANSPOSED,
                     preferred_element_type=F32,
                 )
@@ -181,7 +192,7 @@
             head = t * pairs + pair
             result = inverse[here] * jnp.dot(
                 weights[here],
-                fresh[:, (2 * pair + 1) * DH : (2 * pair + 2) * DH],
+                fresh[:, span + pair * DH : span + (pair + 1) * DH],
                 preferred_element_type=F32,
             )
             logs = jnp.where(lane == head, log[here], logs)
@@ -274,11 +285,11 @@
 def cache_kernel(got_ref, out_ref, sems):
     copies = []
     for pair in range(out_ref.shape[0]):
-        lanes = pl.ds(2 * pair * DH, 2 * DH)
-        copies.append(
-            pltpu.make_async_copy(got_ref.at[:, :, lanes], out_ref.at[pair], sems.at[pair])
-        )
-        copies[-1].start()
+        for part in range(2):
+            source = got_ref.at[:, :, pl.ds((part * out_ref.shape[0] + pair) * DH, DH)]
+            target = out_ref.at[pair, :, :, pl.ds(part * DH, DH)]
+            copies.append(pltpu.make_async_copy(source, target, sems.at[part, pair]))
+            copies[-1].start()
     for copy in copies:
         copy.wait()
 
@@ -347,11 +358,11 @@
         out_specs=HBM,
         scratch_shapes=[
             pltpu.VMEM(keys.shape, BF16),
-            pltpu.VMEM(keys.shape, BF16),
             pltpu.VMEM((1, width), F32),
             pltpu.SMEM(coords.shape, jnp.int32),
             pltpu.VMEM((patches, tok_rows, 2 * pairs_here * DH), BF16),
-            pltpu.SemaphoreType.DMA((4 + videos,)),
+            pltpu.SemaphoreType.DMA((3 + videos,)),
+            pltpu.SemaphoreType.DMA((patches,)),
         ],
     )(keys, values, gains[1], coords)
     cached = lax.all_to_all(fresh, "patch", split_axis=0, concat_axis=0, tiled=True)
@@ -406,7 +417,7 @@
         out_shape=jax.ShapeDtypeStruct((pairs_here, patches, tok_rows, 2 * DH), BF16),
         in_specs=[VMEM],
         out_specs=HBM,
-        scratch_shapes=[pltpu.SemaphoreType.DMA((pairs_here,))],
+        scratch_shapes=[pltpu.SemaphoreType.DMA((2, pairs_here))],
     )(cached)
     attended = kernel(
         functools.partial(join_kernel, groups, videos),

time: 38 us -> 38.6 us (1.016)
  Pallas kernels: 10.6 us -> 11.3 us
    ppermute x9, waiting for transfers between devices: 7.52 us -> 6.79 us  [permuted(): lax.ppermute(array, 'patch', [(i, i ^ offset) for i in range(patches)])]
    all_to_all x1, waiting for transfers between devices: 1.79 us -> 2.45 us  [local(): lax.all_to_all(fresh, 'patch', split_axis=0, concat_axis=0, tiled=True)]
    pallas_call x1, Pallas kernels: 2.4 us -> 3.05 us  [local(): kernel(key_kernel, 'key', 56, out_shape=jax.ShapeDtypeStruct((patches, to...]
  transfers between devices with their start and end apart: 10 -> 10, of which waited for: 5 -> 5; matrix products, arithmetic and copies ran while one was open for 0% -> 0% of each run, Pallas kernels for 21% -> 22%
where the time goes in v23:
time: 38.6 us; the launch traced here: 38.3 us
  starting transfers between devices  16.6 us (43%)
  Pallas kernels  11.3 us (29%)
  waiting for transfers between devices  9.24 us (24%)
  between operations  0.74 us (2%)
  local copies, waits for them, and re-layouts  0.4 us (1%)
    ppermute x9, starting transfers between devices, permuted(): lax.ppermute(array, 'patch', [(i, i ^ offset) for i in range(patches)])  12.1 us
    ppermute x9, waiting for transfers between devices, permuted(): lax.ppermute(array, 'patch', [(i, i ^ offset) for i in range(patches)])  6.79 us
    all_to_all x1, starting transfers between devices, local(): lax.all_to_all(fresh, 'patch', split_axis=0, concat_axis=0, tiled=True)  4.45 us
    pallas_call x1, Pallas kernels, local(): kernel(key_kernel, 'key', 56, out_shape=jax.ShapeDtypeStruct((patches, to...  3.05 us
    all_to_all x1, waiting for transfers between devices, local(): lax.all_to_all(fresh, 'patch', split_axis=0, concat_axis=0, tiled=True)  2.45 us
    pallas_call x1, Pallas kernels, local(): kernel(functools.partial(lay_kernel, groups), 'lay', 56, out_shape=[jax.S...  1.64 us
    pallas_call x1, Pallas kernels, local(): kernel(functools.partial(stale_kernel, groups, videos), 'stale', 32, out_...  1.52 us
    pallas_call x1, Pallas kernels, local(): kernel(query_kernel, 'query', 16, out_shape=jax.ShapeDtypeStruct(queries....  1.22 us
  transfers between devices with their start and end apart: 10, of which 5 were waited for; matrix products, arithmetic and copies ran while one was open for 0% of the time, Pallas kernels for 22%

profile of v23, /device:TPU:0, one launch (start us, length us, event | category | flops | bytes accessed | tf_op | source)
XLA Modules:
  0.0 38.3 jit_solution(7593836609804120394)
XLA Ops:
  0.6 1.6 %lay.1 = (bf16[8,4224]{1,0:T(8,128)(2,1)}, bf16[8,4224]{1,0:T(8,128)(2,1)}, bf16[8,4224]{1,0:T(8,128)(2,1)}, bf16[8,4224]{1,0:T(8,128)(2,1)}) custom-call(bf16[4,8,4096]{2,1,0:T(8,128)(2,1)} %q_ref, s32[3,8]{1,0:T(4,128)} %coords_ref.1), custom_call_target="tpu_custom_call" | custom-call | tf_op jit(solution)/shard_map/lay/pallas_call | solution.py:333
  2.3 3.0 %collective-permute-start.3 = (bf16[8,128,256]{2,1,0:T(8,128)(2,1)}, bf16[8,128,256]{2,1,0:T(8,128)(2,1)S(1)}, u32[]{:S(2)}, u32[]{:S(2)}) collective-permute-start(bf16[8,128,256]{2,1,0:T(8,128)(2,1)} %refs_0_), channel_id=1, source_target_pairs={{0,2},{1,3},{2,0},{3,1},{4,6},{5,7},{6,4},{7,5},{8,10},{9,11},{10,... | collective-permute-start | bytes 1572872 | tf_op jit(solution)/shard_map/ppermute | solution.py:298
  5.3 2.6 %collective-permute-start = (bf16[8,4224]{1,0:T(8,128)(2,1)}, bf16[8,4224]{1,0:T(8,128)(2,1)S(1)}, u32[]{:S(2)}, u32[]{:S(2)}) collective-permute-start(bf16[8,4224]{1,0:T(8,128)(2,1)} %get-tuple-element.32), channel_id=1, source_target_pairs={{0,8},{1,9},{2,10},{3,11},{4,12},{5,13},{6,14},{7,15},{8,0},{9,1},... | collective-permute-start | bytes 202760 | tf_op jit(solution)/shard_map/ppermute | solution.py:298
  7.9 1.3 %collective-permute-start.1 = (bf16[8,4224]{1,0:T(8,128)(2,1)}, bf16[8,4224]{1,0:T(8,128)(2,1)S(1)}, u32[]{:S(2)}, u32[]{:S(2)}) collective-permute-start(bf16[8,4224]{1,0:T(8,128)(2,1)} %get-tuple-element.33), channel_id=1, source_target_pairs={{0,12},{1,13},{2,14},{3,15},{4,8},{5,9},{6,10},{7,11},{8,4},{9,5},... | collective-permute-start | bytes 202760 | tf_op jit(solution)/shard_map/ppermute | solution.py:298
  9.2 0.2 collective-permute-start.2
  9.4 3.1 %key.1.fresh_ref = bf16[16,8,2048]{2,1,0:T(8,128)(2,1)} custom-call(bf16[4,8,4096]{2,1,0:T(8,128)(2,1)} %k_hbm.1, bf16[4,8,4096]{2,1,0:T(8,128)(2,1)} %v_hbm.1, f32[1,4096]{1,0:T(1,128)} %bitcast.6, s32[3,8]{1,0:T(4,128)} %coords_ref.1), custom_call_target="tpu_custom_call" | custom-call | tf_op jit(solution)/shard_map/key/pallas_call | solution.py:352
  12.5 0.0 copy-start.4
  12.5 0.0 copy-start.5
  12.5 4.4 %all-to-all-start = ((bf16[16,8,2048]{2,1,0:T(8,128)(2,1)}), bf16[16,8,2048]{2,1,0:T(8,128)(2,1)S(1)}, u32[]{:S(2)}, u32[]{:S(2)}) async-start(bf16[16,8,2048]{2,1,0:T(8,128)(2,1)} %key.1.fresh_ref), calls=%async_computation | async-start | bytes 1048576 | tf_op jit(solution)/shard_map/all_to_all | solution.py:368
  17.0 0.0 collective-permute-done.refs_0_
  17.0 0.0 collective-permute-done.1.refs_1_
  17.0 0.0 collective-permute-done.2.refs_2_
  17.0 0.4 %collective-permute-done.3.refs_2_ = bf16[8,128,256]{2,1,0:T(8,128)(2,1)S(1)} collective-permute-done((bf16[8,128,256]{2,1,0:T(8,128)(2,1)}, bf16[8,128,256]{2,1,0:T(8,128)(2,1)S(1)}, u32[]{:S(2)}, u32[]{:S(2)}) %collective-permute-start.3) | collective-permute-done | bytes 524320 | tf_op jit(solution)/shard_map/ppermute | solution.py:298
  17.4 0.0 copy-done.4
  17.4 0.0 copy-done.5
  17.4 0.0 copy-start.2
  17.4 0.0 copy-start.3
  17.4 0.7 %turn.1.query_ref = bf16[4,8,4096]{2,1,0:T(8,128)(2,1)S(1)} custom-call(f32[1,4096]{1,0:T(1,128)S(1)} %bitcast.3, bf16[8,4224]{1,0:T(8,128)(2,1)S(1)} %collective-permute-done.refs_0_, bf16[8,4224]{1,0:T(8,128)(2,1)S(1)} %collective-permute-done.1.refs_1_, bf16[8,4224]{1,0:T(8,128)(2,1)S(1)} %collective-permute-done.2.refs_2_, bf16[8,4224]{1,0:T(8,128)(2,1)S(1)} %copy-done.5), custom_call_target="tpu_custom_call" | custom-call | flops 99999997952 | tf_op jit(solution)/shard_map/turn/pallas_call | solution.py:370
  18.1 0.4 copy-done.2
  18.5 0.0 copy-start.1
  18.5 0.0 collective-permute-start.4
  18.5 0.5 %collective-permute-start.5 = (bf16[8,128,256]{2,1,0:T(8,128)(2,1)S(1)}, bf16[8,128,256]{2,1,0:T(8,128)(2,1)S(1)}, u32[]{:S(2)}, u32[]{:S(2)}) collective-permute-start(bf16[8,128,256]{2,1,0:T(8,128)(2,1)S(1)} %collective-permute-done.3.refs_2_), channel_id=1, source_target_pairs={{0,1},{1,0},{2,3},{3,2},{4,5},{5,4},{6,7},{7,6},{8,9},{9,8},{10,11... | collective-permute-start | bytes 1572872 | tf_op jit(solution)/shard_map/ppermute | solution.py:298
  19.0 1.4 %collective-permute-done.4.refs_1_ = bf16[8,128,256]{2,1,0:T(8,128)(2,1)S(1)} collective-permute-done((bf16[8,128,256]{2,1,0:T(8,128)(2,1)S(1)}, bf16[8,128,256]{2,1,0:T(8,128)(2,1)S(1)}, u32[]{:S(2)}, u32[]{:S(2)}) %collective-permute-start.4) | collective-permute-done | bytes 524320 | tf_op jit(solution)/shard_map/ppermute | solution.py:298
  20.4 0.7 %collective-permute-done.5.refs_3_ = bf16[8,128,256]{2,1,0:T(8,128)(2,1)S(1)} collective-permute-done((bf16[8,128,256]{2,1,0:T(8,128)(2,1)S(1)}, bf16[8,128,256]{2,1,0:T(8,128)(2,1)S(1)}, u32[]{:S(2)}, u32[]{:S(2)}) %collective-permute-start.5) | collective-permute-done | bytes 524320 | tf_op jit(solution)/shard_map/ppermute | solution.py:298
  21.1 1.5 %stale.1 = (bf16[8,4224]{1,0:T(8,128)(2,1)S(1)}, bf16[8,4224]{1,0:T(8,128)(2,1)S(1)}, bf16[8,4224]{1,0:T(8,128)(2,1)S(1)}, bf16[8,4224]{1,0:T(8,128)(2,1)S(1)}) custom-call(bf16[4,8,4096]{2,1,0:T(8,128)(2,1)S(1)} %turn.1.query_ref, bf16[8,128,256]{2,1,0:T(8,128)(2,1)S(1)} %copy-done.2, bf16[8,128,256]{2,1,0:T(8,128)(2,1)S(1)} %collective-permute-done.4.refs_1_, ...), custom_call_target="tpu_custom_call" | custom-call | tf_op jit(solution)/shard_map/stale/pallas_call | solution.py:383
  22.6 0.0 copy-start
  22.6 2.9 %collective-permute-start.6 = (bf16[8,4224]{1,0:T(8,128)(2,1)S(1)}, bf16[8,4224]{1,0:T(8,128)(2,1)S(1)}, u32[]{:S(2)}, u32[]{:S(2)}) collective-permute-start(bf16[8,4224]{1,0:T(8,128)(2,1)S(1)} %get-tuple-element.52), channel_id=1, source_target_pairs={{0,8},{1,9},{2,10},{3,11},{4,12},{5,13},{6,14},{7,15},{8,0},{9,1},... | collective-permute-start | bytes 202760 | tf_op jit(solution)/shard_map/ppermute | solution.py:298
  25.5 1.3 %collective-permute-start.7 = (bf16[8,4224]{1,0:T(8,128)(2,1)S(1)}, bf16[8,4224]{1,0:T(8,128)(2,1)S(1)}, u32[]{:S(2)}, u32[]{:S(2)}) collective-permute-start(bf16[8,4224]{1,0:T(8,128)(2,1)S(1)} %get-tuple-element.53), channel_id=1, source_target_pairs={{0,12},{1,13},{2,14},{3,15},{4,8},{5,9},{6,10},{7,11},{8,4},{9,5},... | collective-permute-start | bytes 202760 | tf_op jit(solution)/shard_map/ppermute | solution.py:298
  26.9 0.2 collective-permute-start.8
  27.1 0.0 copy-done.3
  27.1 0.0 copy-done.1
  27.1 1.2 %query.1.query_ref = bf16[4,8,4096]{2,1,0:T(8,128)(2,1)S(1)} custom-call(bf16[4,8,4096]{2,1,0:T(8,128)(2,1)S(1)} %copy-done.1, f32[1,4096]{1,0:T(1,128)S(1)} %bitcast.4, s32[3,8]{1,0:T(4,128)S(1)} %copy-done.3), custom_call_target="tpu_custom_call" | custom-call | tf_op jit(solution)/shard_map/query/pallas_call | solution.py:392
  28.3 0.0 copy-done
  28.4 1.1 %fresh.1 = (f32[4,8,4096]{2,1,0:T(8,128)S(1)}, f32[4,8,128]{2,1,0:T(8,128)S(1)}) custom-call(bf16[4,8,4096]{2,1,0:T(8,128)(2,1)S(1)} %query.1.query_ref, bf16[16,8,2048]{2,1,0:T(8,128)(2,1)S(1)} %copy-done), custom_call_target="tpu_custom_call" | custom-call | tf_op jit(solution)/shard_map/fresh/pallas_call | solution.py:401
  29.5 2.5 %all-to-all-done.got_ref = bf16[16,8,2048]{2,1,0:T(8,128)(2,1)S(1)} async-done(((bf16[16,8,2048]{2,1,0:T(8,128)(2,1)}), bf16[16,8,2048]{2,1,0:T(8,128)(2,1)S(1)}, u32[]{:S(2)}, u32[]{:S(2)}) %all-to-all-start) | async-done | bytes 524320 | tf_op jit(solution)/shard_map/all_to_all | solution.py:368
  31.9 0.9 %cache.1 = bf16[8,16,8,256]{3,2,1,0:T(8,128)(2,1)} custom-call(bf16[16,8,2048]{2,1,0:T(8,128)(2,1)S(1)} %all-to-all-done.got_ref), custom_call_target="tpu_custom_call" | custom-call | tf_op jit(solution)/shard_map/cache/pallas_call | solution.py:413
  32.9 4.2 %collective-permute-done.6.refs_0_ = bf16[8,4224]{1,0:T(8,128)(2,1)S(1)} collective-permute-done((bf16[8,4224]{1,0:T(8,128)(2,1)S(1)}, bf16[8,4224]{1,0:T(8,128)(2,1)S(1)}, u32[]{:S(2)}, u32[]{:S(2)}) %collective-permute-start.6) | collective-permute-done | bytes 67616 | tf_op jit(solution)/shard_map/ppermute | solution.py:298
  37.1 0.0 collective-permute-done.7.refs_1_
  37.1 0.0 collective-permute-done.8.refs_2_
  37.1 1.2 %join.1 = bf16[4,8,4096]{2,1,0:T(8,128)(2,1)} custom-call(bf16[8,4224]{1,0:T(8,128)(2,1)S(1)} %collective-permute-done.6.refs_0_, bf16[8,4224]{1,0:T(8,128)(2,1)S(1)} %collective-permute-done.7.refs_1_, bf16[8,4224]{1,0:T(8,128)(2,1)S(1)} %collective-permute-done.8.refs_2_, bf16[8,4224]{1,0:T(8,128)(2,1)S(1)} %get-tuple-element.55.refs_3_, ...), custom_call_target="tpu_custom_call" | custom-call | tf_op jit(solution)/shard_map/join/pallas_call | solution.py:422
Async XLA Ops:
  2.3 15.1 %collective-permute-start.3 = (bf16[8,128,256]{2,1,0:T(8,128)(2,1)}, bf16[8,128,256]{2,1,0:T(8,128)(2,1)S(1)}, u32[]{:S(2)}, u32[]{:S(2)}) collective-permute-start(bf16[8,128,256]{2,1,0:T(8,128)(2,1)} %refs_0_), channel_id=1, source_target_pairs={{0,2},{1,3},{2,0},{3,1},{4,6},{5,7},{6,4},{7,5},{8,10},{9,11},{10,... | collective-permute-start | bytes 1572872 | tf_op jit(solution)/shard_map/ppermute | solution.py:298
  5.3 11.7 %collective-permute-start = (bf16[8,4224]{1,0:T(8,128)(2,1)}, bf16[8,4224]{1,0:T(8,128)(2,1)S(1)}, u32[]{:S(2)}, u32[]{:S(2)}) collective-permute-start(bf16[8,4224]{1,0:T(8,128)(2,1)} %get-tuple-element.32), channel_id=1, source_target_pairs={{0,8},{1,9},{2,10},{3,11},{4,12},{5,13},{6,14},{7,15},{8,0},{9,1},... | collective-permute-start | bytes 202760 | tf_op jit(solution)/shard_map/ppermute | solution.py:298
  7.9 9.1 %collective-permute-start.1 = (bf16[8,4224]{1,0:T(8,128)(2,1)}, bf16[8,4224]{1,0:T(8,128)(2,1)S(1)}, u32[]{:S(2)}, u32[]{:S(2)}) collective-permute-start(bf16[8,4224]{1,0:T(8,128)(2,1)} %get-tuple-element.33), channel_id=1, source_target_pairs={{0,12},{1,13},{2,14},{3,15},{4,8},{5,9},{6,10},{7,11},{8,4},{9,5},... | collective-permute-start | bytes 202760 | tf_op jit(solution)/shard_map/ppermute | solution.py:298
  9.2 7.8 %collective-permute-start.2 = (bf16[8,4224]{1,0:T(8,128)(2,1)}, bf16[8,4224]{1,0:T(8,128)(2,1)S(1)}, u32[]{:S(2)}, u32[]{:S(2)}) collective-permute-start(bf16[8,4224]{1,0:T(8,128)(2,1)} %get-tuple-element.34), channel_id=1, source_target_pairs={{0,4},{1,5},{2,6},{3,7},{4,0},{5,1},{6,2},{7,3},{8,12},{9,13},{10,... | collective-permute-start | bytes 202760 | tf_op jit(solution)/shard_map/ppermute | solution.py:298
  12.5 4.9 %copy-start.4 = (f32[4096]{0:T(1024)S(1)}, f32[4096]{0:T(1024)}, u32[]{:S(2)}) copy-start(f32[4096]{0:T(1024)} %param.10) | copy-start | bytes 49156
  12.5 4.9 %copy-start.5 = (bf16[8,4224]{1,0:T(8,128)(2,1)S(1)}, bf16[8,4224]{1,0:T(8,128)(2,1)}, u32[]{:S(2)}) copy-start(bf16[8,4224]{1,0:T(8,128)(2,1)} %get-tuple-element.43.refs_3_) | copy-start | bytes 202756
  12.5 19.4 %all-to-all-start = ((bf16[16,8,2048]{2,1,0:T(8,128)(2,1)}), bf16[16,8,2048]{2,1,0:T(8,128)(2,1)S(1)}, u32[]{:S(2)}, u32[]{:S(2)}) async-start(bf16[16,8,2048]{2,1,0:T(8,128)(2,1)} %key.1.fresh_ref), calls=%async_computation | async-start | bytes 1048576 | tf_op jit(solution)/shard_map/all_to_all | solution.py:368
  17.4 1.0 %copy-start.2 = (bf16[8,128,256]{2,1,0:T(8,128)(2,1)S(1)}, bf16[8,128,256]{2,1,0:T(8,128)(2,1)}, u32[]{:S(2)}) copy-start(bf16[8,128,256]{2,1,0:T(8,128)(2,1)} %refs_0_) | copy-start | bytes 1572868
  17.4 9.7 %copy-start.3 = (s32[3,8]{1,0:T(4,128)S(1)}, s32[3,8]{1,0:T(4,128)}, u32[]{:S(2)}) copy-start(s32[3,8]{1,0:T(4,128)} %coords_ref.1) | copy-start | bytes 292
  18.5 8.7 %copy-start.1 = (bf16[4,8,4096]{2,1,0:T(8,128)(2,1)S(1)}, bf16[4,8,4096]{2,1,0:T(8,128)(2,1)}, u32[]{:S(2)}) copy-start(bf16[4,8,4096]{2,1,0:T(8,128)(2,1)} %q_ref) | copy-start | bytes 786436
  18.5 1.9 %collective-permute-start.4 = (bf16[8,128,256]{2,1,0:T(8,128)(2,1)S(1)}, bf16[8,128,256]{2,1,0:T(8,128)(2,1)S(1)}, u32[]{:S(2)}, u32[]{:S(2)}) collective-permute-start(bf16[8,128,256]{2,1,0:T(8,128)(2,1)S(1)} %copy-done.2), channel_id=1, source_target_pairs={{0,1},{1,0},{2,3},{3,2},{4,5},{5,4},{6,7},{7,6},{8,9},{9,8},{10,11... | collective-permute-start | bytes 1572872 | tf_op jit(solution)/shard_map/ppermute | solution.py:298
  18.5 2.6 %collective-permute-start.5 = (bf16[8,128,256]{2,1,0:T(8,128)(2,1)S(1)}, bf16[8,128,256]{2,1,0:T(8,128)(2,1)S(1)}, u32[]{:S(2)}, u32[]{:S(2)}) collective-permute-start(bf16[8,128,256]{2,1,0:T(8,128)(2,1)S(1)} %collective-permute-done.3.refs_2_), channel_id=1, source_target_pairs={{0,1},{1,0},{2,3},{3,2},{4,5},{5,4},{6,7},{7,6},{8,9},{9,8},{10,11... | collective-permute-start | bytes 1572872 | tf_op jit(solution)/shard_map/ppermute | solution.py:298
  22.6 5.7 %copy-start = (bf16[16,8,2048]{2,1,0:T(8,128)(2,1)S(1)}, bf16[16,8,2048]{2,1,0:T(8,128)(2,1)}, u32[]{:S(2)}) copy-start(bf16[16,8,2048]{2,1,0:T(8,128)(2,1)} %key.1.fresh_ref) | copy-start | bytes 1572868
  22.6 14.4 %collective-permute-start.6 = (bf16[8,4224]{1,0:T(8,128)(2,1)S(1)}, bf16[8,4224]{1,0:T(8,128)(2,1)S(1)}, u32[]{:S(2)}, u32[]{:S(2)}) collective-permute-start(bf16[8,4224]{1,0:T(8,128)(2,1)S(1)} %get-tuple-element.52), channel_id=1, source_target_pairs={{0,8},{1,9},{2,10},{3,11},{4,12},{5,13},{6,14},{7,15},{8,0},{9,1},... | collective-permute-start | bytes 202760 | tf_op jit(solution)/shard_map/ppermute | solution.py:298
  25.5 11.6 %collective-permute-start.7 = (bf16[8,4224]{1,0:T(8,128)(2,1)S(1)}, bf16[8,4224]{1,0:T(8,128)(2,1)S(1)}, u32[]{:S(2)}, u32[]{:S(2)}) collective-permute-start(bf16[8,4224]{1,0:T(8,128)(2,1)S(1)} %get-tuple-element.53), channel_id=1, source_target_pairs={{0,12},{1,13},{2,14},{3,15},{4,8},{5,9},{6,10},{7,11},{8,4},{9,5},... | collective-permute-start | bytes 202760 | tf_op jit(solution)/shard_map/ppermute | solution.py:298
  26.9 10.2 %collective-permute-start.8 = (bf16[8,4224]{1,0:T(8,128)(2,1)S(1)}, bf16[8,4224]{1,0:T(8,128)(2,1)S(1)}, u32[]{:S(2)}, u32[]{:S(2)}) collective-permute-start(bf16[8,4224]{1,0:T(8,128)(2,1)S(1)} %get-tuple-element.54), channel_id=1, source_target_pairs={{0,4},{1,5},{2,6},{3,7},{4,0},{5,1},{6,2},{7,3},{8,12},{9,13},{10,... | collective-permute-start | bytes 202760 | tf_op jit(solution)/shard_map/ppermute | solution.py:298

commit v24 on v21

--- a/solution.py
+++ b/solution.py
@@ -66,19 +66,15 @@
     own = lax.axis_index("patch") // groups
     first = pltpu.make_async_copy(coords_hbm, coords_ref, coords_sem)
     first.start()
-    reads = [
-        pltpu.make_async_copy(q_hbm.at[own ^ s], held.at[s, :, pl.ds(0, width)], sems.at[0, s])
-        for s in range(videos)
-    ]
-    writes = [pltpu.make_async_copy(held.at[s], outs[s], sems.at[1, s]) for s in range(videos)]
-    for read in reads:
-        read.start()
+    read = pltpu.make_async_copy(q_hbm, held.at[:, :, pl.ds(0, width)], sems.at[0, 0])
+    writes = [pltpu.make_async_copy(held.at[own ^ s], outs[s], sems.at[1, s]) for s in range(videos)]
+    read.start()
     first.wait()
     place = lane_places(coords_ref, tok_rows).astype(BF16)
     for s in range(videos):
         held[s, :, width:] = place
-    for read, write in zip(reads, writes):
-        read.wait()
+    read.wait()
+    for write in writes:
         write.start()
     for write in writes:
         write.wait()

time: 38 us -> 38 us (level)
  no operation moved by 1% of the time
where the time goes in v24:
time: 38 us; the launch traced here: 37.7 us
  starting transfers between devices  16.6 us (44%)
  Pallas kernels  10.6 us (28%)
  waiting for transfers between devices  9.31 us (24%)
  between operations  0.74 us (2%)
  local copies, waits for them, and re-layouts  0.4 us (1%)
    ppermute x9, starting transfers between devices, permuted(): lax.ppermute(array, 'patch', [(i, i ^ offset) for i in range(patches)])  12.1 us
    ppermute x9, waiting for transfers between devices, permuted(): lax.ppermute(array, 'patch', [(i, i ^ offset) for i in range(patches)])  7.52 us
    all_to_all x1, starting transfers between devices, local(): lax.all_to_all(fresh, 'patch', split_axis=0, concat_axis=0, tiled=True)  4.45 us
    pallas_call x1, Pallas kernels, local(): kernel(key_kernel, 'key', 56, out_shape=jax.ShapeDtypeStruct((patches, to...  2.4 us
    all_to_all x1, waiting for transfers between devices, local(): lax.all_to_all(fresh, 'patch', split_axis=0, concat_axis=0, tiled=True)  1.79 us
    pallas_call x1, Pallas kernels, local(): kernel(functools.partial(lay_kernel, groups), 'lay', 56, out_shape=[jax.S...  1.71 us
    pallas_call x1, Pallas kernels, local(): kernel(functools.partial(stale_kernel, groups, videos), 'stale', 32, out_...  1.52 us
    pallas_call x1, Pallas kernels, local(): kernel(query_kernel, 'query', 16, out_shape=jax.ShapeDtypeStruct(queries....  1.22 us
  transfers between devices with their start and end apart: 10, of which 5 were waited for; matrix products, arithmetic and copies ran while one was open for 0% of the time, Pallas kernels for 21%

profile of v24, /device:TPU:0, one launch (start us, length us, event | category | flops | bytes accessed | tf_op | source)
XLA Modules:
  0.0 37.7 jit_solution(14717906581012254424)
XLA Ops:
  0.6 1.7 %lay.1 = (bf16[8,4224]{1,0:T(8,128)(2,1)}, bf16[8,4224]{1,0:T(8,128)(2,1)}, bf16[8,4224]{1,0:T(8,128)(2,1)}, bf16[8,4224]{1,0:T(8,128)(2,1)}) custom-call(bf16[4,8,4096]{2,1,0:T(8,128)(2,1)} %q_ref, s32[3,8]{1,0:T(4,128)} %coords_ref.1), custom_call_target="tpu_custom_call" | custom-call | tf_op jit(solution)/shard_map/lay/pallas_call | solution.py:318
  2.3 3.0 %collective-permute-start.3 = (bf16[8,128,256]{2,1,0:T(8,128)(2,1)}, bf16[8,128,256]{2,1,0:T(8,128)(2,1)S(1)}, u32[]{:S(2)}, u32[]{:S(2)}) collective-permute-start(bf16[8,128,256]{2,1,0:T(8,128)(2,1)} %refs_0_), channel_id=1, source_target_pairs={{0,2},{1,3},{2,0},{3,1},{4,6},{5,7},{6,4},{7,5},{8,10},{9,11},{10,... | collective-permute-start | bytes 1572872 | tf_op jit(solution)/shard_map/ppermute | solution.py:283
  5.4 2.6 %collective-permute-start = (bf16[8,4224]{1,0:T(8,128)(2,1)}, bf16[8,4224]{1,0:T(8,128)(2,1)S(1)}, u32[]{:S(2)}, u32[]{:S(2)}) collective-permute-start(bf16[8,4224]{1,0:T(8,128)(2,1)} %get-tuple-element.32), channel_id=1, source_target_pairs={{0,8},{1,9},{2,10},{3,11},{4,12},{5,13},{6,14},{7,15},{8,0},{9,1},... | collective-permute-start | bytes 202760 | tf_op jit(solution)/shard_map/ppermute | solution.py:283
  7.9 1.3 %collective-permute-start.1 = (bf16[8,4224]{1,0:T(8,128)(2,1)}, bf16[8,4224]{1,0:T(8,128)(2,1)S(1)}, u32[]{:S(2)}, u32[]{:S(2)}) collective-permute-start(bf16[8,4224]{1,0:T(8,128)(2,1)} %get-tuple-element.33), channel_id=1, source_target_pairs={{0,12},{1,13},{2,14},{3,15},{4,8},{5,9},{6,10},{7,11},{8,4},{9,5},... | collective-permute-start | bytes 202760 | tf_op jit(solution)/shard_map/ppermute | solution.py:283
  9.3 0.2 collective-permute-start.2
  9.5 2.4 %key.1.fresh_ref = bf16[16,8,2048]{2,1,0:T(8,128)(2,1)} custom-call(bf16[4,8,4096]{2,1,0:T(8,128)(2,1)} %k_hbm.1, bf16[4,8,4096]{2,1,0:T(8,128)(2,1)} %v_hbm.1, f32[1,4096]{1,0:T(1,128)} %bitcast.6, s32[3,8]{1,0:T(4,128)} %coords_ref.1), custom_call_target="tpu_custom_call" | custom-call | tf_op jit(solution)/shard_map/key/pallas_call | solution.py:337
  11.9 0.0 copy-start.4
  11.9 0.0 copy-start.5
  12.0 4.4 %all-to-all-start = ((bf16[16,8,2048]{2,1,0:T(8,128)(2,1)}), bf16[16,8,2048]{2,1,0:T(8,128)(2,1)S(1)}, u32[]{:S(2)}, u32[]{:S(2)}) async-start(bf16[16,8,2048]{2,1,0:T(8,128)(2,1)} %key.1.fresh_ref), calls=%async_computation | async-start | bytes 1048576 | tf_op jit(solution)/shard_map/all_to_all | solution.py:353
  16.4 0.0 collective-permute-done.refs_0_
  16.4 0.0 collective-permute-done.1.refs_1_
  16.4 0.0 collective-permute-done.2.refs_2_
  16.4 1.0 %collective-permute-done.3.refs_2_ = bf16[8,128,256]{2,1,0:T(8,128)(2,1)S(1)} collective-permute-done((bf16[8,128,256]{2,1,0:T(8,128)(2,1)}, bf16[8,128,256]{2,1,0:T(8,128)(2,1)S(1)}, u32[]{:S(2)}, u32[]{:S(2)}) %collective-permute-start.3) | collective-permute-done | bytes 524320 | tf_op jit(solution)/shard_map/ppermute | solution.py:283
  17.5 0.0 copy-done.4
  17.5 0.0 copy-done.5
  17.5 0.0 copy-start.2
  17.5 0.0 copy-start.3
  17.5 0.7 %turn.1.query_ref = bf16[4,8,4096]{2,1,0:T(8,128)(2,1)S(1)} custom-call(f32[1,4096]{1,0:T(1,128)S(1)} %bitcast.3, bf16[8,4224]{1,0:T(8,128)(2,1)S(1)} %collective-permute-done.refs_0_, bf16[8,4224]{1,0:T(8,128)(2,1)S(1)} %collective-permute-done.1.refs_1_, bf16[8,4224]{1,0:T(8,128)(2,1)S(1)} %collective-permute-done.2.refs_2_, bf16[8,4224]{1,0:T(8,128)(2,1)S(1)} %copy-done.5), custom_call_target="tpu_custom_call" | custom-call | flops 99999997952 | tf_op jit(solution)/shard_map/turn/pallas_call | solution.py:355
  18.2 0.4 copy-done.2
  18.5 0.0 copy-start.1
  18.5 0.0 collective-permute-start.4
  18.5 0.5 %collective-permute-start.5 = (bf16[8,128,256]{2,1,0:T(8,128)(2,1)S(1)}, bf16[8,128,256]{2,1,0:T(8,128)(2,1)S(1)}, u32[]{:S(2)}, u32[]{:S(2)}) collective-permute-start(bf16[8,128,256]{2,1,0:T(8,128)(2,1)S(1)} %collective-permute-done.3.refs_2_), channel_id=1, source_target_pairs={{0,1},{1,0},{2,3},{3,2},{4,5},{5,4},{6,7},{7,6},{8,9},{9,8},{10,11... | collective-permute-start | bytes 1572872 | tf_op jit(solution)/shard_map/ppermute | solution.py:283
  19.1 1.4 %collective-permute-done.4.refs_1_ = bf16[8,128,256]{2,1,0:T(8,128)(2,1)S(1)} collective-permute-done((bf16[8,128,256]{2,1,0:T(8,128)(2,1)S(1)}, bf16[8,128,256]{2,1,0:T(8,128)(2,1)S(1)}, u32[]{:S(2)}, u32[]{:S(2)}) %collective-permute-start.4) | collective-permute-done | bytes 524320 | tf_op jit(solution)/shard_map/ppermute | solution.py:283
  20.5 0.7 %collective-permute-done.5.refs_3_ = bf16[8,128,256]{2,1,0:T(8,128)(2,1)S(1)} collective-permute-done((bf16[8,128,256]{2,1,0:T(8,128)(2,1)S(1)}, bf16[8,128,256]{2,1,0:T(8,128)(2,1)S(1)}, u32[]{:S(2)}, u32[]{:S(2)}) %collective-permute-start.5) | collective-permute-done | bytes 524320 | tf_op jit(solution)/shard_map/ppermute | solution.py:283
  21.2 1.5 %stale.1 = (bf16[8,4224]{1,0:T(8,128)(2,1)S(1)}, bf16[8,4224]{1,0:T(8,128)(2,1)S(1)}, bf16[8,4224]{1,0:T(8,128)(2,1)S(1)}, bf16[8,4224]{1,0:T(8,128)(2,1)S(1)}) custom-call(bf16[4,8,4096]{2,1,0:T(8,128)(2,1)S(1)} %turn.1.query_ref, bf16[8,128,256]{2,1,0:T(8,128)(2,1)S(1)} %copy-done.2, bf16[8,128,256]{2,1,0:T(8,128)(2,1)S(1)} %collective-permute-done.4.refs_1_, ...), custom_call_target="tpu_custom_call" | custom-call | tf_op jit(solution)/shard_map/stale/pallas_call | solution.py:368
  22.7 0.0 copy-start
  22.7 2.9 %collective-permute-start.6 = (bf16[8,4224]{1,0:T(8,128)(2,1)S(1)}, bf16[8,4224]{1,0:T(8,128)(2,1)S(1)}, u32[]{:S(2)}, u32[]{:S(2)}) collective-permute-start(bf16[8,4224]{1,0:T(8,128)(2,1)S(1)} %get-tuple-element.52), channel_id=1, source_target_pairs={{0,8},{1,9},{2,10},{3,11},{4,12},{5,13},{6,14},{7,15},{8,0},{9,1},... | collective-permute-start | bytes 202760 | tf_op jit(solution)/shard_map/ppermute | solution.py:283
  25.6 1.3 %collective-permute-start.7 = (bf16[8,4224]{1,0:T(8,128)(2,1)S(1)}, bf16[8,4224]{1,0:T(8,128)(2,1)S(1)}, u32[]{:S(2)}, u32[]{:S(2)}) collective-permute-start(bf16[8,4224]{1,0:T(8,128)(2,1)S(1)} %get-tuple-element.53), channel_id=1, source_target_pairs={{0,12},{1,13},{2,14},{3,15},{4,8},{5,9},{6,10},{7,11},{8,4},{9,5},... | collective-permute-start | bytes 202760 | tf_op jit(solution)/shard_map/ppermute | solution.py:283
  27.0 0.2 collective-permute-start.8
  27.2 0.0 copy-done.3
  27.2 0.0 copy-done.1
  27.2 1.2 %query.1.query_ref = bf16[4,8,4096]{2,1,0:T(8,128)(2,1)S(1)} custom-call(bf16[4,8,4096]{2,1,0:T(8,128)(2,1)S(1)} %copy-done.1, f32[1,4096]{1,0:T(1,128)S(1)} %bitcast.4, s32[3,8]{1,0:T(4,128)S(1)} %copy-done.3), custom_call_target="tpu_custom_call" | custom-call | tf_op jit(solution)/shard_map/query/pallas_call | solution.py:377
  28.4 0.0 copy-done
  28.4 1.1 %fresh.1 = (f32[4,8,4096]{2,1,0:T(8,128)S(1)}, f32[4,8,128]{2,1,0:T(8,128)S(1)}) custom-call(bf16[4,8,4096]{2,1,0:T(8,128)(2,1)S(1)} %query.1.query_ref, bf16[16,8,2048]{2,1,0:T(8,128)(2,1)S(1)} %copy-done), custom_call_target="tpu_custom_call" | custom-call | tf_op jit(solution)/shard_map/fresh/pallas_call | solution.py:386
  29.6 1.8 %all-to-all-done.got_ref = bf16[16,8,2048]{2,1,0:T(8,128)(2,1)S(1)} async-done(((bf16[16,8,2048]{2,1,0:T(8,128)(2,1)}), bf16[16,8,2048]{2,1,0:T(8,128)(2,1)S(1)}, u32[]{:S(2)}, u32[]{:S(2)}) %all-to-all-start) | async-done | bytes 524320 | tf_op jit(solution)/shard_map/all_to_all | solution.py:353
  31.3 0.8 %cache.1 = bf16[8,16,8,256]{3,2,1,0:T(8,128)(2,1)} custom-call(bf16[16,8,2048]{2,1,0:T(8,128)(2,1)S(1)} %all-to-all-done.got_ref), custom_call_target="tpu_custom_call" | custom-call | tf_op jit(solution)/shard_map/cache/pallas_call | solution.py:398
  32.2 4.3 %collective-permute-done.6.refs_0_ = bf16[8,4224]{1,0:T(8,128)(2,1)S(1)} collective-permute-done((bf16[8,4224]{1,0:T(8,128)(2,1)S(1)}, bf16[8,4224]{1,0:T(8,128)(2,1)S(1)}, u32[]{:S(2)}, u32[]{:S(2)}) %collective-permute-start.6) | collective-permute-done | bytes 67616 | tf_op jit(solution)/shard_map/ppermute | solution.py:283
  36.5 0.0 collective-permute-done.7.refs_1_
  36.5 0.0 collective-permute-done.8.refs_2_
  36.5 1.2 %join.1 = bf16[4,8,4096]{2,1,0:T(8,128)(2,1)} custom-call(bf16[8,4224]{1,0:T(8,128)(2,1)S(1)} %collective-permute-done.6.refs_0_, bf16[8,4224]{1,0:T(8,128)(2,1)S(1)} %collective-permute-done.7.refs_1_, bf16[8,4224]{1,0:T(8,128)(2,1)S(1)} %collective-permute-done.8.refs_2_, bf16[8,4224]{1,0:T(8,128)(2,1)S(1)} %get-tuple-element.55.refs_3_, ...), custom_call_target="tpu_custom_call" | custom-call | tf_op jit(solution)/shard_map/join/pallas_call | solution.py:407
Async XLA Ops:
  2.3 15.1 %collective-permute-start.3 = (bf16[8,128,256]{2,1,0:T(8,128)(2,1)}, bf16[8,128,256]{2,1,0:T(8,128)(2,1)S(1)}, u32[]{:S(2)}, u32[]{:S(2)}) collective-permute-start(bf16[8,128,256]{2,1,0:T(8,128)(2,1)} %refs_0_), channel_id=1, source_target_pairs={{0,2},{1,3},{2,0},{3,1},{4,6},{5,7},{6,4},{7,5},{8,10},{9,11},{10,... | collective-permute-start | bytes 1572872 | tf_op jit(solution)/shard_map/ppermute | solution.py:283
  5.4 11.1 %collective-permute-start = (bf16[8,4224]{1,0:T(8,128)(2,1)}, bf16[8,4224]{1,0:T(8,128)(2,1)S(1)}, u32[]{:S(2)}, u32[]{:S(2)}) collective-permute-start(bf16[8,4224]{1,0:T(8,128)(2,1)} %get-tuple-element.32), channel_id=1, source_target_pairs={{0,8},{1,9},{2,10},{3,11},{4,12},{5,13},{6,14},{7,15},{8,0},{9,1},... | collective-permute-start | bytes 202760 | tf_op jit(solution)/shard_map/ppermute | solution.py:283
  7.9 8.5 %collective-permute-start.1 = (bf16[8,4224]{1,0:T(8,128)(2,1)}, bf16[8,4224]{1,0:T(8,128)(2,1)S(1)}, u32[]{:S(2)}, u32[]{:S(2)}) collective-permute-start(bf16[8,4224]{1,0:T(8,128)(2,1)} %get-tuple-element.33), channel_id=1, source_target_pairs={{0,12},{1,13},{2,14},{3,15},{4,8},{5,9},{6,10},{7,11},{8,4},{9,5},... | collective-permute-start | bytes 202760 | tf_op jit(solution)/shard_map/ppermute | solution.py:283
  9.3 7.1 %collective-permute-start.2 = (bf16[8,4224]{1,0:T(8,128)(2,1)}, bf16[8,4224]{1,0:T(8,128)(2,1)S(1)}, u32[]{:S(2)}, u32[]{:S(2)}) collective-permute-start(bf16[8,4224]{1,0:T(8,128)(2,1)} %get-tuple-element.34), channel_id=1, source_target_pairs={{0,4},{1,5},{2,6},{3,7},{4,0},{5,1},{6,2},{7,3},{8,12},{9,13},{10,... | collective-permute-start | bytes 202760 | tf_op jit(solution)/shard_map/ppermute | solution.py:283
  11.9 5.6 %copy-start.4 = (f32[4096]{0:T(1024)S(1)}, f32[4096]{0:T(1024)}, u32[]{:S(2)}) copy-start(f32[4096]{0:T(1024)} %param.10) | copy-start | bytes 49156
  11.9 5.6 %copy-start.5 = (bf16[8,4224]{1,0:T(8,128)(2,1)S(1)}, bf16[8,4224]{1,0:T(8,128)(2,1)}, u32[]{:S(2)}) copy-start(bf16[8,4224]{1,0:T(8,128)(2,1)} %get-tuple-element.43.refs_3_) | copy-start | bytes 202756
  12.0 19.4 %all-to-all-start = ((bf16[16,8,2048]{2,1,0:T(8,128)(2,1)}), bf16[16,8,2048]{2,1,0:T(8,128)(2,1)S(1)}, u32[]{:S(2)}, u32[]{:S(2)}) async-start(bf16[16,8,2048]{2,1,0:T(8,128)(2,1)} %key.1.fresh_ref), calls=%async_computation | async-start | bytes 1048576 | tf_op jit(solution)/shard_map/all_to_all | solution.py:353
  17.5 1.0 %copy-start.2 = (bf16[8,128,256]{2,1,0:T(8,128)(2,1)S(1)}, bf16[8,128,256]{2,1,0:T(8,128)(2,1)}, u32[]{:S(2)}) copy-start(bf16[8,128,256]{2,1,0:T(8,128)(2,1)} %refs_0_) | copy-start | bytes 1572868
  17.5 9.7 %copy-start.3 = (s32[3,8]{1,0:T(4,128)S(1)}, s32[3,8]{1,0:T(4,128)}, u32[]{:S(2)}) copy-start(s32[3,8]{1,0:T(4,128)} %coords_ref.1) | copy-start | bytes 292
  18.5 8.7 %copy-start.1 = (bf16[4,8,4096]{2,1,0:T(8,128)(2,1)S(1)}, bf16[4,8,4096]{2,1,0:T(8,128)(2,1)}, u32[]{:S(2)}) copy-start(bf16[4,8,4096]{2,1,0:T(8,128)(2,1)} %q_ref) | copy-start | bytes 786436
  18.5 1.9 %collective-permute-start.4 = (bf16[8,128,256]{2,1,0:T(8,128)(2,1)S(1)}, bf16[8,128,256]{2,1,0:T(8,128)(2,1)S(1)}, u32[]{:S(2)}, u32[]{:S(2)}) collective-permute-start(bf16[8,128,256]{2,1,0:T(8,128)(2,1)S(1)} %copy-done.2), channel_id=1, source_target_pairs={{0,1},{1,0},{2,3},{3,2},{4,5},{5,4},{6,7},{7,6},{8,9},{9,8},{10,11... | collective-permute-start | bytes 1572872 | tf_op jit(solution)/shard_map/ppermute | solution.py:283
  18.5 2.7 %collective-permute-start.5 = (bf16[8,128,256]{2,1,0:T(8,128)(2,1)S(1)}, bf16[8,128,256]{2,1,0:T(8,128)(2,1)S(1)}, u32[]{:S(2)}, u32[]{:S(2)}) collective-permute-start(bf16[8,128,256]{2,1,0:T(8,128)(2,1)S(1)} %collective-permute-done.3.refs_2_), channel_id=1, source_target_pairs={{0,1},{1,0},{2,3},{3,2},{4,5},{5,4},{6,7},{7,6},{8,9},{9,8},{10,11... | collective-permute-start | bytes 1572872 | tf_op jit(solution)/shard_map/ppermute | solution.py:283
  22.7 5.7 %copy-start = (bf16[16,8,2048]{2,1,0:T(8,128)(2,1)S(1)}, bf16[16,8,2048]{2,1,0:T(8,128)(2,1)}, u32[]{:S(2)}) copy-start(bf16[16,8,2048]{2,1,0:T(8,128)(2,1)} %key.1.fresh_ref) | copy-start | bytes 1572868
  22.7 13.8 %collective-permute-start.6 = (bf16[8,4224]{1,0:T(8,128)(2,1)S(1)}, bf16[8,4224]{1,0:T(8,128)(2,1)S(1)}, u32[]{:S(2)}, u32[]{:S(2)}) collective-permute-start(bf16[8,4224]{1,0:T(8,128)(2,1)S(1)} %get-tuple-element.52), channel_id=1, source_target_pairs={{0,8},{1,9},{2,10},{3,11},{4,12},{5,13},{6,14},{7,15},{8,0},{9,1},... | collective-permute-start | bytes 202760 | tf_op jit(solution)/shard_map/ppermute | solution.py:283
  25.6 10.9 %collective-permute-start.7 = (bf16[8,4224]{1,0:T(8,128)(2,1)S(1)}, bf16[8,4224]{1,0:T(8,128)(2,1)S(1)}, u32[]{:S(2)}, u32[]{:S(2)}) collective-permute-start(bf16[8,4224]{1,0:T(8,128)(2,1)S(1)} %get-tuple-element.53), channel_id=1, source_target_pairs={{0,12},{1,13},{2,14},{3,15},{4,8},{5,9},{6,10},{7,11},{8,4},{9,5},... | collective-permute-start | bytes 202760 | tf_op jit(solution)/shard_map/ppermute | solution.py:283
  27.0 9.6 %collective-permute-start.8 = (bf16[8,4224]{1,0:T(8,128)(2,1)S(1)}, bf16[8,4224]{1,0:T(8,128)(2,1)S(1)}, u32[]{:S(2)}, u32[]{:S(2)}) collective-permute-start(bf16[8,4224]{1,0:T(8,128)(2,1)S(1)} %get-tuple-element.54), channel_id=1, source_target_pairs={{0,4},{1,5},{2,6},{3,7},{4,0},{5,1},{6,2},{7,3},{8,12},{9,13},{10,... | collective-permute-start | bytes 202760 | tf_op jit(solution)/shard_map/ppermute | solution.py:283
